TPU v7x, 256 devices: a whole 4x4x8 slice. The times are simulated.
256 devices in a mesh: section: 32 (over z_lo, x, y), dp: 8 (over z_hi, core).
Axes of the slice: x: 4, y: 4, z: 8 (z_hi: 4, z_lo: 2; z = z_hi * 2 + z_lo), core: 2. Of those that a mesh axis runs over, the one named last changes fastest.
Arguments:
- forward_state: bfloat16 [32, 1024, 4096], P('section', 'dp'), may hold values from -6 to 6
- backward_state: bfloat16 [32, 1024, 4096], P('section', 'dp'), may hold values from -6 to 6
- saved: bfloat16 [32, 2, 1024, 4096], P('section', None, 'dp'), may hold values from -6 to 6
- fresh: bfloat16 [1024, 4096], P('dp'), may hold values from -6 to 6
- target: bfloat16 [1024, 4096], P('dp'), may hold values from -6 to 6
- forward_adapter: int32 [32], P('section'), may hold values from 0 to 3
- backward_adapter: int32 [32], P('section'), may hold values from 0 to 3
- value_projection: bfloat16 [32, 4096, 512], P('section', 'dp'), may hold values from -0.09375 to 0.09375
- output_matrix: bfloat16 [32, 512, 4096], P('section', None, 'dp'), may hold values from -0.25 to 0.25
- norm_gain_frozen: float32 [32, 4096], P('section'), may hold values from 0.1 to 1.9
- adapter_down: bfloat16 [32, 4, 4096, 64], P('section'), may hold values from -0.09375 to 0.09375
- adapter_up: bfloat16 [32, 4, 64, 512], P('section'), may hold values from -0.75 to 0.75
Outputs:
- fwd_out: bfloat16 [32, 1024, 4096], P('section', 'dp')
- bwd_out: bfloat16 [32, 1024, 4096], P('section', 'dp')
- grad_down: float32 [32, 4, 4096, 64], P('section', None, 'dp')
- grad_up: float32 [32, 4, 64, 512], P('section', None, None, 'dp')
All inputs are finite; a program needn't handle non-finite values.
Results may differ from a plain program's by a relative error of at most 0.01.
Values may be sent and summed in bfloat16 or wider, within the bound.
No kernel may reach another device: no remote copies, remote signals or barrier semaphores. Data moves between devices by JAX's collectives and lax.ppermute only.
A program may use at most 128 MiB of HBM per device.

v0:
```python
import jax
import jax.numpy as jnp
from jax import lax
from jax.sharding import PartitionSpec as P

adapter_scale = 0.5


def shifted(value, axis, by):
    count = lax.axis_size(axis)
    return lax.ppermute(value, axis, [(i, (i + by) % count) for i in range(count)])


def from_behind(value, axis, steps):
    count = lax.axis_size(axis)
    initial, last = (max(0, -steps), min(count, count - steps))
    return lax.ppermute(value, axis, [(source, source + steps) for source in range(initial, last)])


def normalize(token_rows, gain):
    whole = token_rows.astype(jnp.float32)
    factor = lax.rsqrt(jnp.mean(whole * whole, axis=-1, keepdims=True) + 1e-05)
    scaled = whole * factor
    return ((scaled * gain).astype(jnp.bfloat16), scaled, factor)


def contract_trailing(left, right):
    return lax.dot_general(
        left, right, (((1,), (1,)), ((), ())), preferred_element_type=jnp.float32
    )


def contract_leading(left, right):
    return lax.dot_general(
        left, right, (((0,), (0,)), ((), ())), preferred_element_type=jnp.float32
    )


def forward_layer(token_rows, gain, value_matrix, output_mat, down_mat, up_matrix):
    normalized_input, scaled, factor = normalize(token_rows, gain)
    lowrank_product = jnp.dot(
        normalized_input, down_mat, preferred_element_type=jnp.float32
    ).astype(jnp.bfloat16)
    value_rows = jnp.dot(
        normalized_input, value_matrix, preferred_element_type=jnp.float32
    ) + adapter_scale * jnp.dot(lowrank_product, up_matrix, preferred_element_type=jnp.float32)
    value_rows = value_rows.astype(jnp.bfloat16)
    return (
        token_rows.astype(jnp.float32)
        + jnp.dot(value_rows, output_mat, preferred_element_type=jnp.float32)
    ).astype(jnp.bfloat16)


def backward_layer(token_rows, upstream, gain, value_matrix, output_mat, down_mat, up_matrix):
    normalized_input, scaled, factor = normalize(token_rows, gain)
    lowrank_product = jnp.dot(
        normalized_input, down_mat, preferred_element_type=jnp.float32
    ).astype(jnp.bfloat16)
    gradient_values = contract_trailing(upstream, output_mat).astype(jnp.bfloat16)
    up_product = adapter_scale * contract_leading(lowrank_product, gradient_values)
    gradient_lowrank = (adapter_scale * contract_trailing(gradient_values, up_matrix)).astype(
        jnp.bfloat16
    )
    down_term = contract_leading(normalized_input, gradient_lowrank)
    d_normed = contract_trailing(gradient_values, value_matrix) + contract_trailing(
        gradient_lowrank, down_mat
    )
    d_gained = d_normed * gain
    inner = jnp.mean(d_gained * scaled, axis=-1, keepdims=True)
    d_rows = upstream.astype(jnp.float32) + factor * (d_gained - scaled * inner)
    return (d_rows.astype(jnp.bfloat16), down_term, up_product)


def body(
    forward_state,
    backward_state,
    saved,
    fresh,
    target,
    forward_adapter,
    backward_adapter,
    value_projection,
    output_matrix,
    norm_gain_frozen,
    adapter_down,
    adapter_up,
):
    value_full, output_full = (
        lax.all_gather(value_projection, "dp", axis=1, tiled=True),
        lax.all_gather(output_matrix, "dp", axis=2, tiled=True),
    )
    value_matrix = value_full[0]
    output_mat = output_full[0]
    gain = norm_gain_frozen[0]
    down_factors = adapter_down[0]
    up_factors = adapter_up[0]
    position = lax.axis_index("section")
    is_first = position == 0
    is_last = position == lax.axis_size("section") - 1
    first_out = forward_layer(
        forward_state[0],
        gain,
        value_matrix,
        output_mat,
        down_factors[forward_adapter[0]],
        up_factors[forward_adapter[0]],
    )
    d_first, down_one, up_one = backward_layer(
        saved[0, 0],
        backward_state[0],
        gain,
        value_matrix,
        output_mat,
        down_factors[backward_adapter[0]],
        up_factors[backward_adapter[0]],
    )
    passed, passed_ident = shifted((first_out, forward_adapter), "section", 1)
    returned, returned_ident = from_behind((d_first, backward_adapter), "section", -1)
    loss_grad = (first_out.astype(jnp.float32) - target.astype(jnp.float32)).astype(jnp.bfloat16)
    rows_next = jnp.where(is_first, fresh, passed)
    grad_next = jnp.where(is_last, loss_grad, returned)
    grad_ident = jnp.where(is_last, forward_adapter, returned_ident)
    saved_next = jnp.where(is_last, forward_state[0], saved[0, 1])
    second_out = forward_layer(
        rows_next,
        gain,
        value_matrix,
        output_mat,
        down_factors[passed_ident[0]],
        up_factors[passed_ident[0]],
    )
    d_second, down_two, up_two = backward_layer(
        saved_next,
        grad_next,
        gain,
        value_matrix,
        output_mat,
        down_factors[grad_ident[0]],
        up_factors[grad_ident[0]],
    )
    labels = jnp.arange(down_factors.shape[0])
    pick_first = (labels == backward_adapter[0]).astype(jnp.float32)
    pick_second = (labels == grad_ident[0]).astype(jnp.float32)
    table_down = (
        pick_first[:, None, None] * down_one[None] + pick_second[:, None, None] * down_two[None]
    )
    table_up = pick_first[:, None, None] * up_one[None] + pick_second[:, None, None] * up_two[None]
    grad_down, grad_up = (
        lax.psum_scatter(table_down[None], "dp", scatter_dimension=2, tiled=True),
        lax.psum_scatter(table_up[None], "dp", scatter_dimension=3, tiled=True),
    )
    return (second_out[None], d_second[None], grad_down, grad_up)


def solution(mesh):
    return jax.shard_map(
        body,
        mesh=mesh,
        in_specs=(
            P("section", "dp", None),
            P("section", "dp", None),
            P("section", None, "dp", None),
            P("dp", None),
            P("dp", None),
            P("section"),
            P("section"),
            P("section", "dp", None),
            P("section", None, "dp"),
            P("section", None),
            P("section", None, None, None),
            P("section", None, None, None),
        ),
        out_specs=(
            P("section", "dp", None),
            P("section", "dp", None),
            P("section", None, "dp", None),
            P("section", None, None, "dp"),
        ),
        check_vma=False,
    )
```

profile of v0, /device:TPU:30, one launch (start us, length us, event | category | flops | bytes accessed | tf_op | source)
XLA Modules:
  0.0 280.2 jit_solution(14027299934044613583)
XLA Ops:
  7.2 0.7 all-gather.5.cloned.1.call-update
  8.0 0.7 all-gather.3.cloned.1.call-update
  8.7 0.0 reduce-scatter.7.cloned.1.call-start
  8.7 2.7 collective-permute-start.3
  12.7 0.5 compare_convert_fusion.1
  13.2 1.5 fusion.41
  14.8 3.8 %collective-permute-done.3 = s32[1]{0:T(128)} collective-permute-done((s32[1]{0:T(128)}, s32[1]{0:T(128)}, u32[]{:S(2)}, u32[]{:S(2)}) %collective-permute-start.3) | collective-permute-done | bytes 36 | tf_op jit(solution)/shard_map/ppermute | solution.py:17
  19.2 0.5 compare_convert_fusion
  19.7 45.8 %all-gather.5.cloned.1.call-done = bf16[1,512,4096]{2,1,0:T(8,128)(2,1)} async-done(((bf16[1,512,512]{2,1,0:T(8,128)(2,1)}), bf16[1,512,4096]{2,1,0:T(8,128)(2,1)}) %all-gather.5.cloned.1.call-update) | async-done | bytes 4194320 | tf_op jit(solution)/shard_map/all_gather | solution.py:90
  65.6 3.7 %fusion.53 = bf16[128,512]{1,0:T(8,128)(2,1)S(1)} fusion(bf16[1,512,4096]{2,1,0:T(8,128)(2,1)} %all-gather.5.cloned.1.call-done, bf16[1,128,4096]{2,1,0:T(8,128)(2,1)S(1)} %copy-done.4), kind=kOutput, calls=%fused_computation.66 | convolution fusion | flops 536936448 | bytes 5373952 | tf_op jit(solution)/shard_map/dot_general | solution.py:28
  69.3 1.0 fusion.65
  70.3 48.4 %all-gather.3.cloned.1.call-done = bf16[1,4096,512]{2,1,0:T(8,128)(2,1)} async-done(((bf16[1,512,512]{2,1,0:T(8,128)(2,1)}), bf16[1,4096,512]{2,1,0:T(8,128)(2,1)}) %all-gather.3.cloned.1.call-update) | async-done | bytes 4194320 | tf_op jit(solution)/shard_map/all_gather | solution.py:89
  118.7 3.8 %fusion.13 = f32[128,4096]{1,0:T(8,128)S(1)} fusion(bf16[128,512]{1,0:T(8,128)(2,1)S(1)} %fusion.53, bf16[1,4096,512]{2,1,0:T(8,128)(2,1)} %all-gather.3.cloned.1.call-done), kind=kOutput, calls=%fused_computation.17 | convolution fusion | flops 536870912 | bytes 6422528 | tf_op jit(solution)/shard_map/dot_general | solution.py:28
  122.6 1.3 fusion.34
  123.9 1.6 fusion.39
  125.5 2.6 collective-permute-start.2
  128.1 0.5 add_rsqrt_fusion.3
  128.7 0.6 add_rsqrt_fusion
  129.2 2.6 convolution_multiply_fusion.3
  131.8 1.9 convolution_multiply_fusion.1
  133.8 2.8 %fusion.75 = f32[4096,64]{0,1:T(8,128)} fusion(bf16[128,64]{0,1:T(8,128)(2,1)S(1)} %copy-done.9, f32[128]{0:T(128)S(1)} %copy-done.13, f32[4096]{0:T(1024)S(1)} %bitcast.169, bf16[1,2,128,4096]{3,2,1,0:T(8,128)(2,1)} %param.14), kind=kOutput, calls=%fused_computation.84 | convolution fusion | flops 69206016 | bytes 2130432 | tf_op jit(solution)/shard_map/dot_general | solution.py:34
  136.6 20.6 %collective-permute-done.2 = bf16[128,4096]{1,0:T(8,128)(2,1)} collective-permute-done((bf16[128,4096]{1,0:T(8,128)(2,1)}, bf16[128,4096]{1,0:T(8,128)(2,1)}, u32[]{:S(2)}, u32[]{:S(2)}) %collective-permute-start.2) | collective-permute-done | bytes 1048608 | tf_op jit(solution)/shard_map/ppermute | solution.py:17
  157.2 7.8 %fusion.68 = (bf16[128,4096]{1,0:T(8,128)(2,1)}, bf16[128,4096]{1,0:T(8,128)(2,1)}) fusion(bf16[128,4096]{1,0:T(8,128)(2,1)} %collective-permute-done.2, bf16[128,4096]{1,0:T(8,128)(2,1)} %param.16, pred[]{:T(512)} %eq.27, bf16[1,512,4096]{2,1,0:T(8,128)(2,1)} %all-gather.5.cloned.1.call-done, f32[128,512]{1,0:T(8,128)S(1)} %convolution_multiply_fusion.1, ...), kind=kOutput, calls=%fused_computation.81 | convolution fusion | flops 1080164352 | bytes 13910529 | tf_op jit(solution)/shard_map/dot_general | solution.py:50
  165.1 4.0 %fusion.56 = bf16[128,512]{1,0:T(8,128)(2,1)S(1)} fusion(bf16[128,4096]{1,0:T(8,128)(2,1)} %get-tuple-element.11, bf16[1,512,4096]{2,1,0:T(8,128)(2,1)} %all-gather.5.cloned.1.call-done), kind=kOutput, calls=%fused_computation.67 | convolution fusion | flops 536936448 | bytes 5373952 | tf_op jit(solution)/shard_map/dot_general | solution.py:28
  169.1 1.0 fusion.66
  170.2 2.7 convolution_multiply_fusion.2
  172.8 1.8 multiply_add_fusion.1
  174.7 2.3 copy.16
  177.0 2.7 reshape.157
  179.7 0.0 reduce-scatter.5.cloned.1.call-start
  179.8 0.5 fusion.77
  180.3 0.7 copy-done.3
  181.0 2.6 multiply_add_fusion
  183.6 0.1 collective-permute-start.1
  183.7 3.8 %collective-permute-done.1 = s32[1]{0:T(128)} collective-permute-done((s32[1]{0:T(128)}, s32[1]{0:T(128)}, u32[]{:S(2)}, u32[]{:S(2)}) %collective-permute-start.1) | collective-permute-done | bytes 36 | tf_op jit(solution)/shard_map/ppermute | solution.py:11
  189.3 4.5 %collective-permute-start = (bf16[128,4096]{1,0:T(8,128)(2,1)}, bf16[128,4096]{1,0:T(8,128)(2,1)}, u32[]{:S(2)}, u32[]{:S(2)}) collective-permute-start(bf16[128,4096]{1,0:T(8,128)(2,1)} %get-tuple-element.12), channel_id=1, source_target_pairs={{0,8},{8,16},{16,24},{24,32},{32,40},{40,48},{48,56},{56,64},{64,7... | collective-permute-start | bytes 3145736 | tf_op jit(solution)/shard_map/ppermute | solution.py:11
  193.8 3.7 %fusion.11 = f32[128,4096]{1,0:T(8,128)S(1)} fusion(bf16[128,512]{1,0:T(8,128)(2,1)S(1)} %fusion.56, bf16[1,4096,512]{2,1,0:T(8,128)(2,1)} %all-gather.3.cloned.1.call-done), kind=kOutput, calls=%fused_computation.15 | convolution fusion | flops 536870912 | bytes 6422528 | tf_op jit(solution)/shard_map/dot_general | solution.py:28
  197.5 0.8 fusion.28
  198.3 0.4 copy-done.1
  198.7 1.6 fusion.79
  200.4 15.9 %reduce-scatter.7.cloned.1.call-done = f32[64,256]{1,0:T(8,128)} async-done(((f32[512,256]{1,0:T(8,128)}), f32[64,256]{1,0:T(8,128)}) %reduce-scatter.7.cloned.1.call-update) | async-done | bytes 65552
  216.3 0.9 reshape.158
  217.2 0.8 copy.17
  218.0 1.3 collective-permute-done
  219.3 1.7 fusion.44
  221.0 1.5 convolution_multiply_fusion
  222.5 5.9 %fusion.4 = bf16[1,128,4096]{2,1,0:T(8,128)(2,1)} fusion(bf16[1,512,4096]{2,1,0:T(8,128)(2,1)} %all-gather.5.cloned.1.call-done, bf16[128,4096]{1,0:T(8,128)(2,1)S(1)} %get-tuple-element.7, f32[128,512]{1,0:T(8,128)S(1)} %convolution_multiply_fusion, bf16[1,4096,512]{2,1,0:T(8,128)(2,1)} %all-gather.3.cloned.1.call-done, f32[4096]{0:T(1024)S(1)} %bitcast.175, ...), kind=kOutput, calls=%fused_computation.8 | convolution fusion | flops 1077542912 | bytes 10764800 | tf_op jit(solution)/shard_map/dot_general | solution.py:50
  228.4 45.2 %reduce-scatter.5.cloned.1.call-done = f32[1,4,512,64]{2,3,1,0:T(8,128)} async-done(((f32[1,4,4096,64]{2,3,1,0:T(8,128)}), f32[1,4,512,64]{2,3,1,0:T(8,128)}) %reduce-scatter.5.cloned.1.call-update) | async-done | bytes 524304 | tf_op jit(solution)/shard_map/reduce_scatter | solution.py:149
  (40 shorter events, 0.2 us)
Async XLA Ops:
  7.2 115.4 %copy-start = (bf16[1,4,4096,64]{2,3,1,0:T(8,128)(2,1)S(1)}, bf16[1,4,4096,64]{2,3,1,0:T(8,128)(2,1)}, u32[]{:S(2)}) copy-start(bf16[1,4,4096,64]{2,3,1,0:T(8,128)(2,1)} %param.22) | copy-start | bytes 6291460
  7.2 58.4 %copy-start.4 = (bf16[1,128,4096]{2,1,0:T(8,128)(2,1)S(1)}, bf16[1,128,4096]{2,1,0:T(8,128)(2,1)}, u32[]{:S(2)}) copy-start(bf16[1,128,4096]{2,1,0:T(8,128)(2,1)} %param.13) | copy-start | bytes 3145732
  7.2 58.4 %all-gather.5.cloned.1.call-start = ((), (), s32[]{:S(2)}) async-start(), calls=%async_computation.3 | async-start | bytes 4718592 | tf_op jit(solution)/shard_map/all_gather | solution.py:90
  7.9 110.8 %all-gather.3.cloned.1.call-start = ((), (), s32[]{:S(2)}) async-start(), calls=%async_computation.2 | async-start | bytes 4718592 | tf_op jit(solution)/shard_map/all_gather | solution.py:89
  8.7 207.6 %reduce-scatter.7.cloned.1.call-start = ((), (), s32[]{:S(2)}) async-start(), calls=%async_computation.5 | async-start | bytes 589824
  8.7 9.9 %collective-permute-start.3 = (s32[1]{0:T(128)}, s32[1]{0:T(128)}, u32[]{:S(2)}, u32[]{:S(2)}) collective-permute-start(s32[1]{0:T(128)} %param.18), channel_id=1, source_target_pairs={{8,0},{16,8},{24,16},{32,24},{40,32},{48,40},{56,48},{64,56},{72,6... | collective-permute-start | bytes 20 | tf_op jit(solution)/shard_map/ppermute | solution.py:17
  14.8 114.5 %copy-start.12 = (f32[128]{0:T(128)}, f32[128]{0:T(128)S(1)}, u32[]{:S(2)}) copy-start(f32[128]{0:T(128)S(1)} %add_rsqrt_fusion.1) | copy-start | bytes 1540
  70.3 52.2 %copy-start.8 = (bf16[128,64]{0,1:T(8,128)(2,1)}, bf16[128,64]{0,1:T(8,128)(2,1)S(1)}, u32[]{:S(2)}) copy-start(bf16[128,64]{0,1:T(8,128)(2,1)S(1)} %fusion.65) | copy-start | bytes 49156
  70.3 52.2 %copy-start.7 = (f32[1,4096]{1,0:T(1,128)S(1)}, f32[1,4096]{1,0:T(1,128)}, u32[]{:S(2)}) copy-start(f32[1,4096]{1,0:T(1,128)} %param.21) | copy-start | bytes 49156
  118.7 3.8 %copy-start.2 = (bf16[1,2,128,4096]{3,2,1,0:T(8,128)(2,1)S(1)}, bf16[1,2,128,4096]{3,2,1,0:T(8,128)(2,1)}, u32[]{:S(2)}) copy-start(bf16[1,2,128,4096]{3,2,1,0:T(8,128)(2,1)} %param.14) | copy-start | bytes 6291460
  118.7 3.9 %copy-start.6 = (bf16[1,128,4096]{2,1,0:T(8,128)(2,1)S(1)}, bf16[1,128,4096]{2,1,0:T(8,128)(2,1)}, u32[]{:S(2)}) copy-start(bf16[1,128,4096]{2,1,0:T(8,128)(2,1)} %param.12) | copy-start | bytes 3145732
  122.6 1.3 copy-start.5
  125.5 31.7 %collective-permute-start.2 = (bf16[128,4096]{1,0:T(8,128)(2,1)}, bf16[128,4096]{1,0:T(8,128)(2,1)}, u32[]{:S(2)}, u32[]{:S(2)}) collective-permute-start(bf16[128,4096]{1,0:T(8,128)(2,1)} %fusion.39), channel_id=1, source_target_pairs={{8,0},{16,8},{24,16},{32,24},{40,32},{48,40},{56,48},{64,56},{72,6... | collective-permute-start | bytes 3145736 | tf_op jit(solution)/shard_map/ppermute | solution.py:17
  131.8 2.0 copy-start.9
  131.8 2.0 copy-start.13
  131.8 25.4 %copy-start.16 = (f32[128]{0:T(128)S(1)}, f32[128]{0:T(128)}, u32[]{:S(2)}) copy-start(f32[128]{0:T(128)} %add_rsqrt_fusion.3) | copy-start | bytes 1540
  165.0 5.1 %copy-start.11 = (f32[128]{0:T(128)S(1)}, f32[128]{0:T(128)}, u32[]{:S(2)}) copy-start(f32[128]{0:T(128)} %add_rsqrt_fusion) | copy-start | bytes 1540
  170.1 2.7 copy-start.10
  170.1 2.7 copy-start.14
  170.1 2.7 copy-start.15
  179.7 93.9 %reduce-scatter.5.cloned.1.call-start = ((), (), s32[]{:S(2)}) async-start(), calls=%async_computation.4 | async-start | bytes 4718592 | tf_op jit(solution)/shard_map/reduce_scatter | solution.py:149
  179.8 1.2 copy-start.3
  183.6 3.9 %collective-permute-start.1 = (s32[1]{0:T(128)}, s32[1]{0:T(128)}, u32[]{:S(2)}, u32[]{:S(2)}) collective-permute-start(s32[1]{0:T(128)} %param.17), channel_id=1, source_target_pairs={{0,8},{8,16},{16,24},{24,32},{32,40},{40,48},{48,56},{56,64},{64,7... | collective-permute-start | bytes 20 | tf_op jit(solution)/shard_map/ppermute | solution.py:11
  189.3 29.9 %collective-permute-start = (bf16[128,4096]{1,0:T(8,128)(2,1)}, bf16[128,4096]{1,0:T(8,128)(2,1)}, u32[]{:S(2)}, u32[]{:S(2)}) collective-permute-start(bf16[128,4096]{1,0:T(8,128)(2,1)} %get-tuple-element.12), channel_id=1, source_target_pairs={{0,8},{8,16},{16,24},{24,32},{32,40},{40,48},{48,56},{56,64},{64,7... | collective-permute-start | bytes 3145736 | tf_op jit(solution)/shard_map/ppermute | solution.py:11
  197.5 1.2 copy-start.1
Sparse Core Ops, SparseCore 0:
  9.9 55.6 all-gather.4
  67.4 51.2 all-gather.2
  179.8 36.3 reduce-scatter.6
  219.4 54.1 reduce-scatter.4
where the time goes:
time: 285 us; the launch traced here: 280 us
  waiting for transfers between devices  186 us (65%)
  matrix products  45 us (16%)
  between operations  17.8 us (6%)
  other arithmetic  13.1 us (5%)
  starting transfers between devices  10 us (4%)
  local copies, waits for them, and re-layouts  7.94 us (3%)
    all_gather x1, waiting for transfers between devices, body(): lax.all_gather(value_projection, 'dp', axis=1, tiled=True)  48.4 us
    all_gather x1, waiting for transfers between devices, body(): lax.all_gather(output_matrix, 'dp', axis=2, tiled=True)  45.8 us
    reduce_scatter x1, waiting for transfers between devices, body(): lax.psum_scatter(table_down[None], 'dp', scatter_dimension=2, tiled=True)  45.2 us
    ppermute x2, waiting for transfers between devices, from_behind(): lax.ppermute(value, axis, [(source, source + steps) for source in range(i...  24.4 us
    dot_general x8, matrix products, contract_trailing(): lax.dot_general(left, right, (((1,), (1,)), ((), ())), preferred_element_...  19.3 us
    unnamed x5, waiting for transfers between devices  17.3 us
    dot_general x2, matrix products, forward_layer(): jnp.dot(value_rows, output_mat, preferred_element_type=jnp.float32)  13.7 us
    dot_general x4, matrix products, contract_leading(): lax.dot_general(left, right, (((0,), (0,)), ((), ())), preferred_element_...  8.59 us
  transfers between devices with their start and end apart: 8, of which 8 were waited for; matrix products, arithmetic and copies ran while one was open for 13% of the time, Pallas kernels for 0%

commit v1 on v0

v1 whole, which is shorter than its diff:
```python
import jax
import jax.numpy as jnp
from jax import lax
from jax.experimental import pallas as pl
from jax.experimental.pallas import tpu as pltpu
from jax.sharding import PartitionSpec as P

SCALE = 0.5
EPS = 1e-05
BF = jnp.bfloat16
F32 = jnp.float32
ROWS = 128
WIDTH = 4096
VALUES = 512
PART = 512
RANK = 64
ADAPTERS = 4
PACK = PART + 128
VMEM = 40 * 1024 * 1024


def dot(left, right, dims=((1,), (0,))):
    return lax.dot_general(left, right, (dims, ((), ())), preferred_element_type=F32)


def dot_t(left, right):
    return dot(left, right, ((1,), (1,)))


def t_dot(left, right):
    return dot(left, right, ((0,), (0,)))


def call(kernel, scalars, ins, outs, flops, scratch=()):
    specs, arrays = [], []
    for item in ins:
        array, block, index = item if isinstance(item, tuple) else (item, None, None)
        arrays.append(array)
        if block is None:
            zeros = (0,) * array.ndim
            specs.append(pl.BlockSpec(array.shape, lambda i, *s, z=zeros: z))
        else:
            specs.append(pl.BlockSpec(block, index))
    out_specs = [pl.BlockSpec(o.shape, lambda i, *s, z=(0,) * len(o.shape): z) for o in outs]
    size = sum(a.size * a.dtype.itemsize for a in arrays)
    return pl.pallas_call(
        kernel,
        out_shape=outs,
        grid_spec=pltpu.PrefetchScalarGridSpec(
            num_scalar_prefetch=len(scalars),
            grid=(1,),
            in_specs=specs,
            out_specs=out_specs,
            scratch_shapes=list(scratch),
        ),
        compiler_params=pltpu.CompilerParams(vmem_limit_bytes=VMEM),
        cost_estimate=pl.CostEstimate(flops=flops, bytes_accessed=size, transcendentals=0),
    )(*scalars, *arrays)


def shape(dims, dtype):
    return jax.ShapeDtypeStruct(dims, dtype)


def factor_of(rows):
    return lax.rsqrt(jnp.sum(rows * rows, axis=-1, keepdims=True) * (1.0 / WIDTH) + EPS)


def columns(index):
    return pl.ds(pl.multiple_of(index * PART, PART), PART)


def prepare_kernel(ident, rows, gain, down, normed, factor, low):
    for top in range(0, ROWS, 32):
        part = slice(top, top + 32)
        whole = rows[part, :].astype(F32)
        scale = factor_of(whole)
        normed[part, :] = (whole * scale * gain[...]).astype(BF)
        factor[part, :] = jnp.broadcast_to(scale, (32, 128))
    low[...] = dot_t(normed[...], down[0]).astype(BF)


def down_of(down):
    return (down, (1, RANK, WIDTH), lambda i, ident, *s: (ident[0], 0, 0))


def up_of(up):
    return (up, (1, RANK, VALUES), lambda i, ident, *s: (ident[0], 0, 0))


def prepare(rows, gain, down, ident):
    return call(
        prepare_kernel,
        (ident,),
        [rows, gain, down_of(down)],
        [shape((ROWS, WIDTH), BF), shape((ROWS, 128), F32), shape((ROWS, RANK), BF)],
        2 * ROWS * WIDTH * RANK,
    )


def pack_gradients(where, low, normed, d_values, d_low, mine, other):
    up_term = SCALE * t_dot(low, d_values)
    chip, core = where[0] // 2, where[0] % 2
    for ahead in range(4):
        target = lax.rem(chip + ahead, 4)
        pair = up_term[:, 0:128]
        for k in range(1, 4):
            pair = jnp.where(target == k, up_term[:, 128 * k : 128 * (k + 1)], pair)
        pair = pair.astype(BF)
        for ref, c in ((mine, core), (other, 1 - core)):
            ref[ahead, :, :PART] = t_dot(d_low, normed[:, columns(2 * target + c)]).astype(BF)
            ref[ahead, :, PART:] = pair


PACKED = [shape((4, RANK, PACK), BF), shape((4, RANK, PACK), BF)]


def values_kernel(ident, where, grad, low, normed, up, *refs):
    blocks, (d_values, d_low, mine, other) = refs[:8], refs[8:]
    total = jnp.zeros((ROWS, VALUES), F32)
    for i in range(8):
        total += dot_t(grad[:, columns(where[i])], blocks[i][...])
    values = total.astype(BF)
    lowered = (SCALE * dot_t(values, up[0])).astype(BF)
    d_values[...] = values
    d_low[...] = lowered
    pack_gradients(where, low[...], normed, values, lowered, mine, other)


def first_values(ident, where, grad, low, normed, up, blocks):
    return call(
        values_kernel,
        (ident, where),
        [grad, low, normed, up_of(up), *blocks],
        [shape((ROWS, VALUES), BF), shape((ROWS, RANK), BF), *PACKED],
        2 * ROWS * WIDTH * (VALUES + RANK),
    )


def group_kernel(
    first, ident, where, grad, rows, normed, gain, down, factor, d_values, d_low,
    one, two, inner_in, sum_in, part, inner, total,
):
    scale = factor[:, :1]
    inner_sum = inner_in[...]
    value_sum = sum_in[...]
    for i, block in ((0, one), (1, two)):
        span = columns(where[first + i])
        gained = (
            dot_t(d_values[...], block[...]) + dot(d_low[...], down[0, :, span])
        ) * gain[:, span]
        pre = rows[:, span].astype(F32) * scale
        part[:, i * PART : (i + 1) * PART] = (
            grad[:, span].astype(F32) + scale * gained
        ).astype(BF)
        inner_sum += jnp.sum(gained * pre, axis=-1, keepdims=True)
        value_sum += dot(normed[:, span], block[...])
    if first == 6:
        inner_sum = inner_sum * (scale * scale * (1.0 / WIDTH))
    inner[...] = inner_sum
    total[...] = value_sum


def group(first, ident, where, grad, rows, normed, gain, down, factor, d_values, d_low, pair, inner, total):
    def kernel(*refs):
        group_kernel(first, *refs)

    return call(
        kernel,
        (ident, where),
        [grad, rows, normed, gain, down_of(down), factor, d_values, d_low, *pair, inner, total],
        [shape((ROWS, 2 * PART), BF), shape((ROWS, 128), F32), shape((ROWS, VALUES), F32)],
        8 * ROWS * PART * VALUES,
    )


def output_kernel(ident, where, total, low, up, rows, *refs):
    blocks, out = refs[:8], refs[8]
    values = (total[...] + SCALE * dot(low[...], up[0])).astype(BF)
    for i in range(8):
        span = columns(where[i])
        out[:, span] = (rows[:, span].astype(F32) + dot(values, blocks[i][...])).astype(BF)


def output(ident, where, total, low, up, rows, blocks):
    return call(
        output_kernel,
        (ident, where),
        [total, low, up_of(up), rows, *blocks],
        [shape((ROWS, WIDTH), BF)],
        2 * ROWS * WIDTH * VALUES,
    )[0]


def second_kernel(
    ident, where, p0, p1, p2, p3, mean, behind, out, target, low, normed, up, *refs
):
    blocks, (grad, d_values, d_low, mine, other) = refs[:8], refs[8:]
    last = where[9] == 1
    factor = mean[:, :1]
    parts = (p0, p1, p2, p3)
    total = jnp.zeros((ROWS, VALUES), F32)
    for i in range(8):
        span = columns(where[i])
        piece = parts[i // 2][:, (i % 2) * PART : (i % 2 + 1) * PART].astype(F32)
        relayed = piece - factor * behind[:, span].astype(F32)
        loss = out[:, span].astype(F32) - target[:, span].astype(F32)
        chosen = jnp.where(last, loss, relayed).astype(BF)
        grad[:, span] = chosen
        total += dot_t(chosen, blocks[i][...])
    values = total.astype(BF)
    lowered = (SCALE * dot_t(values, up[0])).astype(BF)
    d_values[...] = values
    d_low[...] = lowered
    pack_gradients(where, low[...], normed, values, lowered, mine, other)


def second_values(ident, where, parts, mean, behind, out, target, low, normed, up, blocks):
    return call(
        second_kernel,
        (ident, where),
        [*parts, mean, behind, out, target, low, normed, up_of(up), *blocks],
        [shape((ROWS, WIDTH), BF), shape((ROWS, VALUES), BF), shape((ROWS, RANK), BF), *PACKED],
        2 * ROWS * WIDTH * (VALUES + RANK),
    )


def input_kernel(ident, where, grad, rows, gain, down, factor, d_values, d_low, *refs):
    blocks, out, kept = refs[:8], refs[8], refs[9]
    scale = factor[:, :1]
    inner = jnp.zeros((ROWS, 1), F32)
    for i in range(8):
        span = columns(where[i])
        gained = (
            dot_t(d_values[...], blocks[i][...]) + dot(d_low[...], down[0, :, span])
        ) * gain[:, span]
        kept[i] = gained
        pre = rows[:, span].astype(F32) * scale
        inner += jnp.sum(gained * pre, axis=-1, keepdims=True)
    inner = inner * (1.0 / WIDTH)
    for i in range(8):
        span = columns(where[i])
        pre = rows[:, span].astype(F32) * scale
        out[:, span] = (
            grad[:, span].astype(F32) + scale * (kept[i] - pre * inner)
        ).astype(BF)


def input_gradient(ident, where, grad, rows, gain, down, factor, d_values, d_low, blocks):
    return call(
        input_kernel,
        (ident, where),
        [grad, rows, gain, down_of(down), factor, d_values, d_low, *blocks],
        [shape((ROWS, WIDTH), BF)],
        2 * ROWS * WIDTH * (VALUES + RANK),
        [pltpu.VMEM((8, ROWS, PART), F32)],
    )[0]


def forward_kernel(ident, where, fresh, passed, gain, down, up, *refs):
    value_blocks, out_blocks, out, rows, normed = refs[:8], refs[8:16], refs[16], refs[17], refs[18]
    first = where[8] == 1
    for top in range(0, ROWS, 32):
        part = slice(top, top + 32)
        whole = jnp.where(first, fresh[part, :], passed[part, :]).astype(F32)
        rows[part, :] = whole.astype(BF)
        normed[part, :] = (whole * factor_of(whole) * gain[...]).astype(BF)
    low = dot_t(normed[...], down[0]).astype(BF)
    total = SCALE * dot(low, up[0])
    for i in range(8):
        total += dot(normed[:, columns(where[i])], value_blocks[i][...])
    values = total.astype(BF)
    for i in range(8):
        span = columns(where[i])
        out[:, span] = (
            rows[:, span].astype(F32) + dot(values, out_blocks[i][...])
        ).astype(BF)


def forward(ident, where, fresh, passed, gain, down, up, value_blocks, out_blocks):
    return call(
        forward_kernel,
        (ident, where),
        [fresh, passed, gain, down_of(down), up_of(up), *value_blocks, *out_blocks],
        [shape((ROWS, WIDTH), BF)],
        4 * ROWS * WIDTH * VALUES,
        [pltpu.VMEM((ROWS, WIDTH), BF), pltpu.VMEM((ROWS, WIDTH), BF)],
    )[0]


def pair_sum_kernel(mine, other, own, one, two, three):
    for ahead, ref in enumerate((own, one, two, three)):
        total = mine[ahead].astype(F32) + other[ahead].astype(F32)
        ref[...] = total.astype(ref.dtype)


def spread(mine, other):
    received = lax.ppermute(other, "dp", CORE)
    block = (RANK, PACK)
    own, one, two, three = call(
        pair_sum_kernel, (), [mine, received],
        [shape(block, F32), shape(block, BF), shape(block, BF), shape(block, BF)], 0,
    )
    return (
        own,
        lax.ppermute(one, "dp", chips(1)),
        lax.ppermute(two, "dp", chips(2)),
        lax.ppermute(three, "dp", chips(3)),
    )


def tables_kernel(ident, other_ident, where, *refs):
    terms, (down, up) = refs[:8], refs[8:]
    core = where[0] % 2
    sums = []
    for tick in range(2):
        total = terms[4 * tick][...]
        for k in range(1, 4):
            total += terms[4 * tick + k][...].astype(F32)
        sums.append(total)
    for label in range(ADAPTERS):
        one = jnp.where(ident[0] == label, 1.0, 0.0)
        two = jnp.where(other_ident[0] == label, 1.0, 0.0)
        total = one * sums[0] + two * sums[1]
        down[label] = total[:, :PART]
        up[label] = jnp.where(core == 0, total[:, PART : PART + 64], total[:, PART + 64 :])


def tables(ident, other_ident, where, terms):
    return call(
        tables_kernel,
        (ident, other_ident, where),
        list(terms),
        [shape((ADAPTERS, RANK, PART), F32), shape((ADAPTERS, RANK, 64), F32)],
        0,
    )


CORE = [(i, i ^ 1) for i in range(8)]


def chips(by):
    return [(i, ((i // 2 + by) % 4) * 2 + i % 2) for i in range(8)]


def split_ring(sign):
    return [(i, ((i // 2 + (sign if i % 2 == 0 else -sign)) % 4) * 2 + i % 2) for i in range(8)]


def gather_blocks(own, gate=None):
    sent = own if gate is None else lax.optimization_barrier((own, gate))[0]
    sibling = lax.ppermute(own, "dp", CORE)
    near = lax.ppermute(sent, "dp", split_ring(1))
    away = lax.ppermute(sent, "dp", split_ring(-1))
    far = lax.ppermute(near, "dp", split_ring(1))
    return (
        own, sibling,
        near, lax.ppermute(near, "dp", CORE),
        away, lax.ppermute(away, "dp", CORE),
        far, lax.ppermute(far, "dp", CORE),
    )


def block_index():
    place = lax.axis_index("dp")
    chip, core = place // 2, place % 2
    other = 1 - core
    step = jnp.where(core == 0, 1, -1)
    block = lambda k, c: 2 * (k % 4) + c
    return [
        block(chip, core), block(chip, other),
        block(chip - step + 4, core), block(chip + step + 4, other),
        block(chip + step + 4, core), block(chip - step + 4, other),
        block(chip + 2, core), block(chip + 2, other),
    ]


def body(
    forward_state, backward_state, saved, fresh, target, forward_adapter, backward_adapter,
    value_projection, output_matrix, norm_gain_frozen, adapter_down, adapter_up,
):
    count = lax.axis_size("section")
    ahead = [(i, (i + 1) % count) for i in range(count)]
    before = [(i, i - 1) for i in range(1, count)]
    position = lax.axis_index("section")
    is_last = position == count - 1
    where = jnp.stack(
        [v.astype(jnp.int32) for v in (*block_index(), position == 0, is_last)]
    )
    gain = norm_gain_frozen
    down = jnp.swapaxes(adapter_down[0], 1, 2)
    up = adapter_up[0]
    rows_f, grad_b, rows_b = forward_state[0], backward_state[0], saved[0, 0]

    outs = gather_blocks(output_matrix[0])
    vals = gather_blocks(value_projection[0], outs[2])
    behind = lax.ppermute(rows_b, "section", before)
    passed_ident = lax.ppermute(forward_adapter, "section", ahead)
    returned_ident = lax.ppermute(backward_adapter, "section", before)
    grad_ident = jnp.where(is_last, forward_adapter, returned_ident)
    rows_n = jnp.where(is_last, rows_f, saved[0, 1])

    normed_f, _, low_f = prepare(rows_f, gain, down, forward_adapter)
    normed_b, factor_b, low_b = prepare(rows_b, gain, down, backward_adapter)
    normed_n, factor_n, low_n = prepare(rows_n, gain, down, grad_ident)

    d_values, d_low, mine, other = first_values(
        backward_adapter, where, grad_b, low_b, normed_b, up, outs
    )
    first_terms = spread(mine, other)

    inner = jnp.zeros((ROWS, 128), F32)
    total = jnp.zeros((ROWS, VALUES), F32)
    parts = []
    for first in range(0, 8, 2):
        part, inner, total = group(
            first, backward_adapter, where, grad_b, rows_b, normed_f, gain, down, factor_b,
            d_values, d_low, vals[first : first + 2], inner, total,
        )
        parts.append(lax.ppermute(part, "section", before))
    mean = lax.ppermute(inner, "section", before)

    first_out = output(forward_adapter, where, total, low_f, up, rows_f, outs)
    passed = lax.ppermute(first_out, "section", ahead)

    grad_n, d_values, d_low, mine, other = second_values(
        grad_ident, where, parts, mean, behind, first_out, target, low_n, normed_n, up, outs
    )
    second_terms = spread(mine, other)
    bwd_out = input_gradient(
        grad_ident, where, grad_n, rows_n, gain, down, factor_n, d_values, d_low, vals
    )
    fwd_out = forward(passed_ident, where, fresh, passed, gain, down, up, vals, outs)
    down_table, up_table = tables(
        backward_adapter, grad_ident, where, (*first_terms, *second_terms)
    )
    return (
        fwd_out[None], bwd_out[None], jnp.swapaxes(down_table, 1, 2)[None], up_table[None]
    )


def solution(mesh):
    return jax.shard_map(
        body,
        mesh=mesh,
        in_specs=(
            P("section", "dp", None),
            P("section", "dp", None),
            P("section", None, "dp", None),
            P("dp", None),
            P("dp", None),
            P("section"),
            P("section"),
            P("section", "dp", None),
            P("section", None, "dp"),
            P("section", None),
            P("section", None, None, None),
            P("section", None, None, None),
        ),
        out_specs=(
            P("section", "dp", None),
            P("section", "dp", None),
            P("section", None, "dp", None),
            P("section", None, None, "dp"),
        ),
        check_vma=False,
    )
```

time: 285 us -> 187 us (0.66)
  waiting for transfers between devices: 186 us -> 77.9 us
  starting transfers between devices: 10 us -> 60.4 us
  matrix products: 45 us -> 0 us
  Pallas kernels: 0 us -> 35.4 us
  between operations: 17.8 us -> 3.05 us
  other arithmetic: 13.1 us -> 0.11 us
    all_gather x2 -> x0, waiting for transfers between devices: 94.2 us -> none  [the longest x1 48.4 us: body(): lax.all_gather(value_projection, 'dp', axis=1, tiled=True)]
    ppermute x4 -> x31, starting transfers between devices: 9.87 us -> 60.4 us  [the longest x2 14 us: gather_blocks(): near = lax.ppermute(sent, 'dp', split_ring(1))]
    ppermute x4 -> x31, waiting for transfers between devices: 29.5 us -> 77.9 us  [the longest x2 33 us: gather_blocks(): near = lax.ppermute(sent, 'dp', split_ring(1))]
    reduce_scatter x1 -> x0, waiting for transfers between devices: 45.2 us -> none  [body(): lax.psum_scatter(table_down[None], 'dp', scatter_dimension=2, tiled=True)]
    dot_general x16 -> x0, matrix products: 45 us -> none  [the longest x8 19.3 us: contract_trailing(): lax.dot_general(left, right, (((1,), (1,)), ((), ())), preferred_element_...]
    pallas_call x0 -> x15, Pallas kernels: none -> 35.4 us  [call(): pl.pallas_call(kernel, out_shape=outs, grid_spec=pltpu.PrefetchScalarGrid...]
    unnamed x5 -> x0, waiting for transfers between devices: 17.3 us -> none
    add x2 -> x0, other arithmetic: 4.45 us -> none  [the longest x1 2.61 us: body(): pick_first[:, None, None] * down_one[None]]
  transfers between devices with their start and end apart: 8 -> 31, of which waited for: 8 -> 11; matrix products, arithmetic and copies ran while one was open for 13% -> 1% of each run, Pallas kernels for 0% -> 15%
where the time goes in v1:
time: 187 us; the launch traced here: 184 us
  waiting for transfers between devices  77.9 us (42%)
  starting transfers between devices  60.4 us (32%)
  Pallas kernels  35.4 us (19%)
  local copies, waits for them, and re-layouts  6.75 us (4%)
  between operations  3.05 us (2%)
    pallas_call x15, Pallas kernels, call(): pl.pallas_call(kernel, out_shape=outs, grid_spec=pltpu.PrefetchScalarGrid...  35.4 us
    ppermute x2, waiting for transfers between devices, gather_blocks(): near = lax.ppermute(sent, 'dp', split_ring(1))  33 us
    ppermute x2, waiting for transfers between devices, gather_blocks(): far = lax.ppermute(near, 'dp', split_ring(1))  15.7 us
    ppermute x2, starting transfers between devices, gather_blocks(): near = lax.ppermute(sent, 'dp', split_ring(1))  14 us
    ppermute x2, waiting for transfers between devices, spread(): lax.ppermute(one, 'dp', chips(1))  9.61 us
    ppermute x4, starting transfers between devices, body(): parts.append(lax.ppermute(part, 'section', before))  8.83 us
    ppermute x1, waiting for transfers between devices, body(): returned_ident = lax.ppermute(backward_adapter, 'section', before)  8.29 us
    ppermute x2, starting transfers between devices, spread(): lax.ppermute(two, 'dp', chips(2))  7.16 us
  transfers between devices with their start and end apart: 31, of which 11 were waited for; matrix products, arithmetic and copies ran while one was open for 1% of the time, Pallas kernels for 15%

profile of v1, /device:TPU:30, one launch (start us, length us, event | category | flops | bytes accessed | tf_op | source)
XLA Modules:
  0.0 183.7 jit_solution(2083418786289996517)
XLA Ops:
  0.7 3.3 %collective-permute-start.2 = (bf16[512,512]{1,0:T(8,128)(2,1)}, bf16[512,512]{1,0:T(8,128)(2,1)S(1)}, u32[]{:S(2)}, u32[]{:S(2)}) collective-permute-start(bf16[512,512]{1,0:T(8,128)(2,1)} %bitcast.45), channel_id=1, source_target_pairs={{0,2},{1,7},{2,4},{3,1},{4,6},{5,3},{6,0},{7,5},{8,10},{9,15},{10,... | collective-permute-start | bytes 1572872 | tf_op jit(solution)/shard_map/ppermute | solution.py:353
  4.0 3.1 %collective-permute-start.4 = (bf16[512,512]{1,0:T(8,128)(2,1)}, bf16[512,512]{1,0:T(8,128)(2,1)S(1)}, u32[]{:S(2)}, u32[]{:S(2)}) collective-permute-start(bf16[512,512]{1,0:T(8,128)(2,1)} %bitcast.46), channel_id=1, source_target_pairs={{0,6},{1,3},{2,0},{3,5},{4,2},{5,7},{6,4},{7,1},{8,14},{9,11},{10,... | collective-permute-start | bytes 1572872 | tf_op jit(solution)/shard_map/ppermute | solution.py:354
  7.1 13.4 %collective-permute-done.2.refs_2_.refs_10_ = bf16[512,512]{1,0:T(8,128)(2,1)S(1)} collective-permute-done((bf16[512,512]{1,0:T(8,128)(2,1)}, bf16[512,512]{1,0:T(8,128)(2,1)S(1)}, u32[]{:S(2)}, u32[]{:S(2)}) %collective-permute-start.2) | collective-permute-done | bytes 524320 | tf_op jit(solution)/shard_map/ppermute | solution.py:353
  20.6 10.7 %collective-permute-start.8 = (bf16[512,512]{1,0:T(8,128)(2,1)}, bf16[512,512]{1,0:T(8,128)(2,1)}, u32[]{:S(2)}, u32[]{:S(2)}) collective-permute-start(bf16[512,512]{1,0:T(8,128)(2,1)} %bitcast.52), channel_id=1, source_target_pairs={{0,2},{1,7},{2,4},{3,1},{4,6},{5,3},{6,0},{7,5},{8,10},{9,15},{10,... | collective-permute-start | bytes 1572872 | tf_op jit(solution)/shard_map/ppermute | solution.py:353
  31.3 4.5 %collective-permute-start.6 = (bf16[512,512]{1,0:T(8,128)(2,1)S(1)}, bf16[512,512]{1,0:T(8,128)(2,1)S(1)}, u32[]{:S(2)}, u32[]{:S(2)}) collective-permute-start(bf16[512,512]{1,0:T(8,128)(2,1)S(1)} %collective-permute-done.2.refs_2_.refs_10_), channel_id=1, source_target_pairs={{0,2},{1,7},{2,4},{3,1},{4,6},{5,3},{6,0},{7,5},{8,10},{9,15},{10,... | collective-permute-start | bytes 1572872 | tf_op jit(solution)/shard_map/ppermute | solution.py:355
  35.9 0.8 copy-done.8
  37.2 19.6 %collective-permute-done.8.refs_10_.refs_2_ = bf16[512,512]{1,0:T(8,128)(2,1)} collective-permute-done((bf16[512,512]{1,0:T(8,128)(2,1)}, bf16[512,512]{1,0:T(8,128)(2,1)}, u32[]{:S(2)}, u32[]{:S(2)}) %collective-permute-start.8) | collective-permute-done | bytes 524320 | tf_op jit(solution)/shard_map/ppermute | solution.py:353
  56.7 1.9 %collective-permute-start.9 = (bf16[512,512]{1,0:T(8,128)(2,1)}, bf16[512,512]{1,0:T(8,128)(2,1)}, u32[]{:S(2)}, u32[]{:S(2)}) collective-permute-start(bf16[512,512]{1,0:T(8,128)(2,1)} %collective-permute-done.8.refs_10_.refs_2_), channel_id=1, source_target_pairs={{0,2},{1,7},{2,4},{3,1},{4,6},{5,3},{6,0},{7,5},{8,10},{9,15},{10,... | collective-permute-start | bytes 1572872 | tf_op jit(solution)/shard_map/ppermute | solution.py:355
  58.7 13.7 %collective-permute-done.6.refs_6_.refs_14_ = bf16[512,512]{1,0:T(8,128)(2,1)S(1)} collective-permute-done((bf16[512,512]{1,0:T(8,128)(2,1)S(1)}, bf16[512,512]{1,0:T(8,128)(2,1)S(1)}, u32[]{:S(2)}, u32[]{:S(2)}) %collective-permute-start.6) | collective-permute-done | bytes 524320 | tf_op jit(solution)/shard_map/ppermute | solution.py:355
  72.4 1.5 slice_bitcast_fusion.rows.refs_3_
  73.9 0.8 copy-done.14
  74.7 2.6 %collective-permute-start.22 = (bf16[128,4096]{1,0:T(8,128)(2,1)S(1)}, bf16[128,4096]{1,0:T(8,128)(2,1)}, u32[]{:S(2)}, u32[]{:S(2)}) collective-permute-start(bf16[128,4096]{1,0:T(8,128)(2,1)S(1)} %slice_bitcast_fusion.rows.refs_3_), channel_id=1, source_target_pairs={{8,0},{16,8},{24,16},{32,24},{40,32},{48,40},{56,48},{64,56},{72,6... | collective-permute-start | bytes 3145736 | tf_op jit(solution)/shard_map/ppermute | solution.py:397
  77.5 0.8 copy-done.12
  78.7 2.1 %collective-permute-done.9.refs_10_.refs_6_ = bf16[512,512]{1,0:T(8,128)(2,1)} collective-permute-done((bf16[512,512]{1,0:T(8,128)(2,1)}, bf16[512,512]{1,0:T(8,128)(2,1)}, u32[]{:S(2)}, u32[]{:S(2)}) %collective-permute-start.9) | collective-permute-done | bytes 524320 | tf_op jit(solution)/shard_map/ppermute | solution.py:355
  80.8 0.8 copy-done.16
  81.6 0.5 collective-permute-start.10
  83.5 0.7 shard_map.148
  84.7 1.2 shard_map.147
  86.5 0.9 copy-done.19
  87.4 2.5 %shard_map.149 = (bf16[128,512]{1,0:T(8,128)(2,1)S(1)}, bf16[128,64]{1,0:T(8,128)(2,1)S(1)}, bf16[4,64,640]{2,1,0:T(8,128)(2,1)S(1)}, bf16[4,64,640]{2,1,0:T(8,128)(2,1)S(1)}) custom-call(s32[1]{0:T(128)S(6)} %copy.17.ident.refs_0_, s32[10]{0:T(128)S(1)} %stack.51.where.refs_1_, bf16[128,4096]{1,0:T(8,128)(2,1)S(1)} %bitcast.38, ...), custom_call_target="tpu_custom_call" | custom-call | flops 603979776 | bytes 6569984 | tf_op jit(solution)/shard_map/pallas_call | solution.py:46
  90.0 2.3 %shard_map.150 = (bf16[128,1024]{1,0:T(8,128)(2,1)S(1)}, f32[128,128]{1,0:T(8,128)S(1)}, f32[128,512]{1,0:T(8,128)S(1)}) custom-call(s32[1]{0:T(128)S(6)} %copy.17.ident.refs_0_, s32[10]{0:T(128)S(1)} %stack.51.where.refs_1_, bf16[128,4096]{1,0:T(8,128)(2,1)S(1)} %bitcast.39, bf16[128,4096]{1,0:T(8,128)(2,1)S(1)} %slice_bitcast_fusion.rows.refs_3_, ...), custom_call_target="tpu_custom_call" | custom-call | flops 268435456 | bytes 6848512 | tf_op jit(solution)/shard_map/pallas_call | solution.py:46
  92.4 2.5 %shard_map.151 = (bf16[128,1024]{1,0:T(8,128)(2,1)S(1)}, f32[128,128]{1,0:T(8,128)S(1)}, f32[128,512]{1,0:T(8,128)S(1)}) custom-call(s32[1]{0:T(128)S(6)} %copy.17.ident.refs_0_, s32[10]{0:T(128)S(1)} %stack.51.where.refs_1_, bf16[128,4096]{1,0:T(8,128)(2,1)S(1)} %bitcast.40, bf16[128,4096]{1,0:T(8,128)(2,1)S(1)} %slice_bitcast_fusion.rows.refs_3_, ...), custom_call_target="tpu_custom_call" | custom-call | flops 268435456 | bytes 6848512 | tf_op jit(solution)/shard_map/pallas_call | solution.py:46
  94.9 2.5 %shard_map.152 = (bf16[128,1024]{1,0:T(8,128)(2,1)S(1)}, f32[128,128]{1,0:T(8,128)S(1)}, f32[128,512]{1,0:T(8,128)S(1)}) custom-call(s32[1]{0:T(128)S(6)} %copy.17.ident.refs_0_, s32[10]{0:T(128)S(1)} %stack.51.where.refs_1_, bf16[128,4096]{1,0:T(8,128)(2,1)S(1)} %bitcast.41, bf16[128,4096]{1,0:T(8,128)(2,1)S(1)} %slice_bitcast_fusion.rows.refs_3_, ...), custom_call_target="tpu_custom_call" | custom-call | flops 268435456 | bytes 6848512 | tf_op jit(solution)/shard_map/pallas_call | solution.py:46
  97.4 2.6 %collective-permute-start.19 = (bf16[128,1024]{1,0:T(8,128)(2,1)S(1)}, bf16[128,1024]{1,0:T(8,128)(2,1)S(1)}, u32[]{:S(2)}, u32[]{:S(2)}) collective-permute-start(bf16[128,1024]{1,0:T(8,128)(2,1)S(1)} %get-tuple-element.61), channel_id=1, source_target_pairs={{8,0},{16,8},{24,16},{32,24},{40,32},{48,40},{56,48},{64,56},{72,6... | collective-permute-start | bytes 786440 | tf_op jit(solution)/shard_map/ppermute | solution.py:420
  100.0 2.4 %collective-permute-start.18 = (bf16[128,1024]{1,0:T(8,128)(2,1)S(1)}, bf16[128,1024]{1,0:T(8,128)(2,1)S(1)}, u32[]{:S(2)}, u32[]{:S(2)}) collective-permute-start(bf16[128,1024]{1,0:T(8,128)(2,1)S(1)} %get-tuple-element.60), channel_id=1, source_target_pairs={{8,0},{16,8},{24,16},{32,24},{40,32},{48,40},{56,48},{64,56},{72,6... | collective-permute-start | bytes 786440 | tf_op jit(solution)/shard_map/ppermute | solution.py:420
  102.4 2.8 %collective-permute-start.16 = (s32[1]{0:T(128)}, s32[1]{0:T(128)}, u32[]{:S(2)}, u32[]{:S(2)}) collective-permute-start(s32[1]{0:T(128)} %param.18), channel_id=1, source_target_pairs={{8,0},{16,8},{24,16},{32,24},{40,32},{48,40},{56,48},{64,56},{72,6... | collective-permute-start | bytes 20 | tf_op jit(solution)/shard_map/ppermute | solution.py:399
  105.4 2.5 %shard_map.153 = (bf16[128,1024]{1,0:T(8,128)(2,1)S(1)}, f32[128,128]{1,0:T(8,128)S(1)}, f32[128,512]{1,0:T(8,128)S(1)}) custom-call(s32[1]{0:T(128)S(6)} %copy.17.ident.refs_0_, s32[10]{0:T(128)S(1)} %stack.51.where.refs_1_, bf16[128,4096]{1,0:T(8,128)(2,1)S(1)} %bitcast.42, bf16[128,4096]{1,0:T(8,128)(2,1)S(1)} %slice_bitcast_fusion.rows.refs_3_, ...), custom_call_target="tpu_custom_call" | custom-call | flops 268435456 | bytes 6848512 | tf_op jit(solution)/shard_map/pallas_call | solution.py:46
  107.9 1.4 shard_map.154.out
  109.3 8.3 %collective-permute-done.16 = s32[1]{0:T(128)} collective-permute-done((s32[1]{0:T(128)}, s32[1]{0:T(128)}, u32[]{:S(2)}, u32[]{:S(2)}) %collective-permute-start.16) | collective-permute-done | bytes 36 | tf_op jit(solution)/shard_map/ppermute | solution.py:399
  117.6 1.9 %collective-permute-start.17 = (bf16[128,1024]{1,0:T(8,128)(2,1)S(1)}, bf16[128,1024]{1,0:T(8,128)(2,1)S(1)}, u32[]{:S(2)}, u32[]{:S(2)}) collective-permute-start(bf16[128,1024]{1,0:T(8,128)(2,1)S(1)} %get-tuple-element.59), channel_id=1, source_target_pairs={{8,0},{16,8},{24,16},{32,24},{40,32},{48,40},{56,48},{64,56},{72,6... | collective-permute-start | bytes 786440 | tf_op jit(solution)/shard_map/ppermute | solution.py:420
  119.5 1.9 %collective-permute-start.21 = (f32[128,128]{1,0:T(8,128)S(1)}, f32[128,128]{1,0:T(8,128)S(1)}, u32[]{:S(2)}, u32[]{:S(2)}) collective-permute-start(f32[128,128]{1,0:T(8,128)S(1)} %get-tuple-element.63), channel_id=1, source_target_pairs={{8,0},{16,8},{24,16},{32,24},{40,32},{48,40},{56,48},{64,56},{72,6... | collective-permute-start | bytes 196616 | tf_op jit(solution)/shard_map/ppermute | solution.py:421
  121.4 1.9 %collective-permute-start.20 = (bf16[128,1024]{1,0:T(8,128)(2,1)S(1)}, bf16[128,1024]{1,0:T(8,128)(2,1)S(1)}, u32[]{:S(2)}, u32[]{:S(2)}) collective-permute-start(bf16[128,1024]{1,0:T(8,128)(2,1)S(1)} %get-tuple-element.62), channel_id=1, source_target_pairs={{8,0},{16,8},{24,16},{32,24},{40,32},{48,40},{56,48},{64,56},{72,6... | collective-permute-start | bytes 786440 | tf_op jit(solution)/shard_map/ppermute | solution.py:420
  123.4 6.3 %collective-permute-start.15 = (bf16[128,4096]{1,0:T(8,128)(2,1)S(1)}, bf16[128,4096]{1,0:T(8,128)(2,1)S(1)}, u32[]{:S(2)}, u32[]{:S(2)}) collective-permute-start(bf16[128,4096]{1,0:T(8,128)(2,1)S(1)} %shard_map.154.out), channel_id=1, source_target_pairs={{0,8},{8,16},{16,24},{24,32},{32,40},{40,48},{48,56},{56,64},{64,7... | collective-permute-start | bytes 3145736 | tf_op jit(solution)/shard_map/ppermute | solution.py:424
  130.5 0.7 shard_map.156
  131.2 1.7 collective-permute-done.17.p0
  132.9 1.4 collective-permute-done.21.mean
  134.3 3.6 %collective-permute-done.20.p3 = bf16[128,1024]{1,0:T(8,128)(2,1)S(1)} collective-permute-done((bf16[128,1024]{1,0:T(8,128)(2,1)S(1)}, bf16[128,1024]{1,0:T(8,128)(2,1)S(1)}, u32[]{:S(2)}, u32[]{:S(2)}) %collective-permute-start.20) | collective-permute-done | bytes 262176 | tf_op jit(solution)/shard_map/ppermute | solution.py:420
  137.9 3.9 %shard_map.157 = (bf16[128,4096]{1,0:T(8,128)(2,1)S(1)}, bf16[128,512]{1,0:T(8,128)(2,1)S(1)}, bf16[128,64]{1,0:T(8,128)(2,1)S(1)}, bf16[4,64,640]{2,1,0:T(8,128)(2,1)S(1)}, bf16[4,64,640]{2,1,0:T(8,128)(2,1)S(1)}) custom-call(s32[1]{0:T(128)S(6)} %select_n.60.ident.other_ident, s32[10]{0:T(128)S(1)} %stack.51.where.refs_1_, ...), custom_call_target="tpu_custom_call" | custom-call | flops 603979776 | bytes 9781248 | tf_op jit(solution)/shard_map/pallas_call | solution.py:46
  142.0 1.0 collective-permute-start.24
  143.0 4.3 %collective-permute-start.25 = (bf16[64,640]{1,0:T(8,128)(2,1)S(1)}, bf16[64,640]{1,0:T(8,128)(2,1)S(1)}, u32[]{:S(2)}, u32[]{:S(2)}) collective-permute-start(bf16[64,640]{1,0:T(8,128)(2,1)S(1)} %get-tuple-element.74), channel_id=1, source_target_pairs={{0,4},{1,5},{2,6},{3,7},{4,0},{5,1},{6,2},{7,3},{8,12},{9,13},{10,... | collective-permute-start | bytes 245768 | tf_op jit(solution)/shard_map/ppermute | solution.py:307
  147.3 4.0 %collective-permute-start.26 = (bf16[64,640]{1,0:T(8,128)(2,1)S(1)}, bf16[64,640]{1,0:T(8,128)(2,1)S(1)}, u32[]{:S(2)}, u32[]{:S(2)}) collective-permute-start(bf16[64,640]{1,0:T(8,128)(2,1)S(1)} %get-tuple-element.75), channel_id=1, source_target_pairs={{0,6},{1,7},{2,0},{3,1},{4,2},{5,3},{6,4},{7,5},{8,14},{9,15},{10,... | collective-permute-start | bytes 245768 | tf_op jit(solution)/shard_map/ppermute | solution.py:308
  151.7 9.6 %collective-permute-done.24.refs_1_ = bf16[64,640]{1,0:T(8,128)(2,1)S(1)} collective-permute-done((bf16[64,640]{1,0:T(8,128)(2,1)S(1)}, bf16[64,640]{1,0:T(8,128)(2,1)S(1)}, u32[]{:S(2)}, u32[]{:S(2)}) %collective-permute-start.24) | collective-permute-done | bytes 81952 | tf_op jit(solution)/shard_map/ppermute | solution.py:306
  161.3 2.9 %collective-permute-start.29 = (bf16[64,640]{1,0:T(8,128)(2,1)S(1)}, bf16[64,640]{1,0:T(8,128)(2,1)S(1)}, u32[]{:S(2)}, u32[]{:S(2)}) collective-permute-start(bf16[64,640]{1,0:T(8,128)(2,1)S(1)} %get-tuple-element.80), channel_id=1, source_target_pairs={{0,4},{1,5},{2,6},{3,7},{4,0},{5,1},{6,2},{7,3},{8,12},{9,13},{10,... | collective-permute-start | bytes 245768 | tf_op jit(solution)/shard_map/ppermute | solution.py:307
  164.2 2.4 %collective-permute-done.25.refs_2_ = bf16[64,640]{1,0:T(8,128)(2,1)S(1)} collective-permute-done((bf16[64,640]{1,0:T(8,128)(2,1)S(1)}, bf16[64,640]{1,0:T(8,128)(2,1)S(1)}, u32[]{:S(2)}, u32[]{:S(2)}) %collective-permute-start.25) | collective-permute-done | bytes 81952 | tf_op jit(solution)/shard_map/ppermute | solution.py:307
  166.6 6.1 %shard_map.158 = bf16[128,4096]{1,0:T(8,128)(2,1)} custom-call(s32[1]{0:T(128)S(6)} %select_n.60.ident.other_ident, s32[10]{0:T(128)S(1)} %stack.51.where.refs_1_, bf16[128,4096]{1,0:T(8,128)(2,1)S(1)} %get-tuple-element.66.grad, bf16[128,4096]{1,0:T(8,128)(2,1)S(1)} %bitcast_select_fusion.rows, f32[1,4096]{1,0:T(1,128)S(1)} %copy-done.20, ...), custom_call_target="tpu_custom_call" | custom-call | flops 603979776 | bytes 8617984 | tf_op jit(solution)/shard_map/pallas_call | solution.py:46
  172.7 1.5 shard_map.161
  174.2 2.1 %collective-permute-done.ident = s32[1]{0:T(128)} collective-permute-done((s32[1]{0:T(128)}, s32[1]{0:T(128)}, u32[]{:S(2)}, u32[]{:S(2)}) %collective-permute-start) | collective-permute-done | bytes 36 | tf_op jit(solution)/shard_map/ppermute | solution.py:398
  176.3 7.4 %shard_map.155 = bf16[128,4096]{1,0:T(8,128)(2,1)} custom-call(s32[1]{0:T(128)} %collective-permute-done.ident, s32[10]{0:T(128)S(1)} %stack.51.where.refs_1_, bf16[128,4096]{1,0:T(8,128)(2,1)S(1)} %copy-done.22, bf16[128,4096]{1,0:T(8,128)(2,1)S(1)} %collective-permute-done.15.passed, f32[1,4096]{1,0:T(1,128)S(1)} %copy-done.20, ...), custom_call_target="tpu_custom_call" | custom-call | flops 1073741824 | bytes 12861440 | tf_op jit(solution)/shard_map/pallas_call | solution.py:46
  (82 shorter events, 3.1 us)
Async XLA Ops:
  0.6 82.8 %copy-start.20 = (f32[1,4096]{1,0:T(1,128)S(1)}, f32[1,4096]{1,0:T(1,128)}, u32[]{:S(2)}) copy-start(f32[1,4096]{1,0:T(1,128)} %gain.9) | copy-start | bytes 49156
  0.6 82.8 %copy-start = (bf16[1,4,4096,64]{2,3,1,0:T(8,128)(2,1)S(1)}, bf16[1,4,4096,64]{2,3,1,0:T(8,128)(2,1)}, u32[]{:S(2)}) copy-start(bf16[1,4,4096,64]{2,3,1,0:T(8,128)(2,1)} %param.22) | copy-start | bytes 6291460
  0.7 19.9 %collective-permute-start.2 = (bf16[512,512]{1,0:T(8,128)(2,1)}, bf16[512,512]{1,0:T(8,128)(2,1)S(1)}, u32[]{:S(2)}, u32[]{:S(2)}) collective-permute-start(bf16[512,512]{1,0:T(8,128)(2,1)} %bitcast.45), channel_id=1, source_target_pairs={{0,2},{1,7},{2,4},{3,1},{4,6},{5,3},{6,0},{7,5},{8,10},{9,15},{10,... | collective-permute-start | bytes 1572872 | tf_op jit(solution)/shard_map/ppermute | solution.py:353
  4.0 31.8 %collective-permute-start.4 = (bf16[512,512]{1,0:T(8,128)(2,1)}, bf16[512,512]{1,0:T(8,128)(2,1)S(1)}, u32[]{:S(2)}, u32[]{:S(2)}) collective-permute-start(bf16[512,512]{1,0:T(8,128)(2,1)} %bitcast.46), channel_id=1, source_target_pairs={{0,6},{1,3},{2,0},{3,5},{4,2},{5,7},{6,4},{7,1},{8,14},{9,11},{10,... | collective-permute-start | bytes 1572872 | tf_op jit(solution)/shard_map/ppermute | solution.py:354
  7.1 28.7 %collective-permute-start.1 = (bf16[512,512]{1,0:T(8,128)(2,1)}, bf16[512,512]{1,0:T(8,128)(2,1)S(1)}, u32[]{:S(2)}, u32[]{:S(2)}) collective-permute-start(bf16[512,512]{1,0:T(8,128)(2,1)} %bitcast.47), channel_id=1, source_target_pairs={{0,1},{1,0},{2,3},{3,2},{4,5},{5,4},{6,7},{7,6},{8,9},{9,8},{10,11... | collective-permute-start | bytes 1572872 | tf_op jit(solution)/shard_map/ppermute | solution.py:352
  20.6 53.3 %copy-start.4 = (bf16[512,512]{1,0:T(8,128)(2,1)}, bf16[512,512]{1,0:T(8,128)(2,1)S(1)}, u32[]{:S(2)}) copy-start(bf16[512,512]{1,0:T(8,128)(2,1)S(1)} %collective-permute-done.2.refs_2_.refs_10_) | copy-start | bytes 1572868
  20.6 36.2 %collective-permute-start.8 = (bf16[512,512]{1,0:T(8,128)(2,1)}, bf16[512,512]{1,0:T(8,128)(2,1)}, u32[]{:S(2)}, u32[]{:S(2)}) collective-permute-start(bf16[512,512]{1,0:T(8,128)(2,1)} %bitcast.52), channel_id=1, source_target_pairs={{0,2},{1,7},{2,4},{3,1},{4,6},{5,3},{6,0},{7,5},{8,10},{9,15},{10,... | collective-permute-start | bytes 1572872 | tf_op jit(solution)/shard_map/ppermute | solution.py:353
  31.3 41.1 %collective-permute-start.6 = (bf16[512,512]{1,0:T(8,128)(2,1)S(1)}, bf16[512,512]{1,0:T(8,128)(2,1)S(1)}, u32[]{:S(2)}, u32[]{:S(2)}) collective-permute-start(bf16[512,512]{1,0:T(8,128)(2,1)S(1)} %collective-permute-done.2.refs_2_.refs_10_), channel_id=1, source_target_pairs={{0,2},{1,7},{2,4},{3,1},{4,6},{5,3},{6,0},{7,5},{8,10},{9,15},{10,... | collective-permute-start | bytes 1572872 | tf_op jit(solution)/shard_map/ppermute | solution.py:355
  35.7 41.6 %collective-permute-start.11 = (bf16[512,512]{1,0:T(8,128)(2,1)}, bf16[512,512]{1,0:T(8,128)(2,1)}, u32[]{:S(2)}, u32[]{:S(2)}) collective-permute-start(bf16[512,512]{1,0:T(8,128)(2,1)} %bitcast.53), channel_id=1, source_target_pairs={{0,6},{1,3},{2,0},{3,5},{4,2},{5,7},{6,4},{7,1},{8,14},{9,11},{10,... | collective-permute-start | bytes 1572872 | tf_op jit(solution)/shard_map/ppermute | solution.py:354
  35.8 41.7 %copy-start.6 = (bf16[512,512]{1,0:T(8,128)(2,1)}, bf16[512,512]{1,0:T(8,128)(2,1)S(1)}, u32[]{:S(2)}) copy-start(bf16[512,512]{1,0:T(8,128)(2,1)S(1)} %collective-permute-done.4.refs_4_.refs_12_) | copy-start | bytes 1572868
  35.8 41.7 %collective-permute-start.3 = (bf16[512,512]{1,0:T(8,128)(2,1)S(1)}, bf16[512,512]{1,0:T(8,128)(2,1)S(1)}, u32[]{:S(2)}, u32[]{:S(2)}) collective-permute-start(bf16[512,512]{1,0:T(8,128)(2,1)S(1)} %collective-permute-done.2.refs_2_.refs_10_), channel_id=1, source_target_pairs={{0,1},{1,0},{2,3},{3,2},{4,5},{5,4},{6,7},{7,6},{8,9},{9,8},{10,11... | collective-permute-start | bytes 1572872 | tf_op jit(solution)/shard_map/ppermute | solution.py:358
  36.7 37.1 %collective-permute-start.5 = (bf16[512,512]{1,0:T(8,128)(2,1)S(1)}, bf16[512,512]{1,0:T(8,128)(2,1)S(1)}, u32[]{:S(2)}, u32[]{:S(2)}) collective-permute-start(bf16[512,512]{1,0:T(8,128)(2,1)S(1)} %collective-permute-done.4.refs_4_.refs_12_), channel_id=1, source_target_pairs={{0,1},{1,0},{2,3},{3,2},{4,5},{5,4},{6,7},{7,6},{8,9},{9,8},{10,11... | collective-permute-start | bytes 1572872 | tf_op jit(solution)/shard_map/ppermute | solution.py:359
  56.7 24.0 %collective-permute-start.9 = (bf16[512,512]{1,0:T(8,128)(2,1)}, bf16[512,512]{1,0:T(8,128)(2,1)}, u32[]{:S(2)}, u32[]{:S(2)}) collective-permute-start(bf16[512,512]{1,0:T(8,128)(2,1)} %collective-permute-done.8.refs_10_.refs_2_), channel_id=1, source_target_pairs={{0,2},{1,7},{2,4},{3,1},{4,6},{5,3},{6,0},{7,5},{8,10},{9,15},{10,... | collective-permute-start | bytes 1572872 | tf_op jit(solution)/shard_map/ppermute | solution.py:355
  72.4 6.4 %copy-start.10 = (bf16[512,512]{1,0:T(8,128)(2,1)}, bf16[512,512]{1,0:T(8,128)(2,1)S(1)}, u32[]{:S(2)}) copy-start(bf16[512,512]{1,0:T(8,128)(2,1)S(1)} %collective-permute-done.6.refs_6_.refs_14_) | copy-start | bytes 1572868
  72.4 8.4 %collective-permute-start.7 = (bf16[512,512]{1,0:T(8,128)(2,1)S(1)}, bf16[512,512]{1,0:T(8,128)(2,1)S(1)}, u32[]{:S(2)}, u32[]{:S(2)}) collective-permute-start(bf16[512,512]{1,0:T(8,128)(2,1)S(1)} %collective-permute-done.6.refs_6_.refs_14_), channel_id=1, source_target_pairs={{0,1},{1,0},{2,3},{3,2},{4,5},{5,4},{6,7},{7,6},{8,9},{9,8},{10,11... | collective-permute-start | bytes 1572872 | tf_op jit(solution)/shard_map/ppermute | solution.py:360
  74.7 44.8 %collective-permute-start.22 = (bf16[128,4096]{1,0:T(8,128)(2,1)S(1)}, bf16[128,4096]{1,0:T(8,128)(2,1)}, u32[]{:S(2)}, u32[]{:S(2)}) collective-permute-start(bf16[128,4096]{1,0:T(8,128)(2,1)S(1)} %slice_bitcast_fusion.rows.refs_3_), channel_id=1, source_target_pairs={{8,0},{16,8},{24,16},{32,24},{40,32},{48,40},{56,48},{64,56},{72,6... | collective-permute-start | bytes 3145736 | tf_op jit(solution)/shard_map/ppermute | solution.py:397
  77.3 12.6 %collective-permute-start.14 = (bf16[512,512]{1,0:T(8,128)(2,1)}, bf16[512,512]{1,0:T(8,128)(2,1)}, u32[]{:S(2)}, u32[]{:S(2)}) collective-permute-start(bf16[512,512]{1,0:T(8,128)(2,1)} %bitcast.54), channel_id=1, source_target_pairs={{0,1},{1,0},{2,3},{3,2},{4,5},{5,4},{6,7},{7,6},{8,9},{9,8},{10,11... | collective-permute-start | bytes 1572872 | tf_op jit(solution)/shard_map/ppermute | solution.py:352
  78.2 14.1 %collective-permute-start.13 = (bf16[512,512]{1,0:T(8,128)(2,1)}, bf16[512,512]{1,0:T(8,128)(2,1)}, u32[]{:S(2)}, u32[]{:S(2)}) collective-permute-start(bf16[512,512]{1,0:T(8,128)(2,1)} %collective-permute-done.8.refs_10_.refs_2_), channel_id=1, source_target_pairs={{0,1},{1,0},{2,3},{3,2},{4,5},{5,4},{6,7},{7,6},{8,9},{9,8},{10,11... | collective-permute-start | bytes 1572872 | tf_op jit(solution)/shard_map/ppermute | solution.py:358
  80.8 14.1 %collective-permute-start.12 = (bf16[512,512]{1,0:T(8,128)(2,1)}, bf16[512,512]{1,0:T(8,128)(2,1)}, u32[]{:S(2)}, u32[]{:S(2)}) collective-permute-start(bf16[512,512]{1,0:T(8,128)(2,1)} %collective-permute-done.11.refs_10_.refs_4_), channel_id=1, source_target_pairs={{0,1},{1,0},{2,3},{3,2},{4,5},{5,4},{6,7},{7,6},{8,9},{9,8},{10,11... | collective-permute-start | bytes 1572872 | tf_op jit(solution)/shard_map/ppermute | solution.py:359
  81.6 23.7 %collective-permute-start.10 = (bf16[512,512]{1,0:T(8,128)(2,1)}, bf16[512,512]{1,0:T(8,128)(2,1)}, u32[]{:S(2)}, u32[]{:S(2)}) collective-permute-start(bf16[512,512]{1,0:T(8,128)(2,1)} %collective-permute-done.9.refs_10_.refs_6_), channel_id=1, source_target_pairs={{0,1},{1,0},{2,3},{3,2},{4,5},{5,4},{6,7},{7,6},{8,9},{9,8},{10,11... | collective-permute-start | bytes 1572872 | tf_op jit(solution)/shard_map/ppermute | solution.py:360
  83.5 2.4 %copy-start.11 = (bf16[512,512]{1,0:T(8,128)(2,1)S(1)}, bf16[512,512]{1,0:T(8,128)(2,1)}, u32[]{:S(2)}) copy-start(bf16[512,512]{1,0:T(8,128)(2,1)} %copy-done.10) | copy-start | bytes 1572868
  83.5 2.4 %copy-start.13 = (bf16[512,512]{1,0:T(8,128)(2,1)S(1)}, bf16[512,512]{1,0:T(8,128)(2,1)}, u32[]{:S(2)}) copy-start(bf16[512,512]{1,0:T(8,128)(2,1)} %copy-done.12) | copy-start | bytes 1572868
  83.5 2.4 %copy-start.15 = (bf16[512,512]{1,0:T(8,128)(2,1)S(1)}, bf16[512,512]{1,0:T(8,128)(2,1)}, u32[]{:S(2)}) copy-start(bf16[512,512]{1,0:T(8,128)(2,1)} %copy-done.14) | copy-start | bytes 1572868
  83.5 2.4 %copy-start.17 = (bf16[512,512]{1,0:T(8,128)(2,1)S(1)}, bf16[512,512]{1,0:T(8,128)(2,1)}, u32[]{:S(2)}) copy-start(bf16[512,512]{1,0:T(8,128)(2,1)} %copy-done.16) | copy-start | bytes 1572868
  84.3 1.7 copy-start.3
  84.3 1.9 %copy-start.5 = (bf16[512,512]{1,0:T(8,128)(2,1)S(1)}, bf16[512,512]{1,0:T(8,128)(2,1)}, u32[]{:S(2)}) copy-start(bf16[512,512]{1,0:T(8,128)(2,1)} %copy-done.4) | copy-start | bytes 1572868
  84.3 2.0 %copy-start.7 = (bf16[512,512]{1,0:T(8,128)(2,1)S(1)}, bf16[512,512]{1,0:T(8,128)(2,1)}, u32[]{:S(2)}) copy-start(bf16[512,512]{1,0:T(8,128)(2,1)} %copy-done.6) | copy-start | bytes 1572868
  84.3 2.2 %copy-start.9 = (bf16[512,512]{1,0:T(8,128)(2,1)S(1)}, bf16[512,512]{1,0:T(8,128)(2,1)}, u32[]{:S(2)}) copy-start(bf16[512,512]{1,0:T(8,128)(2,1)} %copy-done.8) | copy-start | bytes 1572868
  87.4 2.6 %copy-start.18 = (bf16[1,512,512]{2,1,0:T(8,128)(2,1)S(1)}, bf16[1,512,512]{2,1,0:T(8,128)(2,1)}, u32[]{:S(2)}) copy-start(bf16[1,512,512]{2,1,0:T(8,128)(2,1)} %param.19) | copy-start | bytes 1572868
  97.4 24.0 %collective-permute-start.19 = (bf16[128,1024]{1,0:T(8,128)(2,1)S(1)}, bf16[128,1024]{1,0:T(8,128)(2,1)S(1)}, u32[]{:S(2)}, u32[]{:S(2)}) collective-permute-start(bf16[128,1024]{1,0:T(8,128)(2,1)S(1)} %get-tuple-element.61), channel_id=1, source_target_pairs={{8,0},{16,8},{24,16},{32,24},{40,32},{48,40},{56,48},{64,56},{72,6... | collective-permute-start | bytes 786440 | tf_op jit(solution)/shard_map/ppermute | solution.py:420
  100.0 23.3 %collective-permute-start.18 = (bf16[128,1024]{1,0:T(8,128)(2,1)S(1)}, bf16[128,1024]{1,0:T(8,128)(2,1)S(1)}, u32[]{:S(2)}, u32[]{:S(2)}) collective-permute-start(bf16[128,1024]{1,0:T(8,128)(2,1)S(1)} %get-tuple-element.60), channel_id=1, source_target_pairs={{8,0},{16,8},{24,16},{32,24},{40,32},{48,40},{56,48},{64,56},{72,6... | collective-permute-start | bytes 786440 | tf_op jit(solution)/shard_map/ppermute | solution.py:420
  102.4 15.2 %collective-permute-start.16 = (s32[1]{0:T(128)}, s32[1]{0:T(128)}, u32[]{:S(2)}, u32[]{:S(2)}) collective-permute-start(s32[1]{0:T(128)} %param.18), channel_id=1, source_target_pairs={{8,0},{16,8},{24,16},{32,24},{40,32},{48,40},{56,48},{64,56},{72,6... | collective-permute-start | bytes 20 | tf_op jit(solution)/shard_map/ppermute | solution.py:399
  105.3 36.7 %collective-permute-start.23 = (bf16[4,64,640]{2,1,0:T(8,128)(2,1)S(1)}, bf16[4,64,640]{2,1,0:T(8,128)(2,1)S(1)}, u32[]{:S(2)}, u32[]{:S(2)}) collective-permute-start(bf16[4,64,640]{2,1,0:T(8,128)(2,1)S(1)} %get-tuple-element.71), channel_id=1, source_target_pairs={{0,1},{1,0},{2,3},{3,2},{4,5},{5,4},{6,7},{7,6},{8,9},{9,8},{10,11... | collective-permute-start | bytes 983048 | tf_op jit(solution)/shard_map/ppermute | solution.py:298
  107.9 21.8 %copy-start.23 = (bf16[1,2,128,4096]{3,2,1,0:T(8,128)(2,1)S(1)}, bf16[1,2,128,4096]{3,2,1,0:T(8,128)(2,1)}, u32[]{:S(2)}) copy-start(bf16[1,2,128,4096]{3,2,1,0:T(8,128)(2,1)} %param.14) | copy-start | bytes 6291460
  117.6 15.3 %collective-permute-start.17 = (bf16[128,1024]{1,0:T(8,128)(2,1)S(1)}, bf16[128,1024]{1,0:T(8,128)(2,1)S(1)}, u32[]{:S(2)}, u32[]{:S(2)}) collective-permute-start(bf16[128,1024]{1,0:T(8,128)(2,1)S(1)} %get-tuple-element.59), channel_id=1, source_target_pairs={{8,0},{16,8},{24,16},{32,24},{40,32},{48,40},{56,48},{64,56},{72,6... | collective-permute-start | bytes 786440 | tf_op jit(solution)/shard_map/ppermute | solution.py:420
  119.5 14.8 %collective-permute-start.21 = (f32[128,128]{1,0:T(8,128)S(1)}, f32[128,128]{1,0:T(8,128)S(1)}, u32[]{:S(2)}, u32[]{:S(2)}) collective-permute-start(f32[128,128]{1,0:T(8,128)S(1)} %get-tuple-element.63), channel_id=1, source_target_pairs={{8,0},{16,8},{24,16},{32,24},{40,32},{48,40},{56,48},{64,56},{72,6... | collective-permute-start | bytes 196616 | tf_op jit(solution)/shard_map/ppermute | solution.py:421
  121.4 16.5 %collective-permute-start.20 = (bf16[128,1024]{1,0:T(8,128)(2,1)S(1)}, bf16[128,1024]{1,0:T(8,128)(2,1)S(1)}, u32[]{:S(2)}, u32[]{:S(2)}) collective-permute-start(bf16[128,1024]{1,0:T(8,128)(2,1)S(1)} %get-tuple-element.62), channel_id=1, source_target_pairs={{8,0},{16,8},{24,16},{32,24},{40,32},{48,40},{56,48},{64,56},{72,6... | collective-permute-start | bytes 786440 | tf_op jit(solution)/shard_map/ppermute | solution.py:420
  123.4 52.9 %collective-permute-start.15 = (bf16[128,4096]{1,0:T(8,128)(2,1)S(1)}, bf16[128,4096]{1,0:T(8,128)(2,1)S(1)}, u32[]{:S(2)}, u32[]{:S(2)}) collective-permute-start(bf16[128,4096]{1,0:T(8,128)(2,1)S(1)} %shard_map.154.out), channel_id=1, source_target_pairs={{0,8},{8,16},{16,24},{24,32},{32,40},{40,48},{48,56},{56,64},{64,7... | collective-permute-start | bytes 3145736 | tf_op jit(solution)/shard_map/ppermute | solution.py:424
  129.8 8.2 %copy-start.21 = (bf16[128,4096]{1,0:T(8,128)(2,1)S(1)}, bf16[128,4096]{1,0:T(8,128)(2,1)}, u32[]{:S(2)}) copy-start(bf16[128,4096]{1,0:T(8,128)(2,1)} %target.1) | copy-start | bytes 3145732
  141.8 9.5 %collective-permute-start.27 = (bf16[4,64,640]{2,1,0:T(8,128)(2,1)S(1)}, bf16[4,64,640]{2,1,0:T(8,128)(2,1)S(1)}, u32[]{:S(2)}, u32[]{:S(2)}) collective-permute-start(bf16[4,64,640]{2,1,0:T(8,128)(2,1)S(1)} %get-tuple-element.77), channel_id=1, source_target_pairs={{0,1},{1,0},{2,3},{3,2},{4,5},{5,4},{6,7},{7,6},{8,9},{9,8},{10,11... | collective-permute-start | bytes 983048 | tf_op jit(solution)/shard_map/ppermute | solution.py:298
  142.0 19.3 %collective-permute-start.24 = (bf16[64,640]{1,0:T(8,128)(2,1)S(1)}, bf16[64,640]{1,0:T(8,128)(2,1)S(1)}, u32[]{:S(2)}, u32[]{:S(2)}) collective-permute-start(bf16[64,640]{1,0:T(8,128)(2,1)S(1)} %get-tuple-element.73), channel_id=1, source_target_pairs={{0,2},{1,3},{2,4},{3,5},{4,6},{5,7},{6,0},{7,1},{8,10},{9,11},{10,... | collective-permute-start | bytes 245768 | tf_op jit(solution)/shard_map/ppermute | solution.py:306
  143.0 23.6 %collective-permute-start.25 = (bf16[64,640]{1,0:T(8,128)(2,1)S(1)}, bf16[64,640]{1,0:T(8,128)(2,1)S(1)}, u32[]{:S(2)}, u32[]{:S(2)}) collective-permute-start(bf16[64,640]{1,0:T(8,128)(2,1)S(1)} %get-tuple-element.74), channel_id=1, source_target_pairs={{0,4},{1,5},{2,6},{3,7},{4,0},{5,1},{6,2},{7,3},{8,12},{9,13},{10,... | collective-permute-start | bytes 245768 | tf_op jit(solution)/shard_map/ppermute | solution.py:307
  147.3 25.3 %collective-permute-start.26 = (bf16[64,640]{1,0:T(8,128)(2,1)S(1)}, bf16[64,640]{1,0:T(8,128)(2,1)S(1)}, u32[]{:S(2)}, u32[]{:S(2)}) collective-permute-start(bf16[64,640]{1,0:T(8,128)(2,1)S(1)} %get-tuple-element.75), channel_id=1, source_target_pairs={{0,6},{1,7},{2,0},{3,1},{4,2},{5,3},{6,4},{7,5},{8,14},{9,15},{10,... | collective-permute-start | bytes 245768 | tf_op jit(solution)/shard_map/ppermute | solution.py:308
  151.4 21.2 %collective-permute-start.28 = (bf16[64,640]{1,0:T(8,128)(2,1)S(1)}, bf16[64,640]{1,0:T(8,128)(2,1)S(1)}, u32[]{:S(2)}, u32[]{:S(2)}) collective-permute-start(bf16[64,640]{1,0:T(8,128)(2,1)S(1)} %get-tuple-element.79), channel_id=1, source_target_pairs={{0,2},{1,3},{2,4},{3,5},{4,6},{5,7},{6,0},{7,1},{8,10},{9,11},{10,... | collective-permute-start | bytes 245768 | tf_op jit(solution)/shard_map/ppermute | solution.py:306
  161.3 11.3 %collective-permute-start.29 = (bf16[64,640]{1,0:T(8,128)(2,1)S(1)}, bf16[64,640]{1,0:T(8,128)(2,1)S(1)}, u32[]{:S(2)}, u32[]{:S(2)}) collective-permute-start(bf16[64,640]{1,0:T(8,128)(2,1)S(1)} %get-tuple-element.80), channel_id=1, source_target_pairs={{0,4},{1,5},{2,6},{3,7},{4,0},{5,1},{6,2},{7,3},{8,12},{9,13},{10,... | collective-permute-start | bytes 245768 | tf_op jit(solution)/shard_map/ppermute | solution.py:307
  166.6 6.1 %collective-permute-start.30 = (bf16[64,640]{1,0:T(8,128)(2,1)S(1)}, bf16[64,640]{1,0:T(8,128)(2,1)S(1)}, u32[]{:S(2)}, u32[]{:S(2)}) collective-permute-start(bf16[64,640]{1,0:T(8,128)(2,1)S(1)} %get-tuple-element.81), channel_id=1, source_target_pairs={{0,6},{1,7},{2,0},{3,1},{4,2},{5,3},{6,4},{7,5},{8,14},{9,15},{10,... | collective-permute-start | bytes 245768 | tf_op jit(solution)/shard_map/ppermute | solution.py:308
  166.6 9.7 %copy-start.22 = (bf16[128,4096]{1,0:T(8,128)(2,1)S(1)}, bf16[128,4096]{1,0:T(8,128)(2,1)}, u32[]{:S(2)}) copy-start(bf16[128,4096]{1,0:T(8,128)(2,1)} %fresh.1) | copy-start | bytes 3145732
  172.6 3.6 %collective-permute-start = (s32[1]{0:T(128)}, s32[1]{0:T(128)}, u32[]{:S(2)}, u32[]{:S(2)}) collective-permute-start(s32[1]{0:T(128)} %param.17), channel_id=1, source_target_pairs={{0,8},{8,16},{16,24},{24,32},{32,40},{40,48},{48,56},{56,64},{64,7... | collective-permute-start | bytes 20 | tf_op jit(solution)/shard_map/ppermute | solution.py:398
  (7 other events, 7.1 us)

commit v2 on v1

v2 whole, which is shorter than its diff:
```python
import jax
import jax.numpy as jnp
from jax import lax
from jax.experimental import pallas as pl
from jax.experimental.pallas import tpu as pltpu
from jax.sharding import PartitionSpec as P

SCALE = 0.5
EPS = 1e-05
BF = jnp.bfloat16
F32 = jnp.float32
ROWS = 128
WIDTH = 4096
VALUES = 512
PART = 512
RANK = 64
ADAPTERS = 4
PACK = PART + 128
LOWS = 256
WIDE = WIDTH + 128
VMEM = 20 * 1024 * 1024
ONCE = pl.Buffered(1)


def dot(left, right, dims=((1,), (0,))):
    return lax.dot_general(left, right, (dims, ((), ())), preferred_element_type=F32)


def dot_t(left, right):
    return dot(left, right, ((1,), (1,)))


def t_dot(left, right):
    return dot(left, right, ((0,), (0,)))


def call(kernel, scalars, ins, outs, flops, scratch=()):
    specs, arrays = [], []
    for item in ins:
        array, block, index = item if isinstance(item, tuple) else (item, None, None)
        arrays.append(array)
        if block is None:
            zeros = (0,) * array.ndim
            specs.append(pl.BlockSpec(array.shape, lambda i, *s, z=zeros: z, pipeline_mode=ONCE))
        else:
            specs.append(pl.BlockSpec(block, index, pipeline_mode=ONCE))
    out_specs = [
        pl.BlockSpec(o.shape, lambda i, *s, z=(0,) * len(o.shape): z, pipeline_mode=ONCE)
        for o in outs
    ]
    size = sum(a.size * a.dtype.itemsize for a in arrays)
    return pl.pallas_call(
        kernel,
        out_shape=outs,
        grid_spec=pltpu.PrefetchScalarGridSpec(
            num_scalar_prefetch=len(scalars),
            grid=(1,),
            in_specs=specs,
            out_specs=out_specs,
            scratch_shapes=list(scratch),
        ),
        compiler_params=pltpu.CompilerParams(vmem_limit_bytes=VMEM),
        cost_estimate=pl.CostEstimate(
            flops=flops // 1000, bytes_accessed=size // 1000, transcendentals=0
        ),
    )(*scalars, *arrays)


def shape(dims, dtype):
    return jax.ShapeDtypeStruct(dims, dtype)


def factor_of(rows):
    return lax.rsqrt(jnp.sum(rows * rows, axis=-1, keepdims=True) * (1.0 / WIDTH) + EPS)


def columns(index):
    return pl.ds(pl.multiple_of(index * PART, PART), PART)


def only(lows, ident):
    lane = lax.broadcasted_iota(jnp.int32, lows.shape, 1)
    return jnp.where(lane // RANK == ident, lows, jnp.zeros_like(lows))


def compact(lows):
    total = lows[:, :RANK].astype(F32)
    for k in range(1, ADAPTERS):
        total += lows[:, k * RANK : (k + 1) * RANK].astype(F32)
    return total.astype(BF)


def saved_of(saved, which):
    return (saved, (1, 1, ROWS, WIDTH), lambda i, *s: (0, which, 0, 0))


def prepare_kernel(ahead, back, where, rows_f, rows_b, rows_s, gain, down, *refs):
    last = where[9] == 1
    for kind in range(3):
        normed, factor, low = refs[3 * kind : 3 * kind + 3]
        for top in range(0, ROWS, 32):
            part = slice(top, top + 32)
            if kind == 0:
                whole = rows_f[part, :]
            elif kind == 1:
                whole = rows_b[0, 0, part, :]
            else:
                whole = jnp.where(last, rows_f[part, :], rows_s[0, 0, part, :])
            whole = whole.astype(F32)
            scale = factor_of(whole)
            normed[part, :] = (whole * scale * gain[...]).astype(BF)
            factor[part, :] = jnp.broadcast_to(scale, (32, 128))
        lows = dot_t(normed[...], down[...])
        if kind == 0:
            lows = only(lows, ahead[0])
        elif kind == 1:
            lows = only(lows, back[0])
        low[...] = lows.astype(BF)


def prepare(ahead, back, where, rows, saved, gain, down):
    kinds = [shape((ROWS, WIDTH), BF), shape((ROWS, 128), F32), shape((ROWS, LOWS), BF)]
    return call(
        prepare_kernel,
        (ahead, back, where),
        [rows, saved_of(saved, 0), saved_of(saved, 1), gain, down],
        kinds * 3,
        6 * ROWS * WIDTH * LOWS,
    )


def near_kernel(where, grad, normed, *refs):
    outs, vals, (gradients, values) = refs[:6], refs[6:12], refs[12:]
    total = jnp.zeros((ROWS, VALUES), F32)
    for i in range(6):
        total += dot_t(grad[:, columns(where[i])], outs[i][...])
    gradients[...] = total
    total = jnp.zeros((ROWS, VALUES), F32)
    for i in range(6):
        total += dot(normed[:, columns(where[i])], vals[i][...])
    values[...] = total


def near_share(where, grad, normed, outs, vals):
    return call(
        near_kernel,
        (where,),
        [grad, normed, *outs, *vals],
        [shape((ROWS, VALUES), F32)] * 2,
        4 * ROWS * WIDTH * VALUES,
    )


def input_gradient(where, values, lowered, grad, rows, gain, down, scale, blocks, kept, out):
    inner = jnp.zeros((ROWS, 1), F32)
    for i in range(8):
        span = columns(where[i])
        gained = (
            dot_t(values, blocks[i][...]) + dot(lowered, down[:, span])
        ) * gain[:, span]
        kept[i] = gained
        pre = rows(span).astype(F32) * scale
        inner += jnp.sum(gained * pre, axis=-1, keepdims=True)
    inner = inner * (1.0 / WIDTH)
    for i in range(8):
        span = columns(where[i])
        pre = rows(span).astype(F32) * scale
        out[:, span] = (
            grad[:, span].astype(F32) + scale * (kept[i] - pre * inner)
        ).astype(BF)


def first_kernel(
    back, where, share, grad, rows, factor, gain, down, up, far, far_other, *refs
):
    blocks, (out, d_values, d_low, kept) = refs[:8], refs[8:]
    total = share[...]
    total += dot_t(grad[:, columns(where[6])], far[...])
    total += dot_t(grad[:, columns(where[7])], far_other[...])
    values = total.astype(BF)
    lowered = only(SCALE * dot_t(values, up[...]), back[0]).astype(BF)
    d_values[...] = values
    d_low[...] = lowered
    input_gradient(
        where, values, lowered, grad, lambda span: rows[0, 0, :, span], gain, down,
        factor[:, :1], blocks, kept, out,
    )
    out[:, WIDTH:] = jnp.full((ROWS, 128), back[0], jnp.int32).astype(F32).astype(BF)


KEPT = [pltpu.VMEM((8, ROWS, PART), F32)]
GRADS = [shape((ROWS, VALUES), BF), shape((ROWS, LOWS), BF)]


def first_gradient(back, where, share, grad, saved, factor, gain, down, up, outs, vals):
    return call(
        first_kernel,
        (back, where),
        [share, grad, saved_of(saved, 0), factor, gain, down, up, *outs[6:], *vals],
        [shape((ROWS, WIDE), BF), *GRADS],
        2 * ROWS * WIDTH * VALUES,
        KEPT,
    )


def output_kernel(ahead, where, share, normed, low, up, rows, far, far_other, *refs):
    blocks, out = refs[:8], refs[8]
    total = share[...] + SCALE * dot(low[...], up[...])
    total += dot(normed[:, columns(where[6])], far[...])
    total += dot(normed[:, columns(where[7])], far_other[...])
    values = total.astype(BF)
    for i in range(8):
        span = columns(where[i])
        out[:, span] = (rows[:, span].astype(F32) + dot(values, blocks[i][...])).astype(BF)
    out[:, WIDTH:] = jnp.full((ROWS, 128), ahead[0], jnp.int32).astype(F32).astype(BF)


def output(ahead, where, share, normed, low, up, rows, outs, vals):
    return call(
        output_kernel,
        (ahead, where),
        [share, normed, low, up, rows, *vals[6:], *outs],
        [shape((ROWS, WIDE), BF)],
        2 * ROWS * WIDTH * VALUES,
    )[0]


def pack_gradients(where, low, normed, d_values, d_low, mine, other):
    up_term = SCALE * t_dot(low, d_values)
    chip, core = where[0] // 2, where[0] % 2
    for ahead in range(4):
        target = lax.rem(chip + ahead, 4)
        pair = up_term[:, 0:128]
        for k in range(1, 4):
            pair = jnp.where(target == k, up_term[:, 128 * k : 128 * (k + 1)], pair)
        pair = pair.astype(BF)
        for ref, c in ((mine, core), (other, 1 - core)):
            ref[ahead, :, :PART] = t_dot(d_low, normed[:, columns(2 * target + c)]).astype(BF)
            ref[ahead, :, PART:] = pair


PACKED = [shape((4, RANK, PACK), BF)] * 2


def pack_kernel(where, low, normed, d_values, d_low, mine, other):
    pack_gradients(
        where, compact(low[...]), normed, d_values[...], compact(d_low[...]), mine, other
    )


def pack(where, low, normed, d_values, d_low):
    return call(
        pack_kernel, (where,), [low, normed, d_values, d_low], PACKED, 2 * ROWS * WIDTH * RANK
    )


def second_kernel(ahead, where, relayed, out, target, low, normed, up, *refs):
    blocks, (grad, d_values, d_low, mine, other) = refs[:8], refs[8:]
    last = where[9] == 1
    total = jnp.zeros((ROWS, VALUES), F32)
    for i in range(8):
        span = columns(where[i])
        loss = (out[:, span].astype(F32) - target[:, span].astype(F32)).astype(BF)
        chosen = jnp.where(last, loss, relayed[:, span])
        grad[:, span] = chosen
        total += dot_t(chosen, blocks[i][...])
    values = total.astype(BF)
    came = relayed[:, WIDTH : WIDTH + 1].astype(F32).astype(jnp.int32)
    ident = jnp.where(last, ahead[0], came)
    lowered = only(SCALE * dot_t(values, up[...]), ident).astype(BF)
    d_values[...] = values
    d_low[...] = lowered
    pack_gradients(
        where, compact(only(low[...], ident)), normed, values, compact(lowered), mine, other
    )


def second_values(ahead, where, relayed, out, target, low, normed, up, blocks):
    return call(
        second_kernel,
        (ahead, where),
        [relayed, out, target, low, normed, up, *blocks],
        [shape((ROWS, WIDTH), BF), *GRADS, *PACKED],
        2 * ROWS * WIDTH * (VALUES + RANK),
    )


def second_input_kernel(where, grad, rows_f, rows_s, factor, gain, down, d_values, d_low, *refs):
    blocks, (out, kept) = refs[:8], refs[8:]
    last = where[9] == 1
    input_gradient(
        where, d_values[...], d_low[...], grad,
        lambda span: jnp.where(last, rows_f[:, span], rows_s[0, 0, :, span]),
        gain, down, factor[:, :1], blocks, kept, out,
    )


def second_input(where, grad, rows, saved, factor, gain, down, d_values, d_low, blocks):
    return call(
        second_input_kernel,
        (where,),
        [grad, rows, saved_of(saved, 1), factor, gain, down, d_values, d_low, *blocks],
        [shape((ROWS, WIDTH), BF)],
        2 * ROWS * WIDTH * (VALUES + RANK),
        KEPT,
    )[0]


def forward_kernel(where, fresh, passed, gain, down, up, *refs):
    vals, outs, (out, rows, normed) = refs[:8], refs[8:16], refs[16:]
    first = where[8] == 1
    for top in range(0, ROWS, 32):
        part = slice(top, top + 32)
        chosen = jnp.where(first, fresh[part, :], passed[part, :WIDTH])
        whole = chosen.astype(F32)
        rows[part, :] = chosen
        normed[part, :] = (whole * factor_of(whole) * gain[...]).astype(BF)
    ident = passed[:, WIDTH : WIDTH + 1].astype(F32).astype(jnp.int32)
    low = only(dot_t(normed[...], down[...]), ident).astype(BF)
    total = SCALE * dot(low, up[...])
    for i in range(8):
        total += dot(normed[:, columns(where[i])], vals[i][...])
    values = total.astype(BF)
    for i in range(8):
        span = columns(where[i])
        out[:, span] = (rows[:, span].astype(F32) + dot(values, outs[i][...])).astype(BF)


def forward(where, fresh, passed, gain, down, up, vals, outs):
    return call(
        forward_kernel,
        (where,),
        [fresh, passed, gain, down, up, *vals, *outs],
        [shape((ROWS, WIDTH), BF)],
        4 * ROWS * WIDTH * VALUES,
        [pltpu.VMEM((ROWS, WIDTH), BF), pltpu.VMEM((ROWS, WIDTH), BF)],
    )[0]


def pair_sum_kernel(mine, other, own, one, two, three):
    for ahead, ref in enumerate((own, one, two, three)):
        ref[...] = (mine[ahead].astype(F32) + other[ahead].astype(F32)).astype(BF)


def spread(mine, received):
    block = shape((RANK, PACK), BF)
    own, one, two, three = call(pair_sum_kernel, (), [mine, received], [block] * 4, 0)
    return (
        own,
        lax.ppermute(two, "dp", chips(2)),
        lax.ppermute(one, "dp", chips(1)),
        lax.ppermute(three, "dp", chips(3)),
    )


def tables_kernel(ahead, back, where, relayed, *refs):
    terms, (down, up) = refs[:8], refs[8:]
    core = where[0] % 2
    came = relayed[:RANK, :1].astype(F32).astype(jnp.int32)
    ident = jnp.where(where[9] == 1, ahead[0], came)
    sums = []
    for tick in range(2):
        total = terms[4 * tick][...].astype(F32)
        for k in range(1, 4):
            total += terms[4 * tick + k][...].astype(F32)
        sums.append(total)
    for label in range(ADAPTERS):
        one = jnp.where(back[0] == label, 1.0, 0.0)
        two = jnp.where(ident == label, 1.0, 0.0)
        total = one * sums[0] + two * sums[1]
        down[label] = total[:, :PART]
        up[label] = jnp.where(core == 0, total[:, PART : PART + 64], total[:, PART + 64 :])


def tables(ahead, back, where, relayed, terms):
    tail = (relayed, (ROWS, 128), lambda i, *s: (0, WIDTH // 128))
    return call(
        tables_kernel,
        (ahead, back, where),
        [tail, *terms],
        [shape((ADAPTERS, RANK, PART), F32), shape((ADAPTERS, RANK, 64), F32)],
        0,
    )


CORE = [(i, i ^ 1) for i in range(8)]


def chips(by):
    return [(i, ((i // 2 + by) % 4) * 2 + i % 2) for i in range(8)]


def split_ring(sign):
    return [(i, ((i // 2 + (sign if i % 2 == 0 else -sign)) % 4) * 2 + i % 2) for i in range(8)]


def send(block, pairs):
    return lax.ppermute(block, "dp", pairs)


def block_index():
    place = lax.axis_index("dp")
    chip, core = place // 2, place % 2
    other = 1 - core
    step = jnp.where(core == 0, 1, -1)
    block = lambda k, c: 2 * (k % 4) + c
    return [
        block(chip, core), block(chip, other),
        block(chip - step + 4, core), block(chip + step + 4, other),
        block(chip + step + 4, core), block(chip - step + 4, other),
        block(chip + 2, core), block(chip + 2, other),
    ]


def body(
    forward_state, backward_state, saved, fresh, target, forward_adapter, backward_adapter,
    value_projection, output_matrix, norm_gain_frozen, adapter_down, adapter_up,
):
    count = lax.axis_size("section")
    onward = [(i, (i + 1) % count) for i in range(count)]
    before = [(i, i - 1) for i in range(1, count)]
    position = lax.axis_index("section")
    where = jnp.stack(
        [v.astype(jnp.int32) for v in (*block_index(), position == 0, position == count - 1)]
    )
    gain = norm_gain_frozen
    down = jnp.swapaxes(adapter_down[0], 1, 2).reshape(LOWS, WIDTH)
    up = adapter_up[0].reshape(LOWS, VALUES)
    rows, grad = forward_state[0], backward_state[0]
    ahead, back = forward_adapter, backward_adapter

    out_own, val_own = output_matrix[0], value_projection[0]
    out_near, out_away = send(out_own, split_ring(1)), send(out_own, split_ring(-1))
    val_near, val_away = send(val_own, split_ring(1)), send(val_own, split_ring(-1))
    out_sibling, val_sibling = send(out_own, CORE), send(val_own, CORE)

    normed_f, _, low_f, normed_b, factor_b, low_b, normed_n, factor_n, low_n = prepare(
        ahead, back, where, rows, saved, gain, down
    )
    out_near, normed_f = lax.optimization_barrier((out_near, normed_f))
    out_far, val_far = send(out_near, split_ring(1)), send(val_near, split_ring(1))
    outs = [
        out_own, out_sibling, out_near, send(out_near, CORE), out_away, send(out_away, CORE)
    ]
    vals = [
        val_own, val_sibling, val_near, send(val_near, CORE), val_away, send(val_away, CORE)
    ]
    share_b, share_f = near_share(where, grad, normed_f, outs, vals)
    out_far, val_far, share_b = lax.optimization_barrier((out_far, val_far, share_b))
    outs += [out_far, send(out_far, CORE)]
    vals += [val_far, send(val_far, CORE)]

    first_back, d_values, d_low = first_gradient(
        back, where, share_b, grad, saved, factor_b, gain, down, up, outs, vals
    )
    relayed = lax.ppermute(first_back, "section", before)
    share_f, d_values = lax.optimization_barrier((share_f, d_values))
    first_out = output(ahead, where, share_f, normed_f, low_f, up, rows, outs, vals)
    passed = lax.ppermute(first_out, "section", onward)
    d_low, first_out = lax.optimization_barrier((d_low, first_out))
    mine, other = pack(where, low_b, normed_b, d_values, d_low)
    first_terms = spread(mine, send(other, CORE))
    relayed, *first_terms = lax.optimization_barrier((relayed, *first_terms))

    grad_n, d_values, d_low, mine, other = second_values(
        ahead, where, relayed, first_out, target, low_n, normed_n, up, outs
    )
    received = send(other, CORE)
    second_terms = spread(mine, received)
    bwd_out = second_input(
        where, grad_n, rows, saved, factor_n, gain, down, d_values, d_low, vals
    )
    fwd_out = forward(where, fresh, passed, gain, down, up, vals, outs)
    down_table, up_table = tables(ahead, back, where, relayed, (*first_terms, *second_terms))
    return (
        fwd_out[None], bwd_out[None], jnp.swapaxes(down_table, 1, 2)[None], up_table[None]
    )


def solution(mesh):
    return jax.shard_map(
        body,
        mesh=mesh,
        in_specs=(
            P("section", "dp", None),
            P("section", "dp", None),
            P("section", None, "dp", None),
            P("dp", None),
            P("dp", None),
            P("section"),
            P("section"),
            P("section", "dp", None),
            P("section", None, "dp"),
            P("section", None),
            P("section", None, None, None),
            P("section", None, None, None),
        ),
        out_specs=(
            P("section", "dp", None),
            P("section", "dp", None),
            P("section", None, "dp", None),
            P("section", None, None, "dp"),
        ),
        check_vma=False,
    )
```

time: 187 us -> 153 us (0.82); the launches traced: 184 us -> 153 us
  waiting for transfers between devices: 77.9 us -> 53.3 us
  Pallas kernels: 35.4 us -> 26.1 us
  starting transfers between devices: 60.4 us -> 65.9 us
    ppermute x25 -> x18, waiting for transfers between devices: 65.9 us -> 30.6 us  [the longest x16 30.6 us: send(): return lax.ppermute(block, 'dp', pairs)]
    ppermute x2, waiting for transfers between devices: 2.36 us -> 22.7 us  [spread(): lax.ppermute(two, 'dp', chips(2))]
    ppermute x2, waiting for transfers between devices: 9.61 us -> 0.01 us  [spread(): lax.ppermute(one, 'dp', chips(1))]
    pallas_call x15 -> x11, Pallas kernels: 35.4 us -> 26.1 us  [call(): pl.pallas_call(kernel, out_shape=outs, grid_spec=pltpu.PrefetchScalarGrid...]
    ppermute x25 -> x18, starting transfers between devices: 48 us -> 52 us  [the longest x16 43.7 us: send(): return lax.ppermute(block, 'dp', pairs)]
    ppermute x2, starting transfers between devices: 1.29 us -> 3.51 us  [spread(): lax.ppermute(one, 'dp', chips(1))]
    unnamed x48 -> x26, local copies, waits for them, and re-layouts: 5.15 us -> 5.17 us
  transfers between devices with their start and end apart: 31 -> 24, of which waited for: 11 -> 9; matrix products, arithmetic and copies ran while one was open for 1% -> 0% of each run, Pallas kernels for 15% -> 14%
where the time goes in v2:
time: 153 us
  starting transfers between devices  65.9 us (43%)
  waiting for transfers between devices  53.3 us (35%)
  Pallas kernels  26.1 us (17%)
  local copies, waits for them, and re-layouts  5.26 us (3%)
  between operations  2.12 us (1%)
    ppermute x16, starting transfers between devices, send(): return lax.ppermute(block, 'dp', pairs)  43.7 us
    ppermute x16, waiting for transfers between devices, send(): return lax.ppermute(block, 'dp', pairs)  30.6 us
    pallas_call x11, Pallas kernels, call(): pl.pallas_call(kernel, out_shape=outs, grid_spec=pltpu.PrefetchScalarGrid...  26.1 us
    ppermute x2, waiting for transfers between devices, spread(): lax.ppermute(two, 'dp', chips(2))  22.7 us
    ppermute x2, starting transfers between devices, spread(): lax.ppermute(two, 'dp', chips(2))  5.62 us
    ppermute x1, starting transfers between devices, body(): passed = lax.ppermute(first_out, 'section', onward)  5.58 us
    unnamed x26, local copies, waits for them, and re-layouts  5.17 us
    ppermute x2, starting transfers between devices, spread(): lax.ppermute(three, 'dp', chips(3))  4.77 us
  transfers between devices with their start and end apart: 24, of which 9 were waited for; matrix products, arithmetic and copies ran while one was open for 0% of the time, Pallas kernels for 14%

profile of v2, /device:TPU:30, one launch (start us, length us, event | category | flops | bytes accessed | tf_op | source)
XLA Modules:
  0.0 152.7 jit_solution(18244352942150011653)
XLA Ops:
  0.6 3.3 %collective-permute-start = (bf16[512,512]{1,0:T(8,128)(2,1)}, bf16[512,512]{1,0:T(8,128)(2,1)S(1)}, u32[]{:S(2)}, u32[]{:S(2)}) collective-permute-start(bf16[512,512]{1,0:T(8,128)(2,1)} %bitcast.33), channel_id=1, source_target_pairs={{0,2},{1,7},{2,4},{3,1},{4,6},{5,3},{6,0},{7,5},{8,10},{9,15},{10,... | collective-permute-start | bytes 1572872 | tf_op jit(solution)/shard_map/ppermute | solution.py:398
  4.0 4.5 %collective-permute-start.6 = (bf16[512,512]{1,0:T(8,128)(2,1)}, bf16[512,512]{1,0:T(8,128)(2,1)S(1)}, u32[]{:S(2)}, u32[]{:S(2)}) collective-permute-start(bf16[512,512]{1,0:T(8,128)(2,1)} %bitcast.40), channel_id=1, source_target_pairs={{0,2},{1,7},{2,4},{3,1},{4,6},{5,3},{6,0},{7,5},{8,10},{9,15},{10,... | collective-permute-start | bytes 1572872 | tf_op jit(solution)/shard_map/ppermute | solution.py:398
  8.5 1.6 %collective-permute-start.8 = (bf16[512,512]{1,0:T(8,128)(2,1)}, bf16[512,512]{1,0:T(8,128)(2,1)S(1)}, u32[]{:S(2)}, u32[]{:S(2)}) collective-permute-start(bf16[512,512]{1,0:T(8,128)(2,1)} %bitcast.41), channel_id=1, source_target_pairs={{0,6},{1,3},{2,0},{3,5},{4,2},{5,7},{6,4},{7,1},{8,14},{9,11},{10,... | collective-permute-start | bytes 1572872 | tf_op jit(solution)/shard_map/ppermute | solution.py:398
  11.3 0.1 stack.51.where
  11.4 1.6 %copy-done = bf16[1,2,128,4096]{3,2,1,0:T(8,128)(2,1)S(1)} copy-done((bf16[1,2,128,4096]{3,2,1,0:T(8,128)(2,1)S(1)}, bf16[1,2,128,4096]{3,2,1,0:T(8,128)(2,1)}, u32[]{:S(2)}) %copy-start) | copy-done | bytes 2097176
  13.0 1.6 %copy-done.2 = bf16[1,4,4096,64]{2,3,1,0:T(8,128)(2,1)S(1)} copy-done((bf16[1,4,4096,64]{2,3,1,0:T(8,128)(2,1)S(1)}, bf16[1,4,4096,64]{2,3,1,0:T(8,128)(2,1)}, u32[]{:S(2)}) %copy-start.2) | copy-done | bytes 2097176
  14.6 1.2 copy-done.4
  15.8 0.7 copy-done.12
  16.6 4.1 %shard_map.147 = (bf16[128,4096]{1,0:T(8,128)(2,1)S(1)}, f32[128,128]{1,0:T(8,128)}, bf16[128,256]{1,0:T(8,128)(2,1)S(1)}, bf16[128,4096]{1,0:T(8,128)(2,1)S(1)}...) custom-call(s32[1]{0:T(128)S(6)} %copy.16.ahead, ...), custom_call_target="tpu_custom_call" | custom-call | flops 805306 | bytes 7356 | tf_op jit(solution)/shard_map/pallas_call | solution.py:52
  20.7 12.2 %collective-permute-start.5 = (bf16[512,512]{1,0:T(8,128)(2,1)S(1)}, bf16[512,512]{1,0:T(8,128)(2,1)S(1)}, u32[]{:S(2)}, u32[]{:S(2)}) collective-permute-start(bf16[512,512]{1,0:T(8,128)(2,1)S(1)} %bitcast.42), channel_id=1, source_target_pairs={{0,1},{1,0},{2,3},{3,2},{4,5},{5,4},{6,7},{7,6},{8,9},{9,8},{10,11... | collective-permute-start | bytes 1572872 | tf_op jit(solution)/shard_map/ppermute | solution.py:398
  32.9 2.3 %collective-permute-done.6.refs_8_.refs_2_ = bf16[512,512]{1,0:T(8,128)(2,1)S(1)} collective-permute-done((bf16[512,512]{1,0:T(8,128)(2,1)}, bf16[512,512]{1,0:T(8,128)(2,1)S(1)}, u32[]{:S(2)}, u32[]{:S(2)}) %collective-permute-start.6) | collective-permute-done | bytes 524320 | tf_op jit(solution)/shard_map/ppermute | solution.py:398
  35.2 13.5 %collective-permute-start.2 = (bf16[512,512]{1,0:T(8,128)(2,1)S(1)}, bf16[512,512]{1,0:T(8,128)(2,1)S(1)}, u32[]{:S(2)}, u32[]{:S(2)}) collective-permute-start(bf16[512,512]{1,0:T(8,128)(2,1)S(1)} %collective-permute-done.refs_2_.refs_10_), channel_id=1, source_target_pairs={{0,1},{1,0},{2,3},{3,2},{4,5},{5,4},{6,7},{7,6},{8,9},{9,8},{10,11... | collective-permute-start | bytes 1572872 | tf_op jit(solution)/shard_map/ppermute | solution.py:398
  48.7 3.5 %collective-permute-done.8.refs_10_.refs_4_ = bf16[512,512]{1,0:T(8,128)(2,1)S(1)} collective-permute-done((bf16[512,512]{1,0:T(8,128)(2,1)}, bf16[512,512]{1,0:T(8,128)(2,1)S(1)}, u32[]{:S(2)}, u32[]{:S(2)}) %collective-permute-start.8) | collective-permute-done | bytes 524320 | tf_op jit(solution)/shard_map/ppermute | solution.py:398
  52.3 0.5 collective-permute-start.9
  52.8 2.9 %collective-permute-start.10 = (bf16[512,512]{1,0:T(8,128)(2,1)S(1)}, bf16[512,512]{1,0:T(8,128)(2,1)S(1)}, u32[]{:S(2)}, u32[]{:S(2)}) collective-permute-start(bf16[512,512]{1,0:T(8,128)(2,1)S(1)} %collective-permute-done.refs_2_.refs_10_), channel_id=1, source_target_pairs={{0,2},{1,7},{2,4},{3,1},{4,6},{5,3},{6,0},{7,5},{8,10},{9,15},{10,... | collective-permute-start | bytes 1572872 | tf_op jit(solution)/shard_map/ppermute | solution.py:398
  55.7 4.5 %collective-permute-start.11 = (bf16[512,512]{1,0:T(8,128)(2,1)S(1)}, bf16[512,512]{1,0:T(8,128)(2,1)S(1)}, u32[]{:S(2)}, u32[]{:S(2)}) collective-permute-start(bf16[512,512]{1,0:T(8,128)(2,1)S(1)} %collective-permute-done.6.refs_8_.refs_2_), channel_id=1, source_target_pairs={{0,2},{1,7},{2,4},{3,1},{4,6},{5,3},{6,0},{7,5},{8,10},{9,15},{10,... | collective-permute-start | bytes 1572872 | tf_op jit(solution)/shard_map/ppermute | solution.py:398
  60.2 0.0 copy-start.1
  60.2 0.0 copy-start.3
  60.2 0.0 copy-start.9
  60.2 2.1 %shard_map.148 = (f32[128,512]{1,0:T(8,128)S(1)}, f32[128,512]{1,0:T(8,128)S(1)}) custom-call(s32[10]{0:T(128)S(1)} %stack.51.where, bf16[128,4096]{1,0:T(8,128)(2,1)S(1)} %bitcast.47, bf16[128,4096]{1,0:T(8,128)(2,1)S(1)} %get-tuple-element.49.normed, bf16[512,512]{1,0:T(8,128)(2,1)S(1)} %bitcast.36, ...), custom_call_target="tpu_custom_call" | custom-call | flops 1073741 | bytes 8388 | tf_op jit(solution)/shard_map/pallas_call | solution.py:52
  62.4 10.0 %collective-permute-done.10.far.refs_6_.refs_14_ = bf16[512,512]{1,0:T(8,128)(2,1)S(1)} collective-permute-done((bf16[512,512]{1,0:T(8,128)(2,1)S(1)}, bf16[512,512]{1,0:T(8,128)(2,1)S(1)}, u32[]{:S(2)}, u32[]{:S(2)}) %collective-permute-start.10) | collective-permute-done | bytes 524320 | tf_op jit(solution)/shard_map/ppermute | solution.py:398
  72.4 9.3 %collective-permute-done.11.refs_6_.far = bf16[512,512]{1,0:T(8,128)(2,1)S(1)} collective-permute-done((bf16[512,512]{1,0:T(8,128)(2,1)S(1)}, bf16[512,512]{1,0:T(8,128)(2,1)S(1)}, u32[]{:S(2)}, u32[]{:S(2)}) %collective-permute-start.11) | collective-permute-done | bytes 524320 | tf_op jit(solution)/shard_map/ppermute | solution.py:398
  81.7 0.5 collective-permute-start.13
  82.2 1.4 collective-permute-done.12.far_other.refs_7_.refs_15_
  83.6 0.7 collective-permute-done.13.refs_7_.far_other
  84.4 0.0 copy-start.5
  84.4 3.7 %shard_map.149 = (bf16[128,4224]{1,0:T(8,128)(2,1)S(1)}, bf16[128,512]{1,0:T(8,128)(2,1)S(1)}, bf16[128,256]{1,0:T(8,128)(2,1)S(1)}) custom-call(s32[1]{0:T(128)S(6)} %copy.17.back, s32[10]{0:T(128)S(1)} %stack.51.where, f32[128,512]{1,0:T(8,128)S(1)} %get-tuple-element.53.share, bf16[128,4096]{1,0:T(8,128)(2,1)S(1)} %bitcast.48, ...), custom_call_target="tpu_custom_call" | custom-call | flops 536870 | bytes 11091 | tf_op jit(solution)/shard_map/pallas_call | solution.py:52
  88.1 2.7 %collective-permute-start.15 = (bf16[128,4224]{1,0:T(8,128)(2,1)S(1)}, bf16[128,4224]{1,0:T(8,128)(2,1)S(1)}, u32[]{:S(2)}, u32[]{:S(2)}) collective-permute-start(bf16[128,4224]{1,0:T(8,128)(2,1)S(1)} %get-tuple-element.60), channel_id=1, source_target_pairs={{8,0},{16,8},{24,16},{32,24},{40,32},{48,40},{56,48},{64,56},{72,6... | collective-permute-start | bytes 3244040 | tf_op jit(solution)/shard_map/ppermute | solution.py:456
  90.8 1.6 %shard_map.150.out = bf16[128,4224]{1,0:T(8,128)(2,1)S(1)} custom-call(s32[1]{0:T(128)S(6)} %copy.16.ahead, s32[10]{0:T(128)S(1)} %stack.51.where, f32[128,512]{1,0:T(8,128)S(1)} %get-tuple-element.58.share, bf16[128,4096]{1,0:T(8,128)(2,1)S(1)} %get-tuple-element.49.normed, bf16[128,256]{1,0:T(8,128)(2,1)S(1)} %get-tuple-element.59.low, ...), custom_call_target="tpu_custom_call" | custom-call | flops 536870 | bytes 7929 | tf_op jit(solution)/shard_map/pallas_call | solution.py:52
  92.4 5.6 %collective-permute-start.14 = (bf16[128,4224]{1,0:T(8,128)(2,1)S(1)}, bf16[128,4224]{1,0:T(8,128)(2,1)S(1)}, u32[]{:S(2)}, u32[]{:S(2)}) collective-permute-start(bf16[128,4224]{1,0:T(8,128)(2,1)S(1)} %shard_map.150.out), channel_id=1, source_target_pairs={{0,8},{8,16},{16,24},{24,32},{32,40},{40,48},{48,56},{56,64},{64,7... | collective-permute-start | bytes 3244040 | tf_op jit(solution)/shard_map/ppermute | solution.py:459
  97.9 1.0 shard_map.152
  98.9 0.1 collective-permute-start.16
  99.0 1.6 %collective-permute-done.16.other = bf16[4,64,640]{2,1,0:T(8,128)(2,1)S(1)} collective-permute-done((bf16[4,64,640]{2,1,0:T(8,128)(2,1)S(1)}, bf16[4,64,640]{2,1,0:T(8,128)(2,1)S(1)}, u32[]{:S(2)}, u32[]{:S(2)}) %collective-permute-start.16) | collective-permute-done | bytes 327712 | tf_op jit(solution)/shard_map/ppermute | solution.py:398
  100.7 0.1 shard_map.153
  100.7 4.1 %collective-permute-start.17 = (bf16[64,640]{1,0:T(8,128)(2,1)S(1)}, bf16[64,640]{1,0:T(8,128)(2,1)S(1)}, u32[]{:S(2)}, u32[]{:S(2)}) collective-permute-start(bf16[64,640]{1,0:T(8,128)(2,1)S(1)} %get-tuple-element.69), channel_id=1, source_target_pairs={{0,4},{1,5},{2,6},{3,7},{4,0},{5,1},{6,2},{7,3},{8,12},{9,13},{10,... | collective-permute-start | bytes 245768 | tf_op jit(solution)/shard_map/ppermute | solution.py:350
  104.8 1.2 collective-permute-start.18
  106.0 3.0 %collective-permute-start.19 = (bf16[64,640]{1,0:T(8,128)(2,1)S(1)}, bf16[64,640]{1,0:T(8,128)(2,1)S(1)}, u32[]{:S(2)}, u32[]{:S(2)}) collective-permute-start(bf16[64,640]{1,0:T(8,128)(2,1)S(1)} %get-tuple-element.71), channel_id=1, source_target_pairs={{0,6},{1,7},{2,0},{3,1},{4,2},{5,3},{6,4},{7,5},{8,14},{9,15},{10,... | collective-permute-start | bytes 245768 | tf_op jit(solution)/shard_map/ppermute | solution.py:352
  108.9 22.7 %collective-permute-done.17.refs_1_ = bf16[64,640]{1,0:T(8,128)(2,1)S(1)} collective-permute-done((bf16[64,640]{1,0:T(8,128)(2,1)S(1)}, bf16[64,640]{1,0:T(8,128)(2,1)S(1)}, u32[]{:S(2)}, u32[]{:S(2)}) %collective-permute-start.17) | collective-permute-done | bytes 81952 | tf_op jit(solution)/shard_map/ppermute | solution.py:350
  131.7 2.7 %shard_map.154 = (bf16[128,4096]{1,0:T(8,128)(2,1)S(1)}, bf16[128,512]{1,0:T(8,128)(2,1)S(1)}, bf16[128,256]{1,0:T(8,128)(2,1)S(1)}, bf16[4,64,640]{2,1,0:T(8,128)(2,1)S(1)}, bf16[4,64,640]{2,1,0:T(8,128)(2,1)S(1)}) custom-call(s32[1]{0:T(128)S(6)} %copy.16.ahead, s32[10]{0:T(128)S(1)} %stack.51.where, ...), custom_call_target="tpu_custom_call" | custom-call | flops 603979 | bytes 8781 | tf_op jit(solution)/shard_map/pallas_call | solution.py:52
  134.4 0.1 collective-permute-start.20
  134.5 1.6 %collective-permute-done.20.other = bf16[4,64,640]{2,1,0:T(8,128)(2,1)S(1)} collective-permute-done((bf16[4,64,640]{2,1,0:T(8,128)(2,1)S(1)}, bf16[4,64,640]{2,1,0:T(8,128)(2,1)S(1)}, u32[]{:S(2)}, u32[]{:S(2)}) %collective-permute-start.20) | collective-permute-done | bytes 327712 | tf_op jit(solution)/shard_map/ppermute | solution.py:398
  136.1 0.1 shard_map.156
  136.2 1.5 %collective-permute-start.21 = (bf16[64,640]{1,0:T(8,128)(2,1)S(1)}, bf16[64,640]{1,0:T(8,128)(2,1)S(1)}, u32[]{:S(2)}, u32[]{:S(2)}) collective-permute-start(bf16[64,640]{1,0:T(8,128)(2,1)S(1)} %get-tuple-element.87), channel_id=1, source_target_pairs={{0,4},{1,5},{2,6},{3,7},{4,0},{5,1},{6,2},{7,3},{8,12},{9,13},{10,... | collective-permute-start | bytes 245768 | tf_op jit(solution)/shard_map/ppermute | solution.py:350
  137.7 2.3 %collective-permute-start.22 = (bf16[64,640]{1,0:T(8,128)(2,1)S(1)}, bf16[64,640]{1,0:T(8,128)(2,1)S(1)}, u32[]{:S(2)}, u32[]{:S(2)}) collective-permute-start(bf16[64,640]{1,0:T(8,128)(2,1)S(1)} %get-tuple-element.88), channel_id=1, source_target_pairs={{0,2},{1,3},{2,4},{3,5},{4,6},{5,7},{6,0},{7,1},{8,10},{9,11},{10,... | collective-permute-start | bytes 245768 | tf_op jit(solution)/shard_map/ppermute | solution.py:351
  140.1 1.8 %collective-permute-start.23 = (bf16[64,640]{1,0:T(8,128)(2,1)S(1)}, bf16[64,640]{1,0:T(8,128)(2,1)S(1)}, u32[]{:S(2)}, u32[]{:S(2)}) collective-permute-start(bf16[64,640]{1,0:T(8,128)(2,1)S(1)} %get-tuple-element.89), channel_id=1, source_target_pairs={{0,6},{1,7},{2,0},{3,1},{4,2},{5,3},{6,4},{7,5},{8,14},{9,15},{10,... | collective-permute-start | bytes 245768 | tf_op jit(solution)/shard_map/ppermute | solution.py:352
  141.9 4.2 %shard_map.155 = bf16[128,4096]{1,0:T(8,128)(2,1)} custom-call(s32[10]{0:T(128)S(1)} %stack.51.where, bf16[128,4096]{1,0:T(8,128)(2,1)S(1)} %get-tuple-element.76.grad, bf16[128,4096]{1,0:T(8,128)(2,1)S(1)} %bitcast.32, bf16[1,2,128,4096]{3,2,1,0:T(8,128)(2,1)S(1)} %copy-done.1, f32[128,128]{1,0:T(8,128)S(1)} %get-tuple-element.77.factor, ...), custom_call_target="tpu_custom_call" | custom-call | flops 603979 | bytes 10764 | tf_op jit(solution)/shard_map/pallas_call | solution.py:52
  146.1 5.1 %shard_map.151 = bf16[128,4096]{1,0:T(8,128)(2,1)} custom-call(s32[10]{0:T(128)S(1)} %stack.51.where, bf16[128,4096]{1,0:T(8,128)(2,1)S(1)} %copy-done.11, bf16[128,4224]{1,0:T(8,128)(2,1)S(1)} %collective-permute-done.14.passed, f32[1,4096]{1,0:T(1,128)S(1)} %copy-done.12, bf16[256,4096]{1,0:T(8,128)(2,1)S(1)} %bitcast.29, bf16[256,512]{1,0:T(8,128)(2,1)S(1)} %bitcast.52, ...), custom_call_target="tpu_custom_call" | custom-call | flops 1073741 | bytes 12894 | tf_op jit(solution)/shard_map/pallas_call | solution.py:52
  151.2 1.5 %shard_map.157 = (f32[4,64,512]{2,1,0:T(8,128)}, f32[4,64,64]{2,1,0:T(8,128)}) custom-call(s32[1]{0:T(128)S(6)} %copy.16.ahead, s32[1]{0:T(128)S(6)} %copy.17.back, s32[10]{0:T(128)S(1)} %stack.51.where, bf16[128,4224]{1,0:T(8,128)(2,1)S(1)} %collective-permute-done.15.relayed, bf16[64,640]{1,0:T(8,128)(2,1)S(1)} %get-tuple-element.80.refs_0_, ...), custom_call_target="tpu_custom_call" | custom-call | bytes 1736 | tf_op jit(solution)/shard_map/pallas_call | solution.py:52
  (38 shorter events, 0.1 us)
Async XLA Ops:
  0.6 20.1 %collective-permute-start = (bf16[512,512]{1,0:T(8,128)(2,1)}, bf16[512,512]{1,0:T(8,128)(2,1)S(1)}, u32[]{:S(2)}, u32[]{:S(2)}) collective-permute-start(bf16[512,512]{1,0:T(8,128)(2,1)} %bitcast.33), channel_id=1, source_target_pairs={{0,2},{1,7},{2,4},{3,1},{4,6},{5,3},{6,0},{7,5},{8,10},{9,15},{10,... | collective-permute-start | bytes 1572872 | tf_op jit(solution)/shard_map/ppermute | solution.py:398
  4.0 31.3 %collective-permute-start.6 = (bf16[512,512]{1,0:T(8,128)(2,1)}, bf16[512,512]{1,0:T(8,128)(2,1)S(1)}, u32[]{:S(2)}, u32[]{:S(2)}) collective-permute-start(bf16[512,512]{1,0:T(8,128)(2,1)} %bitcast.40), channel_id=1, source_target_pairs={{0,2},{1,7},{2,4},{3,1},{4,6},{5,3},{6,0},{7,5},{8,10},{9,15},{10,... | collective-permute-start | bytes 1572872 | tf_op jit(solution)/shard_map/ppermute | solution.py:398
  8.5 40.3 %collective-permute-start.3 = (bf16[512,512]{1,0:T(8,128)(2,1)}, bf16[512,512]{1,0:T(8,128)(2,1)S(1)}, u32[]{:S(2)}, u32[]{:S(2)}) collective-permute-start(bf16[512,512]{1,0:T(8,128)(2,1)} %bitcast.34), channel_id=1, source_target_pairs={{0,6},{1,3},{2,0},{3,5},{4,2},{5,7},{6,4},{7,1},{8,14},{9,11},{10,... | collective-permute-start | bytes 1572872 | tf_op jit(solution)/shard_map/ppermute | solution.py:398
  8.5 43.8 %collective-permute-start.8 = (bf16[512,512]{1,0:T(8,128)(2,1)}, bf16[512,512]{1,0:T(8,128)(2,1)S(1)}, u32[]{:S(2)}, u32[]{:S(2)}) collective-permute-start(bf16[512,512]{1,0:T(8,128)(2,1)} %bitcast.41), channel_id=1, source_target_pairs={{0,6},{1,3},{2,0},{3,5},{4,2},{5,7},{6,4},{7,1},{8,14},{9,11},{10,... | collective-permute-start | bytes 1572872 | tf_op jit(solution)/shard_map/ppermute | solution.py:398
  10.0 42.2 %collective-permute-start.1 = (bf16[512,512]{1,0:T(8,128)(2,1)}, bf16[512,512]{1,0:T(8,128)(2,1)S(1)}, u32[]{:S(2)}, u32[]{:S(2)}) collective-permute-start(bf16[512,512]{1,0:T(8,128)(2,1)} %bitcast.35), channel_id=1, source_target_pairs={{0,1},{1,0},{2,3},{3,2},{4,5},{5,4},{6,7},{7,6},{8,9},{9,8},{10,11... | collective-permute-start | bytes 1572872 | tf_op jit(solution)/shard_map/ppermute | solution.py:398
  11.4 1.6 %copy-start = (bf16[1,2,128,4096]{3,2,1,0:T(8,128)(2,1)S(1)}, bf16[1,2,128,4096]{3,2,1,0:T(8,128)(2,1)}, u32[]{:S(2)}) copy-start(bf16[1,2,128,4096]{3,2,1,0:T(8,128)(2,1)} %rows_s.3) | copy-start | bytes 6291460
  13.0 1.6 %copy-start.2 = (bf16[1,4,4096,64]{2,3,1,0:T(8,128)(2,1)S(1)}, bf16[1,4,4096,64]{2,3,1,0:T(8,128)(2,1)}, u32[]{:S(2)}) copy-start(bf16[1,4,4096,64]{2,3,1,0:T(8,128)(2,1)} %param.22) | copy-start | bytes 6291460
  14.6 1.2 copy-start.4
  15.8 0.7 copy-start.12
  16.5 4.2 %copy-start.7 = (bf16[1,512,512]{2,1,0:T(8,128)(2,1)S(1)}, bf16[1,512,512]{2,1,0:T(8,128)(2,1)}, u32[]{:S(2)}) copy-start(bf16[1,512,512]{2,1,0:T(8,128)(2,1)} %param.19) | copy-start | bytes 1572868
  16.5 43.6 %copy-start.6 = (bf16[1,512,512]{2,1,0:T(8,128)(2,1)S(1)}, bf16[1,512,512]{2,1,0:T(8,128)(2,1)}, u32[]{:S(2)}) copy-start(bf16[1,512,512]{2,1,0:T(8,128)(2,1)} %param.20) | copy-start | bytes 1572868
  16.5 43.6 %copy-start.8 = (bf16[1,128,4096]{2,1,0:T(8,128)(2,1)S(1)}, bf16[1,128,4096]{2,1,0:T(8,128)(2,1)}, u32[]{:S(2)}) copy-start(bf16[1,128,4096]{2,1,0:T(8,128)(2,1)} %param.13) | copy-start | bytes 3145732
  20.7 32.1 %collective-permute-start.5 = (bf16[512,512]{1,0:T(8,128)(2,1)S(1)}, bf16[512,512]{1,0:T(8,128)(2,1)S(1)}, u32[]{:S(2)}, u32[]{:S(2)}) collective-permute-start(bf16[512,512]{1,0:T(8,128)(2,1)S(1)} %bitcast.42), channel_id=1, source_target_pairs={{0,1},{1,0},{2,3},{3,2},{4,5},{5,4},{6,7},{7,6},{8,9},{9,8},{10,11... | collective-permute-start | bytes 1572872 | tf_op jit(solution)/shard_map/ppermute | solution.py:398
  35.2 20.4 %collective-permute-start.2 = (bf16[512,512]{1,0:T(8,128)(2,1)S(1)}, bf16[512,512]{1,0:T(8,128)(2,1)S(1)}, u32[]{:S(2)}, u32[]{:S(2)}) collective-permute-start(bf16[512,512]{1,0:T(8,128)(2,1)S(1)} %collective-permute-done.refs_2_.refs_10_), channel_id=1, source_target_pairs={{0,1},{1,0},{2,3},{3,2},{4,5},{5,4},{6,7},{7,6},{8,9},{9,8},{10,11... | collective-permute-start | bytes 1572872 | tf_op jit(solution)/shard_map/ppermute | solution.py:398
  48.7 11.4 %collective-permute-start.7 = (bf16[512,512]{1,0:T(8,128)(2,1)S(1)}, bf16[512,512]{1,0:T(8,128)(2,1)S(1)}, u32[]{:S(2)}, u32[]{:S(2)}) collective-permute-start(bf16[512,512]{1,0:T(8,128)(2,1)S(1)} %collective-permute-done.6.refs_8_.refs_2_), channel_id=1, source_target_pairs={{0,1},{1,0},{2,3},{3,2},{4,5},{5,4},{6,7},{7,6},{8,9},{9,8},{10,11... | collective-permute-start | bytes 1572872 | tf_op jit(solution)/shard_map/ppermute | solution.py:398
  52.2 7.9 %collective-permute-start.4 = (bf16[512,512]{1,0:T(8,128)(2,1)S(1)}, bf16[512,512]{1,0:T(8,128)(2,1)S(1)}, u32[]{:S(2)}, u32[]{:S(2)}) collective-permute-start(bf16[512,512]{1,0:T(8,128)(2,1)S(1)} %collective-permute-done.3.refs_4_.refs_12_), channel_id=1, source_target_pairs={{0,1},{1,0},{2,3},{3,2},{4,5},{5,4},{6,7},{7,6},{8,9},{9,8},{10,11... | collective-permute-start | bytes 1572872 | tf_op jit(solution)/shard_map/ppermute | solution.py:398
  52.3 7.9 %collective-permute-start.9 = (bf16[512,512]{1,0:T(8,128)(2,1)S(1)}, bf16[512,512]{1,0:T(8,128)(2,1)S(1)}, u32[]{:S(2)}, u32[]{:S(2)}) collective-permute-start(bf16[512,512]{1,0:T(8,128)(2,1)S(1)} %collective-permute-done.8.refs_10_.refs_4_), channel_id=1, source_target_pairs={{0,1},{1,0},{2,3},{3,2},{4,5},{5,4},{6,7},{7,6},{8,9},{9,8},{10,11... | collective-permute-start | bytes 1572872 | tf_op jit(solution)/shard_map/ppermute | solution.py:398
  52.8 19.6 %collective-permute-start.10 = (bf16[512,512]{1,0:T(8,128)(2,1)S(1)}, bf16[512,512]{1,0:T(8,128)(2,1)S(1)}, u32[]{:S(2)}, u32[]{:S(2)}) collective-permute-start(bf16[512,512]{1,0:T(8,128)(2,1)S(1)} %collective-permute-done.refs_2_.refs_10_), channel_id=1, source_target_pairs={{0,2},{1,7},{2,4},{3,1},{4,6},{5,3},{6,0},{7,5},{8,10},{9,15},{10,... | collective-permute-start | bytes 1572872 | tf_op jit(solution)/shard_map/ppermute | solution.py:398
  55.7 26.0 %collective-permute-start.11 = (bf16[512,512]{1,0:T(8,128)(2,1)S(1)}, bf16[512,512]{1,0:T(8,128)(2,1)S(1)}, u32[]{:S(2)}, u32[]{:S(2)}) collective-permute-start(bf16[512,512]{1,0:T(8,128)(2,1)S(1)} %collective-permute-done.6.refs_8_.refs_2_), channel_id=1, source_target_pairs={{0,2},{1,7},{2,4},{3,1},{4,6},{5,3},{6,0},{7,5},{8,10},{9,15},{10,... | collective-permute-start | bytes 1572872 | tf_op jit(solution)/shard_map/ppermute | solution.py:398
  60.2 24.2 %copy-start.1 = (bf16[1,2,128,4096]{3,2,1,0:T(8,128)(2,1)S(1)}, bf16[1,2,128,4096]{3,2,1,0:T(8,128)(2,1)}, u32[]{:S(2)}) copy-start(bf16[1,2,128,4096]{3,2,1,0:T(8,128)(2,1)} %rows_s.3) | copy-start | bytes 6291460
  60.2 24.2 %copy-start.3 = (bf16[1,4,4096,64]{2,3,1,0:T(8,128)(2,1)S(1)}, bf16[1,4,4096,64]{2,3,1,0:T(8,128)(2,1)}, u32[]{:S(2)}) copy-start(bf16[1,4,4096,64]{2,3,1,0:T(8,128)(2,1)} %param.22) | copy-start | bytes 6291460
  60.2 24.2 %copy-start.9 = (bf16[1,4,64,512]{3,2,1,0:T(8,128)(2,1)S(1)}, bf16[1,4,64,512]{3,2,1,0:T(8,128)(2,1)}, u32[]{:S(2)}) copy-start(bf16[1,4,64,512]{3,2,1,0:T(8,128)(2,1)} %param.23) | copy-start | bytes 786436
  81.7 1.9 %collective-permute-start.12 = (bf16[512,512]{1,0:T(8,128)(2,1)S(1)}, bf16[512,512]{1,0:T(8,128)(2,1)S(1)}, u32[]{:S(2)}, u32[]{:S(2)}) collective-permute-start(bf16[512,512]{1,0:T(8,128)(2,1)S(1)} %collective-permute-done.10.far.refs_6_.refs_14_), channel_id=1, source_target_pairs={{0,1},{1,0},{2,3},{3,2},{4,5},{5,4},{6,7},{7,6},{8,9},{9,8},{10,11... | collective-permute-start | bytes 1572872 | tf_op jit(solution)/shard_map/ppermute | solution.py:398
  81.7 2.7 %collective-permute-start.13 = (bf16[512,512]{1,0:T(8,128)(2,1)S(1)}, bf16[512,512]{1,0:T(8,128)(2,1)S(1)}, u32[]{:S(2)}, u32[]{:S(2)}) collective-permute-start(bf16[512,512]{1,0:T(8,128)(2,1)S(1)} %collective-permute-done.11.refs_6_.far), channel_id=1, source_target_pairs={{0,1},{1,0},{2,3},{3,2},{4,5},{5,4},{6,7},{7,6},{8,9},{9,8},{10,11... | collective-permute-start | bytes 1572872 | tf_op jit(solution)/shard_map/ppermute | solution.py:398
  84.4 6.4 %copy-start.5 = (bf16[1,128,4096]{2,1,0:T(8,128)(2,1)S(1)}, bf16[1,128,4096]{2,1,0:T(8,128)(2,1)}, u32[]{:S(2)}) copy-start(bf16[1,128,4096]{2,1,0:T(8,128)(2,1)} %param.12) | copy-start | bytes 3145732
  88.1 43.6 %collective-permute-start.15 = (bf16[128,4224]{1,0:T(8,128)(2,1)S(1)}, bf16[128,4224]{1,0:T(8,128)(2,1)S(1)}, u32[]{:S(2)}, u32[]{:S(2)}) collective-permute-start(bf16[128,4224]{1,0:T(8,128)(2,1)S(1)} %get-tuple-element.60), channel_id=1, source_target_pairs={{8,0},{16,8},{24,16},{32,24},{40,32},{48,40},{56,48},{64,56},{72,6... | collective-permute-start | bytes 3244040 | tf_op jit(solution)/shard_map/ppermute | solution.py:456
  92.4 39.3 %copy-start.10 = (bf16[128,4096]{1,0:T(8,128)(2,1)S(1)}, bf16[128,4096]{1,0:T(8,128)(2,1)}, u32[]{:S(2)}) copy-start(bf16[128,4096]{1,0:T(8,128)(2,1)} %target.1) | copy-start | bytes 3145732
  92.4 53.7 %collective-permute-start.14 = (bf16[128,4224]{1,0:T(8,128)(2,1)S(1)}, bf16[128,4224]{1,0:T(8,128)(2,1)S(1)}, u32[]{:S(2)}, u32[]{:S(2)}) collective-permute-start(bf16[128,4224]{1,0:T(8,128)(2,1)S(1)} %shard_map.150.out), channel_id=1, source_target_pairs={{0,8},{8,16},{16,24},{24,32},{32,40},{40,48},{48,56},{56,64},{64,7... | collective-permute-start | bytes 3244040 | tf_op jit(solution)/shard_map/ppermute | solution.py:459
  98.9 1.7 %collective-permute-start.16 = (bf16[4,64,640]{2,1,0:T(8,128)(2,1)S(1)}, bf16[4,64,640]{2,1,0:T(8,128)(2,1)S(1)}, u32[]{:S(2)}, u32[]{:S(2)}) collective-permute-start(bf16[4,64,640]{2,1,0:T(8,128)(2,1)S(1)} %get-tuple-element.67), channel_id=1, source_target_pairs={{0,1},{1,0},{2,3},{3,2},{4,5},{5,4},{6,7},{7,6},{8,9},{9,8},{10,11... | collective-permute-start | bytes 983048 | tf_op jit(solution)/shard_map/ppermute | solution.py:398
  100.7 31.0 %collective-permute-start.17 = (bf16[64,640]{1,0:T(8,128)(2,1)S(1)}, bf16[64,640]{1,0:T(8,128)(2,1)S(1)}, u32[]{:S(2)}, u32[]{:S(2)}) collective-permute-start(bf16[64,640]{1,0:T(8,128)(2,1)S(1)} %get-tuple-element.69), channel_id=1, source_target_pairs={{0,4},{1,5},{2,6},{3,7},{4,0},{5,1},{6,2},{7,3},{8,12},{9,13},{10,... | collective-permute-start | bytes 245768 | tf_op jit(solution)/shard_map/ppermute | solution.py:350
  104.8 26.9 %collective-permute-start.18 = (bf16[64,640]{1,0:T(8,128)(2,1)S(1)}, bf16[64,640]{1,0:T(8,128)(2,1)S(1)}, u32[]{:S(2)}, u32[]{:S(2)}) collective-permute-start(bf16[64,640]{1,0:T(8,128)(2,1)S(1)} %get-tuple-element.70), channel_id=1, source_target_pairs={{0,2},{1,3},{2,4},{3,5},{4,6},{5,7},{6,0},{7,1},{8,10},{9,11},{10,... | collective-permute-start | bytes 245768 | tf_op jit(solution)/shard_map/ppermute | solution.py:351
  106.0 25.7 %collective-permute-start.19 = (bf16[64,640]{1,0:T(8,128)(2,1)S(1)}, bf16[64,640]{1,0:T(8,128)(2,1)S(1)}, u32[]{:S(2)}, u32[]{:S(2)}) collective-permute-start(bf16[64,640]{1,0:T(8,128)(2,1)S(1)} %get-tuple-element.71), channel_id=1, source_target_pairs={{0,6},{1,7},{2,0},{3,1},{4,2},{5,3},{6,4},{7,5},{8,14},{9,15},{10,... | collective-permute-start | bytes 245768 | tf_op jit(solution)/shard_map/ppermute | solution.py:352
  134.4 1.7 %collective-permute-start.20 = (bf16[4,64,640]{2,1,0:T(8,128)(2,1)S(1)}, bf16[4,64,640]{2,1,0:T(8,128)(2,1)S(1)}, u32[]{:S(2)}, u32[]{:S(2)}) collective-permute-start(bf16[4,64,640]{2,1,0:T(8,128)(2,1)S(1)} %get-tuple-element.85), channel_id=1, source_target_pairs={{0,1},{1,0},{2,3},{3,2},{4,5},{5,4},{6,7},{7,6},{8,9},{9,8},{10,11... | collective-permute-start | bytes 983048 | tf_op jit(solution)/shard_map/ppermute | solution.py:398
  136.2 15.0 %collective-permute-start.21 = (bf16[64,640]{1,0:T(8,128)(2,1)S(1)}, bf16[64,640]{1,0:T(8,128)(2,1)S(1)}, u32[]{:S(2)}, u32[]{:S(2)}) collective-permute-start(bf16[64,640]{1,0:T(8,128)(2,1)S(1)} %get-tuple-element.87), channel_id=1, source_target_pairs={{0,4},{1,5},{2,6},{3,7},{4,0},{5,1},{6,2},{7,3},{8,12},{9,13},{10,... | collective-permute-start | bytes 245768 | tf_op jit(solution)/shard_map/ppermute | solution.py:350
  137.7 13.4 %collective-permute-start.22 = (bf16[64,640]{1,0:T(8,128)(2,1)S(1)}, bf16[64,640]{1,0:T(8,128)(2,1)S(1)}, u32[]{:S(2)}, u32[]{:S(2)}) collective-permute-start(bf16[64,640]{1,0:T(8,128)(2,1)S(1)} %get-tuple-element.88), channel_id=1, source_target_pairs={{0,2},{1,3},{2,4},{3,5},{4,6},{5,7},{6,0},{7,1},{8,10},{9,11},{10,... | collective-permute-start | bytes 245768 | tf_op jit(solution)/shard_map/ppermute | solution.py:351
  140.1 11.1 %collective-permute-start.23 = (bf16[64,640]{1,0:T(8,128)(2,1)S(1)}, bf16[64,640]{1,0:T(8,128)(2,1)S(1)}, u32[]{:S(2)}, u32[]{:S(2)}) collective-permute-start(bf16[64,640]{1,0:T(8,128)(2,1)S(1)} %get-tuple-element.89), channel_id=1, source_target_pairs={{0,6},{1,7},{2,0},{3,1},{4,2},{5,3},{6,4},{7,5},{8,14},{9,15},{10,... | collective-permute-start | bytes 245768 | tf_op jit(solution)/shard_map/ppermute | solution.py:352
  141.9 4.2 %copy-start.11 = (bf16[128,4096]{1,0:T(8,128)(2,1)S(1)}, bf16[128,4096]{1,0:T(8,128)(2,1)}, u32[]{:S(2)}) copy-start(bf16[128,4096]{1,0:T(8,128)(2,1)} %fresh.1) | copy-start | bytes 3145732

commit v3 on v2

--- a/solution.py
+++ b/solution.py
@@ -129,78 +129,89 @@
     )
 
 
-def near_kernel(where, grad, normed, *refs):
-    outs, vals, (gradients, values) = refs[:6], refs[6:12], refs[12:]
-    total = jnp.zeros((ROWS, VALUES), F32)
-    for i in range(6):
-        total += dot_t(grad[:, columns(where[i])], outs[i][...])
-    gradients[...] = total
-    total = jnp.zeros((ROWS, VALUES), F32)
-    for i in range(6):
-        total += dot(normed[:, columns(where[i])], vals[i][...])
-    values[...] = total
-
-
-def near_share(where, grad, normed, outs, vals):
-    return call(
-        near_kernel,
-        (where,),
-        [grad, normed, *outs, *vals],
-        [shape((ROWS, VALUES), F32)] * 2,
-        4 * ROWS * WIDTH * VALUES,
-    )
-
-
-def input_gradient(where, values, lowered, grad, rows, gain, down, scale, blocks, kept, out):
-    inner = jnp.zeros((ROWS, 1), F32)
-    for i in range(8):
-        span = columns(where[i])
-        gained = (
-            dot_t(values, blocks[i][...]) + dot(lowered, down[:, span])
-        ) * gain[:, span]
-        kept[i] = gained
-        pre = rows(span).astype(F32) * scale
-        inner += jnp.sum(gained * pre, axis=-1, keepdims=True)
+def gained_block(values, lowered, span, gain, down, block):
+    return (dot_t(values, block[...]) + dot(lowered, down[:, span])) * gain[:, span]
+
+
+def input_gradient(where, grad, rows, scale, inner, gained, out):
     inner = inner * (1.0 / WIDTH)
     for i in range(8):
         span = columns(where[i])
         pre = rows(span).astype(F32) * scale
         out[:, span] = (
-            grad[:, span].astype(F32) + scale * (kept[i] - pre * inner)
+            grad[:, span].astype(F32) + scale * (gained(i) - pre * inner)
         ).astype(BF)
 
 
-def first_kernel(
-    back, where, share, grad, rows, factor, gain, down, up, far, far_other, *refs
-):
-    blocks, (out, d_values, d_low, kept) = refs[:8], refs[8:]
-    total = share[...]
-    total += dot_t(grad[:, columns(where[6])], far[...])
-    total += dot_t(grad[:, columns(where[7])], far_other[...])
+def near_kernel(back, where, grad, normed, rows, factor, gain, down, up, *refs):
+    outs, vals, (d_values, d_low, kept, inner, share) = refs[:8], refs[8:14], refs[14:]
+    total = jnp.zeros((ROWS, VALUES), F32)
+    for i in range(8):
+        total += dot_t(grad[:, columns(where[i])], outs[i][...])
     values = total.astype(BF)
     lowered = only(SCALE * dot_t(values, up[...]), back[0]).astype(BF)
     d_values[...] = values
     d_low[...] = lowered
+    scale = factor[:, :1]
+    mean = jnp.zeros((ROWS, 1), F32)
+    for i in range(6):
+        span = columns(where[i])
+        gained = gained_block(values, lowered, span, gain, down, vals[i])
+        kept[i] = gained
+        mean += jnp.sum(
+            gained * (rows[0, 0, :, span].astype(F32) * scale), axis=-1, keepdims=True
+        )
+    inner[...] = jnp.broadcast_to(mean, (ROWS, 128))
+    total = jnp.zeros((ROWS, VALUES), F32)
+    for i in range(6):
+        total += dot(normed[:, columns(where[i])], vals[i][...])
+    share[...] = total
+
+
+GRADS = [shape((ROWS, VALUES), BF), shape((ROWS, LOWS), BF)]
+KEPT = [pltpu.VMEM((8, ROWS, PART), F32)]
+
+
+def near_share(back, where, grad, normed, saved, factor, gain, down, up, outs, vals):
+    return call(
+        near_kernel,
+        (back, where),
+        [grad, normed, saved_of(saved, 0), factor, gain, down, up, *outs, *vals],
+        [*GRADS, shape((6, ROWS, PART), F32), shape((ROWS, 128), F32), shape((ROWS, VALUES), F32)],
+        6 * ROWS * WIDTH * VALUES,
+    )
+
+
+def first_kernel(
+    back, where, kept, inner, values, lowered, grad, rows, factor, gain, down, far, far_other, out
+):
+    scale = factor[:, :1]
+    mean = inner[:, :1]
+    last = []
+    for i, block in ((6, far), (7, far_other)):
+        span = columns(where[i])
+        gained = gained_block(values[...], lowered[...], span, gain, down, block)
+        mean += jnp.sum(
+            gained * (rows[0, 0, :, span].astype(F32) * scale), axis=-1, keepdims=True
+        )
+        last.append(gained)
     input_gradient(
-        where, values, lowered, grad, lambda span: rows[0, 0, :, span], gain, down,
-        factor[:, :1], blocks, kept, out,
+        where, grad, lambda span: rows[0, 0, :, span], scale, mean,
+        lambda i: kept[i] if i < 6 else last[i - 6], out,
     )
     out[:, WIDTH:] = jnp.full((ROWS, 128), back[0], jnp.int32).astype(F32).astype(BF)
 
 
-KEPT = [pltpu.VMEM((8, ROWS, PART), F32)]
-GRADS = [shape((ROWS, VALUES), BF), shape((ROWS, LOWS), BF)]
-
-
-def first_gradient(back, where, share, grad, saved, factor, gain, down, up, outs, vals):
+def first_gradient(back, where, kept, inner, d_values, d_low, grad, saved, factor, gain, down, vals):
     return call(
         first_kernel,
         (back, where),
-        [share, grad, saved_of(saved, 0), factor, gain, down, up, *outs[6:], *vals],
-        [shape((ROWS, WIDE), BF), *GRADS],
-        2 * ROWS * WIDTH * VALUES,
-        KEPT,
-    )
+        [
+            kept, inner, d_values, d_low, grad, saved_of(saved, 0), factor, gain, down, *vals[6:]
+        ],
+        [shape((ROWS, WIDE), BF)],
+        ROWS * WIDTH * VALUES,
+    )[0]
 
 
 def output_kernel(ahead, where, share, normed, low, up, rows, far, far_other, *refs):
@@ -288,11 +299,15 @@
 def second_input_kernel(where, grad, rows_f, rows_s, factor, gain, down, d_values, d_low, *refs):
     blocks, (out, kept) = refs[:8], refs[8:]
     last = where[9] == 1
-    input_gradient(
-        where, d_values[...], d_low[...], grad,
-        lambda span: jnp.where(last, rows_f[:, span], rows_s[0, 0, :, span]),
-        gain, down, factor[:, :1], blocks, kept, out,
-    )
+    scale = factor[:, :1]
+    rows = lambda span: jnp.where(last, rows_f[:, span], rows_s[0, 0, :, span])
+    mean = jnp.zeros((ROWS, 1), F32)
+    for i in range(8):
+        span = columns(where[i])
+        gained = gained_block(d_values[...], d_low[...], span, gain, down, blocks[i])
+        kept[i] = gained
+        mean += jnp.sum(gained * (rows(span).astype(F32) * scale), axis=-1, keepdims=True)
+    input_gradient(where, grad, rows, scale, mean, lambda i: kept[i], out)
 
 
 def second_input(where, grad, rows, saved, factor, gain, down, d_values, d_low, blocks):
@@ -337,14 +352,23 @@
     )[0]
 
 
-def pair_sum_kernel(mine, other, own, one, two, three):
+def pair_sum_kernel(mine, other, total):
+    total[...] = (mine[...].astype(F32) + other[...].astype(F32)).astype(BF)
+
+
+def pair_sum(mine, other):
+    return call(pair_sum_kernel, (), [mine, other], [shape((4, RANK, PACK), BF)], 0)[0]
+
+
+def stack_kernel(first, mine, other, own, one, two, three):
     for ahead, ref in enumerate((own, one, two, three)):
-        ref[...] = (mine[ahead].astype(F32) + other[ahead].astype(F32)).astype(BF)
-
-
-def spread(mine, received):
-    block = shape((RANK, PACK), BF)
-    own, one, two, three = call(pair_sum_kernel, (), [mine, received], [block] * 4, 0)
+        ref[0] = first[ahead]
+        ref[1] = (mine[ahead].astype(F32) + other[ahead].astype(F32)).astype(BF)
+
+
+def spread(first, mine, received):
+    block = shape((2, RANK, PACK), BF)
+    own, one, two, three = call(stack_kernel, (), [first, mine, received], [block] * 4, 0)
     return (
         own,
         lax.ppermute(two, "dp", chips(2)),
@@ -354,15 +378,15 @@
 
 
 def tables_kernel(ahead, back, where, relayed, *refs):
-    terms, (down, up) = refs[:8], refs[8:]
+    terms, (down, up) = refs[:4], refs[4:]
     core = where[0] % 2
     came = relayed[:RANK, :1].astype(F32).astype(jnp.int32)
     ident = jnp.where(where[9] == 1, ahead[0], came)
     sums = []
     for tick in range(2):
-        total = terms[4 * tick][...].astype(F32)
+        total = terms[0][tick].astype(F32)
         for k in range(1, 4):
-            total += terms[4 * tick + k][...].astype(F32)
+            total += terms[k][tick].astype(F32)
         sums.append(total)
     for label in range(ADAPTERS):
         one = jnp.where(back[0] == label, 1.0, 0.0)
@@ -445,33 +469,32 @@
     vals = [
         val_own, val_sibling, val_near, send(val_near, CORE), val_away, send(val_away, CORE)
     ]
-    share_b, share_f = near_share(where, grad, normed_f, outs, vals)
-    out_far, val_far, share_b = lax.optimization_barrier((out_far, val_far, share_b))
     outs += [out_far, send(out_far, CORE)]
+    d_values, d_low, kept, inner, share_f = near_share(
+        back, where, grad, normed_f, saved, factor_b, gain, down, up, outs, vals
+    )
+    mine, other = pack(where, low_b, normed_b, d_values, d_low)
+    first_sums = pair_sum(mine, send(other, CORE))
+    val_far, first_sums = lax.optimization_barrier((val_far, first_sums))
     vals += [val_far, send(val_far, CORE)]
 
-    first_back, d_values, d_low = first_gradient(
-        back, where, share_b, grad, saved, factor_b, gain, down, up, outs, vals
+    first_back = first_gradient(
+        back, where, kept, inner, d_values, d_low, grad, saved, factor_b, gain, down, vals
     )
     relayed = lax.ppermute(first_back, "section", before)
-    share_f, d_values = lax.optimization_barrier((share_f, d_values))
+    share_f, first_back = lax.optimization_barrier((share_f, first_back))
     first_out = output(ahead, where, share_f, normed_f, low_f, up, rows, outs, vals)
     passed = lax.ppermute(first_out, "section", onward)
-    d_low, first_out = lax.optimization_barrier((d_low, first_out))
-    mine, other = pack(where, low_b, normed_b, d_values, d_low)
-    first_terms = spread(mine, send(other, CORE))
-    relayed, *first_terms = lax.optimization_barrier((relayed, *first_terms))
 
     grad_n, d_values, d_low, mine, other = second_values(
         ahead, where, relayed, first_out, target, low_n, normed_n, up, outs
     )
-    received = send(other, CORE)
-    second_terms = spread(mine, received)
+    terms = spread(first_sums, mine, send(other, CORE))
     bwd_out = second_input(
         where, grad_n, rows, saved, factor_n, gain, down, d_values, d_low, vals
     )
     fwd_out = forward(where, fresh, passed, gain, down, up, vals, outs)
-    down_table, up_table = tables(ahead, back, where, relayed, (*first_terms, *second_terms))
+    down_table, up_table = tables(ahead, back, where, relayed, terms)
     return (
         fwd_out[None], bwd_out[None], jnp.swapaxes(down_table, 1, 2)[None], up_table[None]
     )

time: 153 us -> 141 us (0.922)
  starting transfers between devices: 65.9 us -> 47.2 us
  waiting for transfers between devices: 53.3 us -> 58.1 us
    ppermute x2 -> x1, waiting for transfers between devices: 22.7 us -> 0.01 us  [spread(): lax.ppermute(two, 'dp', chips(2))]
    ppermute x1, waiting for transfers between devices: 0.01 us -> 22.2 us  [body(): relayed = lax.ppermute(first_back, 'section', before)]
    ppermute x16, starting transfers between devices: 43.7 us -> 31.6 us  [send(): return lax.ppermute(block, 'dp', pairs)]
    ppermute x16, waiting for transfers between devices: 30.6 us -> 36 us  [send(): return lax.ppermute(block, 'dp', pairs)]
    ppermute x2 -> x1, starting transfers between devices: 3.51 us -> 1.13 us  [spread(): lax.ppermute(one, 'dp', chips(1))]
    ppermute x2 -> x1, starting transfers between devices: 5.62 us -> 3.28 us  [spread(): lax.ppermute(two, 'dp', chips(2))]
    ppermute x2 -> x1, starting transfers between devices: 4.77 us -> 3.01 us  [spread(): lax.ppermute(three, 'dp', chips(3))]
  transfers between devices with their start and end apart: 24 -> 21, of which waited for: 9 -> 9; matrix products, arithmetic and copies ran while one was open for 0% -> 0% of each run, Pallas kernels for 14% -> 17%
where the time goes in v3:
time: 141 us; the launch traced here: 140 us
  waiting for transfers between devices  58.1 us (41%)
  starting transfers between devices  47.2 us (33%)
  Pallas kernels  26.8 us (19%)
  local copies, waits for them, and re-layouts  5.25 us (4%)
  between operations  2.08 us (1%)
    ppermute x16, waiting for transfers between devices, send(): return lax.ppermute(block, 'dp', pairs)  36 us
    ppermute x16, starting transfers between devices, send(): return lax.ppermute(block, 'dp', pairs)  31.6 us
    pallas_call x11, Pallas kernels, call(): pl.pallas_call(kernel, out_shape=outs, grid_spec=pltpu.PrefetchScalarGrid...  26.8 us
    ppermute x1, waiting for transfers between devices, body(): relayed = lax.ppermute(first_back, 'section', before)  22.2 us
    ppermute x1, starting transfers between devices, body(): passed = lax.ppermute(first_out, 'section', onward)  5.58 us
    unnamed x26, local copies, waits for them, and re-layouts  5.17 us
    ppermute x1, starting transfers between devices, spread(): lax.ppermute(two, 'dp', chips(2))  3.28 us
    ppermute x1, starting transfers between devices, spread(): lax.ppermute(three, 'dp', chips(3))  3.01 us
  transfers between devices with their start and end apart: 21, of which 9 were waited for; matrix products, arithmetic and copies ran while one was open for 0% of the time, Pallas kernels for 17%

profile of v3, /device:TPU:30, one launch (start us, length us, event | category | flops | bytes accessed | tf_op | source)
XLA Modules:
  0.0 139.5 jit_solution(18420135347048792019)
XLA Ops:
  0.6 3.3 %collective-permute-start = (bf16[512,512]{1,0:T(8,128)(2,1)}, bf16[512,512]{1,0:T(8,128)(2,1)S(1)}, u32[]{:S(2)}, u32[]{:S(2)}) collective-permute-start(bf16[512,512]{1,0:T(8,128)(2,1)} %bitcast.34), channel_id=1, source_target_pairs={{0,2},{1,7},{2,4},{3,1},{4,6},{5,3},{6,0},{7,5},{8,10},{9,15},{10,... | collective-permute-start | bytes 1572872 | tf_op jit(solution)/shard_map/ppermute | solution.py:422
  4.0 3.1 %collective-permute-start.3 = (bf16[512,512]{1,0:T(8,128)(2,1)}, bf16[512,512]{1,0:T(8,128)(2,1)S(1)}, u32[]{:S(2)}, u32[]{:S(2)}) collective-permute-start(bf16[512,512]{1,0:T(8,128)(2,1)} %bitcast.35), channel_id=1, source_target_pairs={{0,6},{1,3},{2,0},{3,5},{4,2},{5,7},{6,4},{7,1},{8,14},{9,11},{10,... | collective-permute-start | bytes 1572872 | tf_op jit(solution)/shard_map/ppermute | solution.py:422
  7.1 1.4 collective-permute-start.8
  8.5 2.8 %collective-permute-start.10 = (bf16[512,512]{1,0:T(8,128)(2,1)}, bf16[512,512]{1,0:T(8,128)(2,1)S(1)}, u32[]{:S(2)}, u32[]{:S(2)}) collective-permute-start(bf16[512,512]{1,0:T(8,128)(2,1)} %bitcast.42), channel_id=1, source_target_pairs={{0,6},{1,3},{2,0},{3,5},{4,2},{5,7},{6,4},{7,1},{8,14},{9,11},{10,... | collective-permute-start | bytes 1572872 | tf_op jit(solution)/shard_map/ppermute | solution.py:422
  11.2 0.0 collective-permute-start.1
  12.5 0.1 stack.51.where
  12.6 1.6 %copy-done = bf16[1,2,128,4096]{3,2,1,0:T(8,128)(2,1)S(1)} copy-done((bf16[1,2,128,4096]{3,2,1,0:T(8,128)(2,1)S(1)}, bf16[1,2,128,4096]{3,2,1,0:T(8,128)(2,1)}, u32[]{:S(2)}) %copy-start) | copy-done | bytes 2097176
  14.2 1.6 %copy-done.2 = bf16[1,4,4096,64]{2,3,1,0:T(8,128)(2,1)S(1)} copy-done((bf16[1,4,4096,64]{2,3,1,0:T(8,128)(2,1)S(1)}, bf16[1,4,4096,64]{2,3,1,0:T(8,128)(2,1)}, u32[]{:S(2)}) %copy-start.2) | copy-done | bytes 2097176
  15.8 1.2 copy-done.4
  17.0 0.7 copy-done.12
  17.8 0.0 copy-start.8
  17.8 0.0 copy-start.9
  17.8 4.1 %shard_map.147 = (bf16[128,4096]{1,0:T(8,128)(2,1)S(1)}, f32[128,128]{1,0:T(8,128)}, bf16[128,256]{1,0:T(8,128)(2,1)S(1)}, bf16[128,4096]{1,0:T(8,128)(2,1)S(1)}...) custom-call(s32[1]{0:T(128)S(6)} %copy.16.ahead, ...), custom_call_target="tpu_custom_call" | custom-call | flops 805306 | bytes 7356 | tf_op jit(solution)/shard_map/pallas_call | solution.py:52
  21.9 0.0 collective-permute-done.refs_2_.refs_10_
  21.9 11.5 %collective-permute-start.7 = (bf16[512,512]{1,0:T(8,128)(2,1)S(1)}, bf16[512,512]{1,0:T(8,128)(2,1)S(1)}, u32[]{:S(2)}, u32[]{:S(2)}) collective-permute-start(bf16[512,512]{1,0:T(8,128)(2,1)S(1)} %bitcast.43), channel_id=1, source_target_pairs={{0,1},{1,0},{2,3},{3,2},{4,5},{5,4},{6,7},{7,6},{8,9},{9,8},{10,11... | collective-permute-start | bytes 1572872 | tf_op jit(solution)/shard_map/ppermute | solution.py:422
  33.5 7.6 %collective-permute-done.3.refs_4_.refs_12_ = bf16[512,512]{1,0:T(8,128)(2,1)S(1)} collective-permute-done((bf16[512,512]{1,0:T(8,128)(2,1)}, bf16[512,512]{1,0:T(8,128)(2,1)S(1)}, u32[]{:S(2)}, u32[]{:S(2)}) %collective-permute-start.3) | collective-permute-done | bytes 524320 | tf_op jit(solution)/shard_map/ppermute | solution.py:422
  41.1 3.2 %collective-permute-start.5 = (bf16[512,512]{1,0:T(8,128)(2,1)S(1)}, bf16[512,512]{1,0:T(8,128)(2,1)S(1)}, u32[]{:S(2)}, u32[]{:S(2)}) collective-permute-start(bf16[512,512]{1,0:T(8,128)(2,1)S(1)} %collective-permute-done.refs_2_.refs_10_), channel_id=1, source_target_pairs={{0,2},{1,7},{2,4},{3,1},{4,6},{5,3},{6,0},{7,5},{8,10},{9,15},{10,... | collective-permute-start | bytes 1572872 | tf_op jit(solution)/shard_map/ppermute | solution.py:422
  44.3 0.0 collective-permute-done.8.refs_10_.refs_2_
  44.3 5.0 %collective-permute-start.2 = (bf16[512,512]{1,0:T(8,128)(2,1)S(1)}, bf16[512,512]{1,0:T(8,128)(2,1)S(1)}, u32[]{:S(2)}, u32[]{:S(2)}) collective-permute-start(bf16[512,512]{1,0:T(8,128)(2,1)S(1)} %collective-permute-done.refs_2_.refs_10_), channel_id=1, source_target_pairs={{0,1},{1,0},{2,3},{3,2},{4,5},{5,4},{6,7},{7,6},{8,9},{9,8},{10,11... | collective-permute-start | bytes 1572872 | tf_op jit(solution)/shard_map/ppermute | solution.py:422
  49.3 3.0 %collective-permute-done.10.refs_12_.refs_4_ = bf16[512,512]{1,0:T(8,128)(2,1)S(1)} collective-permute-done((bf16[512,512]{1,0:T(8,128)(2,1)}, bf16[512,512]{1,0:T(8,128)(2,1)S(1)}, u32[]{:S(2)}, u32[]{:S(2)}) %collective-permute-start.10) | collective-permute-done | bytes 524320 | tf_op jit(solution)/shard_map/ppermute | solution.py:422
  52.3 0.5 collective-permute-start.9
  52.9 0.1 collective-permute-start.11
  53.0 13.6 %collective-permute-done.5.refs_6_.refs_14_ = bf16[512,512]{1,0:T(8,128)(2,1)S(1)} collective-permute-done((bf16[512,512]{1,0:T(8,128)(2,1)S(1)}, bf16[512,512]{1,0:T(8,128)(2,1)S(1)}, u32[]{:S(2)}, u32[]{:S(2)}) %collective-permute-start.5) | collective-permute-done | bytes 524320 | tf_op jit(solution)/shard_map/ppermute | solution.py:422
  66.6 0.3 collective-permute-start.12
  66.9 1.6 %collective-permute-done.6.refs_7_.refs_15_ = bf16[512,512]{1,0:T(8,128)(2,1)S(1)} collective-permute-done((bf16[512,512]{1,0:T(8,128)(2,1)S(1)}, bf16[512,512]{1,0:T(8,128)(2,1)S(1)}, u32[]{:S(2)}, u32[]{:S(2)}) %collective-permute-start.6) | collective-permute-done | bytes 524320 | tf_op jit(solution)/shard_map/ppermute | solution.py:422
  68.5 4.7 %shard_map.148 = (bf16[128,512]{1,0:T(8,128)(2,1)S(1)}, bf16[128,256]{1,0:T(8,128)(2,1)S(1)}, f32[6,128,512]{2,1,0:T(8,128)S(1)}, f32[128,128]{1,0:T(8,128)S(1)}, f32[128,512]{1,0:T(8,128)S(1)}) custom-call(s32[1]{0:T(128)S(6)} %copy.17.back, s32[10]{0:T(128)S(1)} %stack.51.where, bf16[128,4096]{1,0:T(8,128)(2,1)S(1)} %bitcast.51, ...), custom_call_target="tpu_custom_call" | custom-call | flops 1610612 | bytes 13975 | tf_op jit(solution)/shard_map/pallas_call | solution.py:52
  73.2 1.0 shard_map.149
  74.2 0.2 collective-permute-start.13
  74.4 1.5 %collective-permute-done.13.other = bf16[4,64,640]{2,1,0:T(8,128)(2,1)S(1)} collective-permute-done((bf16[4,64,640]{2,1,0:T(8,128)(2,1)S(1)}, bf16[4,64,640]{2,1,0:T(8,128)(2,1)S(1)}, u32[]{:S(2)}, u32[]{:S(2)}) %collective-permute-start.13) | collective-permute-done | bytes 327712 | tf_op jit(solution)/shard_map/ppermute | solution.py:422
  75.9 0.1 shard_map.150.first
  76.0 5.1 %collective-permute-done.12.far.refs_6_ = bf16[512,512]{1,0:T(8,128)(2,1)S(1)} collective-permute-done((bf16[512,512]{1,0:T(8,128)(2,1)S(1)}, bf16[512,512]{1,0:T(8,128)(2,1)S(1)}, u32[]{:S(2)}, u32[]{:S(2)}) %collective-permute-start.12) | collective-permute-done | bytes 524320 | tf_op jit(solution)/shard_map/ppermute | solution.py:422
  81.1 1.9 %collective-permute-done.14.far_other.refs_7_ = bf16[512,512]{1,0:T(8,128)(2,1)S(1)} collective-permute-done((bf16[512,512]{1,0:T(8,128)(2,1)S(1)}, bf16[512,512]{1,0:T(8,128)(2,1)S(1)}, u32[]{:S(2)}, u32[]{:S(2)}) %collective-permute-start.14) | collective-permute-done | bytes 524320 | tf_op jit(solution)/shard_map/ppermute | solution.py:422
  83.0 1.8 %shard_map.151 = bf16[128,4224]{1,0:T(8,128)(2,1)S(1)} custom-call(s32[1]{0:T(128)S(6)} %copy.17.back, s32[10]{0:T(128)S(1)} %stack.51.where, f32[6,128,512]{2,1,0:T(8,128)S(1)} %get-tuple-element.40.kept, f32[128,128]{1,0:T(8,128)S(1)} %get-tuple-element.41.inner, bf16[128,512]{1,0:T(8,128)(2,1)S(1)} %get-tuple-element.42.d_values.values, ...), custom_call_target="tpu_custom_call" | custom-call | flops 268435 | bytes 8208 | tf_op jit(solution)/shard_map/pallas_call | solution.py:52
  84.8 2.7 %collective-permute-start.16 = (bf16[128,4224]{1,0:T(8,128)(2,1)S(1)}, bf16[128,4224]{1,0:T(8,128)(2,1)S(1)}, u32[]{:S(2)}, u32[]{:S(2)}) collective-permute-start(bf16[128,4224]{1,0:T(8,128)(2,1)S(1)} %shard_map.151), channel_id=1, source_target_pairs={{8,0},{16,8},{24,16},{32,24},{40,32},{48,40},{56,48},{64,56},{72,6... | collective-permute-start | bytes 3244040 | tf_op jit(solution)/shard_map/ppermute | solution.py:484
  87.5 0.0 copy-start.10
  87.5 1.6 %shard_map.152.out = bf16[128,4224]{1,0:T(8,128)(2,1)S(1)} custom-call(s32[1]{0:T(128)S(6)} %copy.16.ahead, s32[10]{0:T(128)S(1)} %stack.51.where, f32[128,512]{1,0:T(8,128)S(1)} %get-tuple-element.49.share, bf16[128,4096]{1,0:T(8,128)(2,1)S(1)} %get-tuple-element.36.normed, bf16[128,256]{1,0:T(8,128)(2,1)S(1)} %get-tuple-element.50.low, ...), custom_call_target="tpu_custom_call" | custom-call | flops 536870 | bytes 7929 | tf_op jit(solution)/shard_map/pallas_call | solution.py:52
  89.1 5.6 %collective-permute-start.15 = (bf16[128,4224]{1,0:T(8,128)(2,1)S(1)}, bf16[128,4224]{1,0:T(8,128)(2,1)S(1)}, u32[]{:S(2)}, u32[]{:S(2)}) collective-permute-start(bf16[128,4224]{1,0:T(8,128)(2,1)S(1)} %shard_map.152.out), channel_id=1, source_target_pairs={{0,8},{8,16},{16,24},{24,32},{32,40},{40,48},{48,56},{56,64},{64,7... | collective-permute-start | bytes 3244040 | tf_op jit(solution)/shard_map/ppermute | solution.py:487
  94.7 22.2 %collective-permute-done.16.relayed = bf16[128,4224]{1,0:T(8,128)(2,1)S(1)} collective-permute-done((bf16[128,4224]{1,0:T(8,128)(2,1)S(1)}, bf16[128,4224]{1,0:T(8,128)(2,1)S(1)}, u32[]{:S(2)}, u32[]{:S(2)}) %collective-permute-start.16) | collective-permute-done | bytes 1081376 | tf_op jit(solution)/shard_map/ppermute | solution.py:484
  116.8 2.6 %shard_map.154 = (bf16[128,4096]{1,0:T(8,128)(2,1)S(1)}, bf16[128,512]{1,0:T(8,128)(2,1)S(1)}, bf16[128,256]{1,0:T(8,128)(2,1)S(1)}, bf16[4,64,640]{2,1,0:T(8,128)(2,1)S(1)}, bf16[4,64,640]{2,1,0:T(8,128)(2,1)S(1)}) custom-call(s32[1]{0:T(128)S(6)} %copy.16.ahead, s32[10]{0:T(128)S(1)} %stack.51.where, ...), custom_call_target="tpu_custom_call" | custom-call | flops 603979 | bytes 8781 | tf_op jit(solution)/shard_map/pallas_call | solution.py:52
  119.5 0.1 collective-permute-start.17
  119.6 1.6 %collective-permute-done.17.other = bf16[4,64,640]{2,1,0:T(8,128)(2,1)S(1)} collective-permute-done((bf16[4,64,640]{2,1,0:T(8,128)(2,1)S(1)}, bf16[4,64,640]{2,1,0:T(8,128)(2,1)S(1)}, u32[]{:S(2)}, u32[]{:S(2)}) %collective-permute-start.17) | collective-permute-done | bytes 327712 | tf_op jit(solution)/shard_map/ppermute | solution.py:422
  121.2 0.1 shard_map.156
  121.3 3.3 %collective-permute-start.18 = (bf16[2,64,640]{2,1,0:T(8,128)(2,1)S(1)}, bf16[2,64,640]{2,1,0:T(8,128)(2,1)S(1)}, u32[]{:S(2)}, u32[]{:S(2)}) collective-permute-start(bf16[2,64,640]{2,1,0:T(8,128)(2,1)S(1)} %get-tuple-element.61), channel_id=1, source_target_pairs={{0,4},{1,5},{2,6},{3,7},{4,0},{5,1},{6,2},{7,3},{8,12},{9,13},{10,... | collective-permute-start | bytes 491528 | tf_op jit(solution)/shard_map/ppermute | solution.py:374
  124.6 1.1 collective-permute-start.19
  125.7 3.0 %collective-permute-start.20 = (bf16[2,64,640]{2,1,0:T(8,128)(2,1)S(1)}, bf16[2,64,640]{2,1,0:T(8,128)(2,1)S(1)}, u32[]{:S(2)}, u32[]{:S(2)}) collective-permute-start(bf16[2,64,640]{2,1,0:T(8,128)(2,1)S(1)} %get-tuple-element.63), channel_id=1, source_target_pairs={{0,6},{1,7},{2,0},{3,1},{4,2},{5,3},{6,4},{7,5},{8,14},{9,15},{10,... | collective-permute-start | bytes 491528 | tf_op jit(solution)/shard_map/ppermute | solution.py:376
  128.7 4.2 %shard_map.155 = bf16[128,4096]{1,0:T(8,128)(2,1)} custom-call(s32[10]{0:T(128)S(1)} %stack.51.where, bf16[128,4096]{1,0:T(8,128)(2,1)S(1)} %get-tuple-element.53.grad, bf16[128,4096]{1,0:T(8,128)(2,1)S(1)} %bitcast.33, bf16[1,2,128,4096]{3,2,1,0:T(8,128)(2,1)S(1)} %copy-done.1, f32[128,128]{1,0:T(8,128)S(1)} %get-tuple-element.54.factor, ...), custom_call_target="tpu_custom_call" | custom-call | flops 603979 | bytes 10764 | tf_op jit(solution)/shard_map/pallas_call | solution.py:52
  132.9 5.1 %shard_map.153 = bf16[128,4096]{1,0:T(8,128)(2,1)} custom-call(s32[10]{0:T(128)S(1)} %stack.51.where, bf16[128,4096]{1,0:T(8,128)(2,1)S(1)} %copy-done.11, bf16[128,4224]{1,0:T(8,128)(2,1)S(1)} %collective-permute-done.15.passed, f32[1,4096]{1,0:T(1,128)S(1)} %copy-done.12, bf16[256,4096]{1,0:T(8,128)(2,1)S(1)} %bitcast.30, bf16[256,512]{1,0:T(8,128)(2,1)S(1)} %bitcast.50, ...), custom_call_target="tpu_custom_call" | custom-call | flops 1073741 | bytes 12894 | tf_op jit(solution)/shard_map/pallas_call | solution.py:52
  138.0 1.5 %shard_map.157 = (f32[4,64,512]{2,1,0:T(8,128)}, f32[4,64,64]{2,1,0:T(8,128)}) custom-call(s32[1]{0:T(128)S(6)} %copy.16.ahead, s32[1]{0:T(128)S(6)} %copy.17.back, s32[10]{0:T(128)S(1)} %stack.51.where, bf16[128,4224]{1,0:T(8,128)(2,1)S(1)} %collective-permute-done.16.relayed, bf16[2,64,640]{2,1,0:T(8,128)(2,1)S(1)} %get-tuple-element.60.refs_0_, ...), custom_call_target="tpu_custom_call" | custom-call | bytes 1736 | tf_op jit(solution)/shard_map/pallas_call | solution.py:52
  (32 shorter events, 0.1 us)
Async XLA Ops:
  0.6 21.3 %collective-permute-start = (bf16[512,512]{1,0:T(8,128)(2,1)}, bf16[512,512]{1,0:T(8,128)(2,1)S(1)}, u32[]{:S(2)}, u32[]{:S(2)}) collective-permute-start(bf16[512,512]{1,0:T(8,128)(2,1)} %bitcast.34), channel_id=1, source_target_pairs={{0,2},{1,7},{2,4},{3,1},{4,6},{5,3},{6,0},{7,5},{8,10},{9,15},{10,... | collective-permute-start | bytes 1572872 | tf_op jit(solution)/shard_map/ppermute | solution.py:422
  4.0 37.1 %collective-permute-start.3 = (bf16[512,512]{1,0:T(8,128)(2,1)}, bf16[512,512]{1,0:T(8,128)(2,1)S(1)}, u32[]{:S(2)}, u32[]{:S(2)}) collective-permute-start(bf16[512,512]{1,0:T(8,128)(2,1)} %bitcast.35), channel_id=1, source_target_pairs={{0,6},{1,3},{2,0},{3,5},{4,2},{5,7},{6,4},{7,1},{8,14},{9,11},{10,... | collective-permute-start | bytes 1572872 | tf_op jit(solution)/shard_map/ppermute | solution.py:422
  7.1 37.2 %collective-permute-start.8 = (bf16[512,512]{1,0:T(8,128)(2,1)}, bf16[512,512]{1,0:T(8,128)(2,1)S(1)}, u32[]{:S(2)}, u32[]{:S(2)}) collective-permute-start(bf16[512,512]{1,0:T(8,128)(2,1)} %bitcast.41), channel_id=1, source_target_pairs={{0,2},{1,7},{2,4},{3,1},{4,6},{5,3},{6,0},{7,5},{8,10},{9,15},{10,... | collective-permute-start | bytes 1572872 | tf_op jit(solution)/shard_map/ppermute | solution.py:422
  8.5 43.9 %collective-permute-start.10 = (bf16[512,512]{1,0:T(8,128)(2,1)}, bf16[512,512]{1,0:T(8,128)(2,1)S(1)}, u32[]{:S(2)}, u32[]{:S(2)}) collective-permute-start(bf16[512,512]{1,0:T(8,128)(2,1)} %bitcast.42), channel_id=1, source_target_pairs={{0,6},{1,3},{2,0},{3,5},{4,2},{5,7},{6,4},{7,1},{8,14},{9,11},{10,... | collective-permute-start | bytes 1572872 | tf_op jit(solution)/shard_map/ppermute | solution.py:422
  11.2 41.1 %collective-permute-start.1 = (bf16[512,512]{1,0:T(8,128)(2,1)}, bf16[512,512]{1,0:T(8,128)(2,1)S(1)}, u32[]{:S(2)}, u32[]{:S(2)}) collective-permute-start(bf16[512,512]{1,0:T(8,128)(2,1)} %bitcast.36), channel_id=1, source_target_pairs={{0,1},{1,0},{2,3},{3,2},{4,5},{5,4},{6,7},{7,6},{8,9},{9,8},{10,11... | collective-permute-start | bytes 1572872 | tf_op jit(solution)/shard_map/ppermute | solution.py:422
  12.6 1.6 %copy-start = (bf16[1,2,128,4096]{3,2,1,0:T(8,128)(2,1)S(1)}, bf16[1,2,128,4096]{3,2,1,0:T(8,128)(2,1)}, u32[]{:S(2)}) copy-start(bf16[1,2,128,4096]{3,2,1,0:T(8,128)(2,1)} %rows_s.3) | copy-start | bytes 6291460
  14.2 1.6 %copy-start.2 = (bf16[1,4,4096,64]{2,3,1,0:T(8,128)(2,1)S(1)}, bf16[1,4,4096,64]{2,3,1,0:T(8,128)(2,1)}, u32[]{:S(2)}) copy-start(bf16[1,4,4096,64]{2,3,1,0:T(8,128)(2,1)} %param.22) | copy-start | bytes 6291460
  15.8 1.2 copy-start.4
  17.0 0.7 copy-start.12
  17.8 4.2 %copy-start.7 = (bf16[1,512,512]{2,1,0:T(8,128)(2,1)S(1)}, bf16[1,512,512]{2,1,0:T(8,128)(2,1)}, u32[]{:S(2)}) copy-start(bf16[1,512,512]{2,1,0:T(8,128)(2,1)} %param.19) | copy-start | bytes 1572868
  17.8 50.7 %copy-start.1 = (bf16[1,2,128,4096]{3,2,1,0:T(8,128)(2,1)S(1)}, bf16[1,2,128,4096]{3,2,1,0:T(8,128)(2,1)}, u32[]{:S(2)}) copy-start(bf16[1,2,128,4096]{3,2,1,0:T(8,128)(2,1)} %rows_s.3) | copy-start | bytes 6291460
  17.8 50.7 %copy-start.3 = (bf16[1,4,4096,64]{2,3,1,0:T(8,128)(2,1)S(1)}, bf16[1,4,4096,64]{2,3,1,0:T(8,128)(2,1)}, u32[]{:S(2)}) copy-start(bf16[1,4,4096,64]{2,3,1,0:T(8,128)(2,1)} %param.22) | copy-start | bytes 6291460
  17.8 50.7 %copy-start.6 = (bf16[1,512,512]{2,1,0:T(8,128)(2,1)S(1)}, bf16[1,512,512]{2,1,0:T(8,128)(2,1)}, u32[]{:S(2)}) copy-start(bf16[1,512,512]{2,1,0:T(8,128)(2,1)} %param.20) | copy-start | bytes 1572868
  17.8 50.7 %copy-start.8 = (bf16[1,4,64,512]{3,2,1,0:T(8,128)(2,1)S(1)}, bf16[1,4,64,512]{3,2,1,0:T(8,128)(2,1)}, u32[]{:S(2)}) copy-start(bf16[1,4,64,512]{3,2,1,0:T(8,128)(2,1)} %param.23) | copy-start | bytes 786436
  17.8 50.7 %copy-start.9 = (bf16[1,128,4096]{2,1,0:T(8,128)(2,1)S(1)}, bf16[1,128,4096]{2,1,0:T(8,128)(2,1)}, u32[]{:S(2)}) copy-start(bf16[1,128,4096]{2,1,0:T(8,128)(2,1)} %param.13) | copy-start | bytes 3145732
  21.9 30.9 %collective-permute-start.7 = (bf16[512,512]{1,0:T(8,128)(2,1)S(1)}, bf16[512,512]{1,0:T(8,128)(2,1)S(1)}, u32[]{:S(2)}, u32[]{:S(2)}) collective-permute-start(bf16[512,512]{1,0:T(8,128)(2,1)S(1)} %bitcast.43), channel_id=1, source_target_pairs={{0,1},{1,0},{2,3},{3,2},{4,5},{5,4},{6,7},{7,6},{8,9},{9,8},{10,11... | collective-permute-start | bytes 1572872 | tf_op jit(solution)/shard_map/ppermute | solution.py:422
  41.1 25.5 %collective-permute-start.5 = (bf16[512,512]{1,0:T(8,128)(2,1)S(1)}, bf16[512,512]{1,0:T(8,128)(2,1)S(1)}, u32[]{:S(2)}, u32[]{:S(2)}) collective-permute-start(bf16[512,512]{1,0:T(8,128)(2,1)S(1)} %collective-permute-done.refs_2_.refs_10_), channel_id=1, source_target_pairs={{0,2},{1,7},{2,4},{3,1},{4,6},{5,3},{6,0},{7,5},{8,10},{9,15},{10,... | collective-permute-start | bytes 1572872 | tf_op jit(solution)/shard_map/ppermute | solution.py:422
  44.3 22.3 %collective-permute-start.2 = (bf16[512,512]{1,0:T(8,128)(2,1)S(1)}, bf16[512,512]{1,0:T(8,128)(2,1)S(1)}, u32[]{:S(2)}, u32[]{:S(2)}) collective-permute-start(bf16[512,512]{1,0:T(8,128)(2,1)S(1)} %collective-permute-done.refs_2_.refs_10_), channel_id=1, source_target_pairs={{0,1},{1,0},{2,3},{3,2},{4,5},{5,4},{6,7},{7,6},{8,9},{9,8},{10,11... | collective-permute-start | bytes 1572872 | tf_op jit(solution)/shard_map/ppermute | solution.py:422
  52.3 14.5 %collective-permute-start.4 = (bf16[512,512]{1,0:T(8,128)(2,1)S(1)}, bf16[512,512]{1,0:T(8,128)(2,1)S(1)}, u32[]{:S(2)}, u32[]{:S(2)}) collective-permute-start(bf16[512,512]{1,0:T(8,128)(2,1)S(1)} %collective-permute-done.3.refs_4_.refs_12_), channel_id=1, source_target_pairs={{0,1},{1,0},{2,3},{3,2},{4,5},{5,4},{6,7},{7,6},{8,9},{9,8},{10,11... | collective-permute-start | bytes 1572872 | tf_op jit(solution)/shard_map/ppermute | solution.py:422
  52.3 14.5 %collective-permute-start.9 = (bf16[512,512]{1,0:T(8,128)(2,1)S(1)}, bf16[512,512]{1,0:T(8,128)(2,1)S(1)}, u32[]{:S(2)}, u32[]{:S(2)}) collective-permute-start(bf16[512,512]{1,0:T(8,128)(2,1)S(1)} %collective-permute-done.8.refs_10_.refs_2_), channel_id=1, source_target_pairs={{0,1},{1,0},{2,3},{3,2},{4,5},{5,4},{6,7},{7,6},{8,9},{9,8},{10,11... | collective-permute-start | bytes 1572872 | tf_op jit(solution)/shard_map/ppermute | solution.py:422
  52.9 14.0 %collective-permute-start.11 = (bf16[512,512]{1,0:T(8,128)(2,1)S(1)}, bf16[512,512]{1,0:T(8,128)(2,1)S(1)}, u32[]{:S(2)}, u32[]{:S(2)}) collective-permute-start(bf16[512,512]{1,0:T(8,128)(2,1)S(1)} %collective-permute-done.10.refs_12_.refs_4_), channel_id=1, source_target_pairs={{0,1},{1,0},{2,3},{3,2},{4,5},{5,4},{6,7},{7,6},{8,9},{9,8},{10,11... | collective-permute-start | bytes 1572872 | tf_op jit(solution)/shard_map/ppermute | solution.py:422
  66.6 1.9 %collective-permute-start.6 = (bf16[512,512]{1,0:T(8,128)(2,1)S(1)}, bf16[512,512]{1,0:T(8,128)(2,1)S(1)}, u32[]{:S(2)}, u32[]{:S(2)}) collective-permute-start(bf16[512,512]{1,0:T(8,128)(2,1)S(1)} %collective-permute-done.5.refs_6_.refs_14_), channel_id=1, source_target_pairs={{0,1},{1,0},{2,3},{3,2},{4,5},{5,4},{6,7},{7,6},{8,9},{9,8},{10,11... | collective-permute-start | bytes 1572872 | tf_op jit(solution)/shard_map/ppermute | solution.py:422
  66.6 14.6 %collective-permute-start.12 = (bf16[512,512]{1,0:T(8,128)(2,1)S(1)}, bf16[512,512]{1,0:T(8,128)(2,1)S(1)}, u32[]{:S(2)}, u32[]{:S(2)}) collective-permute-start(bf16[512,512]{1,0:T(8,128)(2,1)S(1)} %collective-permute-done.8.refs_10_.refs_2_), channel_id=1, source_target_pairs={{0,2},{1,7},{2,4},{3,1},{4,6},{5,3},{6,0},{7,5},{8,10},{9,15},{10,... | collective-permute-start | bytes 1572872 | tf_op jit(solution)/shard_map/ppermute | solution.py:422
  74.2 1.7 %collective-permute-start.13 = (bf16[4,64,640]{2,1,0:T(8,128)(2,1)S(1)}, bf16[4,64,640]{2,1,0:T(8,128)(2,1)S(1)}, u32[]{:S(2)}, u32[]{:S(2)}) collective-permute-start(bf16[4,64,640]{2,1,0:T(8,128)(2,1)S(1)} %get-tuple-element.47), channel_id=1, source_target_pairs={{0,1},{1,0},{2,3},{3,2},{4,5},{5,4},{6,7},{7,6},{8,9},{9,8},{10,11... | collective-permute-start | bytes 983048 | tf_op jit(solution)/shard_map/ppermute | solution.py:422
  81.1 1.9 %collective-permute-start.14 = (bf16[512,512]{1,0:T(8,128)(2,1)S(1)}, bf16[512,512]{1,0:T(8,128)(2,1)S(1)}, u32[]{:S(2)}, u32[]{:S(2)}) collective-permute-start(bf16[512,512]{1,0:T(8,128)(2,1)S(1)} %collective-permute-done.12.far.refs_6_), channel_id=1, source_target_pairs={{0,1},{1,0},{2,3},{3,2},{4,5},{5,4},{6,7},{7,6},{8,9},{9,8},{10,11... | collective-permute-start | bytes 1572872 | tf_op jit(solution)/shard_map/ppermute | solution.py:422
  83.0 4.4 %copy-start.5 = (bf16[1,128,4096]{2,1,0:T(8,128)(2,1)S(1)}, bf16[1,128,4096]{2,1,0:T(8,128)(2,1)}, u32[]{:S(2)}) copy-start(bf16[1,128,4096]{2,1,0:T(8,128)(2,1)} %param.12) | copy-start | bytes 3145732
  84.8 32.0 %collective-permute-start.16 = (bf16[128,4224]{1,0:T(8,128)(2,1)S(1)}, bf16[128,4224]{1,0:T(8,128)(2,1)S(1)}, u32[]{:S(2)}, u32[]{:S(2)}) collective-permute-start(bf16[128,4224]{1,0:T(8,128)(2,1)S(1)} %shard_map.151), channel_id=1, source_target_pairs={{8,0},{16,8},{24,16},{32,24},{40,32},{48,40},{56,48},{64,56},{72,6... | collective-permute-start | bytes 3244040 | tf_op jit(solution)/shard_map/ppermute | solution.py:484
  87.5 29.3 %copy-start.10 = (bf16[128,4096]{1,0:T(8,128)(2,1)S(1)}, bf16[128,4096]{1,0:T(8,128)(2,1)}, u32[]{:S(2)}) copy-start(bf16[128,4096]{1,0:T(8,128)(2,1)} %target.1) | copy-start | bytes 3145732
  89.1 43.8 %collective-permute-start.15 = (bf16[128,4224]{1,0:T(8,128)(2,1)S(1)}, bf16[128,4224]{1,0:T(8,128)(2,1)S(1)}, u32[]{:S(2)}, u32[]{:S(2)}) collective-permute-start(bf16[128,4224]{1,0:T(8,128)(2,1)S(1)} %shard_map.152.out), channel_id=1, source_target_pairs={{0,8},{8,16},{16,24},{24,32},{32,40},{40,48},{48,56},{56,64},{64,7... | collective-permute-start | bytes 3244040 | tf_op jit(solution)/shard_map/ppermute | solution.py:487
  119.5 1.7 %collective-permute-start.17 = (bf16[4,64,640]{2,1,0:T(8,128)(2,1)S(1)}, bf16[4,64,640]{2,1,0:T(8,128)(2,1)S(1)}, u32[]{:S(2)}, u32[]{:S(2)}) collective-permute-start(bf16[4,64,640]{2,1,0:T(8,128)(2,1)S(1)} %get-tuple-element.59), channel_id=1, source_target_pairs={{0,1},{1,0},{2,3},{3,2},{4,5},{5,4},{6,7},{7,6},{8,9},{9,8},{10,11... | collective-permute-start | bytes 983048 | tf_op jit(solution)/shard_map/ppermute | solution.py:422
  121.3 16.7 %collective-permute-start.18 = (bf16[2,64,640]{2,1,0:T(8,128)(2,1)S(1)}, bf16[2,64,640]{2,1,0:T(8,128)(2,1)S(1)}, u32[]{:S(2)}, u32[]{:S(2)}) collective-permute-start(bf16[2,64,640]{2,1,0:T(8,128)(2,1)S(1)} %get-tuple-element.61), channel_id=1, source_target_pairs={{0,4},{1,5},{2,6},{3,7},{4,0},{5,1},{6,2},{7,3},{8,12},{9,13},{10,... | collective-permute-start | bytes 491528 | tf_op jit(solution)/shard_map/ppermute | solution.py:374
  124.6 13.4 %collective-permute-start.19 = (bf16[2,64,640]{2,1,0:T(8,128)(2,1)S(1)}, bf16[2,64,640]{2,1,0:T(8,128)(2,1)S(1)}, u32[]{:S(2)}, u32[]{:S(2)}) collective-permute-start(bf16[2,64,640]{2,1,0:T(8,128)(2,1)S(1)} %get-tuple-element.62), channel_id=1, source_target_pairs={{0,2},{1,3},{2,4},{3,5},{4,6},{5,7},{6,0},{7,1},{8,10},{9,11},{10,... | collective-permute-start | bytes 491528 | tf_op jit(solution)/shard_map/ppermute | solution.py:375
  125.7 12.3 %collective-permute-start.20 = (bf16[2,64,640]{2,1,0:T(8,128)(2,1)S(1)}, bf16[2,64,640]{2,1,0:T(8,128)(2,1)S(1)}, u32[]{:S(2)}, u32[]{:S(2)}) collective-permute-start(bf16[2,64,640]{2,1,0:T(8,128)(2,1)S(1)} %get-tuple-element.63), channel_id=1, source_target_pairs={{0,6},{1,7},{2,0},{3,1},{4,2},{5,3},{6,4},{7,5},{8,14},{9,15},{10,... | collective-permute-start | bytes 491528 | tf_op jit(solution)/shard_map/ppermute | solution.py:376
  128.7 4.2 %copy-start.11 = (bf16[128,4096]{1,0:T(8,128)(2,1)S(1)}, bf16[128,4096]{1,0:T(8,128)(2,1)}, u32[]{:S(2)}) copy-start(bf16[128,4096]{1,0:T(8,128)(2,1)} %fresh.1) | copy-start | bytes 3145732

commit v4 on v3

--- a/solution.py
+++ b/solution.py
@@ -414,8 +414,8 @@
     return [(i, ((i // 2 + by) % 4) * 2 + i % 2) for i in range(8)]
 
 
-def split_ring(sign):
-    return [(i, ((i // 2 + (sign if i % 2 == 0 else -sign)) % 4) * 2 + i % 2) for i in range(8)]
+def split_ring(by):
+    return [(i, ((i // 2 + (by if i % 2 == 0 else -by)) % 4) * 2 + i % 2) for i in range(8)]
 
 
 def send(block, pairs):
@@ -431,8 +431,8 @@
     return [
         block(chip, core), block(chip, other),
         block(chip - step + 4, core), block(chip + step + 4, other),
+        block(chip + 2, core), block(chip + 2, other),
         block(chip + step + 4, core), block(chip - step + 4, other),
-        block(chip + 2, core), block(chip + 2, other),
     ]
 
 
@@ -454,28 +454,25 @@
     ahead, back = forward_adapter, backward_adapter
 
     out_own, val_own = output_matrix[0], value_projection[0]
-    out_near, out_away = send(out_own, split_ring(1)), send(out_own, split_ring(-1))
-    val_near, val_away = send(val_own, split_ring(1)), send(val_own, split_ring(-1))
+    out_one, val_one = send(out_own, split_ring(1)), send(val_own, split_ring(1))
     out_sibling, val_sibling = send(out_own, CORE), send(val_own, CORE)
 
     normed_f, _, low_f, normed_b, factor_b, low_b, normed_n, factor_n, low_n = prepare(
         ahead, back, where, rows, saved, gain, down
     )
-    out_near, normed_f = lax.optimization_barrier((out_near, normed_f))
-    out_far, val_far = send(out_near, split_ring(1)), send(val_near, split_ring(1))
-    outs = [
-        out_own, out_sibling, out_near, send(out_near, CORE), out_away, send(out_away, CORE)
-    ]
-    vals = [
-        val_own, val_sibling, val_near, send(val_near, CORE), val_away, send(val_away, CORE)
-    ]
+    out_one, normed_f, out_sibling, val_sibling = lax.optimization_barrier(
+        (out_one, normed_f, out_sibling, val_sibling)
+    )
+    out_two, val_two = send(out_one, split_ring(1)), send(val_one, split_ring(1))
+    out_far, val_far = send(out_two, split_ring(1)), send(val_two, split_ring(1))
+    outs = [out_own, out_sibling, out_one, send(out_one, CORE), out_two, send(out_two, CORE)]
+    vals = [val_own, val_sibling, val_one, send(val_one, CORE), val_two, send(val_two, CORE)]
     outs += [out_far, send(out_far, CORE)]
     d_values, d_low, kept, inner, share_f = near_share(
         back, where, grad, normed_f, saved, factor_b, gain, down, up, outs, vals
     )
     mine, other = pack(where, low_b, normed_b, d_values, d_low)
-    first_sums = pair_sum(mine, send(other, CORE))
-    val_far, first_sums = lax.optimization_barrier((val_far, first_sums))
+    val_far, mine = lax.optimization_barrier((val_far, mine))
     vals += [val_far, send(val_far, CORE)]
 
     first_back = first_gradient(
@@ -485,6 +482,9 @@
     share_f, first_back = lax.optimization_barrier((share_f, first_back))
     first_out = output(ahead, where, share_f, normed_f, low_f, up, rows, outs, vals)
     passed = lax.ppermute(first_out, "section", onward)
+    first_out, other = lax.optimization_barrier((first_out, other))
+    first_sums = pair_sum(mine, send(other, CORE))
+    relayed, first_sums = lax.optimization_barrier((relayed, first_sums))
 
     grad_n, d_values, d_low, mine, other = second_values(
         ahead, where, relayed, first_out, target, low_n, normed_n, up, outs

time: 141 us -> 143 us (1.014)
  waiting for transfers between devices: 58.1 us -> 63.4 us
  starting transfers between devices: 47.2 us -> 44.5 us
    ppermute x16, waiting for transfers between devices: 36 us -> 42.9 us  [send(): return lax.ppermute(block, 'dp', pairs)]
    ppermute x16, starting transfers between devices: 31.6 us -> 26.3 us  [send(): return lax.ppermute(block, 'dp', pairs)]
    ppermute x1, starting transfers between devices: 3.28 us -> 5.87 us  [spread(): lax.ppermute(two, 'dp', chips(2))]
    ppermute x1, waiting for transfers between devices: 22.2 us -> 20.4 us  [body(): relayed = lax.ppermute(first_back, 'section', before)]
where the time goes in v4:
time: 143 us; the launch traced here: 142 us
  waiting for transfers between devices  63.4 us (44%)
  starting transfers between devices  44.5 us (31%)
  Pallas kernels  26.8 us (19%)
  local copies, waits for them, and re-layouts  5.25 us (4%)
  between operations  2.12 us (1%)
    ppermute x16, waiting for transfers between devices, send(): return lax.ppermute(block, 'dp', pairs)  42.9 us
    pallas_call x11, Pallas kernels, call(): pl.pallas_call(kernel, out_shape=outs, grid_spec=pltpu.PrefetchScalarGrid...  26.8 us
    ppermute x16, starting transfers between devices, send(): return lax.ppermute(block, 'dp', pairs)  26.3 us
    ppermute x1, waiting for transfers between devices, body(): relayed = lax.ppermute(first_back, 'section', before)  20.4 us
    ppermute x1, starting transfers between devices, spread(): lax.ppermute(two, 'dp', chips(2))  5.87 us
    ppermute x1, starting transfers between devices, body(): passed = lax.ppermute(first_out, 'section', onward)  5.58 us
    unnamed x26, local copies, waits for them, and re-layouts  5.17 us
    ppermute x1, starting transfers between devices, spread(): lax.ppermute(three, 'dp', chips(3))  4.13 us
  transfers between devices with their start and end apart: 21, of which 9 were waited for; matrix products, arithmetic and copies ran while one was open for 0% of the time, Pallas kernels for 17%

profile of v4, /device:TPU:30, one launch (start us, length us, event | category | flops | bytes accessed | tf_op | source)
XLA Modules:
  0.0 142.1 jit_solution(3034730068045037217)
XLA Ops:
  0.6 3.3 %collective-permute-start = (bf16[512,512]{1,0:T(8,128)(2,1)}, bf16[512,512]{1,0:T(8,128)(2,1)S(1)}, u32[]{:S(2)}, u32[]{:S(2)}) collective-permute-start(bf16[512,512]{1,0:T(8,128)(2,1)} %bitcast.34), channel_id=1, source_target_pairs={{0,2},{1,7},{2,4},{3,1},{4,6},{5,3},{6,0},{7,5},{8,10},{9,15},{10,... | collective-permute-start | bytes 1572872 | tf_op jit(solution)/shard_map/ppermute | solution.py:422
  4.0 2.6 %collective-permute-start.1 = (bf16[512,512]{1,0:T(8,128)(2,1)}, bf16[512,512]{1,0:T(8,128)(2,1)S(1)}, u32[]{:S(2)}, u32[]{:S(2)}) collective-permute-start(bf16[512,512]{1,0:T(8,128)(2,1)} %bitcast.35), channel_id=1, source_target_pairs={{0,1},{1,0},{2,3},{3,2},{4,5},{5,4},{6,7},{7,6},{8,9},{9,8},{10,11... | collective-permute-start | bytes 1572872 | tf_op jit(solution)/shard_map/ppermute | solution.py:422
  6.6 0.0 collective-permute-start.2
  6.6 2.4 %collective-permute-start.8 = (bf16[512,512]{1,0:T(8,128)(2,1)}, bf16[512,512]{1,0:T(8,128)(2,1)S(1)}, u32[]{:S(2)}, u32[]{:S(2)}) collective-permute-start(bf16[512,512]{1,0:T(8,128)(2,1)} %bitcast.41), channel_id=1, source_target_pairs={{0,2},{1,7},{2,4},{3,1},{4,6},{5,3},{6,0},{7,5},{8,10},{9,15},{10,... | collective-permute-start | bytes 1572872 | tf_op jit(solution)/shard_map/ppermute | solution.py:422
  10.3 0.1 stack.51.where
  10.4 1.6 %copy-done = bf16[1,2,128,4096]{3,2,1,0:T(8,128)(2,1)S(1)} copy-done((bf16[1,2,128,4096]{3,2,1,0:T(8,128)(2,1)S(1)}, bf16[1,2,128,4096]{3,2,1,0:T(8,128)(2,1)}, u32[]{:S(2)}) %copy-start) | copy-done | bytes 2097176
  12.0 1.6 %copy-done.2 = bf16[1,4,4096,64]{2,3,1,0:T(8,128)(2,1)S(1)} copy-done((bf16[1,4,4096,64]{2,3,1,0:T(8,128)(2,1)S(1)}, bf16[1,4,4096,64]{2,3,1,0:T(8,128)(2,1)}, u32[]{:S(2)}) %copy-start.2) | copy-done | bytes 2097176
  13.5 1.2 copy-done.4
  14.8 0.7 copy-done.12
  15.5 0.0 copy-start.8
  15.5 0.0 copy-start.9
  15.5 4.1 %shard_map.147 = (bf16[128,4096]{1,0:T(8,128)(2,1)S(1)}, f32[128,128]{1,0:T(8,128)}, bf16[128,256]{1,0:T(8,128)(2,1)S(1)}, bf16[128,4096]{1,0:T(8,128)(2,1)S(1)}...) custom-call(s32[1]{0:T(128)S(6)} %copy.16.ahead, ...), custom_call_target="tpu_custom_call" | custom-call | flops 805306 | bytes 7356 | tf_op jit(solution)/shard_map/pallas_call | solution.py:52
  19.7 1.5 %collective-permute-start.4 = (bf16[512,512]{1,0:T(8,128)(2,1)S(1)}, bf16[512,512]{1,0:T(8,128)(2,1)S(1)}, u32[]{:S(2)}, u32[]{:S(2)}) collective-permute-start(bf16[512,512]{1,0:T(8,128)(2,1)S(1)} %collective-permute-done.refs_2_.refs_10_), channel_id=1, source_target_pairs={{0,2},{1,7},{2,4},{3,1},{4,6},{5,3},{6,0},{7,5},{8,10},{9,15},{10,... | collective-permute-start | bytes 1572872 | tf_op jit(solution)/shard_map/ppermute | solution.py:422
  21.2 3.2 %collective-permute-done.8.refs_10_.refs_2_ = bf16[512,512]{1,0:T(8,128)(2,1)S(1)} collective-permute-done((bf16[512,512]{1,0:T(8,128)(2,1)}, bf16[512,512]{1,0:T(8,128)(2,1)S(1)}, u32[]{:S(2)}, u32[]{:S(2)}) %collective-permute-start.8) | collective-permute-done | bytes 524320 | tf_op jit(solution)/shard_map/ppermute | solution.py:422
  24.5 6.4 %collective-permute-start.10 = (bf16[512,512]{1,0:T(8,128)(2,1)S(1)}, bf16[512,512]{1,0:T(8,128)(2,1)S(1)}, u32[]{:S(2)}, u32[]{:S(2)}) collective-permute-start(bf16[512,512]{1,0:T(8,128)(2,1)S(1)} %collective-permute-done.8.refs_10_.refs_2_), channel_id=1, source_target_pairs={{0,2},{1,7},{2,4},{3,1},{4,6},{5,3},{6,0},{7,5},{8,10},{9,15},{10,... | collective-permute-start | bytes 1572872 | tf_op jit(solution)/shard_map/ppermute | solution.py:422
  30.9 17.2 %collective-permute-done.4.refs_4_.refs_12_ = bf16[512,512]{1,0:T(8,128)(2,1)S(1)} collective-permute-done((bf16[512,512]{1,0:T(8,128)(2,1)S(1)}, bf16[512,512]{1,0:T(8,128)(2,1)S(1)}, u32[]{:S(2)}, u32[]{:S(2)}) %collective-permute-start.4) | collective-permute-done | bytes 524320 | tf_op jit(solution)/shard_map/ppermute | solution.py:422
  48.1 3.9 %collective-permute-start.6 = (bf16[512,512]{1,0:T(8,128)(2,1)S(1)}, bf16[512,512]{1,0:T(8,128)(2,1)S(1)}, u32[]{:S(2)}, u32[]{:S(2)}) collective-permute-start(bf16[512,512]{1,0:T(8,128)(2,1)S(1)} %collective-permute-done.4.refs_4_.refs_12_), channel_id=1, source_target_pairs={{0,2},{1,7},{2,4},{3,1},{4,6},{5,3},{6,0},{7,5},{8,10},{9,15},{10,... | collective-permute-start | bytes 1572872 | tf_op jit(solution)/shard_map/ppermute | solution.py:422
  51.9 0.0 collective-permute-start.3
  51.9 0.5 collective-permute-start.9
  52.5 7.9 %collective-permute-done.10.refs_12_.refs_4_ = bf16[512,512]{1,0:T(8,128)(2,1)S(1)} collective-permute-done((bf16[512,512]{1,0:T(8,128)(2,1)S(1)}, bf16[512,512]{1,0:T(8,128)(2,1)S(1)}, u32[]{:S(2)}, u32[]{:S(2)}) %collective-permute-start.10) | collective-permute-done | bytes 524320 | tf_op jit(solution)/shard_map/ppermute | solution.py:422
  60.3 0.0 collective-permute-start.11
  60.3 5.6 %collective-permute-done.6.refs_6_.refs_14_ = bf16[512,512]{1,0:T(8,128)(2,1)S(1)} collective-permute-done((bf16[512,512]{1,0:T(8,128)(2,1)S(1)}, bf16[512,512]{1,0:T(8,128)(2,1)S(1)}, u32[]{:S(2)}, u32[]{:S(2)}) %collective-permute-start.6) | collective-permute-done | bytes 524320 | tf_op jit(solution)/shard_map/ppermute | solution.py:422
  65.9 5.5 %collective-permute-start.12 = (bf16[512,512]{1,0:T(8,128)(2,1)S(1)}, bf16[512,512]{1,0:T(8,128)(2,1)S(1)}, u32[]{:S(2)}, u32[]{:S(2)}) collective-permute-start(bf16[512,512]{1,0:T(8,128)(2,1)S(1)} %collective-permute-done.10.refs_12_.refs_4_), channel_id=1, source_target_pairs={{0,2},{1,7},{2,4},{3,1},{4,6},{5,3},{6,0},{7,5},{8,10},{9,15},{10,... | collective-permute-start | bytes 1572872 | tf_op jit(solution)/shard_map/ppermute | solution.py:422
  71.5 0.0 collective-permute-done.7.refs_7_.refs_15_
  71.5 4.7 %shard_map.148 = (bf16[128,512]{1,0:T(8,128)(2,1)S(1)}, bf16[128,256]{1,0:T(8,128)(2,1)S(1)}, f32[6,128,512]{2,1,0:T(8,128)S(1)}, f32[128,128]{1,0:T(8,128)S(1)}, f32[128,512]{1,0:T(8,128)S(1)}) custom-call(s32[1]{0:T(128)S(6)} %copy.17.back, s32[10]{0:T(128)S(1)} %stack.51.where, bf16[128,4096]{1,0:T(8,128)(2,1)S(1)} %bitcast.49, ...), custom_call_target="tpu_custom_call" | custom-call | flops 1610612 | bytes 13975 | tf_op jit(solution)/shard_map/pallas_call | solution.py:52
  76.3 1.0 shard_map.149
  77.2 3.9 %collective-permute-done.12.far.refs_6_ = bf16[512,512]{1,0:T(8,128)(2,1)S(1)} collective-permute-done((bf16[512,512]{1,0:T(8,128)(2,1)S(1)}, bf16[512,512]{1,0:T(8,128)(2,1)S(1)}, u32[]{:S(2)}, u32[]{:S(2)}) %collective-permute-start.12) | collective-permute-done | bytes 524320 | tf_op jit(solution)/shard_map/ppermute | solution.py:422
  81.1 0.0 collective-permute-start.13
  81.1 1.9 %collective-permute-done.13.far_other.refs_7_ = bf16[512,512]{1,0:T(8,128)(2,1)S(1)} collective-permute-done((bf16[512,512]{1,0:T(8,128)(2,1)S(1)}, bf16[512,512]{1,0:T(8,128)(2,1)S(1)}, u32[]{:S(2)}, u32[]{:S(2)}) %collective-permute-start.13) | collective-permute-done | bytes 524320 | tf_op jit(solution)/shard_map/ppermute | solution.py:422
  83.0 1.8 %shard_map.150 = bf16[128,4224]{1,0:T(8,128)(2,1)S(1)} custom-call(s32[1]{0:T(128)S(6)} %copy.17.back, s32[10]{0:T(128)S(1)} %stack.51.where, f32[6,128,512]{2,1,0:T(8,128)S(1)} %get-tuple-element.48.kept, f32[128,128]{1,0:T(8,128)S(1)} %get-tuple-element.49.inner, bf16[128,512]{1,0:T(8,128)(2,1)S(1)} %get-tuple-element.50.d_values.values, ...), custom_call_target="tpu_custom_call" | custom-call | flops 268435 | bytes 8208 | tf_op jit(solution)/shard_map/pallas_call | solution.py:52
  84.8 2.7 %collective-permute-start.15 = (bf16[128,4224]{1,0:T(8,128)(2,1)S(1)}, bf16[128,4224]{1,0:T(8,128)(2,1)S(1)}, u32[]{:S(2)}, u32[]{:S(2)}) collective-permute-start(bf16[128,4224]{1,0:T(8,128)(2,1)S(1)} %shard_map.150), channel_id=1, source_target_pairs={{8,0},{16,8},{24,16},{32,24},{40,32},{48,40},{56,48},{64,56},{72,6... | collective-permute-start | bytes 3244040 | tf_op jit(solution)/shard_map/ppermute | solution.py:481
  87.4 0.0 copy-start.10
  87.5 1.6 %shard_map.151.out = bf16[128,4224]{1,0:T(8,128)(2,1)S(1)} custom-call(s32[1]{0:T(128)S(6)} %copy.16.ahead, s32[10]{0:T(128)S(1)} %stack.51.where, f32[128,512]{1,0:T(8,128)S(1)} %get-tuple-element.56.share, bf16[128,4096]{1,0:T(8,128)(2,1)S(1)} %get-tuple-element.42.normed, bf16[128,256]{1,0:T(8,128)(2,1)S(1)} %get-tuple-element.57.low, ...), custom_call_target="tpu_custom_call" | custom-call | flops 536870 | bytes 7929 | tf_op jit(solution)/shard_map/pallas_call | solution.py:52
  89.0 5.6 %collective-permute-start.14 = (bf16[128,4224]{1,0:T(8,128)(2,1)S(1)}, bf16[128,4224]{1,0:T(8,128)(2,1)S(1)}, u32[]{:S(2)}, u32[]{:S(2)}) collective-permute-start(bf16[128,4224]{1,0:T(8,128)(2,1)S(1)} %shard_map.151.out), channel_id=1, source_target_pairs={{0,8},{8,16},{16,24},{24,32},{32,40},{40,48},{48,56},{56,64},{64,7... | collective-permute-start | bytes 3244040 | tf_op jit(solution)/shard_map/ppermute | solution.py:484
  94.6 0.0 collective-permute-start.16
  94.6 1.6 %collective-permute-done.16.other = bf16[4,64,640]{2,1,0:T(8,128)(2,1)S(1)} collective-permute-done((bf16[4,64,640]{2,1,0:T(8,128)(2,1)S(1)}, bf16[4,64,640]{2,1,0:T(8,128)(2,1)S(1)}, u32[]{:S(2)}, u32[]{:S(2)}) %collective-permute-start.16) | collective-permute-done | bytes 327712 | tf_op jit(solution)/shard_map/ppermute | solution.py:422
  96.3 0.1 shard_map.153.first
  96.3 20.4 %collective-permute-done.15.relayed = bf16[128,4224]{1,0:T(8,128)(2,1)S(1)} collective-permute-done((bf16[128,4224]{1,0:T(8,128)(2,1)S(1)}, bf16[128,4224]{1,0:T(8,128)(2,1)S(1)}, u32[]{:S(2)}, u32[]{:S(2)}) %collective-permute-start.15) | collective-permute-done | bytes 1081376 | tf_op jit(solution)/shard_map/ppermute | solution.py:481
  116.8 2.6 %shard_map.154 = (bf16[128,4096]{1,0:T(8,128)(2,1)S(1)}, bf16[128,512]{1,0:T(8,128)(2,1)S(1)}, bf16[128,256]{1,0:T(8,128)(2,1)S(1)}, bf16[4,64,640]{2,1,0:T(8,128)(2,1)S(1)}, bf16[4,64,640]{2,1,0:T(8,128)(2,1)S(1)}) custom-call(s32[1]{0:T(128)S(6)} %copy.16.ahead, s32[10]{0:T(128)S(1)} %stack.51.where, ...), custom_call_target="tpu_custom_call" | custom-call | flops 603979 | bytes 8781 | tf_op jit(solution)/shard_map/pallas_call | solution.py:52
  119.4 0.1 collective-permute-start.17
  119.5 1.6 %collective-permute-done.17.other = bf16[4,64,640]{2,1,0:T(8,128)(2,1)S(1)} collective-permute-done((bf16[4,64,640]{2,1,0:T(8,128)(2,1)S(1)}, bf16[4,64,640]{2,1,0:T(8,128)(2,1)S(1)}, u32[]{:S(2)}, u32[]{:S(2)}) %collective-permute-start.17) | collective-permute-done | bytes 327712 | tf_op jit(solution)/shard_map/ppermute | solution.py:422
  121.2 0.1 shard_map.156
  121.3 5.9 %collective-permute-start.18 = (bf16[2,64,640]{2,1,0:T(8,128)(2,1)S(1)}, bf16[2,64,640]{2,1,0:T(8,128)(2,1)S(1)}, u32[]{:S(2)}, u32[]{:S(2)}) collective-permute-start(bf16[2,64,640]{2,1,0:T(8,128)(2,1)S(1)} %get-tuple-element.73), channel_id=1, source_target_pairs={{0,4},{1,5},{2,6},{3,7},{4,0},{5,1},{6,2},{7,3},{8,12},{9,13},{10,... | collective-permute-start | bytes 491528 | tf_op jit(solution)/shard_map/ppermute | solution.py:374
  127.1 0.0 collective-permute-start.19
  127.1 4.1 %collective-permute-start.20 = (bf16[2,64,640]{2,1,0:T(8,128)(2,1)S(1)}, bf16[2,64,640]{2,1,0:T(8,128)(2,1)S(1)}, u32[]{:S(2)}, u32[]{:S(2)}) collective-permute-start(bf16[2,64,640]{2,1,0:T(8,128)(2,1)S(1)} %get-tuple-element.75), channel_id=1, source_target_pairs={{0,6},{1,7},{2,0},{3,1},{4,2},{5,3},{6,4},{7,5},{8,14},{9,15},{10,... | collective-permute-start | bytes 491528 | tf_op jit(solution)/shard_map/ppermute | solution.py:376
  131.3 4.2 %shard_map.155 = bf16[128,4096]{1,0:T(8,128)(2,1)} custom-call(s32[10]{0:T(128)S(1)} %stack.51.where, bf16[128,4096]{1,0:T(8,128)(2,1)S(1)} %get-tuple-element.65.grad, bf16[128,4096]{1,0:T(8,128)(2,1)S(1)} %bitcast.33, bf16[1,2,128,4096]{3,2,1,0:T(8,128)(2,1)S(1)} %copy-done.1, f32[128,128]{1,0:T(8,128)S(1)} %get-tuple-element.66.factor, ...), custom_call_target="tpu_custom_call" | custom-call | flops 603979 | bytes 10764 | tf_op jit(solution)/shard_map/pallas_call | solution.py:52
  135.4 5.1 %shard_map.152 = bf16[128,4096]{1,0:T(8,128)(2,1)} custom-call(s32[10]{0:T(128)S(1)} %stack.51.where, bf16[128,4096]{1,0:T(8,128)(2,1)S(1)} %copy-done.11, bf16[128,4224]{1,0:T(8,128)(2,1)S(1)} %collective-permute-done.14.passed, f32[1,4096]{1,0:T(1,128)S(1)} %copy-done.12, bf16[256,4096]{1,0:T(8,128)(2,1)S(1)} %bitcast.30, bf16[256,512]{1,0:T(8,128)(2,1)S(1)} %bitcast.48, ...), custom_call_target="tpu_custom_call" | custom-call | flops 1073741 | bytes 12894 | tf_op jit(solution)/shard_map/pallas_call | solution.py:52
  140.6 1.5 %shard_map.157 = (f32[4,64,512]{2,1,0:T(8,128)}, f32[4,64,64]{2,1,0:T(8,128)}) custom-call(s32[1]{0:T(128)S(6)} %copy.16.ahead, s32[1]{0:T(128)S(6)} %copy.17.back, s32[10]{0:T(128)S(1)} %stack.51.where, bf16[128,4224]{1,0:T(8,128)(2,1)S(1)} %collective-permute-done.15.relayed, bf16[2,64,640]{2,1,0:T(8,128)(2,1)S(1)} %get-tuple-element.72.refs_0_, ...), custom_call_target="tpu_custom_call" | custom-call | bytes 1736 | tf_op jit(solution)/shard_map/pallas_call | solution.py:52
  (32 shorter events, 0.1 us)
Async XLA Ops:
  0.6 19.0 %collective-permute-start = (bf16[512,512]{1,0:T(8,128)(2,1)}, bf16[512,512]{1,0:T(8,128)(2,1)S(1)}, u32[]{:S(2)}, u32[]{:S(2)}) collective-permute-start(bf16[512,512]{1,0:T(8,128)(2,1)} %bitcast.34), channel_id=1, source_target_pairs={{0,2},{1,7},{2,4},{3,1},{4,6},{5,3},{6,0},{7,5},{8,10},{9,15},{10,... | collective-permute-start | bytes 1572872 | tf_op jit(solution)/shard_map/ppermute | solution.py:422
  4.0 15.7 %collective-permute-start.1 = (bf16[512,512]{1,0:T(8,128)(2,1)}, bf16[512,512]{1,0:T(8,128)(2,1)S(1)}, u32[]{:S(2)}, u32[]{:S(2)}) collective-permute-start(bf16[512,512]{1,0:T(8,128)(2,1)} %bitcast.35), channel_id=1, source_target_pairs={{0,1},{1,0},{2,3},{3,2},{4,5},{5,4},{6,7},{7,6},{8,9},{9,8},{10,11... | collective-permute-start | bytes 1572872 | tf_op jit(solution)/shard_map/ppermute | solution.py:422
  6.6 13.1 %collective-permute-start.2 = (bf16[512,512]{1,0:T(8,128)(2,1)}, bf16[512,512]{1,0:T(8,128)(2,1)S(1)}, u32[]{:S(2)}, u32[]{:S(2)}) collective-permute-start(bf16[512,512]{1,0:T(8,128)(2,1)} %bitcast.40), channel_id=1, source_target_pairs={{0,1},{1,0},{2,3},{3,2},{4,5},{5,4},{6,7},{7,6},{8,9},{9,8},{10,11... | collective-permute-start | bytes 1572872 | tf_op jit(solution)/shard_map/ppermute | solution.py:422
  6.6 17.9 %collective-permute-start.8 = (bf16[512,512]{1,0:T(8,128)(2,1)}, bf16[512,512]{1,0:T(8,128)(2,1)S(1)}, u32[]{:S(2)}, u32[]{:S(2)}) collective-permute-start(bf16[512,512]{1,0:T(8,128)(2,1)} %bitcast.41), channel_id=1, source_target_pairs={{0,2},{1,7},{2,4},{3,1},{4,6},{5,3},{6,0},{7,5},{8,10},{9,15},{10,... | collective-permute-start | bytes 1572872 | tf_op jit(solution)/shard_map/ppermute | solution.py:422
  10.4 1.6 %copy-start = (bf16[1,2,128,4096]{3,2,1,0:T(8,128)(2,1)S(1)}, bf16[1,2,128,4096]{3,2,1,0:T(8,128)(2,1)}, u32[]{:S(2)}) copy-start(bf16[1,2,128,4096]{3,2,1,0:T(8,128)(2,1)} %rows_s.3) | copy-start | bytes 6291460
  12.0 1.6 %copy-start.2 = (bf16[1,4,4096,64]{2,3,1,0:T(8,128)(2,1)S(1)}, bf16[1,4,4096,64]{2,3,1,0:T(8,128)(2,1)}, u32[]{:S(2)}) copy-start(bf16[1,4,4096,64]{2,3,1,0:T(8,128)(2,1)} %param.22) | copy-start | bytes 6291460
  13.5 1.2 copy-start.4
  14.8 0.7 copy-start.12
  15.5 56.0 %copy-start.1 = (bf16[1,2,128,4096]{3,2,1,0:T(8,128)(2,1)S(1)}, bf16[1,2,128,4096]{3,2,1,0:T(8,128)(2,1)}, u32[]{:S(2)}) copy-start(bf16[1,2,128,4096]{3,2,1,0:T(8,128)(2,1)} %rows_s.3) | copy-start | bytes 6291460
  15.5 56.0 %copy-start.3 = (bf16[1,4,4096,64]{2,3,1,0:T(8,128)(2,1)S(1)}, bf16[1,4,4096,64]{2,3,1,0:T(8,128)(2,1)}, u32[]{:S(2)}) copy-start(bf16[1,4,4096,64]{2,3,1,0:T(8,128)(2,1)} %param.22) | copy-start | bytes 6291460
  15.5 56.0 %copy-start.6 = (bf16[1,512,512]{2,1,0:T(8,128)(2,1)S(1)}, bf16[1,512,512]{2,1,0:T(8,128)(2,1)}, u32[]{:S(2)}) copy-start(bf16[1,512,512]{2,1,0:T(8,128)(2,1)} %param.20) | copy-start | bytes 1572868
  15.5 56.0 %copy-start.7 = (bf16[1,512,512]{2,1,0:T(8,128)(2,1)S(1)}, bf16[1,512,512]{2,1,0:T(8,128)(2,1)}, u32[]{:S(2)}) copy-start(bf16[1,512,512]{2,1,0:T(8,128)(2,1)} %param.19) | copy-start | bytes 1572868
  15.5 56.0 %copy-start.8 = (bf16[1,4,64,512]{3,2,1,0:T(8,128)(2,1)S(1)}, bf16[1,4,64,512]{3,2,1,0:T(8,128)(2,1)}, u32[]{:S(2)}) copy-start(bf16[1,4,64,512]{3,2,1,0:T(8,128)(2,1)} %param.23) | copy-start | bytes 786436
  15.5 56.0 %copy-start.9 = (bf16[1,128,4096]{2,1,0:T(8,128)(2,1)S(1)}, bf16[1,128,4096]{2,1,0:T(8,128)(2,1)}, u32[]{:S(2)}) copy-start(bf16[1,128,4096]{2,1,0:T(8,128)(2,1)} %param.13) | copy-start | bytes 3145732
  19.7 28.4 %collective-permute-start.4 = (bf16[512,512]{1,0:T(8,128)(2,1)S(1)}, bf16[512,512]{1,0:T(8,128)(2,1)S(1)}, u32[]{:S(2)}, u32[]{:S(2)}) collective-permute-start(bf16[512,512]{1,0:T(8,128)(2,1)S(1)} %collective-permute-done.refs_2_.refs_10_), channel_id=1, source_target_pairs={{0,2},{1,7},{2,4},{3,1},{4,6},{5,3},{6,0},{7,5},{8,10},{9,15},{10,... | collective-permute-start | bytes 1572872 | tf_op jit(solution)/shard_map/ppermute | solution.py:422
  24.5 35.8 %collective-permute-start.10 = (bf16[512,512]{1,0:T(8,128)(2,1)S(1)}, bf16[512,512]{1,0:T(8,128)(2,1)S(1)}, u32[]{:S(2)}, u32[]{:S(2)}) collective-permute-start(bf16[512,512]{1,0:T(8,128)(2,1)S(1)} %collective-permute-done.8.refs_10_.refs_2_), channel_id=1, source_target_pairs={{0,2},{1,7},{2,4},{3,1},{4,6},{5,3},{6,0},{7,5},{8,10},{9,15},{10,... | collective-permute-start | bytes 1572872 | tf_op jit(solution)/shard_map/ppermute | solution.py:422
  48.1 17.9 %collective-permute-start.6 = (bf16[512,512]{1,0:T(8,128)(2,1)S(1)}, bf16[512,512]{1,0:T(8,128)(2,1)S(1)}, u32[]{:S(2)}, u32[]{:S(2)}) collective-permute-start(bf16[512,512]{1,0:T(8,128)(2,1)S(1)} %collective-permute-done.4.refs_4_.refs_12_), channel_id=1, source_target_pairs={{0,2},{1,7},{2,4},{3,1},{4,6},{5,3},{6,0},{7,5},{8,10},{9,15},{10,... | collective-permute-start | bytes 1572872 | tf_op jit(solution)/shard_map/ppermute | solution.py:422
  51.9 14.0 %collective-permute-start.3 = (bf16[512,512]{1,0:T(8,128)(2,1)S(1)}, bf16[512,512]{1,0:T(8,128)(2,1)S(1)}, u32[]{:S(2)}, u32[]{:S(2)}) collective-permute-start(bf16[512,512]{1,0:T(8,128)(2,1)S(1)} %collective-permute-done.refs_2_.refs_10_), channel_id=1, source_target_pairs={{0,1},{1,0},{2,3},{3,2},{4,5},{5,4},{6,7},{7,6},{8,9},{9,8},{10,11... | collective-permute-start | bytes 1572872 | tf_op jit(solution)/shard_map/ppermute | solution.py:422
  51.9 19.5 %collective-permute-start.9 = (bf16[512,512]{1,0:T(8,128)(2,1)S(1)}, bf16[512,512]{1,0:T(8,128)(2,1)S(1)}, u32[]{:S(2)}, u32[]{:S(2)}) collective-permute-start(bf16[512,512]{1,0:T(8,128)(2,1)S(1)} %collective-permute-done.8.refs_10_.refs_2_), channel_id=1, source_target_pairs={{0,1},{1,0},{2,3},{3,2},{4,5},{5,4},{6,7},{7,6},{8,9},{9,8},{10,11... | collective-permute-start | bytes 1572872 | tf_op jit(solution)/shard_map/ppermute | solution.py:422
  52.5 19.0 %collective-permute-start.5 = (bf16[512,512]{1,0:T(8,128)(2,1)S(1)}, bf16[512,512]{1,0:T(8,128)(2,1)S(1)}, u32[]{:S(2)}, u32[]{:S(2)}) collective-permute-start(bf16[512,512]{1,0:T(8,128)(2,1)S(1)} %collective-permute-done.4.refs_4_.refs_12_), channel_id=1, source_target_pairs={{0,1},{1,0},{2,3},{3,2},{4,5},{5,4},{6,7},{7,6},{8,9},{9,8},{10,11... | collective-permute-start | bytes 1572872 | tf_op jit(solution)/shard_map/ppermute | solution.py:422
  60.3 11.1 %collective-permute-start.11 = (bf16[512,512]{1,0:T(8,128)(2,1)S(1)}, bf16[512,512]{1,0:T(8,128)(2,1)S(1)}, u32[]{:S(2)}, u32[]{:S(2)}) collective-permute-start(bf16[512,512]{1,0:T(8,128)(2,1)S(1)} %collective-permute-done.10.refs_12_.refs_4_), channel_id=1, source_target_pairs={{0,1},{1,0},{2,3},{3,2},{4,5},{5,4},{6,7},{7,6},{8,9},{9,8},{10,11... | collective-permute-start | bytes 1572872 | tf_op jit(solution)/shard_map/ppermute | solution.py:422
  65.9 5.5 %collective-permute-start.7 = (bf16[512,512]{1,0:T(8,128)(2,1)S(1)}, bf16[512,512]{1,0:T(8,128)(2,1)S(1)}, u32[]{:S(2)}, u32[]{:S(2)}) collective-permute-start(bf16[512,512]{1,0:T(8,128)(2,1)S(1)} %collective-permute-done.6.refs_6_.refs_14_), channel_id=1, source_target_pairs={{0,1},{1,0},{2,3},{3,2},{4,5},{5,4},{6,7},{7,6},{8,9},{9,8},{10,11... | collective-permute-start | bytes 1572872 | tf_op jit(solution)/shard_map/ppermute | solution.py:422
  65.9 15.1 %collective-permute-start.12 = (bf16[512,512]{1,0:T(8,128)(2,1)S(1)}, bf16[512,512]{1,0:T(8,128)(2,1)S(1)}, u32[]{:S(2)}, u32[]{:S(2)}) collective-permute-start(bf16[512,512]{1,0:T(8,128)(2,1)S(1)} %collective-permute-done.10.refs_12_.refs_4_), channel_id=1, source_target_pairs={{0,2},{1,7},{2,4},{3,1},{4,6},{5,3},{6,0},{7,5},{8,10},{9,15},{10,... | collective-permute-start | bytes 1572872 | tf_op jit(solution)/shard_map/ppermute | solution.py:422
  81.1 1.9 %collective-permute-start.13 = (bf16[512,512]{1,0:T(8,128)(2,1)S(1)}, bf16[512,512]{1,0:T(8,128)(2,1)S(1)}, u32[]{:S(2)}, u32[]{:S(2)}) collective-permute-start(bf16[512,512]{1,0:T(8,128)(2,1)S(1)} %collective-permute-done.12.far.refs_6_), channel_id=1, source_target_pairs={{0,1},{1,0},{2,3},{3,2},{4,5},{5,4},{6,7},{7,6},{8,9},{9,8},{10,11... | collective-permute-start | bytes 1572872 | tf_op jit(solution)/shard_map/ppermute | solution.py:422
  83.0 4.4 %copy-start.5 = (bf16[1,128,4096]{2,1,0:T(8,128)(2,1)S(1)}, bf16[1,128,4096]{2,1,0:T(8,128)(2,1)}, u32[]{:S(2)}) copy-start(bf16[1,128,4096]{2,1,0:T(8,128)(2,1)} %param.12) | copy-start | bytes 3145732
  84.8 32.0 %collective-permute-start.15 = (bf16[128,4224]{1,0:T(8,128)(2,1)S(1)}, bf16[128,4224]{1,0:T(8,128)(2,1)S(1)}, u32[]{:S(2)}, u32[]{:S(2)}) collective-permute-start(bf16[128,4224]{1,0:T(8,128)(2,1)S(1)} %shard_map.150), channel_id=1, source_target_pairs={{8,0},{16,8},{24,16},{32,24},{40,32},{48,40},{56,48},{64,56},{72,6... | collective-permute-start | bytes 3244040 | tf_op jit(solution)/shard_map/ppermute | solution.py:481
  87.4 29.3 %copy-start.10 = (bf16[128,4096]{1,0:T(8,128)(2,1)S(1)}, bf16[128,4096]{1,0:T(8,128)(2,1)}, u32[]{:S(2)}) copy-start(bf16[128,4096]{1,0:T(8,128)(2,1)} %target.1) | copy-start | bytes 3145732
  89.0 46.4 %collective-permute-start.14 = (bf16[128,4224]{1,0:T(8,128)(2,1)S(1)}, bf16[128,4224]{1,0:T(8,128)(2,1)S(1)}, u32[]{:S(2)}, u32[]{:S(2)}) collective-permute-start(bf16[128,4224]{1,0:T(8,128)(2,1)S(1)} %shard_map.151.out), channel_id=1, source_target_pairs={{0,8},{8,16},{16,24},{24,32},{32,40},{40,48},{48,56},{56,64},{64,7... | collective-permute-start | bytes 3244040 | tf_op jit(solution)/shard_map/ppermute | solution.py:484
  94.6 1.6 %collective-permute-start.16 = (bf16[4,64,640]{2,1,0:T(8,128)(2,1)S(1)}, bf16[4,64,640]{2,1,0:T(8,128)(2,1)S(1)}, u32[]{:S(2)}, u32[]{:S(2)}) collective-permute-start(bf16[4,64,640]{2,1,0:T(8,128)(2,1)S(1)} %get-tuple-element.60), channel_id=1, source_target_pairs={{0,1},{1,0},{2,3},{3,2},{4,5},{5,4},{6,7},{7,6},{8,9},{9,8},{10,11... | collective-permute-start | bytes 983048 | tf_op jit(solution)/shard_map/ppermute | solution.py:422
  119.4 1.7 %collective-permute-start.17 = (bf16[4,64,640]{2,1,0:T(8,128)(2,1)S(1)}, bf16[4,64,640]{2,1,0:T(8,128)(2,1)S(1)}, u32[]{:S(2)}, u32[]{:S(2)}) collective-permute-start(bf16[4,64,640]{2,1,0:T(8,128)(2,1)S(1)} %get-tuple-element.71), channel_id=1, source_target_pairs={{0,1},{1,0},{2,3},{3,2},{4,5},{5,4},{6,7},{7,6},{8,9},{9,8},{10,11... | collective-permute-start | bytes 983048 | tf_op jit(solution)/shard_map/ppermute | solution.py:422
  121.3 19.3 %collective-permute-start.18 = (bf16[2,64,640]{2,1,0:T(8,128)(2,1)S(1)}, bf16[2,64,640]{2,1,0:T(8,128)(2,1)S(1)}, u32[]{:S(2)}, u32[]{:S(2)}) collective-permute-start(bf16[2,64,640]{2,1,0:T(8,128)(2,1)S(1)} %get-tuple-element.73), channel_id=1, source_target_pairs={{0,4},{1,5},{2,6},{3,7},{4,0},{5,1},{6,2},{7,3},{8,12},{9,13},{10,... | collective-permute-start | bytes 491528 | tf_op jit(solution)/shard_map/ppermute | solution.py:374
  127.1 13.4 %collective-permute-start.19 = (bf16[2,64,640]{2,1,0:T(8,128)(2,1)S(1)}, bf16[2,64,640]{2,1,0:T(8,128)(2,1)S(1)}, u32[]{:S(2)}, u32[]{:S(2)}) collective-permute-start(bf16[2,64,640]{2,1,0:T(8,128)(2,1)S(1)} %get-tuple-element.74), channel_id=1, source_target_pairs={{0,2},{1,3},{2,4},{3,5},{4,6},{5,7},{6,0},{7,1},{8,10},{9,11},{10,... | collective-permute-start | bytes 491528 | tf_op jit(solution)/shard_map/ppermute | solution.py:375
  127.1 13.4 %collective-permute-start.20 = (bf16[2,64,640]{2,1,0:T(8,128)(2,1)S(1)}, bf16[2,64,640]{2,1,0:T(8,128)(2,1)S(1)}, u32[]{:S(2)}, u32[]{:S(2)}) collective-permute-start(bf16[2,64,640]{2,1,0:T(8,128)(2,1)S(1)} %get-tuple-element.75), channel_id=1, source_target_pairs={{0,6},{1,7},{2,0},{3,1},{4,2},{5,3},{6,4},{7,5},{8,14},{9,15},{10,... | collective-permute-start | bytes 491528 | tf_op jit(solution)/shard_map/ppermute | solution.py:376
  131.3 4.2 %copy-start.11 = (bf16[128,4096]{1,0:T(8,128)(2,1)S(1)}, bf16[128,4096]{1,0:T(8,128)(2,1)}, u32[]{:S(2)}) copy-start(bf16[128,4096]{1,0:T(8,128)(2,1)} %fresh.1) | copy-start | bytes 3145732

commit v5 on v2

--- a/solution.py
+++ b/solution.py
@@ -129,51 +129,48 @@
     )
 
 
-def near_kernel(where, grad, normed, *refs):
-    outs, vals, (gradients, values) = refs[:6], refs[6:12], refs[12:]
+def input_gradient(where, values, lowered, sums, low, grad, rows, scale, gain, down, blocks, out):
+    inner = jnp.sum(values.astype(F32) * sums, axis=-1, keepdims=True)
+    inner += jnp.sum(lowered.astype(F32) * low.astype(F32), axis=-1, keepdims=True)
+    weight = scale * scale * inner * (1.0 / WIDTH)
+    for i in range(8):
+        span = columns(where[i])
+        gained = (dot_t(values, blocks[i][...]) + dot(lowered, down[:, span])) * gain[:, span]
+        out[:, span] = (
+            grad[:, span].astype(F32) + scale * gained - weight * rows(span).astype(F32)
+        ).astype(BF)
+
+
+def near_kernel(where, grad, normed_f, normed_b, *refs):
+    outs, vals, results = refs[:6], refs[6:12], refs[12:]
     total = jnp.zeros((ROWS, VALUES), F32)
     for i in range(6):
         total += dot_t(grad[:, columns(where[i])], outs[i][...])
-    gradients[...] = total
-    total = jnp.zeros((ROWS, VALUES), F32)
-    for i in range(6):
-        total += dot(normed[:, columns(where[i])], vals[i][...])
-    values[...] = total
-
-
-def near_share(where, grad, normed, outs, vals):
+    results[0][...] = total
+    for normed, result in ((normed_f, results[1]), (normed_b, results[2])):
+        total = jnp.zeros((ROWS, VALUES), F32)
+        for i in range(6):
+            total += dot(normed[:, columns(where[i])], vals[i][...])
+        result[...] = total
+
+
+def near_share(where, grad, normed_f, normed_b, outs, vals):
     return call(
         near_kernel,
         (where,),
-        [grad, normed, *outs, *vals],
-        [shape((ROWS, VALUES), F32)] * 2,
-        4 * ROWS * WIDTH * VALUES,
-    )
-
-
-def input_gradient(where, values, lowered, grad, rows, gain, down, scale, blocks, kept, out):
-    inner = jnp.zeros((ROWS, 1), F32)
-    for i in range(8):
-        span = columns(where[i])
-        gained = (
-            dot_t(values, blocks[i][...]) + dot(lowered, down[:, span])
-        ) * gain[:, span]
-        kept[i] = gained
-        pre = rows(span).astype(F32) * scale
-        inner += jnp.sum(gained * pre, axis=-1, keepdims=True)
-    inner = inner * (1.0 / WIDTH)
-    for i in range(8):
-        span = columns(where[i])
-        pre = rows(span).astype(F32) * scale
-        out[:, span] = (
-            grad[:, span].astype(F32) + scale * (kept[i] - pre * inner)
-        ).astype(BF)
+        [grad, normed_f, normed_b, *outs, *vals],
+        [shape((ROWS, VALUES), F32)] * 3,
+        6 * ROWS * WIDTH * VALUES,
+    )
+
+
+GRADS = [shape((ROWS, VALUES), BF), shape((ROWS, LOWS), BF)]
 
 
 def first_kernel(
-    back, where, share, grad, rows, factor, gain, down, up, far, far_other, *refs
+    back, where, share, sums, grad, normed, low, rows, factor, gain, down, up, far, far_other, *refs
 ):
-    blocks, (out, d_values, d_low, kept) = refs[:8], refs[8:]
+    blocks, (out, d_values, d_low) = refs[:8], refs[8:]
     total = share[...]
     total += dot_t(grad[:, columns(where[6])], far[...])
     total += dot_t(grad[:, columns(where[7])], far_other[...])
@@ -181,26 +178,44 @@
     lowered = only(SCALE * dot_t(values, up[...]), back[0]).astype(BF)
     d_values[...] = values
     d_low[...] = lowered
+    total = sums[...]
+    for i in (6, 7):
+        total += dot(normed[:, columns(where[i])], blocks[i][...])
     input_gradient(
-        where, values, lowered, grad, lambda span: rows[0, 0, :, span], gain, down,
-        factor[:, :1], blocks, kept, out,
+        where, values, lowered, total, low[...], grad, lambda span: rows[0, 0, :, span],
+        factor[:, :1], gain, down, blocks, out,
     )
     out[:, WIDTH:] = jnp.full((ROWS, 128), back[0], jnp.int32).astype(F32).astype(BF)
 
 
-KEPT = [pltpu.VMEM((8, ROWS, PART), F32)]
-GRADS = [shape((ROWS, VALUES), BF), shape((ROWS, LOWS), BF)]
-
-
-def first_gradient(back, where, share, grad, saved, factor, gain, down, up, outs, vals):
+def first_gradient(
+    back, where, share, sums, grad, normed, low, saved, factor, gain, down, up, outs, vals
+):
     return call(
         first_kernel,
         (back, where),
-        [share, grad, saved_of(saved, 0), factor, gain, down, up, *outs[6:], *vals],
+        [
+            share, sums, grad, normed, low, saved_of(saved, 0), factor, gain, down, up,
+            *outs[6:], *vals,
+        ],
         [shape((ROWS, WIDE), BF), *GRADS],
         2 * ROWS * WIDTH * VALUES,
-        KEPT,
-    )
+    )
+
+
+def project_kernel(where, normed, *refs):
+    blocks, out = refs[:8], refs[8]
+    total = jnp.zeros((ROWS, VALUES), F32)
+    for i in range(8):
+        total += dot(normed[:, columns(where[i])], blocks[i][...])
+    out[...] = total
+
+
+def project(where, normed, vals):
+    return call(
+        project_kernel, (where,), [normed, *vals], [shape((ROWS, VALUES), F32)],
+        2 * ROWS * WIDTH * VALUES,
+    )[0]
 
 
 def output_kernel(ahead, where, share, normed, low, up, rows, far, far_other, *refs):
@@ -285,28 +300,31 @@
     )
 
 
-def second_input_kernel(where, grad, rows_f, rows_s, factor, gain, down, d_values, d_low, *refs):
-    blocks, (out, kept) = refs[:8], refs[8:]
+def second_input_kernel(
+    where, sums, low, grad, rows_f, rows_s, factor, gain, down, d_values, d_low, *refs
+):
+    blocks, out = refs[:8], refs[8]
     last = where[9] == 1
     input_gradient(
-        where, d_values[...], d_low[...], grad,
+        where, d_values[...], d_low[...], sums[...], low[...], grad,
         lambda span: jnp.where(last, rows_f[:, span], rows_s[0, 0, :, span]),
-        gain, down, factor[:, :1], blocks, kept, out,
-    )
-
-
-def second_input(where, grad, rows, saved, factor, gain, down, d_values, d_low, blocks):
+        factor[:, :1], gain, down, blocks, out,
+    )
+
+
+def second_input(where, sums, low, grad, rows, saved, factor, gain, down, d_values, d_low, blocks):
     return call(
         second_input_kernel,
         (where,),
-        [grad, rows, saved_of(saved, 1), factor, gain, down, d_values, d_low, *blocks],
+        [
+            sums, low, grad, rows, saved_of(saved, 1), factor, gain, down, d_values, d_low, *blocks
+        ],
         [shape((ROWS, WIDTH), BF)],
         2 * ROWS * WIDTH * (VALUES + RANK),
-        KEPT,
     )[0]
 
 
-def forward_kernel(where, fresh, passed, gain, down, up, *refs):
+def forward_kernel(wrapped, where, fresh, passed, gain, down, up, *refs):
     vals, outs, (out, rows, normed) = refs[:8], refs[8:16], refs[16:]
     first = where[8] == 1
     for top in range(0, ROWS, 32):
@@ -315,7 +333,8 @@
         whole = chosen.astype(F32)
         rows[part, :] = chosen
         normed[part, :] = (whole * factor_of(whole) * gain[...]).astype(BF)
-    ident = passed[:, WIDTH : WIDTH + 1].astype(F32).astype(jnp.int32)
+    came = passed[:, WIDTH : WIDTH + 1].astype(F32).astype(jnp.int32)
+    ident = jnp.where(first, wrapped[0], came)
     low = only(dot_t(normed[...], down[...]), ident).astype(BF)
     total = SCALE * dot(low, up[...])
     for i in range(8):
@@ -326,10 +345,10 @@
         out[:, span] = (rows[:, span].astype(F32) + dot(values, outs[i][...])).astype(BF)
 
 
-def forward(where, fresh, passed, gain, down, up, vals, outs):
+def forward(wrapped, where, fresh, passed, gain, down, up, vals, outs):
     return call(
         forward_kernel,
-        (where,),
+        (wrapped, where),
         [fresh, passed, gain, down, up, *vals, *outs],
         [shape((ROWS, WIDTH), BF)],
         4 * ROWS * WIDTH * VALUES,
@@ -390,8 +409,8 @@
     return [(i, ((i // 2 + by) % 4) * 2 + i % 2) for i in range(8)]
 
 
-def split_ring(sign):
-    return [(i, ((i // 2 + (sign if i % 2 == 0 else -sign)) % 4) * 2 + i % 2) for i in range(8)]
+def split_ring(by):
+    return [(i, ((i // 2 + (by if i % 2 == 0 else -by)) % 4) * 2 + i % 2) for i in range(8)]
 
 
 def send(block, pairs):
@@ -407,8 +426,8 @@
     return [
         block(chip, core), block(chip, other),
         block(chip - step + 4, core), block(chip + step + 4, other),
+        block(chip + 2, core), block(chip + 2, other),
         block(chip + step + 4, core), block(chip - step + 4, other),
-        block(chip + 2, core), block(chip + 2, other),
     ]
 
 
@@ -417,7 +436,7 @@
     value_projection, output_matrix, norm_gain_frozen, adapter_down, adapter_up,
 ):
     count = lax.axis_size("section")
-    onward = [(i, (i + 1) % count) for i in range(count)]
+    onward = [(i, i + 1) for i in range(count - 1)]
     before = [(i, i - 1) for i in range(1, count)]
     position = lax.axis_index("section")
     where = jnp.stack(
@@ -430,47 +449,47 @@
     ahead, back = forward_adapter, backward_adapter
 
     out_own, val_own = output_matrix[0], value_projection[0]
-    out_near, out_away = send(out_own, split_ring(1)), send(out_own, split_ring(-1))
-    val_near, val_away = send(val_own, split_ring(1)), send(val_own, split_ring(-1))
+    wrapped = lax.ppermute(ahead, "section", [(count - 1, 0)])
+    out_one, val_one = send(out_own, split_ring(1)), send(val_own, split_ring(1))
     out_sibling, val_sibling = send(out_own, CORE), send(val_own, CORE)
 
     normed_f, _, low_f, normed_b, factor_b, low_b, normed_n, factor_n, low_n = prepare(
         ahead, back, where, rows, saved, gain, down
     )
-    out_near, normed_f = lax.optimization_barrier((out_near, normed_f))
-    out_far, val_far = send(out_near, split_ring(1)), send(val_near, split_ring(1))
-    outs = [
-        out_own, out_sibling, out_near, send(out_near, CORE), out_away, send(out_away, CORE)
-    ]
-    vals = [
-        val_own, val_sibling, val_near, send(val_near, CORE), val_away, send(val_away, CORE)
-    ]
-    share_b, share_f = near_share(where, grad, normed_f, outs, vals)
+    out_one, normed_f, out_sibling, val_sibling, wrapped = lax.optimization_barrier(
+        (out_one, normed_f, out_sibling, val_sibling, wrapped)
+    )
+    out_two, val_two = send(out_one, split_ring(1)), send(val_one, split_ring(1))
+    out_far, val_far = send(out_two, split_ring(1)), send(val_two, split_ring(1))
+    outs = [out_own, out_sibling, out_one, send(out_one, CORE), out_two, send(out_two, CORE)]
+    vals = [val_own, val_sibling, val_one, send(val_one, CORE), val_two, send(val_two, CORE)]
+    share_b, share_f, sums_b = near_share(where, grad, normed_f, normed_b, outs, vals)
     out_far, val_far, share_b = lax.optimization_barrier((out_far, val_far, share_b))
     outs += [out_far, send(out_far, CORE)]
     vals += [val_far, send(val_far, CORE)]
 
     first_back, d_values, d_low = first_gradient(
-        back, where, share_b, grad, saved, factor_b, gain, down, up, outs, vals
+        back, where, share_b, sums_b, grad, normed_b, low_b, saved, factor_b, gain, down, up,
+        outs, vals,
     )
     relayed = lax.ppermute(first_back, "section", before)
-    share_f, d_values = lax.optimization_barrier((share_f, d_values))
+    share_f, first_back = lax.optimization_barrier((share_f, first_back))
     first_out = output(ahead, where, share_f, normed_f, low_f, up, rows, outs, vals)
     passed = lax.ppermute(first_out, "section", onward)
-    d_low, first_out = lax.optimization_barrier((d_low, first_out))
+    first_out, d_low, normed_n = lax.optimization_barrier((first_out, d_low, normed_n))
     mine, other = pack(where, low_b, normed_b, d_values, d_low)
     first_terms = spread(mine, send(other, CORE))
-    relayed, *first_terms = lax.optimization_barrier((relayed, *first_terms))
+    sums_n = project(where, normed_n, vals)
+    relayed, sums_n, *first_terms = lax.optimization_barrier((relayed, sums_n, *first_terms))
 
     grad_n, d_values, d_low, mine, other = second_values(
         ahead, where, relayed, first_out, target, low_n, normed_n, up, outs
     )
-    received = send(other, CORE)
-    second_terms = spread(mine, received)
+    second_terms = spread(mine, send(other, CORE))
     bwd_out = second_input(
-        where, grad_n, rows, saved, factor_n, gain, down, d_values, d_low, vals
-    )
-    fwd_out = forward(where, fresh, passed, gain, down, up, vals, outs)
+        where, sums_n, low_n, grad_n, rows, saved, factor_n, gain, down, d_values, d_low, vals
+    )
+    fwd_out = forward(wrapped, where, fresh, passed, gain, down, up, vals, outs)
     down_table, up_table = tables(ahead, back, where, relayed, (*first_terms, *second_terms))
     return (
         fwd_out[None], bwd_out[None], jnp.swapaxes(down_table, 1, 2)[None], up_table[None]

time: 153 us -> 157 us (1.026)
  waiting for transfers between devices: 53.3 us -> 71.2 us
  starting transfers between devices: 65.9 us -> 50.9 us
    ppermute x16, waiting for transfers between devices: 30.6 us -> 48.1 us  [send(): return lax.ppermute(block, 'dp', pairs)]
    ppermute x16, starting transfers between devices: 43.7 us -> 26.3 us  [send(): return lax.ppermute(block, 'dp', pairs)]
    ppermute x1, starting transfers between devices: 5.58 us -> 8.14 us  [body(): passed = lax.ppermute(first_out, 'section', onward)]
    pallas_call x11 -> x12, Pallas kernels: 26.1 us -> 27.5 us  [call(): pl.pallas_call(kernel, out_shape=outs, grid_spec=pltpu.PrefetchScalarGrid...]
  transfers between devices with their start and end apart: 24 -> 25, of which waited for: 9 -> 10; matrix products, arithmetic and copies ran while one was open for 0% -> 0% of each run, Pallas kernels for 14% -> 14%
where the time goes in v5:
time: 157 us
  waiting for transfers between devices  71.2 us (45%)
  starting transfers between devices  50.9 us (32%)
  Pallas kernels  27.5 us (18%)
  local copies, waits for them, and re-layouts  5.26 us (3%)
  between operations  2.15 us (1%)
    ppermute x16, waiting for transfers between devices, send(): return lax.ppermute(block, 'dp', pairs)  48.1 us
    pallas_call x12, Pallas kernels, call(): pl.pallas_call(kernel, out_shape=outs, grid_spec=pltpu.PrefetchScalarGrid...  27.5 us
    ppermute x16, starting transfers between devices, send(): return lax.ppermute(block, 'dp', pairs)  26.3 us
    ppermute x2, waiting for transfers between devices, spread(): lax.ppermute(two, 'dp', chips(2))  23.1 us
    ppermute x1, starting transfers between devices, body(): passed = lax.ppermute(first_out, 'section', onward)  8.14 us
    ppermute x2, starting transfers between devices, spread(): lax.ppermute(three, 'dp', chips(3))  5.76 us
    unnamed x26, local copies, waits for them, and re-layouts  5.17 us
    ppermute x2, starting transfers between devices, spread(): lax.ppermute(two, 'dp', chips(2))  5.09 us
  transfers between devices with their start and end apart: 25, of which 10 were waited for; matrix products, arithmetic and copies ran while one was open for 0% of the time, Pallas kernels for 14%

profile of v5, /device:TPU:30, one launch (start us, length us, event | category | flops | bytes accessed | tf_op | source)
XLA Modules:
  0.0 157.0 jit_solution(9934875026977419609)
XLA Ops:
  0.6 0.1 collective-permute-start.2
  0.7 3.3 %collective-permute-start = (bf16[512,512]{1,0:T(8,128)(2,1)}, bf16[512,512]{1,0:T(8,128)(2,1)S(1)}, u32[]{:S(2)}, u32[]{:S(2)}) collective-permute-start(bf16[512,512]{1,0:T(8,128)(2,1)} %bitcast.40), channel_id=1, source_target_pairs={{0,2},{1,7},{2,4},{3,1},{4,6},{5,3},{6,0},{7,5},{8,10},{9,15},{10,... | collective-permute-start | bytes 1572872 | tf_op jit(solution)/shard_map/ppermute | solution.py:417
  4.1 3.2 %collective-permute-start.1 = (bf16[512,512]{1,0:T(8,128)(2,1)}, bf16[512,512]{1,0:T(8,128)(2,1)S(1)}, u32[]{:S(2)}, u32[]{:S(2)}) collective-permute-start(bf16[512,512]{1,0:T(8,128)(2,1)} %bitcast.41), channel_id=1, source_target_pairs={{0,1},{1,0},{2,3},{3,2},{4,5},{5,4},{6,7},{7,6},{8,9},{9,8},{10,11... | collective-permute-start | bytes 1572872 | tf_op jit(solution)/shard_map/ppermute | solution.py:417
  7.2 1.3 collective-permute-start.7
  8.6 1.2 collective-permute-start.3
  11.1 0.1 stack.51.where
  11.2 1.6 %copy-done = bf16[1,2,128,4096]{3,2,1,0:T(8,128)(2,1)S(1)} copy-done((bf16[1,2,128,4096]{3,2,1,0:T(8,128)(2,1)S(1)}, bf16[1,2,128,4096]{3,2,1,0:T(8,128)(2,1)}, u32[]{:S(2)}) %copy-start) | copy-done | bytes 2097176
  12.8 1.6 %copy-done.2 = bf16[1,4,4096,64]{2,3,1,0:T(8,128)(2,1)S(1)} copy-done((bf16[1,4,4096,64]{2,3,1,0:T(8,128)(2,1)S(1)}, bf16[1,4,4096,64]{2,3,1,0:T(8,128)(2,1)}, u32[]{:S(2)}) %copy-start.2) | copy-done | bytes 2097176
  14.4 1.2 copy-done.5
  15.6 0.7 copy-done.12
  16.3 4.1 %shard_map.147 = (bf16[128,4096]{1,0:T(8,128)(2,1)S(1)}, f32[128,128]{1,0:T(8,128)}, bf16[128,256]{1,0:T(8,128)(2,1)S(1)}, bf16[128,4096]{1,0:T(8,128)(2,1)S(1)}...) custom-call(s32[1]{0:T(128)S(6)} %copy.16.ahead, ...), custom_call_target="tpu_custom_call" | custom-call | flops 805306 | bytes 7356 | tf_op jit(solution)/shard_map/pallas_call | solution.py:52
  20.5 1.5 collective-permute-start.5
  22.0 2.6 %collective-permute-done.7.refs_8_.refs_2_ = bf16[512,512]{1,0:T(8,128)(2,1)S(1)} collective-permute-done((bf16[512,512]{1,0:T(8,128)(2,1)}, bf16[512,512]{1,0:T(8,128)(2,1)S(1)}, u32[]{:S(2)}, u32[]{:S(2)}) %collective-permute-start.7) | collective-permute-done | bytes 524320 | tf_op jit(solution)/shard_map/ppermute | solution.py:417
  24.6 11.4 %collective-permute-start.9 = (bf16[512,512]{1,0:T(8,128)(2,1)S(1)}, bf16[512,512]{1,0:T(8,128)(2,1)S(1)}, u32[]{:S(2)}, u32[]{:S(2)}) collective-permute-start(bf16[512,512]{1,0:T(8,128)(2,1)S(1)} %collective-permute-done.7.refs_8_.refs_2_), channel_id=1, source_target_pairs={{0,2},{1,7},{2,4},{3,1},{4,6},{5,3},{6,0},{7,5},{8,10},{9,15},{10,... | collective-permute-start | bytes 1572872 | tf_op jit(solution)/shard_map/ppermute | solution.py:417
  36.0 0.5 collective-permute-start.8
  36.5 13.0 %collective-permute-done.5.refs_4_.refs_12_ = bf16[512,512]{1,0:T(8,128)(2,1)S(1)} collective-permute-done((bf16[512,512]{1,0:T(8,128)(2,1)S(1)}, bf16[512,512]{1,0:T(8,128)(2,1)S(1)}, u32[]{:S(2)}, u32[]{:S(2)}) %collective-permute-start.5) | collective-permute-done | bytes 524320 | tf_op jit(solution)/shard_map/ppermute | solution.py:417
  49.5 5.6 %collective-permute-done.9.refs_10_.refs_4_ = bf16[512,512]{1,0:T(8,128)(2,1)S(1)} collective-permute-done((bf16[512,512]{1,0:T(8,128)(2,1)S(1)}, bf16[512,512]{1,0:T(8,128)(2,1)S(1)}, u32[]{:S(2)}, u32[]{:S(2)}) %collective-permute-start.9) | collective-permute-done | bytes 524320 | tf_op jit(solution)/shard_map/ppermute | solution.py:417
  55.1 0.2 collective-permute-start.11
  55.3 4.0 %collective-permute-start.12 = (bf16[512,512]{1,0:T(8,128)(2,1)S(1)}, bf16[512,512]{1,0:T(8,128)(2,1)S(1)}, u32[]{:S(2)}, u32[]{:S(2)}) collective-permute-start(bf16[512,512]{1,0:T(8,128)(2,1)S(1)} %collective-permute-done.9.refs_10_.refs_4_), channel_id=1, source_target_pairs={{0,2},{1,7},{2,4},{3,1},{4,6},{5,3},{6,0},{7,5},{8,10},{9,15},{10,... | collective-permute-start | bytes 1572872 | tf_op jit(solution)/shard_map/ppermute | solution.py:417
  59.3 0.0 copy-start.1
  59.4 2.5 %shard_map.148 = (f32[128,512]{1,0:T(8,128)S(1)}, f32[128,512]{1,0:T(8,128)S(1)}, f32[128,512]{1,0:T(8,128)S(1)}) custom-call(s32[10]{0:T(128)S(1)} %stack.51.where, bf16[128,4096]{1,0:T(8,128)(2,1)S(1)} %bitcast.46, bf16[128,4096]{1,0:T(8,128)(2,1)S(1)} %get-tuple-element.55.normed_f.normed, bf16[128,4096]{1,0:T(8,128)(2,1)S(1)} %get-tuple-element.56.normed_b.normed, ...), custom_call_target="tpu_custom_call" | custom-call | flops 1610612 | bytes 9437 | tf_op jit(solution)/shard_map/pallas_call | solution.py:52
  61.9 8.6 %collective-permute-done.11.far.refs_6_.refs_14_ = bf16[512,512]{1,0:T(8,128)(2,1)S(1)} collective-permute-done((bf16[512,512]{1,0:T(8,128)(2,1)S(1)}, bf16[512,512]{1,0:T(8,128)(2,1)S(1)}, u32[]{:S(2)}, u32[]{:S(2)}) %collective-permute-start.11) | collective-permute-done | bytes 524320 | tf_op jit(solution)/shard_map/ppermute | solution.py:417
  70.6 12.9 %collective-permute-done.12.refs_6_.far = bf16[512,512]{1,0:T(8,128)(2,1)S(1)} collective-permute-done((bf16[512,512]{1,0:T(8,128)(2,1)S(1)}, bf16[512,512]{1,0:T(8,128)(2,1)S(1)}, u32[]{:S(2)}, u32[]{:S(2)}) %collective-permute-start.12) | collective-permute-done | bytes 524320 | tf_op jit(solution)/shard_map/ppermute | solution.py:417
  83.4 0.5 collective-permute-start.14
  83.9 1.4 collective-permute-done.13.far_other.refs_7_.refs_15_
  85.3 0.7 collective-permute-done.14.refs_7_.far_other
  86.1 3.3 %shard_map.149 = (bf16[128,4224]{1,0:T(8,128)(2,1)S(1)}, bf16[128,512]{1,0:T(8,128)(2,1)S(1)}, bf16[128,256]{1,0:T(8,128)(2,1)S(1)}) custom-call(s32[1]{0:T(128)S(6)} %copy.17.back, s32[10]{0:T(128)S(1)} %stack.51.where, f32[128,512]{1,0:T(8,128)S(1)} %get-tuple-element.62.share, f32[128,512]{1,0:T(8,128)S(1)} %get-tuple-element.63.sums, ...), custom_call_target="tpu_custom_call" | custom-call | flops 536870 | bytes 12468 | tf_op jit(solution)/shard_map/pallas_call | solution.py:52
  89.4 1.9 %collective-permute-start.16 = (bf16[128,4224]{1,0:T(8,128)(2,1)S(1)}, bf16[128,4224]{1,0:T(8,128)(2,1)S(1)}, u32[]{:S(2)}, u32[]{:S(2)}) collective-permute-start(bf16[128,4224]{1,0:T(8,128)(2,1)S(1)} %get-tuple-element.68), channel_id=1, source_target_pairs={{8,0},{16,8},{24,16},{32,24},{40,32},{48,40},{56,48},{64,56},{72,6... | collective-permute-start | bytes 3244040 | tf_op jit(solution)/shard_map/ppermute | solution.py:475
  91.4 1.6 %shard_map.150.out = bf16[128,4224]{1,0:T(8,128)(2,1)S(1)} custom-call(s32[1]{0:T(128)S(6)} %copy.16.ahead, s32[10]{0:T(128)S(1)} %stack.51.where, f32[128,512]{1,0:T(8,128)S(1)} %get-tuple-element.69.share, bf16[128,4096]{1,0:T(8,128)(2,1)S(1)} %get-tuple-element.55.normed_f.normed, bf16[128,256]{1,0:T(8,128)(2,1)S(1)} %get-tuple-element.70.low, ...), custom_call_target="tpu_custom_call" | custom-call | flops 536870 | bytes 7929 | tf_op jit(solution)/shard_map/pallas_call | solution.py:52
  93.0 8.1 %collective-permute-start.15 = (bf16[128,4224]{1,0:T(8,128)(2,1)S(1)}, bf16[128,4224]{1,0:T(8,128)(2,1)S(1)}, u32[]{:S(2)}, u32[]{:S(2)}) collective-permute-start(bf16[128,4224]{1,0:T(8,128)(2,1)S(1)} %shard_map.150.out), channel_id=1, source_target_pairs={{0,8},{8,16},{16,24},{24,32},{32,40},{40,48},{48,56},{56,64},{64,7... | collective-permute-start | bytes 3244040 | tf_op jit(solution)/shard_map/ppermute | solution.py:478
  101.1 1.0 shard_map.153
  102.1 0.1 collective-permute-start.17
  102.2 1.6 %collective-permute-done.17.other = bf16[4,64,640]{2,1,0:T(8,128)(2,1)S(1)} collective-permute-done((bf16[4,64,640]{2,1,0:T(8,128)(2,1)S(1)}, bf16[4,64,640]{2,1,0:T(8,128)(2,1)S(1)}, u32[]{:S(2)}, u32[]{:S(2)}) %collective-permute-start.17) | collective-permute-done | bytes 327712 | tf_op jit(solution)/shard_map/ppermute | solution.py:417
  103.8 0.1 shard_map.154
  103.9 3.6 %collective-permute-start.18 = (bf16[64,640]{1,0:T(8,128)(2,1)S(1)}, bf16[64,640]{1,0:T(8,128)(2,1)S(1)}, u32[]{:S(2)}, u32[]{:S(2)}) collective-permute-start(bf16[64,640]{1,0:T(8,128)(2,1)S(1)} %get-tuple-element.79), channel_id=1, source_target_pairs={{0,4},{1,5},{2,6},{3,7},{4,0},{5,1},{6,2},{7,3},{8,12},{9,13},{10,... | collective-permute-start | bytes 245768 | tf_op jit(solution)/shard_map/ppermute | solution.py:369
  107.5 4.1 %collective-permute-start.20 = (bf16[64,640]{1,0:T(8,128)(2,1)S(1)}, bf16[64,640]{1,0:T(8,128)(2,1)S(1)}, u32[]{:S(2)}, u32[]{:S(2)}) collective-permute-start(bf16[64,640]{1,0:T(8,128)(2,1)S(1)} %get-tuple-element.81), channel_id=1, source_target_pairs={{0,6},{1,7},{2,0},{3,1},{4,2},{5,3},{6,4},{7,5},{8,14},{9,15},{10,... | collective-permute-start | bytes 245768 | tf_op jit(solution)/shard_map/ppermute | solution.py:371
  111.7 1.3 shard_map.152.sums
  112.9 23.1 %collective-permute-done.18.refs_1_ = bf16[64,640]{1,0:T(8,128)(2,1)S(1)} collective-permute-done((bf16[64,640]{1,0:T(8,128)(2,1)S(1)}, bf16[64,640]{1,0:T(8,128)(2,1)S(1)}, u32[]{:S(2)}, u32[]{:S(2)}) %collective-permute-start.18) | collective-permute-done | bytes 81952 | tf_op jit(solution)/shard_map/ppermute | solution.py:369
  136.0 2.7 %shard_map.155 = (bf16[128,4096]{1,0:T(8,128)(2,1)S(1)}, bf16[128,512]{1,0:T(8,128)(2,1)S(1)}, bf16[128,256]{1,0:T(8,128)(2,1)S(1)}, bf16[4,64,640]{2,1,0:T(8,128)(2,1)S(1)}, bf16[4,64,640]{2,1,0:T(8,128)(2,1)S(1)}) custom-call(s32[1]{0:T(128)S(6)} %copy.16.ahead, s32[10]{0:T(128)S(1)} %stack.51.where, ...), custom_call_target="tpu_custom_call" | custom-call | flops 603979 | bytes 8781 | tf_op jit(solution)/shard_map/pallas_call | solution.py:52
  138.7 0.1 collective-permute-start.21
  138.8 1.6 %collective-permute-done.21.other = bf16[4,64,640]{2,1,0:T(8,128)(2,1)S(1)} collective-permute-done((bf16[4,64,640]{2,1,0:T(8,128)(2,1)S(1)}, bf16[4,64,640]{2,1,0:T(8,128)(2,1)S(1)}, u32[]{:S(2)}, u32[]{:S(2)}) %collective-permute-start.21) | collective-permute-done | bytes 327712 | tf_op jit(solution)/shard_map/ppermute | solution.py:417
  140.4 0.1 shard_map.157
  140.5 1.5 collective-permute-start.22
  142.0 2.5 %collective-permute-start.23 = (bf16[64,640]{1,0:T(8,128)(2,1)S(1)}, bf16[64,640]{1,0:T(8,128)(2,1)S(1)}, u32[]{:S(2)}, u32[]{:S(2)}) collective-permute-start(bf16[64,640]{1,0:T(8,128)(2,1)S(1)} %get-tuple-element.98), channel_id=1, source_target_pairs={{0,2},{1,3},{2,4},{3,5},{4,6},{5,7},{6,0},{7,1},{8,10},{9,11},{10,... | collective-permute-start | bytes 245768 | tf_op jit(solution)/shard_map/ppermute | solution.py:370
  144.5 1.6 %collective-permute-start.24 = (bf16[64,640]{1,0:T(8,128)(2,1)S(1)}, bf16[64,640]{1,0:T(8,128)(2,1)S(1)}, u32[]{:S(2)}, u32[]{:S(2)}) collective-permute-start(bf16[64,640]{1,0:T(8,128)(2,1)S(1)} %get-tuple-element.99), channel_id=1, source_target_pairs={{0,6},{1,7},{2,0},{3,1},{4,2},{5,3},{6,4},{7,5},{8,14},{9,15},{10,... | collective-permute-start | bytes 245768 | tf_op jit(solution)/shard_map/ppermute | solution.py:371
  146.1 3.5 %shard_map.156 = bf16[128,4096]{1,0:T(8,128)(2,1)} custom-call(s32[10]{0:T(128)S(1)} %stack.51.where, f32[128,512]{1,0:T(8,128)S(1)} %shard_map.152.sums, bf16[128,256]{1,0:T(8,128)(2,1)S(1)} %get-tuple-element.83.low, bf16[128,4096]{1,0:T(8,128)(2,1)S(1)} %get-tuple-element.86.grad, bf16[128,4096]{1,0:T(8,128)(2,1)S(1)} %bitcast.39, ...), custom_call_target="tpu_custom_call" | custom-call | flops 603979 | bytes 11091 | tf_op jit(solution)/shard_map/pallas_call | solution.py:52
  149.7 5.8 %shard_map.151 = bf16[128,4096]{1,0:T(8,128)(2,1)} custom-call(s32[1]{0:T(128)} %collective-permute-done.3.wrapped, s32[10]{0:T(128)S(1)} %stack.51.where, bf16[128,4096]{1,0:T(8,128)(2,1)S(1)} %copy-done.11, bf16[128,4224]{1,0:T(8,128)(2,1)S(1)} %collective-permute-done.15.passed, f32[1,4096]{1,0:T(1,128)S(1)} %copy-done.12, ...), custom_call_target="tpu_custom_call" | custom-call | flops 1073741 | bytes 12894 | tf_op jit(solution)/shard_map/pallas_call | solution.py:52
  155.4 1.5 shard_map.158
  (41 shorter events, 0.1 us)
Async XLA Ops:
  0.6 19.8 %collective-permute-start.2 = (bf16[512,512]{1,0:T(8,128)(2,1)}, bf16[512,512]{1,0:T(8,128)(2,1)S(1)}, u32[]{:S(2)}, u32[]{:S(2)}) collective-permute-start(bf16[512,512]{1,0:T(8,128)(2,1)} %bitcast.30), channel_id=1, source_target_pairs={{0,1},{1,0},{2,3},{3,2},{4,5},{5,4},{6,7},{7,6},{8,9},{9,8},{10,11... | collective-permute-start | bytes 1572872 | tf_op jit(solution)/shard_map/ppermute | solution.py:417
  0.7 19.7 %collective-permute-start = (bf16[512,512]{1,0:T(8,128)(2,1)}, bf16[512,512]{1,0:T(8,128)(2,1)S(1)}, u32[]{:S(2)}, u32[]{:S(2)}) collective-permute-start(bf16[512,512]{1,0:T(8,128)(2,1)} %bitcast.40), channel_id=1, source_target_pairs={{0,2},{1,7},{2,4},{3,1},{4,6},{5,3},{6,0},{7,5},{8,10},{9,15},{10,... | collective-permute-start | bytes 1572872 | tf_op jit(solution)/shard_map/ppermute | solution.py:417
  4.1 16.4 %collective-permute-start.1 = (bf16[512,512]{1,0:T(8,128)(2,1)}, bf16[512,512]{1,0:T(8,128)(2,1)S(1)}, u32[]{:S(2)}, u32[]{:S(2)}) collective-permute-start(bf16[512,512]{1,0:T(8,128)(2,1)} %bitcast.41), channel_id=1, source_target_pairs={{0,1},{1,0},{2,3},{3,2},{4,5},{5,4},{6,7},{7,6},{8,9},{9,8},{10,11... | collective-permute-start | bytes 1572872 | tf_op jit(solution)/shard_map/ppermute | solution.py:417
  7.2 17.3 %collective-permute-start.7 = (bf16[512,512]{1,0:T(8,128)(2,1)}, bf16[512,512]{1,0:T(8,128)(2,1)S(1)}, u32[]{:S(2)}, u32[]{:S(2)}) collective-permute-start(bf16[512,512]{1,0:T(8,128)(2,1)} %bitcast.31), channel_id=1, source_target_pairs={{0,2},{1,7},{2,4},{3,1},{4,6},{5,3},{6,0},{7,5},{8,10},{9,15},{10,... | collective-permute-start | bytes 1572872 | tf_op jit(solution)/shard_map/ppermute | solution.py:417
  8.6 11.9 %collective-permute-start.3 = (s32[1]{0:T(128)}, s32[1]{0:T(128)}, u32[]{:S(2)}, u32[]{:S(2)}) collective-permute-start(s32[1]{0:T(128)} %param.17), channel_id=1, source_target_pairs={{248,0},{249,1},{250,2},{251,3},{252,4},{253,5},{254,6},{255,7}} | collective-permute-start | bytes 20 | tf_op jit(solution)/shard_map/ppermute | solution.py:452
  11.2 1.6 %copy-start = (bf16[1,2,128,4096]{3,2,1,0:T(8,128)(2,1)S(1)}, bf16[1,2,128,4096]{3,2,1,0:T(8,128)(2,1)}, u32[]{:S(2)}) copy-start(bf16[1,2,128,4096]{3,2,1,0:T(8,128)(2,1)} %rows_s.3) | copy-start | bytes 6291460
  12.8 1.6 %copy-start.2 = (bf16[1,4,4096,64]{2,3,1,0:T(8,128)(2,1)S(1)}, bf16[1,4,4096,64]{2,3,1,0:T(8,128)(2,1)}, u32[]{:S(2)}) copy-start(bf16[1,4,4096,64]{2,3,1,0:T(8,128)(2,1)} %param.22) | copy-start | bytes 6291460
  14.4 1.2 copy-start.5
  15.6 0.7 copy-start.12
  16.3 43.0 %copy-start.4 = (bf16[1,512,512]{2,1,0:T(8,128)(2,1)S(1)}, bf16[1,512,512]{2,1,0:T(8,128)(2,1)}, u32[]{:S(2)}) copy-start(bf16[1,512,512]{2,1,0:T(8,128)(2,1)} %param.19) | copy-start | bytes 1572868
  16.3 43.0 %copy-start.7 = (bf16[1,512,512]{2,1,0:T(8,128)(2,1)S(1)}, bf16[1,512,512]{2,1,0:T(8,128)(2,1)}, u32[]{:S(2)}) copy-start(bf16[1,512,512]{2,1,0:T(8,128)(2,1)} %param.20) | copy-start | bytes 1572868
  16.3 43.0 %copy-start.8 = (bf16[1,128,4096]{2,1,0:T(8,128)(2,1)S(1)}, bf16[1,128,4096]{2,1,0:T(8,128)(2,1)}, u32[]{:S(2)}) copy-start(bf16[1,128,4096]{2,1,0:T(8,128)(2,1)} %param.13) | copy-start | bytes 3145732
  20.5 29.0 %collective-permute-start.5 = (bf16[512,512]{1,0:T(8,128)(2,1)S(1)}, bf16[512,512]{1,0:T(8,128)(2,1)S(1)}, u32[]{:S(2)}, u32[]{:S(2)}) collective-permute-start(bf16[512,512]{1,0:T(8,128)(2,1)S(1)} %collective-permute-done.refs_2_.refs_10_), channel_id=1, source_target_pairs={{0,2},{1,7},{2,4},{3,1},{4,6},{5,3},{6,0},{7,5},{8,10},{9,15},{10,... | collective-permute-start | bytes 1572872 | tf_op jit(solution)/shard_map/ppermute | solution.py:417
  24.6 30.5 %collective-permute-start.9 = (bf16[512,512]{1,0:T(8,128)(2,1)S(1)}, bf16[512,512]{1,0:T(8,128)(2,1)S(1)}, u32[]{:S(2)}, u32[]{:S(2)}) collective-permute-start(bf16[512,512]{1,0:T(8,128)(2,1)S(1)} %collective-permute-done.7.refs_8_.refs_2_), channel_id=1, source_target_pairs={{0,2},{1,7},{2,4},{3,1},{4,6},{5,3},{6,0},{7,5},{8,10},{9,15},{10,... | collective-permute-start | bytes 1572872 | tf_op jit(solution)/shard_map/ppermute | solution.py:417
  36.0 19.3 %collective-permute-start.4 = (bf16[512,512]{1,0:T(8,128)(2,1)S(1)}, bf16[512,512]{1,0:T(8,128)(2,1)S(1)}, u32[]{:S(2)}, u32[]{:S(2)}) collective-permute-start(bf16[512,512]{1,0:T(8,128)(2,1)S(1)} %collective-permute-done.refs_2_.refs_10_), channel_id=1, source_target_pairs={{0,1},{1,0},{2,3},{3,2},{4,5},{5,4},{6,7},{7,6},{8,9},{9,8},{10,11... | collective-permute-start | bytes 1572872 | tf_op jit(solution)/shard_map/ppermute | solution.py:417
  36.0 23.3 %collective-permute-start.8 = (bf16[512,512]{1,0:T(8,128)(2,1)S(1)}, bf16[512,512]{1,0:T(8,128)(2,1)S(1)}, u32[]{:S(2)}, u32[]{:S(2)}) collective-permute-start(bf16[512,512]{1,0:T(8,128)(2,1)S(1)} %collective-permute-done.7.refs_8_.refs_2_), channel_id=1, source_target_pairs={{0,1},{1,0},{2,3},{3,2},{4,5},{5,4},{6,7},{7,6},{8,9},{9,8},{10,11... | collective-permute-start | bytes 1572872 | tf_op jit(solution)/shard_map/ppermute | solution.py:417
  49.5 9.8 %collective-permute-start.6 = (bf16[512,512]{1,0:T(8,128)(2,1)S(1)}, bf16[512,512]{1,0:T(8,128)(2,1)S(1)}, u32[]{:S(2)}, u32[]{:S(2)}) collective-permute-start(bf16[512,512]{1,0:T(8,128)(2,1)S(1)} %collective-permute-done.5.refs_4_.refs_12_), channel_id=1, source_target_pairs={{0,1},{1,0},{2,3},{3,2},{4,5},{5,4},{6,7},{7,6},{8,9},{9,8},{10,11... | collective-permute-start | bytes 1572872 | tf_op jit(solution)/shard_map/ppermute | solution.py:417
  55.1 4.2 %collective-permute-start.10 = (bf16[512,512]{1,0:T(8,128)(2,1)S(1)}, bf16[512,512]{1,0:T(8,128)(2,1)S(1)}, u32[]{:S(2)}, u32[]{:S(2)}) collective-permute-start(bf16[512,512]{1,0:T(8,128)(2,1)S(1)} %collective-permute-done.9.refs_10_.refs_4_), channel_id=1, source_target_pairs={{0,1},{1,0},{2,3},{3,2},{4,5},{5,4},{6,7},{7,6},{8,9},{9,8},{10,11... | collective-permute-start | bytes 1572872 | tf_op jit(solution)/shard_map/ppermute | solution.py:417
  55.1 15.4 %collective-permute-start.11 = (bf16[512,512]{1,0:T(8,128)(2,1)S(1)}, bf16[512,512]{1,0:T(8,128)(2,1)S(1)}, u32[]{:S(2)}, u32[]{:S(2)}) collective-permute-start(bf16[512,512]{1,0:T(8,128)(2,1)S(1)} %collective-permute-done.5.refs_4_.refs_12_), channel_id=1, source_target_pairs={{0,2},{1,7},{2,4},{3,1},{4,6},{5,3},{6,0},{7,5},{8,10},{9,15},{10,... | collective-permute-start | bytes 1572872 | tf_op jit(solution)/shard_map/ppermute | solution.py:417
  55.3 28.2 %collective-permute-start.12 = (bf16[512,512]{1,0:T(8,128)(2,1)S(1)}, bf16[512,512]{1,0:T(8,128)(2,1)S(1)}, u32[]{:S(2)}, u32[]{:S(2)}) collective-permute-start(bf16[512,512]{1,0:T(8,128)(2,1)S(1)} %collective-permute-done.9.refs_10_.refs_4_), channel_id=1, source_target_pairs={{0,2},{1,7},{2,4},{3,1},{4,6},{5,3},{6,0},{7,5},{8,10},{9,15},{10,... | collective-permute-start | bytes 1572872 | tf_op jit(solution)/shard_map/ppermute | solution.py:417
  59.3 26.8 %copy-start.1 = (bf16[1,2,128,4096]{3,2,1,0:T(8,128)(2,1)S(1)}, bf16[1,2,128,4096]{3,2,1,0:T(8,128)(2,1)}, u32[]{:S(2)}) copy-start(bf16[1,2,128,4096]{3,2,1,0:T(8,128)(2,1)} %rows_s.3) | copy-start | bytes 6291460
  59.4 26.7 %copy-start.3 = (bf16[1,4,4096,64]{2,3,1,0:T(8,128)(2,1)S(1)}, bf16[1,4,4096,64]{2,3,1,0:T(8,128)(2,1)}, u32[]{:S(2)}) copy-start(bf16[1,4,4096,64]{2,3,1,0:T(8,128)(2,1)} %param.22) | copy-start | bytes 6291460
  59.4 26.7 %copy-start.9 = (bf16[1,4,64,512]{3,2,1,0:T(8,128)(2,1)S(1)}, bf16[1,4,64,512]{3,2,1,0:T(8,128)(2,1)}, u32[]{:S(2)}) copy-start(bf16[1,4,64,512]{3,2,1,0:T(8,128)(2,1)} %param.23) | copy-start | bytes 786436
  83.4 1.9 %collective-permute-start.13 = (bf16[512,512]{1,0:T(8,128)(2,1)S(1)}, bf16[512,512]{1,0:T(8,128)(2,1)S(1)}, u32[]{:S(2)}, u32[]{:S(2)}) collective-permute-start(bf16[512,512]{1,0:T(8,128)(2,1)S(1)} %collective-permute-done.11.far.refs_6_.refs_14_), channel_id=1, source_target_pairs={{0,1},{1,0},{2,3},{3,2},{4,5},{5,4},{6,7},{7,6},{8,9},{9,8},{10,11... | collective-permute-start | bytes 1572872 | tf_op jit(solution)/shard_map/ppermute | solution.py:417
  83.4 2.7 %collective-permute-start.14 = (bf16[512,512]{1,0:T(8,128)(2,1)S(1)}, bf16[512,512]{1,0:T(8,128)(2,1)S(1)}, u32[]{:S(2)}, u32[]{:S(2)}) collective-permute-start(bf16[512,512]{1,0:T(8,128)(2,1)S(1)} %collective-permute-done.12.refs_6_.far), channel_id=1, source_target_pairs={{0,1},{1,0},{2,3},{3,2},{4,5},{5,4},{6,7},{7,6},{8,9},{9,8},{10,11... | collective-permute-start | bytes 1572872 | tf_op jit(solution)/shard_map/ppermute | solution.py:417
  86.1 5.3 %copy-start.6 = (bf16[1,128,4096]{2,1,0:T(8,128)(2,1)S(1)}, bf16[1,128,4096]{2,1,0:T(8,128)(2,1)}, u32[]{:S(2)}) copy-start(bf16[1,128,4096]{2,1,0:T(8,128)(2,1)} %param.12) | copy-start | bytes 3145732
  89.4 46.6 %collective-permute-start.16 = (bf16[128,4224]{1,0:T(8,128)(2,1)S(1)}, bf16[128,4224]{1,0:T(8,128)(2,1)S(1)}, u32[]{:S(2)}, u32[]{:S(2)}) collective-permute-start(bf16[128,4224]{1,0:T(8,128)(2,1)S(1)} %get-tuple-element.68), channel_id=1, source_target_pairs={{8,0},{16,8},{24,16},{32,24},{40,32},{48,40},{56,48},{64,56},{72,6... | collective-permute-start | bytes 3244040 | tf_op jit(solution)/shard_map/ppermute | solution.py:475
  93.0 56.7 %collective-permute-start.15 = (bf16[128,4224]{1,0:T(8,128)(2,1)S(1)}, bf16[128,4224]{1,0:T(8,128)(2,1)S(1)}, u32[]{:S(2)}, u32[]{:S(2)}) collective-permute-start(bf16[128,4224]{1,0:T(8,128)(2,1)S(1)} %shard_map.150.out), channel_id=1, source_target_pairs={{0,8},{8,16},{16,24},{24,32},{32,40},{40,48},{48,56},{56,64},{64,7... | collective-permute-start | bytes 3244040 | tf_op jit(solution)/shard_map/ppermute | solution.py:478
  102.1 1.7 %collective-permute-start.17 = (bf16[4,64,640]{2,1,0:T(8,128)(2,1)S(1)}, bf16[4,64,640]{2,1,0:T(8,128)(2,1)S(1)}, u32[]{:S(2)}, u32[]{:S(2)}) collective-permute-start(bf16[4,64,640]{2,1,0:T(8,128)(2,1)S(1)} %get-tuple-element.77), channel_id=1, source_target_pairs={{0,1},{1,0},{2,3},{3,2},{4,5},{5,4},{6,7},{7,6},{8,9},{9,8},{10,11... | collective-permute-start | bytes 983048 | tf_op jit(solution)/shard_map/ppermute | solution.py:417
  103.9 32.1 %collective-permute-start.18 = (bf16[64,640]{1,0:T(8,128)(2,1)S(1)}, bf16[64,640]{1,0:T(8,128)(2,1)S(1)}, u32[]{:S(2)}, u32[]{:S(2)}) collective-permute-start(bf16[64,640]{1,0:T(8,128)(2,1)S(1)} %get-tuple-element.79), channel_id=1, source_target_pairs={{0,4},{1,5},{2,6},{3,7},{4,0},{5,1},{6,2},{7,3},{8,12},{9,13},{10,... | collective-permute-start | bytes 245768 | tf_op jit(solution)/shard_map/ppermute | solution.py:369
  107.5 28.5 %collective-permute-start.19 = (bf16[64,640]{1,0:T(8,128)(2,1)S(1)}, bf16[64,640]{1,0:T(8,128)(2,1)S(1)}, u32[]{:S(2)}, u32[]{:S(2)}) collective-permute-start(bf16[64,640]{1,0:T(8,128)(2,1)S(1)} %get-tuple-element.80), channel_id=1, source_target_pairs={{0,2},{1,3},{2,4},{3,5},{4,6},{5,7},{6,0},{7,1},{8,10},{9,11},{10,... | collective-permute-start | bytes 245768 | tf_op jit(solution)/shard_map/ppermute | solution.py:370
  107.5 28.5 %copy-start.10 = (bf16[128,4096]{1,0:T(8,128)(2,1)S(1)}, bf16[128,4096]{1,0:T(8,128)(2,1)}, u32[]{:S(2)}) copy-start(bf16[128,4096]{1,0:T(8,128)(2,1)} %target.1) | copy-start | bytes 3145732
  107.5 28.5 %collective-permute-start.20 = (bf16[64,640]{1,0:T(8,128)(2,1)S(1)}, bf16[64,640]{1,0:T(8,128)(2,1)S(1)}, u32[]{:S(2)}, u32[]{:S(2)}) collective-permute-start(bf16[64,640]{1,0:T(8,128)(2,1)S(1)} %get-tuple-element.81), channel_id=1, source_target_pairs={{0,6},{1,7},{2,0},{3,1},{4,2},{5,3},{6,4},{7,5},{8,14},{9,15},{10,... | collective-permute-start | bytes 245768 | tf_op jit(solution)/shard_map/ppermute | solution.py:371
  138.7 1.7 %collective-permute-start.21 = (bf16[4,64,640]{2,1,0:T(8,128)(2,1)S(1)}, bf16[4,64,640]{2,1,0:T(8,128)(2,1)S(1)}, u32[]{:S(2)}, u32[]{:S(2)}) collective-permute-start(bf16[4,64,640]{2,1,0:T(8,128)(2,1)S(1)} %get-tuple-element.95), channel_id=1, source_target_pairs={{0,1},{1,0},{2,3},{3,2},{4,5},{5,4},{6,7},{7,6},{8,9},{9,8},{10,11... | collective-permute-start | bytes 983048 | tf_op jit(solution)/shard_map/ppermute | solution.py:417
  140.5 14.9 %collective-permute-start.22 = (bf16[64,640]{1,0:T(8,128)(2,1)S(1)}, bf16[64,640]{1,0:T(8,128)(2,1)S(1)}, u32[]{:S(2)}, u32[]{:S(2)}) collective-permute-start(bf16[64,640]{1,0:T(8,128)(2,1)S(1)} %get-tuple-element.97), channel_id=1, source_target_pairs={{0,4},{1,5},{2,6},{3,7},{4,0},{5,1},{6,2},{7,3},{8,12},{9,13},{10,... | collective-permute-start | bytes 245768 | tf_op jit(solution)/shard_map/ppermute | solution.py:369
  142.0 13.5 %collective-permute-start.23 = (bf16[64,640]{1,0:T(8,128)(2,1)S(1)}, bf16[64,640]{1,0:T(8,128)(2,1)S(1)}, u32[]{:S(2)}, u32[]{:S(2)}) collective-permute-start(bf16[64,640]{1,0:T(8,128)(2,1)S(1)} %get-tuple-element.98), channel_id=1, source_target_pairs={{0,2},{1,3},{2,4},{3,5},{4,6},{5,7},{6,0},{7,1},{8,10},{9,11},{10,... | collective-permute-start | bytes 245768 | tf_op jit(solution)/shard_map/ppermute | solution.py:370
  144.5 11.0 %collective-permute-start.24 = (bf16[64,640]{1,0:T(8,128)(2,1)S(1)}, bf16[64,640]{1,0:T(8,128)(2,1)S(1)}, u32[]{:S(2)}, u32[]{:S(2)}) collective-permute-start(bf16[64,640]{1,0:T(8,128)(2,1)S(1)} %get-tuple-element.99), channel_id=1, source_target_pairs={{0,6},{1,7},{2,0},{3,1},{4,2},{5,3},{6,4},{7,5},{8,14},{9,15},{10,... | collective-permute-start | bytes 245768 | tf_op jit(solution)/shard_map/ppermute | solution.py:371
  146.1 3.5 %copy-start.11 = (bf16[128,4096]{1,0:T(8,128)(2,1)S(1)}, bf16[128,4096]{1,0:T(8,128)(2,1)}, u32[]{:S(2)}) copy-start(bf16[128,4096]{1,0:T(8,128)(2,1)} %fresh.1) | copy-start | bytes 3145732

commit v6 on v5

--- a/solution.py
+++ b/solution.py
@@ -324,7 +324,7 @@
     )[0]
 
 
-def forward_kernel(wrapped, where, fresh, passed, gain, down, up, *refs):
+def forward_kernel(where, fresh, passed, gain, down, up, *refs):
     vals, outs, (out, rows, normed) = refs[:8], refs[8:16], refs[16:]
     first = where[8] == 1
     for top in range(0, ROWS, 32):
@@ -333,8 +333,7 @@
         whole = chosen.astype(F32)
         rows[part, :] = chosen
         normed[part, :] = (whole * factor_of(whole) * gain[...]).astype(BF)
-    came = passed[:, WIDTH : WIDTH + 1].astype(F32).astype(jnp.int32)
-    ident = jnp.where(first, wrapped[0], came)
+    ident = passed[:, WIDTH : WIDTH + 1].astype(F32).astype(jnp.int32)
     low = only(dot_t(normed[...], down[...]), ident).astype(BF)
     total = SCALE * dot(low, up[...])
     for i in range(8):
@@ -345,10 +344,10 @@
         out[:, span] = (rows[:, span].astype(F32) + dot(values, outs[i][...])).astype(BF)
 
 
-def forward(wrapped, where, fresh, passed, gain, down, up, vals, outs):
+def forward(where, fresh, passed, gain, down, up, vals, outs):
     return call(
         forward_kernel,
-        (wrapped, where),
+        (where,),
         [fresh, passed, gain, down, up, *vals, *outs],
         [shape((ROWS, WIDTH), BF)],
         4 * ROWS * WIDTH * VALUES,
@@ -356,14 +355,23 @@
     )[0]
 
 
-def pair_sum_kernel(mine, other, own, one, two, three):
+def pair_sum_kernel(mine, other, total):
+    total[...] = (mine[...].astype(F32) + other[...].astype(F32)).astype(BF)
+
+
+def pair_sum(mine, other):
+    return call(pair_sum_kernel, (), [mine, other], [shape((4, RANK, PACK), BF)], 0)[0]
+
+
+def stack_kernel(first, mine, other, own, one, two, three):
     for ahead, ref in enumerate((own, one, two, three)):
-        ref[...] = (mine[ahead].astype(F32) + other[ahead].astype(F32)).astype(BF)
-
-
-def spread(mine, received):
-    block = shape((RANK, PACK), BF)
-    own, one, two, three = call(pair_sum_kernel, (), [mine, received], [block] * 4, 0)
+        ref[0] = first[ahead]
+        ref[1] = (mine[ahead].astype(F32) + other[ahead].astype(F32)).astype(BF)
+
+
+def spread(first, mine, received):
+    block = shape((2, RANK, PACK), BF)
+    own, one, two, three = call(stack_kernel, (), [first, mine, received], [block] * 4, 0)
     return (
         own,
         lax.ppermute(two, "dp", chips(2)),
@@ -373,15 +381,15 @@
 
 
 def tables_kernel(ahead, back, where, relayed, *refs):
-    terms, (down, up) = refs[:8], refs[8:]
+    terms, (down, up) = refs[:4], refs[4:]
     core = where[0] % 2
     came = relayed[:RANK, :1].astype(F32).astype(jnp.int32)
     ident = jnp.where(where[9] == 1, ahead[0], came)
     sums = []
     for tick in range(2):
-        total = terms[4 * tick][...].astype(F32)
+        total = terms[0][tick].astype(F32)
         for k in range(1, 4):
-            total += terms[4 * tick + k][...].astype(F32)
+            total += terms[k][tick].astype(F32)
         sums.append(total)
     for label in range(ADAPTERS):
         one = jnp.where(back[0] == label, 1.0, 0.0)
@@ -436,7 +444,7 @@
     value_projection, output_matrix, norm_gain_frozen, adapter_down, adapter_up,
 ):
     count = lax.axis_size("section")
-    onward = [(i, i + 1) for i in range(count - 1)]
+    onward = [(i, (i + 1) % count) for i in range(count)]
     before = [(i, i - 1) for i in range(1, count)]
     position = lax.axis_index("section")
     where = jnp.stack(
@@ -449,15 +457,14 @@
     ahead, back = forward_adapter, backward_adapter
 
     out_own, val_own = output_matrix[0], value_projection[0]
-    wrapped = lax.ppermute(ahead, "section", [(count - 1, 0)])
     out_one, val_one = send(out_own, split_ring(1)), send(val_own, split_ring(1))
     out_sibling, val_sibling = send(out_own, CORE), send(val_own, CORE)
 
     normed_f, _, low_f, normed_b, factor_b, low_b, normed_n, factor_n, low_n = prepare(
         ahead, back, where, rows, saved, gain, down
     )
-    out_one, normed_f, out_sibling, val_sibling, wrapped = lax.optimization_barrier(
-        (out_one, normed_f, out_sibling, val_sibling, wrapped)
+    out_one, normed_f, out_sibling, val_sibling = lax.optimization_barrier(
+        (out_one, normed_f, out_sibling, val_sibling)
     )
     out_two, val_two = send(out_one, split_ring(1)), send(val_one, split_ring(1))
     out_far, val_far = send(out_two, split_ring(1)), send(val_two, split_ring(1))
@@ -478,19 +485,19 @@
     passed = lax.ppermute(first_out, "section", onward)
     first_out, d_low, normed_n = lax.optimization_barrier((first_out, d_low, normed_n))
     mine, other = pack(where, low_b, normed_b, d_values, d_low)
-    first_terms = spread(mine, send(other, CORE))
+    first_sums = pair_sum(mine, send(other, CORE))
     sums_n = project(where, normed_n, vals)
-    relayed, sums_n, *first_terms = lax.optimization_barrier((relayed, sums_n, *first_terms))
+    relayed, sums_n, first_sums = lax.optimization_barrier((relayed, sums_n, first_sums))
 
     grad_n, d_values, d_low, mine, other = second_values(
         ahead, where, relayed, first_out, target, low_n, normed_n, up, outs
     )
-    second_terms = spread(mine, send(other, CORE))
+    terms = spread(first_sums, mine, send(other, CORE))
     bwd_out = second_input(
         where, sums_n, low_n, grad_n, rows, saved, factor_n, gain, down, d_values, d_low, vals
     )
-    fwd_out = forward(wrapped, where, fresh, passed, gain, down, up, vals, outs)
-    down_table, up_table = tables(ahead, back, where, relayed, (*first_terms, *second_terms))
+    fwd_out = forward(where, fresh, passed, gain, down, up, vals, outs)
+    down_table, up_table = tables(ahead, back, where, relayed, terms)
     return (
         fwd_out[None], bwd_out[None], jnp.swapaxes(down_table, 1, 2)[None], up_table[None]
     )

time: 157 us -> 143 us (0.911); the launches traced: 157 us -> 141 us
  waiting for transfers between devices: 71.2 us -> 56.4 us
    ppermute x2 -> x1, waiting for transfers between devices: 23.1 us -> 0.01 us  [spread(): lax.ppermute(two, 'dp', chips(2))]
    ppermute x1, waiting for transfers between devices: 0.01 us -> 19.4 us  [body(): relayed = lax.ppermute(first_back, 'section', before)]
    ppermute x16, waiting for transfers between devices: 48.1 us -> 37 us  [send(): return lax.ppermute(block, 'dp', pairs)]
    ppermute x16, starting transfers between devices: 26.3 us -> 35.6 us  [send(): return lax.ppermute(block, 'dp', pairs)]
    ppermute x2 -> x1, starting transfers between devices: 5.76 us -> 1.81 us  [spread(): lax.ppermute(three, 'dp', chips(3))]
    ppermute x2 -> x1, starting transfers between devices: 5.09 us -> 2.42 us  [spread(): lax.ppermute(two, 'dp', chips(2))]
    ppermute x1, starting transfers between devices: 8.14 us -> 5.58 us  [body(): passed = lax.ppermute(first_out, 'section', onward)]
  transfers between devices with their start and end apart: 25 -> 21, of which waited for: 10 -> 9; matrix products, arithmetic and copies ran while one was open for 0% -> 0% of each run, Pallas kernels for 14% -> 16%
where the time goes in v6:
time: 143 us; the launch traced here: 141 us
  waiting for transfers between devices  56.4 us (39%)
  starting transfers between devices  50.4 us (35%)
  Pallas kernels  26.8 us (19%)
  local copies, waits for them, and re-layouts  5.26 us (4%)
  between operations  2.13 us (1%)
    ppermute x16, waiting for transfers between devices, send(): return lax.ppermute(block, 'dp', pairs)  37 us
    ppermute x16, starting transfers between devices, send(): return lax.ppermute(block, 'dp', pairs)  35.6 us
    pallas_call x12, Pallas kernels, call(): pl.pallas_call(kernel, out_shape=outs, grid_spec=pltpu.PrefetchScalarGrid...  26.8 us
    ppermute x1, waiting for transfers between devices, body(): relayed = lax.ppermute(first_back, 'section', before)  19.4 us
    ppermute x1, starting transfers between devices, body(): passed = lax.ppermute(first_out, 'section', onward)  5.58 us
    unnamed x26, local copies, waits for them, and re-layouts  5.17 us
  transfers between devices with their start and end apart: 21, of which 9 were waited for; matrix products, arithmetic and copies ran while one was open for 0% of the time, Pallas kernels for 16%

profile of v6, /device:TPU:30, one launch (start us, length us, event | category | flops | bytes accessed | tf_op | source)
XLA Modules:
  0.0 141.0 jit_solution(16898345372738145717)
XLA Ops:
  0.6 0.1 collective-permute-start.2
  0.7 3.3 %collective-permute-start = (bf16[512,512]{1,0:T(8,128)(2,1)}, bf16[512,512]{1,0:T(8,128)(2,1)S(1)}, u32[]{:S(2)}, u32[]{:S(2)}) collective-permute-start(bf16[512,512]{1,0:T(8,128)(2,1)} %bitcast.40), channel_id=1, source_target_pairs={{0,2},{1,7},{2,4},{3,1},{4,6},{5,3},{6,0},{7,5},{8,10},{9,15},{10,... | collective-permute-start | bytes 1572872 | tf_op jit(solution)/shard_map/ppermute | solution.py:425
  4.1 3.2 %collective-permute-start.1 = (bf16[512,512]{1,0:T(8,128)(2,1)}, bf16[512,512]{1,0:T(8,128)(2,1)S(1)}, u32[]{:S(2)}, u32[]{:S(2)}) collective-permute-start(bf16[512,512]{1,0:T(8,128)(2,1)} %bitcast.41), channel_id=1, source_target_pairs={{0,1},{1,0},{2,3},{3,2},{4,5},{5,4},{6,7},{7,6},{8,9},{9,8},{10,11... | collective-permute-start | bytes 1572872 | tf_op jit(solution)/shard_map/ppermute | solution.py:425
  7.2 1.3 collective-permute-start.6
  9.9 0.1 stack.51.where
  10.0 1.6 %copy-done = bf16[1,2,128,4096]{3,2,1,0:T(8,128)(2,1)S(1)} copy-done((bf16[1,2,128,4096]{3,2,1,0:T(8,128)(2,1)S(1)}, bf16[1,2,128,4096]{3,2,1,0:T(8,128)(2,1)}, u32[]{:S(2)}) %copy-start) | copy-done | bytes 2097176
  11.6 1.6 %copy-done.2 = bf16[1,4,4096,64]{2,3,1,0:T(8,128)(2,1)S(1)} copy-done((bf16[1,4,4096,64]{2,3,1,0:T(8,128)(2,1)S(1)}, bf16[1,4,4096,64]{2,3,1,0:T(8,128)(2,1)}, u32[]{:S(2)}) %copy-start.2) | copy-done | bytes 2097176
  13.1 1.2 copy-done.5
  14.4 0.7 copy-done.12
  15.1 4.1 %shard_map.147 = (bf16[128,4096]{1,0:T(8,128)(2,1)S(1)}, f32[128,128]{1,0:T(8,128)}, bf16[128,256]{1,0:T(8,128)(2,1)S(1)}, bf16[128,4096]{1,0:T(8,128)(2,1)S(1)}...) custom-call(s32[1]{0:T(128)S(6)} %copy.16.ahead, ...), custom_call_target="tpu_custom_call" | custom-call | flops 805306 | bytes 7356 | tf_op jit(solution)/shard_map/pallas_call | solution.py:52
  19.2 1.5 %collective-permute-start.4 = (bf16[512,512]{1,0:T(8,128)(2,1)S(1)}, bf16[512,512]{1,0:T(8,128)(2,1)S(1)}, u32[]{:S(2)}, u32[]{:S(2)}) collective-permute-start(bf16[512,512]{1,0:T(8,128)(2,1)S(1)} %collective-permute-done.refs_2_.refs_10_), channel_id=1, source_target_pairs={{0,2},{1,7},{2,4},{3,1},{4,6},{5,3},{6,0},{7,5},{8,10},{9,15},{10,... | collective-permute-start | bytes 1572872 | tf_op jit(solution)/shard_map/ppermute | solution.py:425
  20.8 3.8 %collective-permute-done.6.refs_8_.refs_2_ = bf16[512,512]{1,0:T(8,128)(2,1)S(1)} collective-permute-done((bf16[512,512]{1,0:T(8,128)(2,1)}, bf16[512,512]{1,0:T(8,128)(2,1)S(1)}, u32[]{:S(2)}, u32[]{:S(2)}) %collective-permute-start.6) | collective-permute-done | bytes 524320 | tf_op jit(solution)/shard_map/ppermute | solution.py:425
  24.6 5.2 %collective-permute-start.8 = (bf16[512,512]{1,0:T(8,128)(2,1)S(1)}, bf16[512,512]{1,0:T(8,128)(2,1)S(1)}, u32[]{:S(2)}, u32[]{:S(2)}) collective-permute-start(bf16[512,512]{1,0:T(8,128)(2,1)S(1)} %collective-permute-done.6.refs_8_.refs_2_), channel_id=1, source_target_pairs={{0,2},{1,7},{2,4},{3,1},{4,6},{5,3},{6,0},{7,5},{8,10},{9,15},{10,... | collective-permute-start | bytes 1572872 | tf_op jit(solution)/shard_map/ppermute | solution.py:425
  29.8 11.8 %collective-permute-start.3 = (bf16[512,512]{1,0:T(8,128)(2,1)S(1)}, bf16[512,512]{1,0:T(8,128)(2,1)S(1)}, u32[]{:S(2)}, u32[]{:S(2)}) collective-permute-start(bf16[512,512]{1,0:T(8,128)(2,1)S(1)} %collective-permute-done.refs_2_.refs_10_), channel_id=1, source_target_pairs={{0,1},{1,0},{2,3},{3,2},{4,5},{5,4},{6,7},{7,6},{8,9},{9,8},{10,11... | collective-permute-start | bytes 1572872 | tf_op jit(solution)/shard_map/ppermute | solution.py:425
  41.6 3.4 %collective-permute-start.5 = (bf16[512,512]{1,0:T(8,128)(2,1)S(1)}, bf16[512,512]{1,0:T(8,128)(2,1)S(1)}, u32[]{:S(2)}, u32[]{:S(2)}) collective-permute-start(bf16[512,512]{1,0:T(8,128)(2,1)S(1)} %collective-permute-done.4.refs_4_.refs_12_), channel_id=1, source_target_pairs={{0,1},{1,0},{2,3},{3,2},{4,5},{5,4},{6,7},{7,6},{8,9},{9,8},{10,11... | collective-permute-start | bytes 1572872 | tf_op jit(solution)/shard_map/ppermute | solution.py:425
  45.0 9.3 %collective-permute-done.8.refs_10_.refs_4_ = bf16[512,512]{1,0:T(8,128)(2,1)S(1)} collective-permute-done((bf16[512,512]{1,0:T(8,128)(2,1)S(1)}, bf16[512,512]{1,0:T(8,128)(2,1)S(1)}, u32[]{:S(2)}, u32[]{:S(2)}) %collective-permute-start.8) | collective-permute-done | bytes 524320 | tf_op jit(solution)/shard_map/ppermute | solution.py:425
  54.3 0.7 collective-permute-start.10
  55.0 4.3 %collective-permute-start.11 = (bf16[512,512]{1,0:T(8,128)(2,1)S(1)}, bf16[512,512]{1,0:T(8,128)(2,1)S(1)}, u32[]{:S(2)}, u32[]{:S(2)}) collective-permute-start(bf16[512,512]{1,0:T(8,128)(2,1)S(1)} %collective-permute-done.8.refs_10_.refs_4_), channel_id=1, source_target_pairs={{0,2},{1,7},{2,4},{3,1},{4,6},{5,3},{6,0},{7,5},{8,10},{9,15},{10,... | collective-permute-start | bytes 1572872 | tf_op jit(solution)/shard_map/ppermute | solution.py:425
  59.3 0.0 copy-start.1
  59.4 0.0 copy-start.3
  59.4 2.5 %shard_map.148 = (f32[128,512]{1,0:T(8,128)S(1)}, f32[128,512]{1,0:T(8,128)S(1)}, f32[128,512]{1,0:T(8,128)S(1)}) custom-call(s32[10]{0:T(128)S(1)} %stack.51.where, bf16[128,4096]{1,0:T(8,128)(2,1)S(1)} %bitcast.46, bf16[128,4096]{1,0:T(8,128)(2,1)S(1)} %get-tuple-element.46.normed_f.normed, bf16[128,4096]{1,0:T(8,128)(2,1)S(1)} %get-tuple-element.47.normed_b.normed, ...), custom_call_target="tpu_custom_call" | custom-call | flops 1610612 | bytes 9437 | tf_op jit(solution)/shard_map/pallas_call | solution.py:52
  61.9 14.2 %collective-permute-done.10.far.refs_6_.refs_14_ = bf16[512,512]{1,0:T(8,128)(2,1)S(1)} collective-permute-done((bf16[512,512]{1,0:T(8,128)(2,1)S(1)}, bf16[512,512]{1,0:T(8,128)(2,1)S(1)}, u32[]{:S(2)}, u32[]{:S(2)}) %collective-permute-start.10) | collective-permute-done | bytes 524320 | tf_op jit(solution)/shard_map/ppermute | solution.py:425
  76.2 5.6 %collective-permute-done.11.refs_6_.far = bf16[512,512]{1,0:T(8,128)(2,1)S(1)} collective-permute-done((bf16[512,512]{1,0:T(8,128)(2,1)S(1)}, bf16[512,512]{1,0:T(8,128)(2,1)S(1)}, u32[]{:S(2)}, u32[]{:S(2)}) %collective-permute-start.11) | collective-permute-done | bytes 524320 | tf_op jit(solution)/shard_map/ppermute | solution.py:425
  81.8 0.5 collective-permute-start.13
  82.3 1.4 collective-permute-done.12.far_other.refs_7_.refs_15_
  83.7 0.7 collective-permute-done.13.refs_7_.far_other
  84.4 0.0 copy-start.6
  84.5 3.3 %shard_map.149 = (bf16[128,4224]{1,0:T(8,128)(2,1)S(1)}, bf16[128,512]{1,0:T(8,128)(2,1)S(1)}, bf16[128,256]{1,0:T(8,128)(2,1)S(1)}) custom-call(s32[1]{0:T(128)S(6)} %copy.17.back, s32[10]{0:T(128)S(1)} %stack.51.where, f32[128,512]{1,0:T(8,128)S(1)} %get-tuple-element.53.share, f32[128,512]{1,0:T(8,128)S(1)} %get-tuple-element.54.sums, ...), custom_call_target="tpu_custom_call" | custom-call | flops 536870 | bytes 12468 | tf_op jit(solution)/shard_map/pallas_call | solution.py:52
  87.8 2.7 %collective-permute-start.15 = (bf16[128,4224]{1,0:T(8,128)(2,1)S(1)}, bf16[128,4224]{1,0:T(8,128)(2,1)S(1)}, u32[]{:S(2)}, u32[]{:S(2)}) collective-permute-start(bf16[128,4224]{1,0:T(8,128)(2,1)S(1)} %get-tuple-element.59), channel_id=1, source_target_pairs={{8,0},{16,8},{24,16},{32,24},{40,32},{48,40},{56,48},{64,56},{72,6... | collective-permute-start | bytes 3244040 | tf_op jit(solution)/shard_map/ppermute | solution.py:482
  90.4 1.6 %shard_map.150.out = bf16[128,4224]{1,0:T(8,128)(2,1)S(1)} custom-call(s32[1]{0:T(128)S(6)} %copy.16.ahead, s32[10]{0:T(128)S(1)} %stack.51.where, f32[128,512]{1,0:T(8,128)S(1)} %get-tuple-element.60.share, bf16[128,4096]{1,0:T(8,128)(2,1)S(1)} %get-tuple-element.46.normed_f.normed, bf16[128,256]{1,0:T(8,128)(2,1)S(1)} %get-tuple-element.61.low, ...), custom_call_target="tpu_custom_call" | custom-call | flops 536870 | bytes 7929 | tf_op jit(solution)/shard_map/pallas_call | solution.py:52
  92.0 5.6 %collective-permute-start.14 = (bf16[128,4224]{1,0:T(8,128)(2,1)S(1)}, bf16[128,4224]{1,0:T(8,128)(2,1)S(1)}, u32[]{:S(2)}, u32[]{:S(2)}) collective-permute-start(bf16[128,4224]{1,0:T(8,128)(2,1)S(1)} %shard_map.150.out), channel_id=1, source_target_pairs={{0,8},{8,16},{16,24},{24,32},{32,40},{40,48},{48,56},{56,64},{64,7... | collective-permute-start | bytes 3244040 | tf_op jit(solution)/shard_map/ppermute | solution.py:485
  97.6 1.0 shard_map.153
  98.6 0.1 collective-permute-start.16
  98.7 0.0 copy-start.10
  98.7 1.3 shard_map.152.sums
  100.0 0.3 collective-permute-done.16.other
  100.3 0.1 shard_map.154.first
  100.4 19.4 %collective-permute-done.15.relayed = bf16[128,4224]{1,0:T(8,128)(2,1)S(1)} collective-permute-done((bf16[128,4224]{1,0:T(8,128)(2,1)S(1)}, bf16[128,4224]{1,0:T(8,128)(2,1)S(1)}, u32[]{:S(2)}, u32[]{:S(2)}) %collective-permute-start.15) | collective-permute-done | bytes 1081376 | tf_op jit(solution)/shard_map/ppermute | solution.py:482
  119.8 2.6 %shard_map.155 = (bf16[128,4096]{1,0:T(8,128)(2,1)S(1)}, bf16[128,512]{1,0:T(8,128)(2,1)S(1)}, bf16[128,256]{1,0:T(8,128)(2,1)S(1)}, bf16[4,64,640]{2,1,0:T(8,128)(2,1)S(1)}, bf16[4,64,640]{2,1,0:T(8,128)(2,1)S(1)}) custom-call(s32[1]{0:T(128)S(6)} %copy.16.ahead, s32[10]{0:T(128)S(1)} %stack.51.where, ...), custom_call_target="tpu_custom_call" | custom-call | flops 603979 | bytes 8781 | tf_op jit(solution)/shard_map/pallas_call | solution.py:52
  122.5 0.1 collective-permute-start.17
  122.6 1.6 %collective-permute-done.17.other = bf16[4,64,640]{2,1,0:T(8,128)(2,1)S(1)} collective-permute-done((bf16[4,64,640]{2,1,0:T(8,128)(2,1)S(1)}, bf16[4,64,640]{2,1,0:T(8,128)(2,1)S(1)}, u32[]{:S(2)}, u32[]{:S(2)}) %collective-permute-start.17) | collective-permute-done | bytes 327712 | tf_op jit(solution)/shard_map/ppermute | solution.py:425
  124.2 0.1 shard_map.157
  124.3 2.4 %collective-permute-start.18 = (bf16[2,64,640]{2,1,0:T(8,128)(2,1)S(1)}, bf16[2,64,640]{2,1,0:T(8,128)(2,1)S(1)}, u32[]{:S(2)}, u32[]{:S(2)}) collective-permute-start(bf16[2,64,640]{2,1,0:T(8,128)(2,1)S(1)} %get-tuple-element.81), channel_id=1, source_target_pairs={{0,4},{1,5},{2,6},{3,7},{4,0},{5,1},{6,2},{7,3},{8,12},{9,13},{10,... | collective-permute-start | bytes 491528 | tf_op jit(solution)/shard_map/ppermute | solution.py:377
  126.7 2.3 %collective-permute-start.19 = (bf16[2,64,640]{2,1,0:T(8,128)(2,1)S(1)}, bf16[2,64,640]{2,1,0:T(8,128)(2,1)S(1)}, u32[]{:S(2)}, u32[]{:S(2)}) collective-permute-start(bf16[2,64,640]{2,1,0:T(8,128)(2,1)S(1)} %get-tuple-element.82), channel_id=1, source_target_pairs={{0,2},{1,3},{2,4},{3,5},{4,6},{5,7},{6,0},{7,1},{8,10},{9,11},{10,... | collective-permute-start | bytes 491528 | tf_op jit(solution)/shard_map/ppermute | solution.py:378
  129.0 1.8 %collective-permute-start.20 = (bf16[2,64,640]{2,1,0:T(8,128)(2,1)S(1)}, bf16[2,64,640]{2,1,0:T(8,128)(2,1)S(1)}, u32[]{:S(2)}, u32[]{:S(2)}) collective-permute-start(bf16[2,64,640]{2,1,0:T(8,128)(2,1)S(1)} %get-tuple-element.83), channel_id=1, source_target_pairs={{0,6},{1,7},{2,0},{3,1},{4,2},{5,3},{6,4},{7,5},{8,14},{9,15},{10,... | collective-permute-start | bytes 491528 | tf_op jit(solution)/shard_map/ppermute | solution.py:379
  130.8 3.5 %shard_map.156 = bf16[128,4096]{1,0:T(8,128)(2,1)} custom-call(s32[10]{0:T(128)S(1)} %stack.51.where, f32[128,512]{1,0:T(8,128)S(1)} %shard_map.152.sums, bf16[128,256]{1,0:T(8,128)(2,1)S(1)} %get-tuple-element.70.low, bf16[128,4096]{1,0:T(8,128)(2,1)S(1)} %get-tuple-element.73.grad, bf16[128,4096]{1,0:T(8,128)(2,1)S(1)} %bitcast.39, ...), custom_call_target="tpu_custom_call" | custom-call | flops 603979 | bytes 11091 | tf_op jit(solution)/shard_map/pallas_call | solution.py:52
  134.4 5.1 %shard_map.151 = bf16[128,4096]{1,0:T(8,128)(2,1)} custom-call(s32[10]{0:T(128)S(1)} %stack.51.where, bf16[128,4096]{1,0:T(8,128)(2,1)S(1)} %copy-done.11, bf16[128,4224]{1,0:T(8,128)(2,1)S(1)} %collective-permute-done.14.passed, f32[1,4096]{1,0:T(1,128)S(1)} %copy-done.12, bf16[256,4096]{1,0:T(8,128)(2,1)S(1)} %bitcast.29, bf16[256,512]{1,0:T(8,128)(2,1)S(1)} %bitcast.51, ...), custom_call_target="tpu_custom_call" | custom-call | flops 1073741 | bytes 12894 | tf_op jit(solution)/shard_map/pallas_call | solution.py:52
  139.5 1.5 %shard_map.158 = (f32[4,64,512]{2,1,0:T(8,128)}, f32[4,64,64]{2,1,0:T(8,128)}) custom-call(s32[1]{0:T(128)S(6)} %copy.16.ahead, s32[1]{0:T(128)S(6)} %copy.17.back, s32[10]{0:T(128)S(1)} %stack.51.where, bf16[128,4224]{1,0:T(8,128)(2,1)S(1)} %collective-permute-done.15.relayed, bf16[2,64,640]{2,1,0:T(8,128)(2,1)S(1)} %get-tuple-element.80.refs_0_, ...), custom_call_target="tpu_custom_call" | custom-call | bytes 1736 | tf_op jit(solution)/shard_map/pallas_call | solution.py:52
  (33 shorter events, 0.1 us)
Async XLA Ops:
  0.6 18.6 %collective-permute-start.2 = (bf16[512,512]{1,0:T(8,128)(2,1)}, bf16[512,512]{1,0:T(8,128)(2,1)S(1)}, u32[]{:S(2)}, u32[]{:S(2)}) collective-permute-start(bf16[512,512]{1,0:T(8,128)(2,1)} %bitcast.30), channel_id=1, source_target_pairs={{0,1},{1,0},{2,3},{3,2},{4,5},{5,4},{6,7},{7,6},{8,9},{9,8},{10,11... | collective-permute-start | bytes 1572872 | tf_op jit(solution)/shard_map/ppermute | solution.py:425
  0.7 18.5 %collective-permute-start = (bf16[512,512]{1,0:T(8,128)(2,1)}, bf16[512,512]{1,0:T(8,128)(2,1)S(1)}, u32[]{:S(2)}, u32[]{:S(2)}) collective-permute-start(bf16[512,512]{1,0:T(8,128)(2,1)} %bitcast.40), channel_id=1, source_target_pairs={{0,2},{1,7},{2,4},{3,1},{4,6},{5,3},{6,0},{7,5},{8,10},{9,15},{10,... | collective-permute-start | bytes 1572872 | tf_op jit(solution)/shard_map/ppermute | solution.py:425
  4.1 15.2 %collective-permute-start.1 = (bf16[512,512]{1,0:T(8,128)(2,1)}, bf16[512,512]{1,0:T(8,128)(2,1)S(1)}, u32[]{:S(2)}, u32[]{:S(2)}) collective-permute-start(bf16[512,512]{1,0:T(8,128)(2,1)} %bitcast.41), channel_id=1, source_target_pairs={{0,1},{1,0},{2,3},{3,2},{4,5},{5,4},{6,7},{7,6},{8,9},{9,8},{10,11... | collective-permute-start | bytes 1572872 | tf_op jit(solution)/shard_map/ppermute | solution.py:425
  7.2 17.3 %collective-permute-start.6 = (bf16[512,512]{1,0:T(8,128)(2,1)}, bf16[512,512]{1,0:T(8,128)(2,1)S(1)}, u32[]{:S(2)}, u32[]{:S(2)}) collective-permute-start(bf16[512,512]{1,0:T(8,128)(2,1)} %bitcast.31), channel_id=1, source_target_pairs={{0,2},{1,7},{2,4},{3,1},{4,6},{5,3},{6,0},{7,5},{8,10},{9,15},{10,... | collective-permute-start | bytes 1572872 | tf_op jit(solution)/shard_map/ppermute | solution.py:425
  10.0 1.6 %copy-start = (bf16[1,2,128,4096]{3,2,1,0:T(8,128)(2,1)S(1)}, bf16[1,2,128,4096]{3,2,1,0:T(8,128)(2,1)}, u32[]{:S(2)}) copy-start(bf16[1,2,128,4096]{3,2,1,0:T(8,128)(2,1)} %rows_s.3) | copy-start | bytes 6291460
  11.5 1.6 %copy-start.2 = (bf16[1,4,4096,64]{2,3,1,0:T(8,128)(2,1)S(1)}, bf16[1,4,4096,64]{2,3,1,0:T(8,128)(2,1)}, u32[]{:S(2)}) copy-start(bf16[1,4,4096,64]{2,3,1,0:T(8,128)(2,1)} %param.22) | copy-start | bytes 6291460
  13.1 1.2 copy-start.5
  14.4 0.7 copy-start.12
  15.1 44.2 %copy-start.4 = (bf16[1,512,512]{2,1,0:T(8,128)(2,1)S(1)}, bf16[1,512,512]{2,1,0:T(8,128)(2,1)}, u32[]{:S(2)}) copy-start(bf16[1,512,512]{2,1,0:T(8,128)(2,1)} %param.19) | copy-start | bytes 1572868
  15.1 44.2 %copy-start.7 = (bf16[1,512,512]{2,1,0:T(8,128)(2,1)S(1)}, bf16[1,512,512]{2,1,0:T(8,128)(2,1)}, u32[]{:S(2)}) copy-start(bf16[1,512,512]{2,1,0:T(8,128)(2,1)} %param.20) | copy-start | bytes 1572868
  15.1 44.2 %copy-start.8 = (bf16[1,128,4096]{2,1,0:T(8,128)(2,1)S(1)}, bf16[1,128,4096]{2,1,0:T(8,128)(2,1)}, u32[]{:S(2)}) copy-start(bf16[1,128,4096]{2,1,0:T(8,128)(2,1)} %param.13) | copy-start | bytes 3145732
  19.2 22.4 %collective-permute-start.4 = (bf16[512,512]{1,0:T(8,128)(2,1)S(1)}, bf16[512,512]{1,0:T(8,128)(2,1)S(1)}, u32[]{:S(2)}, u32[]{:S(2)}) collective-permute-start(bf16[512,512]{1,0:T(8,128)(2,1)S(1)} %collective-permute-done.refs_2_.refs_10_), channel_id=1, source_target_pairs={{0,2},{1,7},{2,4},{3,1},{4,6},{5,3},{6,0},{7,5},{8,10},{9,15},{10,... | collective-permute-start | bytes 1572872 | tf_op jit(solution)/shard_map/ppermute | solution.py:425
  24.6 29.7 %collective-permute-start.8 = (bf16[512,512]{1,0:T(8,128)(2,1)S(1)}, bf16[512,512]{1,0:T(8,128)(2,1)S(1)}, u32[]{:S(2)}, u32[]{:S(2)}) collective-permute-start(bf16[512,512]{1,0:T(8,128)(2,1)S(1)} %collective-permute-done.6.refs_8_.refs_2_), channel_id=1, source_target_pairs={{0,2},{1,7},{2,4},{3,1},{4,6},{5,3},{6,0},{7,5},{8,10},{9,15},{10,... | collective-permute-start | bytes 1572872 | tf_op jit(solution)/shard_map/ppermute | solution.py:425
  29.8 25.2 %collective-permute-start.3 = (bf16[512,512]{1,0:T(8,128)(2,1)S(1)}, bf16[512,512]{1,0:T(8,128)(2,1)S(1)}, u32[]{:S(2)}, u32[]{:S(2)}) collective-permute-start(bf16[512,512]{1,0:T(8,128)(2,1)S(1)} %collective-permute-done.refs_2_.refs_10_), channel_id=1, source_target_pairs={{0,1},{1,0},{2,3},{3,2},{4,5},{5,4},{6,7},{7,6},{8,9},{9,8},{10,11... | collective-permute-start | bytes 1572872 | tf_op jit(solution)/shard_map/ppermute | solution.py:425
  41.6 17.7 %collective-permute-start.7 = (bf16[512,512]{1,0:T(8,128)(2,1)S(1)}, bf16[512,512]{1,0:T(8,128)(2,1)S(1)}, u32[]{:S(2)}, u32[]{:S(2)}) collective-permute-start(bf16[512,512]{1,0:T(8,128)(2,1)S(1)} %collective-permute-done.6.refs_8_.refs_2_), channel_id=1, source_target_pairs={{0,1},{1,0},{2,3},{3,2},{4,5},{5,4},{6,7},{7,6},{8,9},{9,8},{10,11... | collective-permute-start | bytes 1572872 | tf_op jit(solution)/shard_map/ppermute | solution.py:425
  41.6 17.7 %collective-permute-start.5 = (bf16[512,512]{1,0:T(8,128)(2,1)S(1)}, bf16[512,512]{1,0:T(8,128)(2,1)S(1)}, u32[]{:S(2)}, u32[]{:S(2)}) collective-permute-start(bf16[512,512]{1,0:T(8,128)(2,1)S(1)} %collective-permute-done.4.refs_4_.refs_12_), channel_id=1, source_target_pairs={{0,1},{1,0},{2,3},{3,2},{4,5},{5,4},{6,7},{7,6},{8,9},{9,8},{10,11... | collective-permute-start | bytes 1572872 | tf_op jit(solution)/shard_map/ppermute | solution.py:425
  54.3 5.0 %collective-permute-start.9 = (bf16[512,512]{1,0:T(8,128)(2,1)S(1)}, bf16[512,512]{1,0:T(8,128)(2,1)S(1)}, u32[]{:S(2)}, u32[]{:S(2)}) collective-permute-start(bf16[512,512]{1,0:T(8,128)(2,1)S(1)} %collective-permute-done.8.refs_10_.refs_4_), channel_id=1, source_target_pairs={{0,1},{1,0},{2,3},{3,2},{4,5},{5,4},{6,7},{7,6},{8,9},{9,8},{10,11... | collective-permute-start | bytes 1572872 | tf_op jit(solution)/shard_map/ppermute | solution.py:425
  54.3 21.9 %collective-permute-start.10 = (bf16[512,512]{1,0:T(8,128)(2,1)S(1)}, bf16[512,512]{1,0:T(8,128)(2,1)S(1)}, u32[]{:S(2)}, u32[]{:S(2)}) collective-permute-start(bf16[512,512]{1,0:T(8,128)(2,1)S(1)} %collective-permute-done.4.refs_4_.refs_12_), channel_id=1, source_target_pairs={{0,2},{1,7},{2,4},{3,1},{4,6},{5,3},{6,0},{7,5},{8,10},{9,15},{10,... | collective-permute-start | bytes 1572872 | tf_op jit(solution)/shard_map/ppermute | solution.py:425
  55.0 26.8 %collective-permute-start.11 = (bf16[512,512]{1,0:T(8,128)(2,1)S(1)}, bf16[512,512]{1,0:T(8,128)(2,1)S(1)}, u32[]{:S(2)}, u32[]{:S(2)}) collective-permute-start(bf16[512,512]{1,0:T(8,128)(2,1)S(1)} %collective-permute-done.8.refs_10_.refs_4_), channel_id=1, source_target_pairs={{0,2},{1,7},{2,4},{3,1},{4,6},{5,3},{6,0},{7,5},{8,10},{9,15},{10,... | collective-permute-start | bytes 1572872 | tf_op jit(solution)/shard_map/ppermute | solution.py:425
  59.3 25.1 %copy-start.1 = (bf16[1,2,128,4096]{3,2,1,0:T(8,128)(2,1)S(1)}, bf16[1,2,128,4096]{3,2,1,0:T(8,128)(2,1)}, u32[]{:S(2)}) copy-start(bf16[1,2,128,4096]{3,2,1,0:T(8,128)(2,1)} %rows_s.3) | copy-start | bytes 6291460
  59.4 25.1 %copy-start.3 = (bf16[1,4,4096,64]{2,3,1,0:T(8,128)(2,1)S(1)}, bf16[1,4,4096,64]{2,3,1,0:T(8,128)(2,1)}, u32[]{:S(2)}) copy-start(bf16[1,4,4096,64]{2,3,1,0:T(8,128)(2,1)} %param.22) | copy-start | bytes 6291460
  59.4 25.1 %copy-start.9 = (bf16[1,4,64,512]{3,2,1,0:T(8,128)(2,1)S(1)}, bf16[1,4,64,512]{3,2,1,0:T(8,128)(2,1)}, u32[]{:S(2)}) copy-start(bf16[1,4,64,512]{3,2,1,0:T(8,128)(2,1)} %param.23) | copy-start | bytes 786436
  81.8 1.9 %collective-permute-start.12 = (bf16[512,512]{1,0:T(8,128)(2,1)S(1)}, bf16[512,512]{1,0:T(8,128)(2,1)S(1)}, u32[]{:S(2)}, u32[]{:S(2)}) collective-permute-start(bf16[512,512]{1,0:T(8,128)(2,1)S(1)} %collective-permute-done.10.far.refs_6_.refs_14_), channel_id=1, source_target_pairs={{0,1},{1,0},{2,3},{3,2},{4,5},{5,4},{6,7},{7,6},{8,9},{9,8},{10,11... | collective-permute-start | bytes 1572872 | tf_op jit(solution)/shard_map/ppermute | solution.py:425
  81.8 2.7 %collective-permute-start.13 = (bf16[512,512]{1,0:T(8,128)(2,1)S(1)}, bf16[512,512]{1,0:T(8,128)(2,1)S(1)}, u32[]{:S(2)}, u32[]{:S(2)}) collective-permute-start(bf16[512,512]{1,0:T(8,128)(2,1)S(1)} %collective-permute-done.11.refs_6_.far), channel_id=1, source_target_pairs={{0,1},{1,0},{2,3},{3,2},{4,5},{5,4},{6,7},{7,6},{8,9},{9,8},{10,11... | collective-permute-start | bytes 1572872 | tf_op jit(solution)/shard_map/ppermute | solution.py:425
  84.4 6.0 %copy-start.6 = (bf16[1,128,4096]{2,1,0:T(8,128)(2,1)S(1)}, bf16[1,128,4096]{2,1,0:T(8,128)(2,1)}, u32[]{:S(2)}) copy-start(bf16[1,128,4096]{2,1,0:T(8,128)(2,1)} %param.12) | copy-start | bytes 3145732
  87.8 32.0 %collective-permute-start.15 = (bf16[128,4224]{1,0:T(8,128)(2,1)S(1)}, bf16[128,4224]{1,0:T(8,128)(2,1)S(1)}, u32[]{:S(2)}, u32[]{:S(2)}) collective-permute-start(bf16[128,4224]{1,0:T(8,128)(2,1)S(1)} %get-tuple-element.59), channel_id=1, source_target_pairs={{8,0},{16,8},{24,16},{32,24},{40,32},{48,40},{56,48},{64,56},{72,6... | collective-permute-start | bytes 3244040 | tf_op jit(solution)/shard_map/ppermute | solution.py:482
  92.0 42.3 %collective-permute-start.14 = (bf16[128,4224]{1,0:T(8,128)(2,1)S(1)}, bf16[128,4224]{1,0:T(8,128)(2,1)S(1)}, u32[]{:S(2)}, u32[]{:S(2)}) collective-permute-start(bf16[128,4224]{1,0:T(8,128)(2,1)S(1)} %shard_map.150.out), channel_id=1, source_target_pairs={{0,8},{8,16},{16,24},{24,32},{32,40},{40,48},{48,56},{56,64},{64,7... | collective-permute-start | bytes 3244040 | tf_op jit(solution)/shard_map/ppermute | solution.py:485
  98.6 1.7 %collective-permute-start.16 = (bf16[4,64,640]{2,1,0:T(8,128)(2,1)S(1)}, bf16[4,64,640]{2,1,0:T(8,128)(2,1)S(1)}, u32[]{:S(2)}, u32[]{:S(2)}) collective-permute-start(bf16[4,64,640]{2,1,0:T(8,128)(2,1)S(1)} %get-tuple-element.68), channel_id=1, source_target_pairs={{0,1},{1,0},{2,3},{3,2},{4,5},{5,4},{6,7},{7,6},{8,9},{9,8},{10,11... | collective-permute-start | bytes 983048 | tf_op jit(solution)/shard_map/ppermute | solution.py:425
  98.7 21.1 %copy-start.10 = (bf16[128,4096]{1,0:T(8,128)(2,1)S(1)}, bf16[128,4096]{1,0:T(8,128)(2,1)}, u32[]{:S(2)}) copy-start(bf16[128,4096]{1,0:T(8,128)(2,1)} %target.1) | copy-start | bytes 3145732
  122.5 1.7 %collective-permute-start.17 = (bf16[4,64,640]{2,1,0:T(8,128)(2,1)S(1)}, bf16[4,64,640]{2,1,0:T(8,128)(2,1)S(1)}, u32[]{:S(2)}, u32[]{:S(2)}) collective-permute-start(bf16[4,64,640]{2,1,0:T(8,128)(2,1)S(1)} %get-tuple-element.79), channel_id=1, source_target_pairs={{0,1},{1,0},{2,3},{3,2},{4,5},{5,4},{6,7},{7,6},{8,9},{9,8},{10,11... | collective-permute-start | bytes 983048 | tf_op jit(solution)/shard_map/ppermute | solution.py:425
  124.3 15.2 %collective-permute-start.18 = (bf16[2,64,640]{2,1,0:T(8,128)(2,1)S(1)}, bf16[2,64,640]{2,1,0:T(8,128)(2,1)S(1)}, u32[]{:S(2)}, u32[]{:S(2)}) collective-permute-start(bf16[2,64,640]{2,1,0:T(8,128)(2,1)S(1)} %get-tuple-element.81), channel_id=1, source_target_pairs={{0,4},{1,5},{2,6},{3,7},{4,0},{5,1},{6,2},{7,3},{8,12},{9,13},{10,... | collective-permute-start | bytes 491528 | tf_op jit(solution)/shard_map/ppermute | solution.py:377
  126.7 12.8 %collective-permute-start.19 = (bf16[2,64,640]{2,1,0:T(8,128)(2,1)S(1)}, bf16[2,64,640]{2,1,0:T(8,128)(2,1)S(1)}, u32[]{:S(2)}, u32[]{:S(2)}) collective-permute-start(bf16[2,64,640]{2,1,0:T(8,128)(2,1)S(1)} %get-tuple-element.82), channel_id=1, source_target_pairs={{0,2},{1,3},{2,4},{3,5},{4,6},{5,7},{6,0},{7,1},{8,10},{9,11},{10,... | collective-permute-start | bytes 491528 | tf_op jit(solution)/shard_map/ppermute | solution.py:378
  129.0 10.5 %collective-permute-start.20 = (bf16[2,64,640]{2,1,0:T(8,128)(2,1)S(1)}, bf16[2,64,640]{2,1,0:T(8,128)(2,1)S(1)}, u32[]{:S(2)}, u32[]{:S(2)}) collective-permute-start(bf16[2,64,640]{2,1,0:T(8,128)(2,1)S(1)} %get-tuple-element.83), channel_id=1, source_target_pairs={{0,6},{1,7},{2,0},{3,1},{4,2},{5,3},{6,4},{7,5},{8,14},{9,15},{10,... | collective-permute-start | bytes 491528 | tf_op jit(solution)/shard_map/ppermute | solution.py:379
  130.8 3.6 %copy-start.11 = (bf16[128,4096]{1,0:T(8,128)(2,1)S(1)}, bf16[128,4096]{1,0:T(8,128)(2,1)}, u32[]{:S(2)}) copy-start(bf16[128,4096]{1,0:T(8,128)(2,1)} %fresh.1) | copy-start | bytes 3145732

commit v7 on v3

--- a/solution.py
+++ b/solution.py
@@ -169,7 +169,6 @@
 
 
 GRADS = [shape((ROWS, VALUES), BF), shape((ROWS, LOWS), BF)]
-KEPT = [pltpu.VMEM((8, ROWS, PART), F32)]
 
 
 def near_share(back, where, grad, normed, saved, factor, gain, down, up, outs, vals):
@@ -296,28 +295,47 @@
     )
 
 
-def second_input_kernel(where, grad, rows_f, rows_s, factor, gain, down, d_values, d_low, *refs):
-    blocks, (out, kept) = refs[:8], refs[8:]
+def project_kernel(where, normed, *refs):
+    blocks, out = refs[:8], refs[8]
+    total = jnp.zeros((ROWS, VALUES), F32)
+    for i in range(8):
+        total += dot(normed[:, columns(where[i])], blocks[i][...])
+    out[...] = total
+
+
+def project(where, normed, vals):
+    return call(
+        project_kernel, (where,), [normed, *vals], [shape((ROWS, VALUES), F32)],
+        2 * ROWS * WIDTH * VALUES,
+    )[0]
+
+
+def second_input_kernel(
+    where, sums, low, grad, rows_f, rows_s, factor, gain, down, d_values, d_low, *refs
+):
+    blocks, out = refs[:8], refs[8]
     last = where[9] == 1
     scale = factor[:, :1]
-    rows = lambda span: jnp.where(last, rows_f[:, span], rows_s[0, 0, :, span])
-    mean = jnp.zeros((ROWS, 1), F32)
-    for i in range(8):
-        span = columns(where[i])
-        gained = gained_block(d_values[...], d_low[...], span, gain, down, blocks[i])
-        kept[i] = gained
-        mean += jnp.sum(gained * (rows(span).astype(F32) * scale), axis=-1, keepdims=True)
-    input_gradient(where, grad, rows, scale, mean, lambda i: kept[i], out)
-
-
-def second_input(where, grad, rows, saved, factor, gain, down, d_values, d_low, blocks):
+    values, lowered = d_values[...], d_low[...]
+    inner = jnp.sum(values.astype(F32) * sums[...], axis=-1, keepdims=True)
+    inner += jnp.sum(lowered.astype(F32) * low[...].astype(F32), axis=-1, keepdims=True)
+    weight = scale * scale * inner * (1.0 / WIDTH)
+    for i in range(8):
+        span = columns(where[i])
+        rows = jnp.where(last, rows_f[:, span], rows_s[0, 0, :, span]).astype(F32)
+        gained = gained_block(values, lowered, span, gain, down, blocks[i])
+        out[:, span] = (grad[:, span].astype(F32) + scale * gained - weight * rows).astype(BF)
+
+
+def second_input(where, sums, low, grad, rows, saved, factor, gain, down, d_values, d_low, blocks):
     return call(
         second_input_kernel,
         (where,),
-        [grad, rows, saved_of(saved, 1), factor, gain, down, d_values, d_low, *blocks],
+        [
+            sums, low, grad, rows, saved_of(saved, 1), factor, gain, down, d_values, d_low, *blocks
+        ],
         [shape((ROWS, WIDTH), BF)],
         2 * ROWS * WIDTH * (VALUES + RANK),
-        KEPT,
     )[0]
 
 
@@ -352,41 +370,29 @@
     )[0]
 
 
-def pair_sum_kernel(mine, other, total):
-    total[...] = (mine[...].astype(F32) + other[...].astype(F32)).astype(BF)
-
-
-def pair_sum(mine, other):
-    return call(pair_sum_kernel, (), [mine, other], [shape((4, RANK, PACK), BF)], 0)[0]
-
-
-def stack_kernel(first, mine, other, own, one, two, three):
+def pair_sum_kernel(mine, other, own, one, two, three):
     for ahead, ref in enumerate((own, one, two, three)):
-        ref[0] = first[ahead]
-        ref[1] = (mine[ahead].astype(F32) + other[ahead].astype(F32)).astype(BF)
-
-
-def spread(first, mine, received):
-    block = shape((2, RANK, PACK), BF)
-    own, one, two, three = call(stack_kernel, (), [first, mine, received], [block] * 4, 0)
-    return (
-        own,
-        lax.ppermute(two, "dp", chips(2)),
-        lax.ppermute(one, "dp", chips(1)),
-        lax.ppermute(three, "dp", chips(3)),
-    )
+        ref[...] = (mine[ahead].astype(F32) + other[ahead].astype(F32)).astype(BF)
+
+
+def chip_sums(mine, received):
+    return call(pair_sum_kernel, (), [mine, received], [shape((RANK, PACK), BF)] * 4, 0)
+
+
+def spread(own, one, two, three):
+    return (own, *(send(block, chips(k)) for k, block in ((2, two), (1, one), (3, three))))
 
 
 def tables_kernel(ahead, back, where, relayed, *refs):
-    terms, (down, up) = refs[:4], refs[4:]
+    terms, (down, up) = refs[:8], refs[8:]
     core = where[0] % 2
     came = relayed[:RANK, :1].astype(F32).astype(jnp.int32)
     ident = jnp.where(where[9] == 1, ahead[0], came)
     sums = []
     for tick in range(2):
-        total = terms[0][tick].astype(F32)
+        total = terms[4 * tick][...].astype(F32)
         for k in range(1, 4):
-            total += terms[k][tick].astype(F32)
+            total += terms[4 * tick + k][...].astype(F32)
         sums.append(total)
     for label in range(ADAPTERS):
         one = jnp.where(back[0] == label, 1.0, 0.0)
@@ -474,27 +480,33 @@
         back, where, grad, normed_f, saved, factor_b, gain, down, up, outs, vals
     )
     mine, other = pack(where, low_b, normed_b, d_values, d_low)
-    first_sums = pair_sum(mine, send(other, CORE))
-    val_far, first_sums = lax.optimization_barrier((val_far, first_sums))
+    first_sums = chip_sums(mine, send(other, CORE))
+    val_far, *first_sums = lax.optimization_barrier((val_far, *first_sums))
     vals += [val_far, send(val_far, CORE)]
 
     first_back = first_gradient(
         back, where, kept, inner, d_values, d_low, grad, saved, factor_b, gain, down, vals
     )
     relayed = lax.ppermute(first_back, "section", before)
-    share_f, first_back = lax.optimization_barrier((share_f, first_back))
+    share_f, first_back, *first_sums = lax.optimization_barrier(
+        (share_f, first_back, *first_sums)
+    )
+    first_terms = list(spread(*first_sums))
+    share_f, first_terms[2] = lax.optimization_barrier((share_f, first_terms[2]))
     first_out = output(ahead, where, share_f, normed_f, low_f, up, rows, outs, vals)
     passed = lax.ppermute(first_out, "section", onward)
+    sums_n = project(where, normed_n, vals)
+    relayed, sums_n, *first_terms = lax.optimization_barrier((relayed, sums_n, *first_terms))
 
     grad_n, d_values, d_low, mine, other = second_values(
         ahead, where, relayed, first_out, target, low_n, normed_n, up, outs
     )
-    terms = spread(first_sums, mine, send(other, CORE))
+    second_terms = spread(*chip_sums(mine, send(other, CORE)))
     bwd_out = second_input(
-        where, grad_n, rows, saved, factor_n, gain, down, d_values, d_low, vals
+        where, sums_n, low_n, grad_n, rows, saved, factor_n, gain, down, d_values, d_low, vals
     )
     fwd_out = forward(where, fresh, passed, gain, down, up, vals, outs)
-    down_table, up_table = tables(ahead, back, where, relayed, terms)
+    down_table, up_table = tables(ahead, back, where, relayed, (*first_terms, *second_terms))
     return (
         fwd_out[None], bwd_out[None], jnp.swapaxes(down_table, 1, 2)[None], up_table[None]
     )

time: 141 us -> 155 us (1.099)
  starting transfers between devices: 47.2 us -> 63.7 us
  waiting for transfers between devices: 58.1 us -> 56.4 us
    ppermute x16 -> x22, starting transfers between devices: 31.6 us -> 56 us  [send(): return lax.ppermute(block, 'dp', pairs)]
    ppermute x1, waiting for transfers between devices: 22.2 us -> 0.01 us  [body(): relayed = lax.ppermute(first_back, 'section', before)]
    ppermute x16 -> x22, waiting for transfers between devices: 36 us -> 56.4 us  [send(): return lax.ppermute(block, 'dp', pairs)]
    ppermute x3 -> x0, starting transfers between devices: 7.42 us -> none  [the longest x1 3.28 us: spread(): lax.ppermute(two, 'dp', chips(2))]
    pallas_call x11 -> x12, Pallas kernels: 26.8 us -> 27.5 us  [call(): pl.pallas_call(kernel, out_shape=outs, grid_spec=pltpu.PrefetchScalarGrid...]
  transfers between devices with their start and end apart: 21 -> 24, of which waited for: 9 -> 9; matrix products, arithmetic and copies ran while one was open for 0% -> 0% of each run, Pallas kernels for 17% -> 16%
where the time goes in v7:
time: 155 us
  starting transfers between devices  63.7 us (41%)
  waiting for transfers between devices  56.4 us (36%)
  Pallas kernels  27.5 us (18%)
  local copies, waits for them, and re-layouts  5.25 us (3%)
  between operations  2.08 us (1%)
    ppermute x22, waiting for transfers between devices, send(): return lax.ppermute(block, 'dp', pairs)  56.4 us
    ppermute x22, starting transfers between devices, send(): return lax.ppermute(block, 'dp', pairs)  56 us
    pallas_call x12, Pallas kernels, call(): pl.pallas_call(kernel, out_shape=outs, grid_spec=pltpu.PrefetchScalarGrid...  27.5 us
    unnamed x26, local copies, waits for them, and re-layouts  5.16 us
    ppermute x1, starting transfers between devices, body(): passed = lax.ppermute(first_out, 'section', onward)  5.05 us
  transfers between devices with their start and end apart: 24, of which 9 were waited for; matrix products, arithmetic and copies ran while one was open for 0% of the time, Pallas kernels for 16%

profile of v7, /device:TPU:30, one launch (start us, length us, event | category | flops | bytes accessed | tf_op | source)
XLA Modules:
  0.0 154.9 jit_solution(14621499428810096727)
XLA Ops:
  0.6 3.3 %collective-permute-start = (bf16[512,512]{1,0:T(8,128)(2,1)}, bf16[512,512]{1,0:T(8,128)(2,1)S(1)}, u32[]{:S(2)}, u32[]{:S(2)}) collective-permute-start(bf16[512,512]{1,0:T(8,128)(2,1)} %bitcast.34), channel_id=1, source_target_pairs={{0,2},{1,7},{2,4},{3,1},{4,6},{5,3},{6,0},{7,5},{8,10},{9,15},{10,... | collective-permute-start | bytes 1572872 | tf_op jit(solution)/shard_map/ppermute | solution.py:428
  4.0 4.5 %collective-permute-start.8 = (bf16[512,512]{1,0:T(8,128)(2,1)}, bf16[512,512]{1,0:T(8,128)(2,1)S(1)}, u32[]{:S(2)}, u32[]{:S(2)}) collective-permute-start(bf16[512,512]{1,0:T(8,128)(2,1)} %bitcast.41), channel_id=1, source_target_pairs={{0,2},{1,7},{2,4},{3,1},{4,6},{5,3},{6,0},{7,5},{8,10},{9,15},{10,... | collective-permute-start | bytes 1572872 | tf_op jit(solution)/shard_map/ppermute | solution.py:428
  8.5 1.6 %collective-permute-start.3 = (bf16[512,512]{1,0:T(8,128)(2,1)}, bf16[512,512]{1,0:T(8,128)(2,1)S(1)}, u32[]{:S(2)}, u32[]{:S(2)}) collective-permute-start(bf16[512,512]{1,0:T(8,128)(2,1)} %bitcast.35), channel_id=1, source_target_pairs={{0,6},{1,3},{2,0},{3,5},{4,2},{5,7},{6,4},{7,1},{8,14},{9,11},{10,... | collective-permute-start | bytes 1572872 | tf_op jit(solution)/shard_map/ppermute | solution.py:428
  11.3 0.1 stack.51.where
  11.4 1.6 %copy-done = bf16[1,2,128,4096]{3,2,1,0:T(8,128)(2,1)S(1)} copy-done((bf16[1,2,128,4096]{3,2,1,0:T(8,128)(2,1)S(1)}, bf16[1,2,128,4096]{3,2,1,0:T(8,128)(2,1)}, u32[]{:S(2)}) %copy-start) | copy-done | bytes 2097176
  13.0 1.6 %copy-done.2 = bf16[1,4,4096,64]{2,3,1,0:T(8,128)(2,1)S(1)} copy-done((bf16[1,4,4096,64]{2,3,1,0:T(8,128)(2,1)S(1)}, bf16[1,4,4096,64]{2,3,1,0:T(8,128)(2,1)}, u32[]{:S(2)}) %copy-start.2) | copy-done | bytes 2097176
  14.6 1.2 copy-done.4
  15.8 0.7 copy-done.12
  16.6 0.0 copy-start.8
  16.6 0.0 copy-start.9
  16.6 4.1 %shard_map.147 = (bf16[128,4096]{1,0:T(8,128)(2,1)S(1)}, f32[128,128]{1,0:T(8,128)}, bf16[128,256]{1,0:T(8,128)(2,1)S(1)}, bf16[128,4096]{1,0:T(8,128)(2,1)S(1)}...) custom-call(s32[1]{0:T(128)S(6)} %copy.16.ahead, ...), custom_call_target="tpu_custom_call" | custom-call | flops 805306 | bytes 7356 | tf_op jit(solution)/shard_map/pallas_call | solution.py:52
  20.7 0.0 collective-permute-done.refs_2_.refs_10_
  20.7 12.2 %collective-permute-start.7 = (bf16[512,512]{1,0:T(8,128)(2,1)S(1)}, bf16[512,512]{1,0:T(8,128)(2,1)S(1)}, u32[]{:S(2)}, u32[]{:S(2)}) collective-permute-start(bf16[512,512]{1,0:T(8,128)(2,1)S(1)} %bitcast.43), channel_id=1, source_target_pairs={{0,1},{1,0},{2,3},{3,2},{4,5},{5,4},{6,7},{7,6},{8,9},{9,8},{10,11... | collective-permute-start | bytes 1572872 | tf_op jit(solution)/shard_map/ppermute | solution.py:428
  32.9 2.3 %collective-permute-done.8.refs_10_.refs_2_ = bf16[512,512]{1,0:T(8,128)(2,1)S(1)} collective-permute-done((bf16[512,512]{1,0:T(8,128)(2,1)}, bf16[512,512]{1,0:T(8,128)(2,1)S(1)}, u32[]{:S(2)}, u32[]{:S(2)}) %collective-permute-start.8) | collective-permute-done | bytes 524320 | tf_op jit(solution)/shard_map/ppermute | solution.py:428
  35.2 19.4 %collective-permute-start.5 = (bf16[512,512]{1,0:T(8,128)(2,1)S(1)}, bf16[512,512]{1,0:T(8,128)(2,1)S(1)}, u32[]{:S(2)}, u32[]{:S(2)}) collective-permute-start(bf16[512,512]{1,0:T(8,128)(2,1)S(1)} %collective-permute-done.refs_2_.refs_10_), channel_id=1, source_target_pairs={{0,2},{1,7},{2,4},{3,1},{4,6},{5,3},{6,0},{7,5},{8,10},{9,15},{10,... | collective-permute-start | bytes 1572872 | tf_op jit(solution)/shard_map/ppermute | solution.py:428
  54.6 0.5 collective-permute-start.9
  55.1 0.1 collective-permute-start.11
  55.2 0.4 collective-permute-start.4
  55.6 13.7 %collective-permute-done.5.refs_6_.refs_14_ = bf16[512,512]{1,0:T(8,128)(2,1)S(1)} collective-permute-done((bf16[512,512]{1,0:T(8,128)(2,1)S(1)}, bf16[512,512]{1,0:T(8,128)(2,1)S(1)}, u32[]{:S(2)}, u32[]{:S(2)}) %collective-permute-start.5) | collective-permute-done | bytes 524320 | tf_op jit(solution)/shard_map/ppermute | solution.py:428
  69.4 1.0 collective-permute-start.12
  70.4 0.9 collective-permute-done.6.refs_7_.refs_15_
  71.3 4.7 %shard_map.148 = (bf16[128,512]{1,0:T(8,128)(2,1)S(1)}, bf16[128,256]{1,0:T(8,128)(2,1)S(1)}, f32[6,128,512]{2,1,0:T(8,128)S(1)}, f32[128,128]{1,0:T(8,128)S(1)}, f32[128,512]{1,0:T(8,128)S(1)}) custom-call(s32[1]{0:T(128)S(6)} %copy.17.back, s32[10]{0:T(128)S(1)} %stack.51.where, bf16[128,4096]{1,0:T(8,128)(2,1)S(1)} %bitcast.52, ...), custom_call_target="tpu_custom_call" | custom-call | flops 1610612 | bytes 13975 | tf_op jit(solution)/shard_map/pallas_call | solution.py:52
  76.0 1.0 shard_map.149
  77.0 1.3 collective-permute-start.13
  78.3 1.3 collective-permute-done.13.other
  79.6 0.1 shard_map.150
  79.7 4.3 %collective-permute-done.12.far.refs_6_ = bf16[512,512]{1,0:T(8,128)(2,1)S(1)} collective-permute-done((bf16[512,512]{1,0:T(8,128)(2,1)S(1)}, bf16[512,512]{1,0:T(8,128)(2,1)S(1)}, u32[]{:S(2)}, u32[]{:S(2)}) %collective-permute-start.12) | collective-permute-done | bytes 524320 | tf_op jit(solution)/shard_map/ppermute | solution.py:428
  84.0 0.1 collective-permute-start.14
  84.0 1.9 %collective-permute-done.14.far_other.refs_7_ = bf16[512,512]{1,0:T(8,128)(2,1)S(1)} collective-permute-done((bf16[512,512]{1,0:T(8,128)(2,1)S(1)}, bf16[512,512]{1,0:T(8,128)(2,1)S(1)}, u32[]{:S(2)}, u32[]{:S(2)}) %collective-permute-start.14) | collective-permute-done | bytes 524320 | tf_op jit(solution)/shard_map/ppermute | solution.py:428
  85.9 1.8 %shard_map.151 = bf16[128,4224]{1,0:T(8,128)(2,1)S(1)} custom-call(s32[1]{0:T(128)S(6)} %copy.17.back, s32[10]{0:T(128)S(1)} %stack.51.where, f32[6,128,512]{2,1,0:T(8,128)S(1)} %get-tuple-element.59.kept, f32[128,128]{1,0:T(8,128)S(1)} %get-tuple-element.60.inner, bf16[128,512]{1,0:T(8,128)(2,1)S(1)} %get-tuple-element.61.d_values.values, ...), custom_call_target="tpu_custom_call" | custom-call | flops 268435 | bytes 8208 | tf_op jit(solution)/shard_map/pallas_call | solution.py:52
  87.7 2.7 %collective-permute-start.17 = (bf16[128,4224]{1,0:T(8,128)(2,1)S(1)}, bf16[128,4224]{1,0:T(8,128)(2,1)S(1)}, u32[]{:S(2)}, u32[]{:S(2)}) collective-permute-start(bf16[128,4224]{1,0:T(8,128)(2,1)S(1)} %shard_map.151), channel_id=1, source_target_pairs={{8,0},{16,8},{24,16},{32,24},{40,32},{48,40},{56,48},{64,56},{72,6... | collective-permute-start | bytes 3244040 | tf_op jit(solution)/shard_map/ppermute | solution.py:490
  90.3 1.4 collective-permute-start.15
  91.7 5.8 %collective-permute-done.15.refs_2_ = bf16[64,640]{1,0:T(8,128)(2,1)S(1)} collective-permute-done((bf16[64,640]{1,0:T(8,128)(2,1)S(1)}, bf16[64,640]{1,0:T(8,128)(2,1)S(1)}, u32[]{:S(2)}, u32[]{:S(2)}) %collective-permute-start.15) | collective-permute-done | bytes 81952 | tf_op jit(solution)/shard_map/ppermute | solution.py:428
  97.5 1.6 %shard_map.152.out = bf16[128,4224]{1,0:T(8,128)(2,1)S(1)} custom-call(s32[1]{0:T(128)S(6)} %copy.16.ahead, s32[10]{0:T(128)S(1)} %stack.51.where, f32[128,512]{1,0:T(8,128)S(1)} %get-tuple-element.78.share, bf16[128,4096]{1,0:T(8,128)(2,1)S(1)} %get-tuple-element.55.normed, bf16[128,256]{1,0:T(8,128)(2,1)S(1)} %get-tuple-element.79.low, ...), custom_call_target="tpu_custom_call" | custom-call | flops 536870 | bytes 7929 | tf_op jit(solution)/shard_map/pallas_call | solution.py:52
  99.1 5.0 %collective-permute-start.16 = (bf16[128,4224]{1,0:T(8,128)(2,1)S(1)}, bf16[128,4224]{1,0:T(8,128)(2,1)S(1)}, u32[]{:S(2)}, u32[]{:S(2)}) collective-permute-start(bf16[128,4224]{1,0:T(8,128)(2,1)S(1)} %shard_map.152.out), channel_id=1, source_target_pairs={{0,8},{8,16},{16,24},{24,32},{32,40},{40,48},{48,56},{56,64},{64,7... | collective-permute-start | bytes 3244040 | tf_op jit(solution)/shard_map/ppermute | solution.py:497
  104.1 3.8 %collective-permute-start.18 = (bf16[64,640]{1,0:T(8,128)(2,1)S(1)}, bf16[64,640]{1,0:T(8,128)(2,1)S(1)}, u32[]{:S(2)}, u32[]{:S(2)}) collective-permute-start(bf16[64,640]{1,0:T(8,128)(2,1)S(1)} %get-tuple-element.82), channel_id=1, source_target_pairs={{0,4},{1,5},{2,6},{3,7},{4,0},{5,1},{6,2},{7,3},{8,12},{9,13},{10,... | collective-permute-start | bytes 245768 | tf_op jit(solution)/shard_map/ppermute | solution.py:428
  107.9 1.3 shard_map.154.sums
  109.1 24.7 %collective-permute-done.18.refs_1_ = bf16[64,640]{1,0:T(8,128)(2,1)S(1)} collective-permute-done((bf16[64,640]{1,0:T(8,128)(2,1)S(1)}, bf16[64,640]{1,0:T(8,128)(2,1)S(1)}, u32[]{:S(2)}, u32[]{:S(2)}) %collective-permute-start.18) | collective-permute-done | bytes 81952 | tf_op jit(solution)/shard_map/ppermute | solution.py:428
  133.8 2.7 %shard_map.155 = (bf16[128,4096]{1,0:T(8,128)(2,1)S(1)}, bf16[128,512]{1,0:T(8,128)(2,1)S(1)}, bf16[128,256]{1,0:T(8,128)(2,1)S(1)}, bf16[4,64,640]{2,1,0:T(8,128)(2,1)S(1)}, bf16[4,64,640]{2,1,0:T(8,128)(2,1)S(1)}) custom-call(s32[1]{0:T(128)S(6)} %copy.16.ahead, s32[10]{0:T(128)S(1)} %stack.51.where, ...), custom_call_target="tpu_custom_call" | custom-call | flops 603979 | bytes 8781 | tf_op jit(solution)/shard_map/pallas_call | solution.py:52
  136.5 0.1 collective-permute-start.20
  136.6 1.6 %collective-permute-done.20.other = bf16[4,64,640]{2,1,0:T(8,128)(2,1)S(1)} collective-permute-done((bf16[4,64,640]{2,1,0:T(8,128)(2,1)S(1)}, bf16[4,64,640]{2,1,0:T(8,128)(2,1)S(1)}, u32[]{:S(2)}, u32[]{:S(2)}) %collective-permute-start.20) | collective-permute-done | bytes 327712 | tf_op jit(solution)/shard_map/ppermute | solution.py:428
  138.2 0.1 shard_map.157
  138.3 2.3 %collective-permute-start.21 = (bf16[64,640]{1,0:T(8,128)(2,1)S(1)}, bf16[64,640]{1,0:T(8,128)(2,1)S(1)}, u32[]{:S(2)}, u32[]{:S(2)}) collective-permute-start(bf16[64,640]{1,0:T(8,128)(2,1)S(1)} %get-tuple-element.99), channel_id=1, source_target_pairs={{0,4},{1,5},{2,6},{3,7},{4,0},{5,1},{6,2},{7,3},{8,12},{9,13},{10,... | collective-permute-start | bytes 245768 | tf_op jit(solution)/shard_map/ppermute | solution.py:428
  140.6 0.0 collective-permute-start.22
  140.6 4.1 %collective-permute-start.23 = (bf16[64,640]{1,0:T(8,128)(2,1)S(1)}, bf16[64,640]{1,0:T(8,128)(2,1)S(1)}, u32[]{:S(2)}, u32[]{:S(2)}) collective-permute-start(bf16[64,640]{1,0:T(8,128)(2,1)S(1)} %get-tuple-element.101), channel_id=1, source_target_pairs={{0,6},{1,7},{2,0},{3,1},{4,2},{5,3},{6,4},{7,5},{8,14},{9,15},{10,... | collective-permute-start | bytes 245768 | tf_op jit(solution)/shard_map/ppermute | solution.py:428
  144.7 3.6 %shard_map.156 = bf16[128,4096]{1,0:T(8,128)(2,1)} custom-call(s32[10]{0:T(128)S(1)} %stack.51.where, f32[128,512]{1,0:T(8,128)S(1)} %shard_map.154.sums, bf16[128,256]{1,0:T(8,128)(2,1)S(1)} %get-tuple-element.86.low, bf16[128,4096]{1,0:T(8,128)(2,1)S(1)} %get-tuple-element.88.grad, bf16[128,4096]{1,0:T(8,128)(2,1)S(1)} %bitcast.33, ...), custom_call_target="tpu_custom_call" | custom-call | flops 603979 | bytes 11091 | tf_op jit(solution)/shard_map/pallas_call | solution.py:52
  148.3 5.1 %shard_map.153 = bf16[128,4096]{1,0:T(8,128)(2,1)} custom-call(s32[10]{0:T(128)S(1)} %stack.51.where, bf16[128,4096]{1,0:T(8,128)(2,1)S(1)} %copy-done.11, bf16[128,4224]{1,0:T(8,128)(2,1)S(1)} %collective-permute-done.16.passed, f32[1,4096]{1,0:T(1,128)S(1)} %copy-done.12, bf16[256,4096]{1,0:T(8,128)(2,1)S(1)} %bitcast.30, bf16[256,512]{1,0:T(8,128)(2,1)S(1)} %bitcast.51, ...), custom_call_target="tpu_custom_call" | custom-call | flops 1073741 | bytes 12894 | tf_op jit(solution)/shard_map/pallas_call | solution.py:52
  153.4 1.5 shard_map.158
  (39 shorter events, 0.1 us)
Async XLA Ops:
  0.6 20.1 %collective-permute-start = (bf16[512,512]{1,0:T(8,128)(2,1)}, bf16[512,512]{1,0:T(8,128)(2,1)S(1)}, u32[]{:S(2)}, u32[]{:S(2)}) collective-permute-start(bf16[512,512]{1,0:T(8,128)(2,1)} %bitcast.34), channel_id=1, source_target_pairs={{0,2},{1,7},{2,4},{3,1},{4,6},{5,3},{6,0},{7,5},{8,10},{9,15},{10,... | collective-permute-start | bytes 1572872 | tf_op jit(solution)/shard_map/ppermute | solution.py:428
  4.0 31.3 %collective-permute-start.8 = (bf16[512,512]{1,0:T(8,128)(2,1)}, bf16[512,512]{1,0:T(8,128)(2,1)S(1)}, u32[]{:S(2)}, u32[]{:S(2)}) collective-permute-start(bf16[512,512]{1,0:T(8,128)(2,1)} %bitcast.41), channel_id=1, source_target_pairs={{0,2},{1,7},{2,4},{3,1},{4,6},{5,3},{6,0},{7,5},{8,10},{9,15},{10,... | collective-permute-start | bytes 1572872 | tf_op jit(solution)/shard_map/ppermute | solution.py:428
  8.5 46.2 %collective-permute-start.10 = (bf16[512,512]{1,0:T(8,128)(2,1)}, bf16[512,512]{1,0:T(8,128)(2,1)S(1)}, u32[]{:S(2)}, u32[]{:S(2)}) collective-permute-start(bf16[512,512]{1,0:T(8,128)(2,1)} %bitcast.42), channel_id=1, source_target_pairs={{0,6},{1,3},{2,0},{3,5},{4,2},{5,7},{6,4},{7,1},{8,14},{9,11},{10,... | collective-permute-start | bytes 1572872 | tf_op jit(solution)/shard_map/ppermute | solution.py:428
  8.5 46.2 %collective-permute-start.3 = (bf16[512,512]{1,0:T(8,128)(2,1)}, bf16[512,512]{1,0:T(8,128)(2,1)S(1)}, u32[]{:S(2)}, u32[]{:S(2)}) collective-permute-start(bf16[512,512]{1,0:T(8,128)(2,1)} %bitcast.35), channel_id=1, source_target_pairs={{0,6},{1,3},{2,0},{3,5},{4,2},{5,7},{6,4},{7,1},{8,14},{9,11},{10,... | collective-permute-start | bytes 1572872 | tf_op jit(solution)/shard_map/ppermute | solution.py:428
  10.0 45.1 %collective-permute-start.1 = (bf16[512,512]{1,0:T(8,128)(2,1)}, bf16[512,512]{1,0:T(8,128)(2,1)S(1)}, u32[]{:S(2)}, u32[]{:S(2)}) collective-permute-start(bf16[512,512]{1,0:T(8,128)(2,1)} %bitcast.36), channel_id=1, source_target_pairs={{0,1},{1,0},{2,3},{3,2},{4,5},{5,4},{6,7},{7,6},{8,9},{9,8},{10,11... | collective-permute-start | bytes 1572872 | tf_op jit(solution)/shard_map/ppermute | solution.py:428
  11.4 1.6 %copy-start = (bf16[1,2,128,4096]{3,2,1,0:T(8,128)(2,1)S(1)}, bf16[1,2,128,4096]{3,2,1,0:T(8,128)(2,1)}, u32[]{:S(2)}) copy-start(bf16[1,2,128,4096]{3,2,1,0:T(8,128)(2,1)} %rows_s.3) | copy-start | bytes 6291460
  13.0 1.6 %copy-start.2 = (bf16[1,4,4096,64]{2,3,1,0:T(8,128)(2,1)S(1)}, bf16[1,4,4096,64]{2,3,1,0:T(8,128)(2,1)}, u32[]{:S(2)}) copy-start(bf16[1,4,4096,64]{2,3,1,0:T(8,128)(2,1)} %param.22) | copy-start | bytes 6291460
  14.6 1.2 copy-start.4
  15.8 0.7 copy-start.12
  16.5 4.2 %copy-start.7 = (bf16[1,512,512]{2,1,0:T(8,128)(2,1)S(1)}, bf16[1,512,512]{2,1,0:T(8,128)(2,1)}, u32[]{:S(2)}) copy-start(bf16[1,512,512]{2,1,0:T(8,128)(2,1)} %param.19) | copy-start | bytes 1572868
  16.5 54.7 %copy-start.1 = (bf16[1,2,128,4096]{3,2,1,0:T(8,128)(2,1)S(1)}, bf16[1,2,128,4096]{3,2,1,0:T(8,128)(2,1)}, u32[]{:S(2)}) copy-start(bf16[1,2,128,4096]{3,2,1,0:T(8,128)(2,1)} %rows_s.3) | copy-start | bytes 6291460
  16.5 54.7 %copy-start.3 = (bf16[1,4,4096,64]{2,3,1,0:T(8,128)(2,1)S(1)}, bf16[1,4,4096,64]{2,3,1,0:T(8,128)(2,1)}, u32[]{:S(2)}) copy-start(bf16[1,4,4096,64]{2,3,1,0:T(8,128)(2,1)} %param.22) | copy-start | bytes 6291460
  16.6 54.7 %copy-start.6 = (bf16[1,512,512]{2,1,0:T(8,128)(2,1)S(1)}, bf16[1,512,512]{2,1,0:T(8,128)(2,1)}, u32[]{:S(2)}) copy-start(bf16[1,512,512]{2,1,0:T(8,128)(2,1)} %param.20) | copy-start | bytes 1572868
  16.6 54.7 %copy-start.8 = (bf16[1,4,64,512]{3,2,1,0:T(8,128)(2,1)S(1)}, bf16[1,4,64,512]{3,2,1,0:T(8,128)(2,1)}, u32[]{:S(2)}) copy-start(bf16[1,4,64,512]{3,2,1,0:T(8,128)(2,1)} %param.23) | copy-start | bytes 786436
  16.6 54.7 %copy-start.9 = (bf16[1,128,4096]{2,1,0:T(8,128)(2,1)S(1)}, bf16[1,128,4096]{2,1,0:T(8,128)(2,1)}, u32[]{:S(2)}) copy-start(bf16[1,128,4096]{2,1,0:T(8,128)(2,1)} %param.13) | copy-start | bytes 3145732
  20.7 34.5 %collective-permute-start.7 = (bf16[512,512]{1,0:T(8,128)(2,1)S(1)}, bf16[512,512]{1,0:T(8,128)(2,1)S(1)}, u32[]{:S(2)}, u32[]{:S(2)}) collective-permute-start(bf16[512,512]{1,0:T(8,128)(2,1)S(1)} %bitcast.43), channel_id=1, source_target_pairs={{0,1},{1,0},{2,3},{3,2},{4,5},{5,4},{6,7},{7,6},{8,9},{9,8},{10,11... | collective-permute-start | bytes 1572872 | tf_op jit(solution)/shard_map/ppermute | solution.py:428
  35.2 34.1 %collective-permute-start.5 = (bf16[512,512]{1,0:T(8,128)(2,1)S(1)}, bf16[512,512]{1,0:T(8,128)(2,1)S(1)}, u32[]{:S(2)}, u32[]{:S(2)}) collective-permute-start(bf16[512,512]{1,0:T(8,128)(2,1)S(1)} %collective-permute-done.refs_2_.refs_10_), channel_id=1, source_target_pairs={{0,2},{1,7},{2,4},{3,1},{4,6},{5,3},{6,0},{7,5},{8,10},{9,15},{10,... | collective-permute-start | bytes 1572872 | tf_op jit(solution)/shard_map/ppermute | solution.py:428
  54.6 14.8 %collective-permute-start.2 = (bf16[512,512]{1,0:T(8,128)(2,1)S(1)}, bf16[512,512]{1,0:T(8,128)(2,1)S(1)}, u32[]{:S(2)}, u32[]{:S(2)}) collective-permute-start(bf16[512,512]{1,0:T(8,128)(2,1)S(1)} %collective-permute-done.refs_2_.refs_10_), channel_id=1, source_target_pairs={{0,1},{1,0},{2,3},{3,2},{4,5},{5,4},{6,7},{7,6},{8,9},{9,8},{10,11... | collective-permute-start | bytes 1572872 | tf_op jit(solution)/shard_map/ppermute | solution.py:428
  54.6 15.7 %collective-permute-start.9 = (bf16[512,512]{1,0:T(8,128)(2,1)S(1)}, bf16[512,512]{1,0:T(8,128)(2,1)S(1)}, u32[]{:S(2)}, u32[]{:S(2)}) collective-permute-start(bf16[512,512]{1,0:T(8,128)(2,1)S(1)} %collective-permute-done.8.refs_10_.refs_2_), channel_id=1, source_target_pairs={{0,1},{1,0},{2,3},{3,2},{4,5},{5,4},{6,7},{7,6},{8,9},{9,8},{10,11... | collective-permute-start | bytes 1572872 | tf_op jit(solution)/shard_map/ppermute | solution.py:428
  55.1 15.2 %collective-permute-start.11 = (bf16[512,512]{1,0:T(8,128)(2,1)S(1)}, bf16[512,512]{1,0:T(8,128)(2,1)S(1)}, u32[]{:S(2)}, u32[]{:S(2)}) collective-permute-start(bf16[512,512]{1,0:T(8,128)(2,1)S(1)} %collective-permute-done.10.refs_12_.refs_4_), channel_id=1, source_target_pairs={{0,1},{1,0},{2,3},{3,2},{4,5},{5,4},{6,7},{7,6},{8,9},{9,8},{10,11... | collective-permute-start | bytes 1572872 | tf_op jit(solution)/shard_map/ppermute | solution.py:428
  55.2 15.1 %collective-permute-start.4 = (bf16[512,512]{1,0:T(8,128)(2,1)S(1)}, bf16[512,512]{1,0:T(8,128)(2,1)S(1)}, u32[]{:S(2)}, u32[]{:S(2)}) collective-permute-start(bf16[512,512]{1,0:T(8,128)(2,1)S(1)} %collective-permute-done.3.refs_4_.refs_12_), channel_id=1, source_target_pairs={{0,1},{1,0},{2,3},{3,2},{4,5},{5,4},{6,7},{7,6},{8,9},{9,8},{10,11... | collective-permute-start | bytes 1572872 | tf_op jit(solution)/shard_map/ppermute | solution.py:428
  69.4 1.9 %collective-permute-start.6 = (bf16[512,512]{1,0:T(8,128)(2,1)S(1)}, bf16[512,512]{1,0:T(8,128)(2,1)S(1)}, u32[]{:S(2)}, u32[]{:S(2)}) collective-permute-start(bf16[512,512]{1,0:T(8,128)(2,1)S(1)} %collective-permute-done.5.refs_6_.refs_14_), channel_id=1, source_target_pairs={{0,1},{1,0},{2,3},{3,2},{4,5},{5,4},{6,7},{7,6},{8,9},{9,8},{10,11... | collective-permute-start | bytes 1572872 | tf_op jit(solution)/shard_map/ppermute | solution.py:428
  69.4 14.6 %collective-permute-start.12 = (bf16[512,512]{1,0:T(8,128)(2,1)S(1)}, bf16[512,512]{1,0:T(8,128)(2,1)S(1)}, u32[]{:S(2)}, u32[]{:S(2)}) collective-permute-start(bf16[512,512]{1,0:T(8,128)(2,1)S(1)} %collective-permute-done.8.refs_10_.refs_2_), channel_id=1, source_target_pairs={{0,2},{1,7},{2,4},{3,1},{4,6},{5,3},{6,0},{7,5},{8,10},{9,15},{10,... | collective-permute-start | bytes 1572872 | tf_op jit(solution)/shard_map/ppermute | solution.py:428
  77.0 2.6 %collective-permute-start.13 = (bf16[4,64,640]{2,1,0:T(8,128)(2,1)S(1)}, bf16[4,64,640]{2,1,0:T(8,128)(2,1)S(1)}, u32[]{:S(2)}, u32[]{:S(2)}) collective-permute-start(bf16[4,64,640]{2,1,0:T(8,128)(2,1)S(1)} %get-tuple-element.66), channel_id=1, source_target_pairs={{0,1},{1,0},{2,3},{3,2},{4,5},{5,4},{6,7},{7,6},{8,9},{9,8},{10,11... | collective-permute-start | bytes 983048 | tf_op jit(solution)/shard_map/ppermute | solution.py:428
  84.0 1.9 %collective-permute-start.14 = (bf16[512,512]{1,0:T(8,128)(2,1)S(1)}, bf16[512,512]{1,0:T(8,128)(2,1)S(1)}, u32[]{:S(2)}, u32[]{:S(2)}) collective-permute-start(bf16[512,512]{1,0:T(8,128)(2,1)S(1)} %collective-permute-done.12.far.refs_6_), channel_id=1, source_target_pairs={{0,1},{1,0},{2,3},{3,2},{4,5},{5,4},{6,7},{7,6},{8,9},{9,8},{10,11... | collective-permute-start | bytes 1572872 | tf_op jit(solution)/shard_map/ppermute | solution.py:428
  85.9 11.6 %copy-start.5 = (bf16[1,128,4096]{2,1,0:T(8,128)(2,1)S(1)}, bf16[1,128,4096]{2,1,0:T(8,128)(2,1)}, u32[]{:S(2)}) copy-start(bf16[1,128,4096]{2,1,0:T(8,128)(2,1)} %param.12) | copy-start | bytes 3145732
  87.7 46.2 %collective-permute-start.17 = (bf16[128,4224]{1,0:T(8,128)(2,1)S(1)}, bf16[128,4224]{1,0:T(8,128)(2,1)S(1)}, u32[]{:S(2)}, u32[]{:S(2)}) collective-permute-start(bf16[128,4224]{1,0:T(8,128)(2,1)S(1)} %shard_map.151), channel_id=1, source_target_pairs={{8,0},{16,8},{24,16},{32,24},{40,32},{48,40},{56,48},{64,56},{72,6... | collective-permute-start | bytes 3244040 | tf_op jit(solution)/shard_map/ppermute | solution.py:490
  90.3 7.2 %collective-permute-start.15 = (bf16[64,640]{1,0:T(8,128)(2,1)S(1)}, bf16[64,640]{1,0:T(8,128)(2,1)S(1)}, u32[]{:S(2)}, u32[]{:S(2)}) collective-permute-start(bf16[64,640]{1,0:T(8,128)(2,1)S(1)} %get-tuple-element.77), channel_id=1, source_target_pairs={{0,2},{1,3},{2,4},{3,5},{4,6},{5,7},{6,0},{7,1},{8,10},{9,11},{10,... | collective-permute-start | bytes 245768 | tf_op jit(solution)/shard_map/ppermute | solution.py:428
  99.1 49.2 %collective-permute-start.16 = (bf16[128,4224]{1,0:T(8,128)(2,1)S(1)}, bf16[128,4224]{1,0:T(8,128)(2,1)S(1)}, u32[]{:S(2)}, u32[]{:S(2)}) collective-permute-start(bf16[128,4224]{1,0:T(8,128)(2,1)S(1)} %shard_map.152.out), channel_id=1, source_target_pairs={{0,8},{8,16},{16,24},{24,32},{32,40},{40,48},{48,56},{56,64},{64,7... | collective-permute-start | bytes 3244040 | tf_op jit(solution)/shard_map/ppermute | solution.py:497
  104.1 29.7 %collective-permute-start.18 = (bf16[64,640]{1,0:T(8,128)(2,1)S(1)}, bf16[64,640]{1,0:T(8,128)(2,1)S(1)}, u32[]{:S(2)}, u32[]{:S(2)}) collective-permute-start(bf16[64,640]{1,0:T(8,128)(2,1)S(1)} %get-tuple-element.82), channel_id=1, source_target_pairs={{0,4},{1,5},{2,6},{3,7},{4,0},{5,1},{6,2},{7,3},{8,12},{9,13},{10,... | collective-permute-start | bytes 245768 | tf_op jit(solution)/shard_map/ppermute | solution.py:428
  107.9 26.0 %collective-permute-start.19 = (bf16[64,640]{1,0:T(8,128)(2,1)S(1)}, bf16[64,640]{1,0:T(8,128)(2,1)S(1)}, u32[]{:S(2)}, u32[]{:S(2)}) collective-permute-start(bf16[64,640]{1,0:T(8,128)(2,1)S(1)} %get-tuple-element.84), channel_id=1, source_target_pairs={{0,6},{1,7},{2,0},{3,1},{4,2},{5,3},{6,4},{7,5},{8,14},{9,15},{10,... | collective-permute-start | bytes 245768 | tf_op jit(solution)/shard_map/ppermute | solution.py:428
  107.9 26.0 %copy-start.10 = (bf16[128,4096]{1,0:T(8,128)(2,1)S(1)}, bf16[128,4096]{1,0:T(8,128)(2,1)}, u32[]{:S(2)}) copy-start(bf16[128,4096]{1,0:T(8,128)(2,1)} %target.1) | copy-start | bytes 3145732
  136.5 1.7 %collective-permute-start.20 = (bf16[4,64,640]{2,1,0:T(8,128)(2,1)S(1)}, bf16[4,64,640]{2,1,0:T(8,128)(2,1)S(1)}, u32[]{:S(2)}, u32[]{:S(2)}) collective-permute-start(bf16[4,64,640]{2,1,0:T(8,128)(2,1)S(1)} %get-tuple-element.97), channel_id=1, source_target_pairs={{0,1},{1,0},{2,3},{3,2},{4,5},{5,4},{6,7},{7,6},{8,9},{9,8},{10,11... | collective-permute-start | bytes 983048 | tf_op jit(solution)/shard_map/ppermute | solution.py:428
  138.3 15.1 %collective-permute-start.21 = (bf16[64,640]{1,0:T(8,128)(2,1)S(1)}, bf16[64,640]{1,0:T(8,128)(2,1)S(1)}, u32[]{:S(2)}, u32[]{:S(2)}) collective-permute-start(bf16[64,640]{1,0:T(8,128)(2,1)S(1)} %get-tuple-element.99), channel_id=1, source_target_pairs={{0,4},{1,5},{2,6},{3,7},{4,0},{5,1},{6,2},{7,3},{8,12},{9,13},{10,... | collective-permute-start | bytes 245768 | tf_op jit(solution)/shard_map/ppermute | solution.py:428
  140.6 12.8 %collective-permute-start.22 = (bf16[64,640]{1,0:T(8,128)(2,1)S(1)}, bf16[64,640]{1,0:T(8,128)(2,1)S(1)}, u32[]{:S(2)}, u32[]{:S(2)}) collective-permute-start(bf16[64,640]{1,0:T(8,128)(2,1)S(1)} %get-tuple-element.100), channel_id=1, source_target_pairs={{0,2},{1,3},{2,4},{3,5},{4,6},{5,7},{6,0},{7,1},{8,10},{9,11},{10,... | collective-permute-start | bytes 245768 | tf_op jit(solution)/shard_map/ppermute | solution.py:428
  140.6 12.8 %collective-permute-start.23 = (bf16[64,640]{1,0:T(8,128)(2,1)S(1)}, bf16[64,640]{1,0:T(8,128)(2,1)S(1)}, u32[]{:S(2)}, u32[]{:S(2)}) collective-permute-start(bf16[64,640]{1,0:T(8,128)(2,1)S(1)} %get-tuple-element.101), channel_id=1, source_target_pairs={{0,6},{1,7},{2,0},{3,1},{4,2},{5,3},{6,4},{7,5},{8,14},{9,15},{10,... | collective-permute-start | bytes 245768 | tf_op jit(solution)/shard_map/ppermute | solution.py:428
  144.7 3.6 %copy-start.11 = (bf16[128,4096]{1,0:T(8,128)(2,1)S(1)}, bf16[128,4096]{1,0:T(8,128)(2,1)}, u32[]{:S(2)}) copy-start(bf16[128,4096]{1,0:T(8,128)(2,1)} %fresh.1) | copy-start | bytes 3145732

commit v8 on v3

--- a/solution.py
+++ b/solution.py
@@ -169,7 +169,6 @@
 
 
 GRADS = [shape((ROWS, VALUES), BF), shape((ROWS, LOWS), BF)]
-KEPT = [pltpu.VMEM((8, ROWS, PART), F32)]
 
 
 def near_share(back, where, grad, normed, saved, factor, gain, down, up, outs, vals):
@@ -296,32 +295,51 @@
     )
 
 
-def second_input_kernel(where, grad, rows_f, rows_s, factor, gain, down, d_values, d_low, *refs):
-    blocks, (out, kept) = refs[:8], refs[8:]
+def project_kernel(where, normed, *refs):
+    blocks, out = refs[:8], refs[8]
+    total = jnp.zeros((ROWS, VALUES), F32)
+    for i in range(8):
+        total += dot(normed[:, columns(where[i])], blocks[i][...])
+    out[...] = total
+
+
+def project(where, normed, vals):
+    return call(
+        project_kernel, (where,), [normed, *vals], [shape((ROWS, VALUES), F32)],
+        2 * ROWS * WIDTH * VALUES,
+    )[0]
+
+
+def second_input_kernel(
+    where, sums, low, grad, rows_f, rows_s, factor, gain, down, d_values, d_low, *refs
+):
+    blocks, out = refs[:8], refs[8]
     last = where[9] == 1
     scale = factor[:, :1]
-    rows = lambda span: jnp.where(last, rows_f[:, span], rows_s[0, 0, :, span])
-    mean = jnp.zeros((ROWS, 1), F32)
-    for i in range(8):
-        span = columns(where[i])
-        gained = gained_block(d_values[...], d_low[...], span, gain, down, blocks[i])
-        kept[i] = gained
-        mean += jnp.sum(gained * (rows(span).astype(F32) * scale), axis=-1, keepdims=True)
-    input_gradient(where, grad, rows, scale, mean, lambda i: kept[i], out)
-
-
-def second_input(where, grad, rows, saved, factor, gain, down, d_values, d_low, blocks):
+    values, lowered = d_values[...], d_low[...]
+    inner = jnp.sum(values.astype(F32) * sums[...], axis=-1, keepdims=True)
+    inner += jnp.sum(lowered.astype(F32) * low[...].astype(F32), axis=-1, keepdims=True)
+    weight = scale * scale * inner * (1.0 / WIDTH)
+    for i in range(8):
+        span = columns(where[i])
+        rows = jnp.where(last, rows_f[:, span], rows_s[0, 0, :, span]).astype(F32)
+        gained = gained_block(values, lowered, span, gain, down, blocks[i])
+        out[:, span] = (grad[:, span].astype(F32) + scale * gained - weight * rows).astype(BF)
+
+
+def second_input(where, sums, low, grad, rows, saved, factor, gain, down, d_values, d_low, blocks):
     return call(
         second_input_kernel,
         (where,),
-        [grad, rows, saved_of(saved, 1), factor, gain, down, d_values, d_low, *blocks],
+        [
+            sums, low, grad, rows, saved_of(saved, 1), factor, gain, down, d_values, d_low, *blocks
+        ],
         [shape((ROWS, WIDTH), BF)],
         2 * ROWS * WIDTH * (VALUES + RANK),
-        KEPT,
     )[0]
 
 
-def forward_kernel(where, fresh, passed, gain, down, up, *refs):
+def forward_kernel(wrapped, where, fresh, passed, gain, down, up, *refs):
     vals, outs, (out, rows, normed) = refs[:8], refs[8:16], refs[16:]
     first = where[8] == 1
     for top in range(0, ROWS, 32):
@@ -330,7 +348,8 @@
         whole = chosen.astype(F32)
         rows[part, :] = chosen
         normed[part, :] = (whole * factor_of(whole) * gain[...]).astype(BF)
-    ident = passed[:, WIDTH : WIDTH + 1].astype(F32).astype(jnp.int32)
+    came = passed[:, WIDTH : WIDTH + 1].astype(F32).astype(jnp.int32)
+    ident = jnp.where(first, wrapped[0], came)
     low = only(dot_t(normed[...], down[...]), ident).astype(BF)
     total = SCALE * dot(low, up[...])
     for i in range(8):
@@ -341,10 +360,10 @@
         out[:, span] = (rows[:, span].astype(F32) + dot(values, outs[i][...])).astype(BF)
 
 
-def forward(where, fresh, passed, gain, down, up, vals, outs):
+def forward(wrapped, where, fresh, passed, gain, down, up, vals, outs):
     return call(
         forward_kernel,
-        (where,),
+        (wrapped, where),
         [fresh, passed, gain, down, up, *vals, *outs],
         [shape((ROWS, WIDTH), BF)],
         4 * ROWS * WIDTH * VALUES,
@@ -441,7 +460,7 @@
     value_projection, output_matrix, norm_gain_frozen, adapter_down, adapter_up,
 ):
     count = lax.axis_size("section")
-    onward = [(i, (i + 1) % count) for i in range(count)]
+    onward = [(i, i + 1) for i in range(count - 1)]
     before = [(i, i - 1) for i in range(1, count)]
     position = lax.axis_index("section")
     where = jnp.stack(
@@ -461,7 +480,9 @@
     normed_f, _, low_f, normed_b, factor_b, low_b, normed_n, factor_n, low_n = prepare(
         ahead, back, where, rows, saved, gain, down
     )
-    out_near, normed_f = lax.optimization_barrier((out_near, normed_f))
+    out_near, out_away, normed_f, out_sibling, val_sibling = lax.optimization_barrier(
+        (out_near, out_away, normed_f, out_sibling, val_sibling)
+    )
     out_far, val_far = send(out_near, split_ring(1)), send(val_near, split_ring(1))
     outs = [
         out_own, out_sibling, out_near, send(out_near, CORE), out_away, send(out_away, CORE)
@@ -485,15 +506,19 @@
     share_f, first_back = lax.optimization_barrier((share_f, first_back))
     first_out = output(ahead, where, share_f, normed_f, low_f, up, rows, outs, vals)
     passed = lax.ppermute(first_out, "section", onward)
+    first_out, sent, normed_n = lax.optimization_barrier((first_out, ahead, normed_n))
+    wrapped = lax.ppermute(sent, "section", [(count - 1, 0)])
+    sums_n = project(where, normed_n, vals)
+    relayed, sums_n, wrapped = lax.optimization_barrier((relayed, sums_n, wrapped))
 
     grad_n, d_values, d_low, mine, other = second_values(
         ahead, where, relayed, first_out, target, low_n, normed_n, up, outs
     )
     terms = spread(first_sums, mine, send(other, CORE))
     bwd_out = second_input(
-        where, grad_n, rows, saved, factor_n, gain, down, d_values, d_low, vals
-    )
-    fwd_out = forward(where, fresh, passed, gain, down, up, vals, outs)
+        where, sums_n, low_n, grad_n, rows, saved, factor_n, gain, down, d_values, d_low, vals
+    )
+    fwd_out = forward(wrapped, where, fresh, passed, gain, down, up, vals, outs)
     down_table, up_table = tables(ahead, back, where, relayed, terms)
     return (
         fwd_out[None], bwd_out[None], jnp.swapaxes(down_table, 1, 2)[None], up_table[None]

time: 141 us -> 141 us (level)
  waiting for transfers between devices: 58.1 us -> 41.6 us
  starting transfers between devices: 47.2 us -> 63 us
    ppermute x16, starting transfers between devices: 31.6 us -> 43.8 us  [send(): return lax.ppermute(block, 'dp', pairs)]
    ppermute x16, waiting for transfers between devices: 36 us -> 23.9 us  [send(): return lax.ppermute(block, 'dp', pairs)]
    ppermute x1, waiting for transfers between devices: 22.2 us -> 17.7 us  [body(): relayed = lax.ppermute(first_back, 'section', before)]
    ppermute x1, starting transfers between devices: 5.58 us -> 7.41 us  [body(): passed = lax.ppermute(first_out, 'section', onward)]
    pallas_call x11 -> x12, Pallas kernels: 26.8 us -> 28.1 us  [call(): pl.pallas_call(kernel, out_shape=outs, grid_spec=pltpu.PrefetchScalarGrid...]
  transfers between devices with their start and end apart: 21 -> 22, of which waited for: 9 -> 10; matrix products, arithmetic and copies ran while one was open for 0% -> 0% of each run, Pallas kernels for 17% -> 18%
where the time goes in v8:
time: 141 us; the launch traced here: 140 us
  starting transfers between devices  63 us (45%)
  waiting for transfers between devices  41.6 us (30%)
  Pallas kernels  28.1 us (20%)
  local copies, waits for them, and re-layouts  5.25 us (4%)
  between operations  2.1 us (1%)
    ppermute x16, starting transfers between devices, send(): return lax.ppermute(block, 'dp', pairs)  43.8 us
    pallas_call x12, Pallas kernels, call(): pl.pallas_call(kernel, out_shape=outs, grid_spec=pltpu.PrefetchScalarGrid...  28.1 us
    ppermute x16, waiting for transfers between devices, send(): return lax.ppermute(block, 'dp', pairs)  23.9 us
    ppermute x1, waiting for transfers between devices, body(): relayed = lax.ppermute(first_back, 'section', before)  17.7 us
    ppermute x1, starting transfers between devices, body(): passed = lax.ppermute(first_out, 'section', onward)  7.41 us
    unnamed x26, local copies, waits for them, and re-layouts  5.17 us
    ppermute x1, starting transfers between devices, spread(): lax.ppermute(two, 'dp', chips(2))  3.61 us
    ppermute x1, starting transfers between devices, spread(): lax.ppermute(three, 'dp', chips(3))  3.43 us
  transfers between devices with their start and end apart: 22, of which 10 were waited for; matrix products, arithmetic and copies ran while one was open for 0% of the time, Pallas kernels for 18%

profile of v8, /device:TPU:30, one launch (start us, length us, event | category | flops | bytes accessed | tf_op | source)
XLA Modules:
  0.0 140.1 jit_solution(10590034215991930758)
XLA Ops:
  0.6 3.3 %collective-permute-start = (bf16[512,512]{1,0:T(8,128)(2,1)}, bf16[512,512]{1,0:T(8,128)(2,1)S(1)}, u32[]{:S(2)}, u32[]{:S(2)}) collective-permute-start(bf16[512,512]{1,0:T(8,128)(2,1)} %bitcast.34), channel_id=1, source_target_pairs={{0,2},{1,7},{2,4},{3,1},{4,6},{5,3},{6,0},{7,5},{8,10},{9,15},{10,... | collective-permute-start | bytes 1572872 | tf_op jit(solution)/shard_map/ppermute | solution.py:441
  4.0 3.1 %collective-permute-start.1 = (bf16[512,512]{1,0:T(8,128)(2,1)}, bf16[512,512]{1,0:T(8,128)(2,1)S(1)}, u32[]{:S(2)}, u32[]{:S(2)}) collective-permute-start(bf16[512,512]{1,0:T(8,128)(2,1)} %bitcast.35), channel_id=1, source_target_pairs={{0,6},{1,3},{2,0},{3,5},{4,2},{5,7},{6,4},{7,1},{8,14},{9,11},{10,... | collective-permute-start | bytes 1572872 | tf_op jit(solution)/shard_map/ppermute | solution.py:441
  7.1 0.5 collective-permute-start.3
  7.6 1.4 collective-permute-start.8
  10.3 0.1 stack.51.where
  10.4 1.6 %copy-done = bf16[1,2,128,4096]{3,2,1,0:T(8,128)(2,1)S(1)} copy-done((bf16[1,2,128,4096]{3,2,1,0:T(8,128)(2,1)S(1)}, bf16[1,2,128,4096]{3,2,1,0:T(8,128)(2,1)}, u32[]{:S(2)}) %copy-start) | copy-done | bytes 2097176
  12.0 1.6 %copy-done.2 = bf16[1,4,4096,64]{2,3,1,0:T(8,128)(2,1)S(1)} copy-done((bf16[1,4,4096,64]{2,3,1,0:T(8,128)(2,1)S(1)}, bf16[1,4,4096,64]{2,3,1,0:T(8,128)(2,1)}, u32[]{:S(2)}) %copy-start.2) | copy-done | bytes 2097176
  13.5 1.2 copy-done.4
  14.8 0.7 copy-done.12
  15.5 0.0 copy-start.8
  15.5 0.0 copy-start.9
  15.5 4.1 %shard_map.147 = (bf16[128,4096]{1,0:T(8,128)(2,1)S(1)}, f32[128,128]{1,0:T(8,128)}, bf16[128,256]{1,0:T(8,128)(2,1)S(1)}, bf16[128,4096]{1,0:T(8,128)(2,1)S(1)}...) custom-call(s32[1]{0:T(128)S(6)} %copy.16.ahead, ...), custom_call_target="tpu_custom_call" | custom-call | flops 805306 | bytes 7356 | tf_op jit(solution)/shard_map/pallas_call | solution.py:52
  19.7 0.9 collective-permute-done.refs_2_.refs_10_
  20.5 6.2 %collective-permute-start.10 = (bf16[512,512]{1,0:T(8,128)(2,1)S(1)}, bf16[512,512]{1,0:T(8,128)(2,1)S(1)}, u32[]{:S(2)}, u32[]{:S(2)}) collective-permute-start(bf16[512,512]{1,0:T(8,128)(2,1)S(1)} %bitcast.43), channel_id=1, source_target_pairs={{0,6},{1,3},{2,0},{3,5},{4,2},{5,7},{6,4},{7,1},{8,14},{9,11},{10,... | collective-permute-start | bytes 1572872 | tf_op jit(solution)/shard_map/ppermute | solution.py:441
  26.8 8.6 %collective-permute-done.1.refs_4_.refs_12_ = bf16[512,512]{1,0:T(8,128)(2,1)S(1)} collective-permute-done((bf16[512,512]{1,0:T(8,128)(2,1)}, bf16[512,512]{1,0:T(8,128)(2,1)S(1)}, u32[]{:S(2)}, u32[]{:S(2)}) %collective-permute-start.1) | collective-permute-done | bytes 524320 | tf_op jit(solution)/shard_map/ppermute | solution.py:441
  35.4 4.0 %collective-permute-start.6 = (bf16[512,512]{1,0:T(8,128)(2,1)S(1)}, bf16[512,512]{1,0:T(8,128)(2,1)S(1)}, u32[]{:S(2)}, u32[]{:S(2)}) collective-permute-start(bf16[512,512]{1,0:T(8,128)(2,1)S(1)} %collective-permute-done.refs_2_.refs_10_), channel_id=1, source_target_pairs={{0,2},{1,7},{2,4},{3,1},{4,6},{5,3},{6,0},{7,5},{8,10},{9,15},{10,... | collective-permute-start | bytes 1572872 | tf_op jit(solution)/shard_map/ppermute | solution.py:441
  39.4 0.5 collective-permute-start.5
  39.9 3.8 %collective-permute-start.9 = (bf16[512,512]{1,0:T(8,128)(2,1)S(1)}, bf16[512,512]{1,0:T(8,128)(2,1)S(1)}, u32[]{:S(2)}, u32[]{:S(2)}) collective-permute-start(bf16[512,512]{1,0:T(8,128)(2,1)S(1)} %collective-permute-done.8.refs_10_.refs_2_), channel_id=1, source_target_pairs={{0,1},{1,0},{2,3},{3,2},{4,5},{5,4},{6,7},{7,6},{8,9},{9,8},{10,11... | collective-permute-start | bytes 1572872 | tf_op jit(solution)/shard_map/ppermute | solution.py:441
  43.7 3.0 %collective-permute-done.10.refs_12_.refs_4_ = bf16[512,512]{1,0:T(8,128)(2,1)S(1)} collective-permute-done((bf16[512,512]{1,0:T(8,128)(2,1)S(1)}, bf16[512,512]{1,0:T(8,128)(2,1)S(1)}, u32[]{:S(2)}, u32[]{:S(2)}) %collective-permute-start.10) | collective-permute-done | bytes 524320 | tf_op jit(solution)/shard_map/ppermute | solution.py:441
  46.7 19.9 %collective-permute-start.11 = (bf16[512,512]{1,0:T(8,128)(2,1)S(1)}, bf16[512,512]{1,0:T(8,128)(2,1)S(1)}, u32[]{:S(2)}, u32[]{:S(2)}) collective-permute-start(bf16[512,512]{1,0:T(8,128)(2,1)S(1)} %collective-permute-done.10.refs_12_.refs_4_), channel_id=1, source_target_pairs={{0,1},{1,0},{2,3},{3,2},{4,5},{5,4},{6,7},{7,6},{8,9},{9,8},{10,11... | collective-permute-start | bytes 1572872 | tf_op jit(solution)/shard_map/ppermute | solution.py:441
  66.6 0.0 collective-permute-start.7
  66.6 0.5 collective-permute-start.12
  67.1 1.0 collective-permute-done.11.refs_13_.refs_5_
  68.1 0.7 collective-permute-done.7.refs_7_.refs_15_
  68.9 4.7 %shard_map.148 = (bf16[128,512]{1,0:T(8,128)(2,1)S(1)}, bf16[128,256]{1,0:T(8,128)(2,1)S(1)}, f32[6,128,512]{2,1,0:T(8,128)S(1)}, f32[128,128]{1,0:T(8,128)S(1)}, f32[128,512]{1,0:T(8,128)S(1)}) custom-call(s32[1]{0:T(128)S(6)} %copy.17.back, s32[10]{0:T(128)S(1)} %stack.51.where, bf16[128,4096]{1,0:T(8,128)(2,1)S(1)} %bitcast.52, ...), custom_call_target="tpu_custom_call" | custom-call | flops 1610612 | bytes 13975 | tf_op jit(solution)/shard_map/pallas_call | solution.py:52
  73.6 1.0 shard_map.149
  74.6 0.5 collective-permute-start.13
  75.1 1.3 collective-permute-done.13.other
  76.3 0.1 shard_map.150.first
  76.4 4.9 %collective-permute-done.12.far.refs_6_ = bf16[512,512]{1,0:T(8,128)(2,1)S(1)} collective-permute-done((bf16[512,512]{1,0:T(8,128)(2,1)S(1)}, bf16[512,512]{1,0:T(8,128)(2,1)S(1)}, u32[]{:S(2)}, u32[]{:S(2)}) %collective-permute-start.12) | collective-permute-done | bytes 524320 | tf_op jit(solution)/shard_map/ppermute | solution.py:441
  81.3 1.9 %collective-permute-done.14.far_other.refs_7_ = bf16[512,512]{1,0:T(8,128)(2,1)S(1)} collective-permute-done((bf16[512,512]{1,0:T(8,128)(2,1)S(1)}, bf16[512,512]{1,0:T(8,128)(2,1)S(1)}, u32[]{:S(2)}, u32[]{:S(2)}) %collective-permute-start.14) | collective-permute-done | bytes 524320 | tf_op jit(solution)/shard_map/ppermute | solution.py:441
  83.2 1.8 %shard_map.151 = bf16[128,4224]{1,0:T(8,128)(2,1)S(1)} custom-call(s32[1]{0:T(128)S(6)} %copy.17.back, s32[10]{0:T(128)S(1)} %stack.51.where, f32[6,128,512]{2,1,0:T(8,128)S(1)} %get-tuple-element.51.kept, f32[128,128]{1,0:T(8,128)S(1)} %get-tuple-element.52.inner, bf16[128,512]{1,0:T(8,128)(2,1)S(1)} %get-tuple-element.53.d_values.values, ...), custom_call_target="tpu_custom_call" | custom-call | flops 268435 | bytes 8208 | tf_op jit(solution)/shard_map/pallas_call | solution.py:52
  85.0 2.7 %collective-permute-start.15 = (bf16[128,4224]{1,0:T(8,128)(2,1)S(1)}, bf16[128,4224]{1,0:T(8,128)(2,1)S(1)}, u32[]{:S(2)}, u32[]{:S(2)}) collective-permute-start(bf16[128,4224]{1,0:T(8,128)(2,1)S(1)} %shard_map.151), channel_id=1, source_target_pairs={{8,0},{16,8},{24,16},{32,24},{40,32},{48,40},{56,48},{64,56},{72,6... | collective-permute-start | bytes 3244040 | tf_op jit(solution)/shard_map/ppermute | solution.py:505
  87.6 1.6 %shard_map.152.out = bf16[128,4224]{1,0:T(8,128)(2,1)S(1)} custom-call(s32[1]{0:T(128)S(6)} %copy.16.ahead, s32[10]{0:T(128)S(1)} %stack.51.where, f32[128,512]{1,0:T(8,128)S(1)} %get-tuple-element.61.share, bf16[128,4096]{1,0:T(8,128)(2,1)S(1)} %get-tuple-element.45.normed, bf16[128,256]{1,0:T(8,128)(2,1)S(1)} %get-tuple-element.62.low, ...), custom_call_target="tpu_custom_call" | custom-call | flops 536870 | bytes 7929 | tf_op jit(solution)/shard_map/pallas_call | solution.py:52
  89.2 7.4 %collective-permute-start.17 = (bf16[128,4224]{1,0:T(8,128)(2,1)S(1)}, bf16[128,4224]{1,0:T(8,128)(2,1)S(1)}, u32[]{:S(2)}, u32[]{:S(2)}) collective-permute-start(bf16[128,4224]{1,0:T(8,128)(2,1)S(1)} %shard_map.152.out), channel_id=1, source_target_pairs={{0,8},{8,16},{16,24},{24,32},{32,40},{40,48},{48,56},{56,64},{64,7... | collective-permute-start | bytes 3244040 | tf_op jit(solution)/shard_map/ppermute | solution.py:508
  96.7 1.4 collective-permute-start.16
  98.0 1.3 shard_map.153.sums
  99.3 17.7 %collective-permute-done.15.relayed = bf16[128,4224]{1,0:T(8,128)(2,1)S(1)} collective-permute-done((bf16[128,4224]{1,0:T(8,128)(2,1)S(1)}, bf16[128,4224]{1,0:T(8,128)(2,1)S(1)}, u32[]{:S(2)}, u32[]{:S(2)}) %collective-permute-start.15) | collective-permute-done | bytes 1081376 | tf_op jit(solution)/shard_map/ppermute | solution.py:505
  117.0 2.7 %shard_map.155 = (bf16[128,4096]{1,0:T(8,128)(2,1)S(1)}, bf16[128,512]{1,0:T(8,128)(2,1)S(1)}, bf16[128,256]{1,0:T(8,128)(2,1)S(1)}, bf16[4,64,640]{2,1,0:T(8,128)(2,1)S(1)}, bf16[4,64,640]{2,1,0:T(8,128)(2,1)S(1)}) custom-call(s32[1]{0:T(128)S(6)} %copy.16.ahead, s32[10]{0:T(128)S(1)} %stack.51.where, ...), custom_call_target="tpu_custom_call" | custom-call | flops 603979 | bytes 8781 | tf_op jit(solution)/shard_map/pallas_call | solution.py:52
  119.6 0.1 collective-permute-start.18
  119.7 1.6 %collective-permute-done.18.other = bf16[4,64,640]{2,1,0:T(8,128)(2,1)S(1)} collective-permute-done((bf16[4,64,640]{2,1,0:T(8,128)(2,1)S(1)}, bf16[4,64,640]{2,1,0:T(8,128)(2,1)S(1)}, u32[]{:S(2)}, u32[]{:S(2)}) %collective-permute-start.18) | collective-permute-done | bytes 327712 | tf_op jit(solution)/shard_map/ppermute | solution.py:441
  121.4 0.1 shard_map.157
  121.4 3.6 %collective-permute-start.19 = (bf16[2,64,640]{2,1,0:T(8,128)(2,1)S(1)}, bf16[2,64,640]{2,1,0:T(8,128)(2,1)S(1)}, u32[]{:S(2)}, u32[]{:S(2)}) collective-permute-start(bf16[2,64,640]{2,1,0:T(8,128)(2,1)S(1)} %get-tuple-element.79), channel_id=1, source_target_pairs={{0,4},{1,5},{2,6},{3,7},{4,0},{5,1},{6,2},{7,3},{8,12},{9,13},{10,... | collective-permute-start | bytes 491528 | tf_op jit(solution)/shard_map/ppermute | solution.py:393
  125.1 0.7 collective-permute-start.20
  125.8 3.4 %collective-permute-start.21 = (bf16[2,64,640]{2,1,0:T(8,128)(2,1)S(1)}, bf16[2,64,640]{2,1,0:T(8,128)(2,1)S(1)}, u32[]{:S(2)}, u32[]{:S(2)}) collective-permute-start(bf16[2,64,640]{2,1,0:T(8,128)(2,1)S(1)} %get-tuple-element.81), channel_id=1, source_target_pairs={{0,6},{1,7},{2,0},{3,1},{4,2},{5,3},{6,4},{7,5},{8,14},{9,15},{10,... | collective-permute-start | bytes 491528 | tf_op jit(solution)/shard_map/ppermute | solution.py:395
  129.2 3.6 %shard_map.156 = bf16[128,4096]{1,0:T(8,128)(2,1)} custom-call(s32[10]{0:T(128)S(1)} %stack.51.where, f32[128,512]{1,0:T(8,128)S(1)} %shard_map.153.sums, bf16[128,256]{1,0:T(8,128)(2,1)S(1)} %get-tuple-element.68.low, bf16[128,4096]{1,0:T(8,128)(2,1)S(1)} %get-tuple-element.71.grad, bf16[128,4096]{1,0:T(8,128)(2,1)S(1)} %bitcast.33, ...), custom_call_target="tpu_custom_call" | custom-call | flops 603979 | bytes 11091 | tf_op jit(solution)/shard_map/pallas_call | solution.py:52
  132.8 5.7 %shard_map.154 = bf16[128,4096]{1,0:T(8,128)(2,1)} custom-call(s32[1]{0:T(128)} %collective-permute-done.16.wrapped, s32[10]{0:T(128)S(1)} %stack.51.where, bf16[128,4096]{1,0:T(8,128)(2,1)S(1)} %copy-done.11, bf16[128,4224]{1,0:T(8,128)(2,1)S(1)} %collective-permute-done.17.passed, f32[1,4096]{1,0:T(1,128)S(1)} %copy-done.12, ...), custom_call_target="tpu_custom_call" | custom-call | flops 1073741 | bytes 12894 | tf_op jit(solution)/shard_map/pallas_call | solution.py:52
  138.5 1.5 %shard_map.158 = (f32[4,64,512]{2,1,0:T(8,128)}, f32[4,64,64]{2,1,0:T(8,128)}) custom-call(s32[1]{0:T(128)S(6)} %copy.16.ahead, s32[1]{0:T(128)S(6)} %copy.17.back, s32[10]{0:T(128)S(1)} %stack.51.where, bf16[128,4224]{1,0:T(8,128)(2,1)S(1)} %collective-permute-done.15.relayed, bf16[2,64,640]{2,1,0:T(8,128)(2,1)S(1)} %get-tuple-element.78.refs_0_, ...), custom_call_target="tpu_custom_call" | custom-call | bytes 1736 | tf_op jit(solution)/shard_map/pallas_call | solution.py:52
  (35 shorter events, 0.1 us)
Async XLA Ops:
  0.6 19.9 %collective-permute-start = (bf16[512,512]{1,0:T(8,128)(2,1)}, bf16[512,512]{1,0:T(8,128)(2,1)S(1)}, u32[]{:S(2)}, u32[]{:S(2)}) collective-permute-start(bf16[512,512]{1,0:T(8,128)(2,1)} %bitcast.34), channel_id=1, source_target_pairs={{0,2},{1,7},{2,4},{3,1},{4,6},{5,3},{6,0},{7,5},{8,10},{9,15},{10,... | collective-permute-start | bytes 1572872 | tf_op jit(solution)/shard_map/ppermute | solution.py:441
  4.0 31.4 %collective-permute-start.1 = (bf16[512,512]{1,0:T(8,128)(2,1)}, bf16[512,512]{1,0:T(8,128)(2,1)S(1)}, u32[]{:S(2)}, u32[]{:S(2)}) collective-permute-start(bf16[512,512]{1,0:T(8,128)(2,1)} %bitcast.35), channel_id=1, source_target_pairs={{0,6},{1,3},{2,0},{3,5},{4,2},{5,7},{6,4},{7,1},{8,14},{9,11},{10,... | collective-permute-start | bytes 1572872 | tf_op jit(solution)/shard_map/ppermute | solution.py:441
  7.1 28.2 %collective-permute-start.2 = (bf16[512,512]{1,0:T(8,128)(2,1)}, bf16[512,512]{1,0:T(8,128)(2,1)S(1)}, u32[]{:S(2)}, u32[]{:S(2)}) collective-permute-start(bf16[512,512]{1,0:T(8,128)(2,1)} %bitcast.36), channel_id=1, source_target_pairs={{0,1},{1,0},{2,3},{3,2},{4,5},{5,4},{6,7},{7,6},{8,9},{9,8},{10,11... | collective-permute-start | bytes 1572872 | tf_op jit(solution)/shard_map/ppermute | solution.py:441
  7.1 28.2 %collective-permute-start.3 = (bf16[512,512]{1,0:T(8,128)(2,1)}, bf16[512,512]{1,0:T(8,128)(2,1)S(1)}, u32[]{:S(2)}, u32[]{:S(2)}) collective-permute-start(bf16[512,512]{1,0:T(8,128)(2,1)} %bitcast.41), channel_id=1, source_target_pairs={{0,1},{1,0},{2,3},{3,2},{4,5},{5,4},{6,7},{7,6},{8,9},{9,8},{10,11... | collective-permute-start | bytes 1572872 | tf_op jit(solution)/shard_map/ppermute | solution.py:441
  7.6 32.3 %collective-permute-start.8 = (bf16[512,512]{1,0:T(8,128)(2,1)}, bf16[512,512]{1,0:T(8,128)(2,1)S(1)}, u32[]{:S(2)}, u32[]{:S(2)}) collective-permute-start(bf16[512,512]{1,0:T(8,128)(2,1)} %bitcast.42), channel_id=1, source_target_pairs={{0,2},{1,7},{2,4},{3,1},{4,6},{5,3},{6,0},{7,5},{8,10},{9,15},{10,... | collective-permute-start | bytes 1572872 | tf_op jit(solution)/shard_map/ppermute | solution.py:441
  10.4 1.6 %copy-start = (bf16[1,2,128,4096]{3,2,1,0:T(8,128)(2,1)S(1)}, bf16[1,2,128,4096]{3,2,1,0:T(8,128)(2,1)}, u32[]{:S(2)}) copy-start(bf16[1,2,128,4096]{3,2,1,0:T(8,128)(2,1)} %rows_s.3) | copy-start | bytes 6291460
  12.0 1.6 %copy-start.2 = (bf16[1,4,4096,64]{2,3,1,0:T(8,128)(2,1)S(1)}, bf16[1,4,4096,64]{2,3,1,0:T(8,128)(2,1)}, u32[]{:S(2)}) copy-start(bf16[1,4,4096,64]{2,3,1,0:T(8,128)(2,1)} %param.22) | copy-start | bytes 6291460
  13.5 1.2 copy-start.4
  14.8 0.7 copy-start.12
  15.5 5.1 %copy-start.7 = (bf16[1,512,512]{2,1,0:T(8,128)(2,1)S(1)}, bf16[1,512,512]{2,1,0:T(8,128)(2,1)}, u32[]{:S(2)}) copy-start(bf16[1,512,512]{2,1,0:T(8,128)(2,1)} %param.19) | copy-start | bytes 1572868
  15.5 53.4 %copy-start.1 = (bf16[1,2,128,4096]{3,2,1,0:T(8,128)(2,1)S(1)}, bf16[1,2,128,4096]{3,2,1,0:T(8,128)(2,1)}, u32[]{:S(2)}) copy-start(bf16[1,2,128,4096]{3,2,1,0:T(8,128)(2,1)} %rows_s.3) | copy-start | bytes 6291460
  15.5 53.4 %copy-start.3 = (bf16[1,4,4096,64]{2,3,1,0:T(8,128)(2,1)S(1)}, bf16[1,4,4096,64]{2,3,1,0:T(8,128)(2,1)}, u32[]{:S(2)}) copy-start(bf16[1,4,4096,64]{2,3,1,0:T(8,128)(2,1)} %param.22) | copy-start | bytes 6291460
  15.5 53.4 %copy-start.6 = (bf16[1,512,512]{2,1,0:T(8,128)(2,1)S(1)}, bf16[1,512,512]{2,1,0:T(8,128)(2,1)}, u32[]{:S(2)}) copy-start(bf16[1,512,512]{2,1,0:T(8,128)(2,1)} %param.20) | copy-start | bytes 1572868
  15.5 53.4 %copy-start.8 = (bf16[1,4,64,512]{3,2,1,0:T(8,128)(2,1)S(1)}, bf16[1,4,64,512]{3,2,1,0:T(8,128)(2,1)}, u32[]{:S(2)}) copy-start(bf16[1,4,64,512]{3,2,1,0:T(8,128)(2,1)} %param.23) | copy-start | bytes 786436
  15.5 53.4 %copy-start.9 = (bf16[1,128,4096]{2,1,0:T(8,128)(2,1)S(1)}, bf16[1,128,4096]{2,1,0:T(8,128)(2,1)}, u32[]{:S(2)}) copy-start(bf16[1,128,4096]{2,1,0:T(8,128)(2,1)} %param.13) | copy-start | bytes 3145732
  20.5 26.2 %collective-permute-start.10 = (bf16[512,512]{1,0:T(8,128)(2,1)S(1)}, bf16[512,512]{1,0:T(8,128)(2,1)S(1)}, u32[]{:S(2)}, u32[]{:S(2)}) collective-permute-start(bf16[512,512]{1,0:T(8,128)(2,1)S(1)} %bitcast.43), channel_id=1, source_target_pairs={{0,6},{1,3},{2,0},{3,5},{4,2},{5,7},{6,4},{7,1},{8,14},{9,11},{10,... | collective-permute-start | bytes 1572872 | tf_op jit(solution)/shard_map/ppermute | solution.py:441
  35.4 31.2 %collective-permute-start.6 = (bf16[512,512]{1,0:T(8,128)(2,1)S(1)}, bf16[512,512]{1,0:T(8,128)(2,1)S(1)}, u32[]{:S(2)}, u32[]{:S(2)}) collective-permute-start(bf16[512,512]{1,0:T(8,128)(2,1)S(1)} %collective-permute-done.refs_2_.refs_10_), channel_id=1, source_target_pairs={{0,2},{1,7},{2,4},{3,1},{4,6},{5,3},{6,0},{7,5},{8,10},{9,15},{10,... | collective-permute-start | bytes 1572872 | tf_op jit(solution)/shard_map/ppermute | solution.py:441
  39.4 27.2 %collective-permute-start.4 = (bf16[512,512]{1,0:T(8,128)(2,1)S(1)}, bf16[512,512]{1,0:T(8,128)(2,1)S(1)}, u32[]{:S(2)}, u32[]{:S(2)}) collective-permute-start(bf16[512,512]{1,0:T(8,128)(2,1)S(1)} %collective-permute-done.refs_2_.refs_10_), channel_id=1, source_target_pairs={{0,1},{1,0},{2,3},{3,2},{4,5},{5,4},{6,7},{7,6},{8,9},{9,8},{10,11... | collective-permute-start | bytes 1572872 | tf_op jit(solution)/shard_map/ppermute | solution.py:441
  39.4 27.7 %collective-permute-start.5 = (bf16[512,512]{1,0:T(8,128)(2,1)S(1)}, bf16[512,512]{1,0:T(8,128)(2,1)S(1)}, u32[]{:S(2)}, u32[]{:S(2)}) collective-permute-start(bf16[512,512]{1,0:T(8,128)(2,1)S(1)} %collective-permute-done.1.refs_4_.refs_12_), channel_id=1, source_target_pairs={{0,1},{1,0},{2,3},{3,2},{4,5},{5,4},{6,7},{7,6},{8,9},{9,8},{10,11... | collective-permute-start | bytes 1572872 | tf_op jit(solution)/shard_map/ppermute | solution.py:441
  39.9 27.2 %collective-permute-start.9 = (bf16[512,512]{1,0:T(8,128)(2,1)S(1)}, bf16[512,512]{1,0:T(8,128)(2,1)S(1)}, u32[]{:S(2)}, u32[]{:S(2)}) collective-permute-start(bf16[512,512]{1,0:T(8,128)(2,1)S(1)} %collective-permute-done.8.refs_10_.refs_2_), channel_id=1, source_target_pairs={{0,1},{1,0},{2,3},{3,2},{4,5},{5,4},{6,7},{7,6},{8,9},{9,8},{10,11... | collective-permute-start | bytes 1572872 | tf_op jit(solution)/shard_map/ppermute | solution.py:441
  46.7 21.4 %collective-permute-start.11 = (bf16[512,512]{1,0:T(8,128)(2,1)S(1)}, bf16[512,512]{1,0:T(8,128)(2,1)S(1)}, u32[]{:S(2)}, u32[]{:S(2)}) collective-permute-start(bf16[512,512]{1,0:T(8,128)(2,1)S(1)} %collective-permute-done.10.refs_12_.refs_4_), channel_id=1, source_target_pairs={{0,1},{1,0},{2,3},{3,2},{4,5},{5,4},{6,7},{7,6},{8,9},{9,8},{10,11... | collective-permute-start | bytes 1572872 | tf_op jit(solution)/shard_map/ppermute | solution.py:441
  66.6 2.3 %collective-permute-start.7 = (bf16[512,512]{1,0:T(8,128)(2,1)S(1)}, bf16[512,512]{1,0:T(8,128)(2,1)S(1)}, u32[]{:S(2)}, u32[]{:S(2)}) collective-permute-start(bf16[512,512]{1,0:T(8,128)(2,1)S(1)} %collective-permute-done.6.refs_6_.refs_14_), channel_id=1, source_target_pairs={{0,1},{1,0},{2,3},{3,2},{4,5},{5,4},{6,7},{7,6},{8,9},{9,8},{10,11... | collective-permute-start | bytes 1572872 | tf_op jit(solution)/shard_map/ppermute | solution.py:441
  66.6 14.7 %collective-permute-start.12 = (bf16[512,512]{1,0:T(8,128)(2,1)S(1)}, bf16[512,512]{1,0:T(8,128)(2,1)S(1)}, u32[]{:S(2)}, u32[]{:S(2)}) collective-permute-start(bf16[512,512]{1,0:T(8,128)(2,1)S(1)} %collective-permute-done.8.refs_10_.refs_2_), channel_id=1, source_target_pairs={{0,2},{1,7},{2,4},{3,1},{4,6},{5,3},{6,0},{7,5},{8,10},{9,15},{10,... | collective-permute-start | bytes 1572872 | tf_op jit(solution)/shard_map/ppermute | solution.py:441
  74.6 1.7 %collective-permute-start.13 = (bf16[4,64,640]{2,1,0:T(8,128)(2,1)S(1)}, bf16[4,64,640]{2,1,0:T(8,128)(2,1)S(1)}, u32[]{:S(2)}, u32[]{:S(2)}) collective-permute-start(bf16[4,64,640]{2,1,0:T(8,128)(2,1)S(1)} %get-tuple-element.58), channel_id=1, source_target_pairs={{0,1},{1,0},{2,3},{3,2},{4,5},{5,4},{6,7},{7,6},{8,9},{9,8},{10,11... | collective-permute-start | bytes 983048 | tf_op jit(solution)/shard_map/ppermute | solution.py:441
  81.3 1.9 %collective-permute-start.14 = (bf16[512,512]{1,0:T(8,128)(2,1)S(1)}, bf16[512,512]{1,0:T(8,128)(2,1)S(1)}, u32[]{:S(2)}, u32[]{:S(2)}) collective-permute-start(bf16[512,512]{1,0:T(8,128)(2,1)S(1)} %collective-permute-done.12.far.refs_6_), channel_id=1, source_target_pairs={{0,1},{1,0},{2,3},{3,2},{4,5},{5,4},{6,7},{7,6},{8,9},{9,8},{10,11... | collective-permute-start | bytes 1572872 | tf_op jit(solution)/shard_map/ppermute | solution.py:441
  83.2 4.4 %copy-start.5 = (bf16[1,128,4096]{2,1,0:T(8,128)(2,1)S(1)}, bf16[1,128,4096]{2,1,0:T(8,128)(2,1)}, u32[]{:S(2)}) copy-start(bf16[1,128,4096]{2,1,0:T(8,128)(2,1)} %param.12) | copy-start | bytes 3145732
  85.0 32.0 %collective-permute-start.15 = (bf16[128,4224]{1,0:T(8,128)(2,1)S(1)}, bf16[128,4224]{1,0:T(8,128)(2,1)S(1)}, u32[]{:S(2)}, u32[]{:S(2)}) collective-permute-start(bf16[128,4224]{1,0:T(8,128)(2,1)S(1)} %shard_map.151), channel_id=1, source_target_pairs={{8,0},{16,8},{24,16},{32,24},{40,32},{48,40},{56,48},{64,56},{72,6... | collective-permute-start | bytes 3244040 | tf_op jit(solution)/shard_map/ppermute | solution.py:505
  89.2 43.5 %collective-permute-start.17 = (bf16[128,4224]{1,0:T(8,128)(2,1)S(1)}, bf16[128,4224]{1,0:T(8,128)(2,1)S(1)}, u32[]{:S(2)}, u32[]{:S(2)}) collective-permute-start(bf16[128,4224]{1,0:T(8,128)(2,1)S(1)} %shard_map.152.out), channel_id=1, source_target_pairs={{0,8},{8,16},{16,24},{24,32},{32,40},{40,48},{48,56},{56,64},{64,7... | collective-permute-start | bytes 3244040 | tf_op jit(solution)/shard_map/ppermute | solution.py:508
  96.6 20.3 %copy-start.10 = (bf16[128,4096]{1,0:T(8,128)(2,1)S(1)}, bf16[128,4096]{1,0:T(8,128)(2,1)}, u32[]{:S(2)}) copy-start(bf16[128,4096]{1,0:T(8,128)(2,1)} %target.1) | copy-start | bytes 3145732
  96.7 2.6 %collective-permute-start.16 = (s32[1]{0:T(128)}, s32[1]{0:T(128)}, u32[]{:S(2)}, u32[]{:S(2)}) collective-permute-start(s32[1]{0:T(128)} %param.17), channel_id=1, source_target_pairs={{248,0},{249,1},{250,2},{251,3},{252,4},{253,5},{254,6},{255,7}} | collective-permute-start | bytes 20 | tf_op jit(solution)/shard_map/ppermute | solution.py:510
  119.6 1.7 %collective-permute-start.18 = (bf16[4,64,640]{2,1,0:T(8,128)(2,1)S(1)}, bf16[4,64,640]{2,1,0:T(8,128)(2,1)S(1)}, u32[]{:S(2)}, u32[]{:S(2)}) collective-permute-start(bf16[4,64,640]{2,1,0:T(8,128)(2,1)S(1)} %get-tuple-element.77), channel_id=1, source_target_pairs={{0,1},{1,0},{2,3},{3,2},{4,5},{5,4},{6,7},{7,6},{8,9},{9,8},{10,11... | collective-permute-start | bytes 983048 | tf_op jit(solution)/shard_map/ppermute | solution.py:441
  121.4 17.1 %collective-permute-start.19 = (bf16[2,64,640]{2,1,0:T(8,128)(2,1)S(1)}, bf16[2,64,640]{2,1,0:T(8,128)(2,1)S(1)}, u32[]{:S(2)}, u32[]{:S(2)}) collective-permute-start(bf16[2,64,640]{2,1,0:T(8,128)(2,1)S(1)} %get-tuple-element.79), channel_id=1, source_target_pairs={{0,4},{1,5},{2,6},{3,7},{4,0},{5,1},{6,2},{7,3},{8,12},{9,13},{10,... | collective-permute-start | bytes 491528 | tf_op jit(solution)/shard_map/ppermute | solution.py:393
  125.1 13.5 %collective-permute-start.20 = (bf16[2,64,640]{2,1,0:T(8,128)(2,1)S(1)}, bf16[2,64,640]{2,1,0:T(8,128)(2,1)S(1)}, u32[]{:S(2)}, u32[]{:S(2)}) collective-permute-start(bf16[2,64,640]{2,1,0:T(8,128)(2,1)S(1)} %get-tuple-element.80), channel_id=1, source_target_pairs={{0,2},{1,3},{2,4},{3,5},{4,6},{5,7},{6,0},{7,1},{8,10},{9,11},{10,... | collective-permute-start | bytes 491528 | tf_op jit(solution)/shard_map/ppermute | solution.py:394
  125.8 12.8 %collective-permute-start.21 = (bf16[2,64,640]{2,1,0:T(8,128)(2,1)S(1)}, bf16[2,64,640]{2,1,0:T(8,128)(2,1)S(1)}, u32[]{:S(2)}, u32[]{:S(2)}) collective-permute-start(bf16[2,64,640]{2,1,0:T(8,128)(2,1)S(1)} %get-tuple-element.81), channel_id=1, source_target_pairs={{0,6},{1,7},{2,0},{3,1},{4,2},{5,3},{6,4},{7,5},{8,14},{9,15},{10,... | collective-permute-start | bytes 491528 | tf_op jit(solution)/shard_map/ppermute | solution.py:395
  129.2 3.6 %copy-start.11 = (bf16[128,4096]{1,0:T(8,128)(2,1)S(1)}, bf16[128,4096]{1,0:T(8,128)(2,1)}, u32[]{:S(2)}) copy-start(bf16[128,4096]{1,0:T(8,128)(2,1)} %fresh.1) | copy-start | bytes 3145732

commit v9 on v8

--- a/solution.py
+++ b/solution.py
@@ -235,37 +235,35 @@
     )[0]
 
 
-def pack_gradients(where, low, normed, d_values, d_low, mine, other):
+def pack_gradients(where, low, normed, d_values, d_low, core, ref):
     up_term = SCALE * t_dot(low, d_values)
-    chip, core = where[0] // 2, where[0] % 2
+    chip = where[0] // 2
     for ahead in range(4):
         target = lax.rem(chip + ahead, 4)
         pair = up_term[:, 0:128]
         for k in range(1, 4):
             pair = jnp.where(target == k, up_term[:, 128 * k : 128 * (k + 1)], pair)
-        pair = pair.astype(BF)
-        for ref, c in ((mine, core), (other, 1 - core)):
-            ref[ahead, :, :PART] = t_dot(d_low, normed[:, columns(2 * target + c)]).astype(BF)
-            ref[ahead, :, PART:] = pair
-
-
-PACKED = [shape((4, RANK, PACK), BF)] * 2
-
-
-def pack_kernel(where, low, normed, d_values, d_low, mine, other):
-    pack_gradients(
-        where, compact(low[...]), normed, d_values[...], compact(d_low[...]), mine, other
-    )
-
-
-def pack(where, low, normed, d_values, d_low):
-    return call(
-        pack_kernel, (where,), [low, normed, d_values, d_low], PACKED, 2 * ROWS * WIDTH * RANK
-    )
+        ref[ahead, :, :PART] = t_dot(d_low, normed[:, columns(2 * target + core)]).astype(BF)
+        ref[ahead, :, PART:] = pair.astype(BF)
+
+
+PACKED = [shape((4, RANK, PACK), BF)]
+
+
+def pack(where, low, normed, d_values, d_low, other):
+    def kernel(where, low, normed, d_values, d_low, ref):
+        core = 1 - where[0] % 2 if other else where[0] % 2
+        pack_gradients(
+            where, compact(low[...]), normed, d_values[...], compact(d_low[...]), core, ref
+        )
+
+    return call(
+        kernel, (where,), [low, normed, d_values, d_low], PACKED, ROWS * WIDTH * RANK
+    )[0]
 
 
 def second_kernel(ahead, where, relayed, out, target, low, normed, up, *refs):
-    blocks, (grad, d_values, d_low, mine, other) = refs[:8], refs[8:]
+    blocks, (grad, d_values, d_low, chosen_low, other) = refs[:8], refs[8:]
     last = where[9] == 1
     total = jnp.zeros((ROWS, VALUES), F32)
     for i in range(8):
@@ -280,8 +278,10 @@
     lowered = only(SCALE * dot_t(values, up[...]), ident).astype(BF)
     d_values[...] = values
     d_low[...] = lowered
+    chosen = only(low[...], ident)
+    chosen_low[...] = chosen
     pack_gradients(
-        where, compact(only(low[...], ident)), normed, values, compact(lowered), mine, other
+        where, compact(chosen), normed, values, compact(lowered), 1 - where[0] % 2, other
     )
 
 
@@ -290,7 +290,7 @@
         second_kernel,
         (ahead, where),
         [relayed, out, target, low, normed, up, *blocks],
-        [shape((ROWS, WIDTH), BF), *GRADS, *PACKED],
+        [shape((ROWS, WIDTH), BF), *GRADS, shape((ROWS, LOWS), BF), *PACKED],
         2 * ROWS * WIDTH * (VALUES + RANK),
     )
 
@@ -339,7 +339,7 @@
     )[0]
 
 
-def forward_kernel(wrapped, where, fresh, passed, gain, down, up, *refs):
+def forward_kernel(where, fresh, passed, gain, down, up, *refs):
     vals, outs, (out, rows, normed) = refs[:8], refs[8:16], refs[16:]
     first = where[8] == 1
     for top in range(0, ROWS, 32):
@@ -348,8 +348,7 @@
         whole = chosen.astype(F32)
         rows[part, :] = chosen
         normed[part, :] = (whole * factor_of(whole) * gain[...]).astype(BF)
-    came = passed[:, WIDTH : WIDTH + 1].astype(F32).astype(jnp.int32)
-    ident = jnp.where(first, wrapped[0], came)
+    ident = passed[:, WIDTH : WIDTH + 1].astype(F32).astype(jnp.int32)
     low = only(dot_t(normed[...], down[...]), ident).astype(BF)
     total = SCALE * dot(low, up[...])
     for i in range(8):
@@ -360,10 +359,10 @@
         out[:, span] = (rows[:, span].astype(F32) + dot(values, outs[i][...])).astype(BF)
 
 
-def forward(wrapped, where, fresh, passed, gain, down, up, vals, outs):
+def forward(where, fresh, passed, gain, down, up, vals, outs):
     return call(
         forward_kernel,
-        (wrapped, where),
+        (where,),
         [fresh, passed, gain, down, up, *vals, *outs],
         [shape((ROWS, WIDTH), BF)],
         4 * ROWS * WIDTH * VALUES,
@@ -379,15 +378,24 @@
     return call(pair_sum_kernel, (), [mine, other], [shape((4, RANK, PACK), BF)], 0)[0]
 
 
-def stack_kernel(first, mine, other, own, one, two, three):
+def stack_kernel(where, first, mine, other, own, one, two, three):
+    core = where[0] % 2
     for ahead, ref in enumerate((own, one, two, three)):
-        ref[0] = first[ahead]
-        ref[1] = (mine[ahead].astype(F32) + other[ahead].astype(F32)).astype(BF)
-
-
-def spread(first, mine, received):
-    block = shape((2, RANK, PACK), BF)
-    own, one, two, three = call(stack_kernel, (), [first, mine, received], [block] * 4, 0)
+        sums = (mine[ahead].astype(F32) + other[ahead].astype(F32)).astype(BF)
+        ref[:, :PART] = first[ahead, :, :PART]
+        ref[:, PART : 2 * PART] = sums[:, :PART]
+        ups = [
+            jnp.where(core == 0, pair[:, : RANK].astype(F32), pair[:, RANK:].astype(F32))
+            for pair in (first[ahead, :, PART:], sums[:, PART:])
+        ]
+        ref[:, 2 * PART :] = jnp.concatenate(ups, axis=1).astype(BF)
+
+
+def spread(where, first, mine, received):
+    block = shape((RANK, 2 * PART + 128), BF)
+    own, one, two, three = call(
+        stack_kernel, (where,), [first, mine, received], [block] * 4, 0
+    )
     return (
         own,
         lax.ppermute(two, "dp", chips(2)),
@@ -398,21 +406,17 @@
 
 def tables_kernel(ahead, back, where, relayed, *refs):
     terms, (down, up) = refs[:4], refs[4:]
-    core = where[0] % 2
     came = relayed[:RANK, :1].astype(F32).astype(jnp.int32)
     ident = jnp.where(where[9] == 1, ahead[0], came)
-    sums = []
-    for tick in range(2):
-        total = terms[0][tick].astype(F32)
-        for k in range(1, 4):
-            total += terms[k][tick].astype(F32)
-        sums.append(total)
+    total = terms[0][...].astype(F32)
+    for k in range(1, 4):
+        total += terms[k][...].astype(F32)
+    end = 2 * PART
     for label in range(ADAPTERS):
         one = jnp.where(back[0] == label, 1.0, 0.0)
         two = jnp.where(ident == label, 1.0, 0.0)
-        total = one * sums[0] + two * sums[1]
-        down[label] = total[:, :PART]
-        up[label] = jnp.where(core == 0, total[:, PART : PART + 64], total[:, PART + 64 :])
+        down[label] = one * total[:, :PART] + two * total[:, PART:end]
+        up[label] = one * total[:, end : end + RANK] + two * total[:, end + RANK :]
 
 
 def tables(ahead, back, where, relayed, terms):
@@ -460,7 +464,7 @@
     value_projection, output_matrix, norm_gain_frozen, adapter_down, adapter_up,
 ):
     count = lax.axis_size("section")
-    onward = [(i, i + 1) for i in range(count - 1)]
+    onward = [(i, (i + 1) % count) for i in range(count)]
     before = [(i, i - 1) for i in range(1, count)]
     position = lax.axis_index("section")
     where = jnp.stack(
@@ -494,7 +498,8 @@
     d_values, d_low, kept, inner, share_f = near_share(
         back, where, grad, normed_f, saved, factor_b, gain, down, up, outs, vals
     )
-    mine, other = pack(where, low_b, normed_b, d_values, d_low)
+    other = pack(where, low_b, normed_b, d_values, d_low, True)
+    mine = pack(where, low_b, normed_b, d_values, d_low, False)
     first_sums = pair_sum(mine, send(other, CORE))
     val_far, first_sums = lax.optimization_barrier((val_far, first_sums))
     vals += [val_far, send(val_far, CORE)]
@@ -506,19 +511,20 @@
     share_f, first_back = lax.optimization_barrier((share_f, first_back))
     first_out = output(ahead, where, share_f, normed_f, low_f, up, rows, outs, vals)
     passed = lax.ppermute(first_out, "section", onward)
-    first_out, sent, normed_n = lax.optimization_barrier((first_out, ahead, normed_n))
-    wrapped = lax.ppermute(sent, "section", [(count - 1, 0)])
+    first_out, normed_n = lax.optimization_barrier((first_out, normed_n))
     sums_n = project(where, normed_n, vals)
-    relayed, sums_n, wrapped = lax.optimization_barrier((relayed, sums_n, wrapped))
-
-    grad_n, d_values, d_low, mine, other = second_values(
+    relayed, sums_n = lax.optimization_barrier((relayed, sums_n))
+
+    grad_n, d_values, d_low, chosen_low, other = second_values(
         ahead, where, relayed, first_out, target, low_n, normed_n, up, outs
     )
-    terms = spread(first_sums, mine, send(other, CORE))
+    received = send(other, CORE)
+    mine = pack(where, chosen_low, normed_n, d_values, d_low, False)
+    terms = spread(where, first_sums, mine, received)
     bwd_out = second_input(
         where, sums_n, low_n, grad_n, rows, saved, factor_n, gain, down, d_values, d_low, vals
     )
-    fwd_out = forward(wrapped, where, fresh, passed, gain, down, up, vals, outs)
+    fwd_out = forward(where, fresh, passed, gain, down, up, vals, outs)
     down_table, up_table = tables(ahead, back, where, relayed, terms)
     return (
         fwd_out[None], bwd_out[None], jnp.swapaxes(down_table, 1, 2)[None], up_table[None]

time: 141 us -> 140 us (level)
  starting transfers between devices: 63 us -> 59.8 us
  Pallas kernels: 28.1 us -> 29.7 us
  waiting for transfers between devices: 41.6 us -> 43.1 us
    ppermute x1, waiting for transfers between devices: 17.7 us -> 20.9 us  [body(): relayed = lax.ppermute(first_back, 'section', before)]
    ppermute x1, starting transfers between devices: 7.41 us -> 5.58 us  [body(): passed = lax.ppermute(first_out, 'section', onward)]
    ppermute x16, waiting for transfers between devices: 23.9 us -> 22.2 us  [send(): return lax.ppermute(block, 'dp', pairs)]
    pallas_call x12 -> x14, Pallas kernels: 28.1 us -> 29.7 us  [call(): pl.pallas_call(kernel, out_shape=outs, grid_spec=pltpu.PrefetchScalarGrid...]
  transfers between devices with their start and end apart: 22 -> 21, of which waited for: 10 -> 10; matrix products, arithmetic and copies ran while one was open for 0% -> 0% of each run, Pallas kernels for 18% -> 19%
where the time goes in v9:
time: 140 us
  starting transfers between devices  59.8 us (43%)
  waiting for transfers between devices  43.1 us (31%)
  Pallas kernels  29.7 us (21%)
  local copies, waits for them, and re-layouts  5.25 us (4%)
  between operations  2.09 us (1%)
    ppermute x16, starting transfers between devices, send(): return lax.ppermute(block, 'dp', pairs)  43.8 us
    pallas_call x14, Pallas kernels, call(): pl.pallas_call(kernel, out_shape=outs, grid_spec=pltpu.PrefetchScalarGrid...  29.7 us
    ppermute x16, waiting for transfers between devices, send(): return lax.ppermute(block, 'dp', pairs)  22.2 us
    ppermute x1, waiting for transfers between devices, body(): relayed = lax.ppermute(first_back, 'section', before)  20.9 us
    ppermute x1, starting transfers between devices, body(): passed = lax.ppermute(first_out, 'section', onward)  5.58 us
    unnamed x26, local copies, waits for them, and re-layouts  5.16 us
    ppermute x1, starting transfers between devices, spread(): lax.ppermute(two, 'dp', chips(2))  3.61 us
    ppermute x1, starting transfers between devices, spread(): lax.ppermute(three, 'dp', chips(3))  3.43 us
  transfers between devices with their start and end apart: 21, of which 10 were waited for; matrix products, arithmetic and copies ran while one was open for 0% of the time, Pallas kernels for 19%

profile of v9, /device:TPU:30, one launch (start us, length us, event | category | flops | bytes accessed | tf_op | source)
XLA Modules:
  0.0 139.9 jit_solution(1819557343226555897)
XLA Ops:
  0.6 3.3 %collective-permute-start = (bf16[512,512]{1,0:T(8,128)(2,1)}, bf16[512,512]{1,0:T(8,128)(2,1)S(1)}, u32[]{:S(2)}, u32[]{:S(2)}) collective-permute-start(bf16[512,512]{1,0:T(8,128)(2,1)} %bitcast.34), channel_id=1, source_target_pairs={{0,2},{1,7},{2,4},{3,1},{4,6},{5,3},{6,0},{7,5},{8,10},{9,15},{10,... | collective-permute-start | bytes 1572872 | tf_op jit(solution)/shard_map/ppermute | solution.py:445
  4.0 3.1 %collective-permute-start.1 = (bf16[512,512]{1,0:T(8,128)(2,1)}, bf16[512,512]{1,0:T(8,128)(2,1)S(1)}, u32[]{:S(2)}, u32[]{:S(2)}) collective-permute-start(bf16[512,512]{1,0:T(8,128)(2,1)} %bitcast.35), channel_id=1, source_target_pairs={{0,6},{1,3},{2,0},{3,5},{4,2},{5,7},{6,4},{7,1},{8,14},{9,11},{10,... | collective-permute-start | bytes 1572872 | tf_op jit(solution)/shard_map/ppermute | solution.py:445
  7.1 0.5 collective-permute-start.3
  7.6 1.4 collective-permute-start.8
  10.3 0.1 stack.51.where
  10.4 1.6 %copy-done = bf16[1,2,128,4096]{3,2,1,0:T(8,128)(2,1)S(1)} copy-done((bf16[1,2,128,4096]{3,2,1,0:T(8,128)(2,1)S(1)}, bf16[1,2,128,4096]{3,2,1,0:T(8,128)(2,1)}, u32[]{:S(2)}) %copy-start) | copy-done | bytes 2097176
  12.0 1.6 %copy-done.2 = bf16[1,4,4096,64]{2,3,1,0:T(8,128)(2,1)S(1)} copy-done((bf16[1,4,4096,64]{2,3,1,0:T(8,128)(2,1)S(1)}, bf16[1,4,4096,64]{2,3,1,0:T(8,128)(2,1)}, u32[]{:S(2)}) %copy-start.2) | copy-done | bytes 2097176
  13.5 1.2 copy-done.4
  14.8 0.7 copy-done.12
  15.5 0.0 copy-start.8
  15.5 0.0 copy-start.9
  15.5 4.1 %shard_map.147 = (bf16[128,4096]{1,0:T(8,128)(2,1)S(1)}, f32[128,128]{1,0:T(8,128)}, bf16[128,256]{1,0:T(8,128)(2,1)S(1)}, bf16[128,4096]{1,0:T(8,128)(2,1)S(1)}...) custom-call(s32[1]{0:T(128)S(6)} %copy.16.ahead, ...), custom_call_target="tpu_custom_call" | custom-call | flops 805306 | bytes 7356 | tf_op jit(solution)/shard_map/pallas_call | solution.py:52
  19.7 0.9 collective-permute-done.refs_2_.refs_10_
  20.5 6.2 %collective-permute-start.10 = (bf16[512,512]{1,0:T(8,128)(2,1)S(1)}, bf16[512,512]{1,0:T(8,128)(2,1)S(1)}, u32[]{:S(2)}, u32[]{:S(2)}) collective-permute-start(bf16[512,512]{1,0:T(8,128)(2,1)S(1)} %bitcast.43), channel_id=1, source_target_pairs={{0,6},{1,3},{2,0},{3,5},{4,2},{5,7},{6,4},{7,1},{8,14},{9,11},{10,... | collective-permute-start | bytes 1572872 | tf_op jit(solution)/shard_map/ppermute | solution.py:445
  26.8 8.6 %collective-permute-done.1.refs_4_.refs_12_ = bf16[512,512]{1,0:T(8,128)(2,1)S(1)} collective-permute-done((bf16[512,512]{1,0:T(8,128)(2,1)}, bf16[512,512]{1,0:T(8,128)(2,1)S(1)}, u32[]{:S(2)}, u32[]{:S(2)}) %collective-permute-start.1) | collective-permute-done | bytes 524320 | tf_op jit(solution)/shard_map/ppermute | solution.py:445
  35.4 4.0 %collective-permute-start.6 = (bf16[512,512]{1,0:T(8,128)(2,1)S(1)}, bf16[512,512]{1,0:T(8,128)(2,1)S(1)}, u32[]{:S(2)}, u32[]{:S(2)}) collective-permute-start(bf16[512,512]{1,0:T(8,128)(2,1)S(1)} %collective-permute-done.refs_2_.refs_10_), channel_id=1, source_target_pairs={{0,2},{1,7},{2,4},{3,1},{4,6},{5,3},{6,0},{7,5},{8,10},{9,15},{10,... | collective-permute-start | bytes 1572872 | tf_op jit(solution)/shard_map/ppermute | solution.py:445
  39.4 0.5 collective-permute-start.5
  39.9 3.8 %collective-permute-start.9 = (bf16[512,512]{1,0:T(8,128)(2,1)S(1)}, bf16[512,512]{1,0:T(8,128)(2,1)S(1)}, u32[]{:S(2)}, u32[]{:S(2)}) collective-permute-start(bf16[512,512]{1,0:T(8,128)(2,1)S(1)} %collective-permute-done.8.refs_10_.refs_2_), channel_id=1, source_target_pairs={{0,1},{1,0},{2,3},{3,2},{4,5},{5,4},{6,7},{7,6},{8,9},{9,8},{10,11... | collective-permute-start | bytes 1572872 | tf_op jit(solution)/shard_map/ppermute | solution.py:445
  43.7 3.0 %collective-permute-done.10.refs_12_.refs_4_ = bf16[512,512]{1,0:T(8,128)(2,1)S(1)} collective-permute-done((bf16[512,512]{1,0:T(8,128)(2,1)S(1)}, bf16[512,512]{1,0:T(8,128)(2,1)S(1)}, u32[]{:S(2)}, u32[]{:S(2)}) %collective-permute-start.10) | collective-permute-done | bytes 524320 | tf_op jit(solution)/shard_map/ppermute | solution.py:445
  46.7 19.9 %collective-permute-start.11 = (bf16[512,512]{1,0:T(8,128)(2,1)S(1)}, bf16[512,512]{1,0:T(8,128)(2,1)S(1)}, u32[]{:S(2)}, u32[]{:S(2)}) collective-permute-start(bf16[512,512]{1,0:T(8,128)(2,1)S(1)} %collective-permute-done.10.refs_12_.refs_4_), channel_id=1, source_target_pairs={{0,1},{1,0},{2,3},{3,2},{4,5},{5,4},{6,7},{7,6},{8,9},{9,8},{10,11... | collective-permute-start | bytes 1572872 | tf_op jit(solution)/shard_map/ppermute | solution.py:445
  66.6 0.5 collective-permute-start.12
  67.1 1.0 collective-permute-done.11.refs_13_.refs_5_
  68.1 0.7 collective-permute-done.7.refs_7_.refs_15_
  68.9 4.7 %shard_map.148 = (bf16[128,512]{1,0:T(8,128)(2,1)S(1)}, bf16[128,256]{1,0:T(8,128)(2,1)S(1)}, f32[6,128,512]{2,1,0:T(8,128)S(1)}, f32[128,128]{1,0:T(8,128)S(1)}, f32[128,512]{1,0:T(8,128)S(1)}) custom-call(s32[1]{0:T(128)S(6)} %copy.17.back, s32[10]{0:T(128)S(1)} %stack.51.where, bf16[128,4096]{1,0:T(8,128)(2,1)S(1)} %bitcast.52, ...), custom_call_target="tpu_custom_call" | custom-call | flops 1610612 | bytes 13975 | tf_op jit(solution)/shard_map/pallas_call | solution.py:52
  73.6 0.9 shard_map.150
  74.5 0.5 collective-permute-start.13
  75.0 0.9 shard_map.149.mine
  75.9 0.4 collective-permute-done.13.other
  76.2 0.1 shard_map.151.first
  76.3 5.0 %collective-permute-done.12.far.refs_6_ = bf16[512,512]{1,0:T(8,128)(2,1)S(1)} collective-permute-done((bf16[512,512]{1,0:T(8,128)(2,1)S(1)}, bf16[512,512]{1,0:T(8,128)(2,1)S(1)}, u32[]{:S(2)}, u32[]{:S(2)}) %collective-permute-start.12) | collective-permute-done | bytes 524320 | tf_op jit(solution)/shard_map/ppermute | solution.py:445
  81.3 1.9 %collective-permute-done.14.far_other.refs_7_ = bf16[512,512]{1,0:T(8,128)(2,1)S(1)} collective-permute-done((bf16[512,512]{1,0:T(8,128)(2,1)S(1)}, bf16[512,512]{1,0:T(8,128)(2,1)S(1)}, u32[]{:S(2)}, u32[]{:S(2)}) %collective-permute-start.14) | collective-permute-done | bytes 524320 | tf_op jit(solution)/shard_map/ppermute | solution.py:445
  83.2 1.8 %shard_map.152 = bf16[128,4224]{1,0:T(8,128)(2,1)S(1)} custom-call(s32[1]{0:T(128)S(6)} %copy.17.back, s32[10]{0:T(128)S(1)} %stack.51.where, f32[6,128,512]{2,1,0:T(8,128)S(1)} %get-tuple-element.48.kept, f32[128,128]{1,0:T(8,128)S(1)} %get-tuple-element.49.inner, bf16[128,512]{1,0:T(8,128)(2,1)S(1)} %get-tuple-element.50.d_values.values, ...), custom_call_target="tpu_custom_call" | custom-call | flops 268435 | bytes 8208 | tf_op jit(solution)/shard_map/pallas_call | solution.py:52
  85.0 2.7 %collective-permute-start.16 = (bf16[128,4224]{1,0:T(8,128)(2,1)S(1)}, bf16[128,4224]{1,0:T(8,128)(2,1)S(1)}, u32[]{:S(2)}, u32[]{:S(2)}) collective-permute-start(bf16[128,4224]{1,0:T(8,128)(2,1)S(1)} %shard_map.152), channel_id=1, source_target_pairs={{8,0},{16,8},{24,16},{32,24},{40,32},{48,40},{56,48},{64,56},{72,6... | collective-permute-start | bytes 3244040 | tf_op jit(solution)/shard_map/ppermute | solution.py:510
  87.6 1.6 %shard_map.153.out = bf16[128,4224]{1,0:T(8,128)(2,1)S(1)} custom-call(s32[1]{0:T(128)S(6)} %copy.16.ahead, s32[10]{0:T(128)S(1)} %stack.51.where, f32[128,512]{1,0:T(8,128)S(1)} %get-tuple-element.55.share, bf16[128,4096]{1,0:T(8,128)(2,1)S(1)} %get-tuple-element.41.normed, bf16[128,256]{1,0:T(8,128)(2,1)S(1)} %get-tuple-element.56.low, ...), custom_call_target="tpu_custom_call" | custom-call | flops 536870 | bytes 7929 | tf_op jit(solution)/shard_map/pallas_call | solution.py:52
  89.2 5.6 %collective-permute-start.15 = (bf16[128,4224]{1,0:T(8,128)(2,1)S(1)}, bf16[128,4224]{1,0:T(8,128)(2,1)S(1)}, u32[]{:S(2)}, u32[]{:S(2)}) collective-permute-start(bf16[128,4224]{1,0:T(8,128)(2,1)S(1)} %shard_map.153.out), channel_id=1, source_target_pairs={{0,8},{8,16},{16,24},{24,32},{32,40},{40,48},{48,56},{56,64},{64,7... | collective-permute-start | bytes 3244040 | tf_op jit(solution)/shard_map/ppermute | solution.py:513
  94.8 1.3 shard_map.155.sums
  96.1 20.9 %collective-permute-done.16.relayed = bf16[128,4224]{1,0:T(8,128)(2,1)S(1)} collective-permute-done((bf16[128,4224]{1,0:T(8,128)(2,1)S(1)}, bf16[128,4224]{1,0:T(8,128)(2,1)S(1)}, u32[]{:S(2)}, u32[]{:S(2)}) %collective-permute-start.16) | collective-permute-done | bytes 1081376 | tf_op jit(solution)/shard_map/ppermute | solution.py:510
  117.0 2.6 %shard_map.156 = (bf16[128,4096]{1,0:T(8,128)(2,1)S(1)}, bf16[128,512]{1,0:T(8,128)(2,1)S(1)}, bf16[128,256]{1,0:T(8,128)(2,1)S(1)}, bf16[128,256]{1,0:T(8,128)(2,1)S(1)}, bf16[4,64,640]{2,1,0:T(8,128)(2,1)S(1)}) custom-call(s32[1]{0:T(128)S(6)} %copy.16.ahead, s32[10]{0:T(128)S(1)} %stack.51.where, bf16[128,4224]{1,0:T(8,128)(2,1)S(1)} %collective-permute-done.16.relayed, ...), custom_call_target="tpu_custom_call" | custom-call | flops 603979 | bytes 8781 | tf_op jit(solution)/shard_map/pallas_call | solution.py:52
  119.6 0.1 collective-permute-start.17
  119.7 0.9 shard_map.158.mine
  120.6 0.7 collective-permute-done.17.other
  121.3 0.7 shard_map.159
  122.0 3.6 %collective-permute-start.18 = (bf16[64,1152]{1,0:T(8,128)(2,1)S(1)}, bf16[64,1152]{1,0:T(8,128)(2,1)S(1)}, u32[]{:S(2)}, u32[]{:S(2)}) collective-permute-start(bf16[64,1152]{1,0:T(8,128)(2,1)S(1)} %get-tuple-element.71), channel_id=1, source_target_pairs={{0,4},{1,5},{2,6},{3,7},{4,0},{5,1},{6,2},{7,3},{8,12},{9,13},{10,... | collective-permute-start | bytes 442376 | tf_op jit(solution)/shard_map/ppermute | solution.py:401
  125.6 0.7 collective-permute-start.19
  126.3 3.4 %collective-permute-start.20 = (bf16[64,1152]{1,0:T(8,128)(2,1)S(1)}, bf16[64,1152]{1,0:T(8,128)(2,1)S(1)}, u32[]{:S(2)}, u32[]{:S(2)}) collective-permute-start(bf16[64,1152]{1,0:T(8,128)(2,1)S(1)} %get-tuple-element.73), channel_id=1, source_target_pairs={{0,6},{1,7},{2,0},{3,1},{4,2},{5,3},{6,4},{7,5},{8,14},{9,15},{10,... | collective-permute-start | bytes 442376 | tf_op jit(solution)/shard_map/ppermute | solution.py:403
  129.8 3.5 %shard_map.157 = bf16[128,4096]{1,0:T(8,128)(2,1)} custom-call(s32[10]{0:T(128)S(1)} %stack.51.where, f32[128,512]{1,0:T(8,128)S(1)} %shard_map.155.sums, bf16[128,256]{1,0:T(8,128)(2,1)S(1)} %get-tuple-element.60.low, bf16[128,4096]{1,0:T(8,128)(2,1)S(1)} %get-tuple-element.63.grad, bf16[128,4096]{1,0:T(8,128)(2,1)S(1)} %bitcast.33, ...), custom_call_target="tpu_custom_call" | custom-call | flops 603979 | bytes 11091 | tf_op jit(solution)/shard_map/pallas_call | solution.py:52
  133.3 5.1 %shard_map.154 = bf16[128,4096]{1,0:T(8,128)(2,1)} custom-call(s32[10]{0:T(128)S(1)} %stack.51.where, bf16[128,4096]{1,0:T(8,128)(2,1)S(1)} %copy-done.11, bf16[128,4224]{1,0:T(8,128)(2,1)S(1)} %collective-permute-done.15.passed, f32[1,4096]{1,0:T(1,128)S(1)} %copy-done.12, bf16[256,4096]{1,0:T(8,128)(2,1)S(1)} %bitcast.30, bf16[256,512]{1,0:T(8,128)(2,1)S(1)} %bitcast.51, ...), custom_call_target="tpu_custom_call" | custom-call | flops 1073741 | bytes 12894 | tf_op jit(solution)/shard_map/pallas_call | solution.py:52
  138.4 1.5 %shard_map.160 = (f32[4,64,512]{2,1,0:T(8,128)}, f32[4,64,64]{2,1,0:T(8,128)}) custom-call(s32[1]{0:T(128)S(6)} %copy.16.ahead, s32[1]{0:T(128)S(6)} %copy.17.back, s32[10]{0:T(128)S(1)} %stack.51.where, bf16[128,4224]{1,0:T(8,128)(2,1)S(1)} %collective-permute-done.16.relayed, bf16[64,1152]{1,0:T(8,128)(2,1)S(1)} %get-tuple-element.70.refs_0_, ...), custom_call_target="tpu_custom_call" | custom-call | bytes 1671 | tf_op jit(solution)/shard_map/pallas_call | solution.py:52
  (35 shorter events, 0.1 us)
Async XLA Ops:
  0.6 19.9 %collective-permute-start = (bf16[512,512]{1,0:T(8,128)(2,1)}, bf16[512,512]{1,0:T(8,128)(2,1)S(1)}, u32[]{:S(2)}, u32[]{:S(2)}) collective-permute-start(bf16[512,512]{1,0:T(8,128)(2,1)} %bitcast.34), channel_id=1, source_target_pairs={{0,2},{1,7},{2,4},{3,1},{4,6},{5,3},{6,0},{7,5},{8,10},{9,15},{10,... | collective-permute-start | bytes 1572872 | tf_op jit(solution)/shard_map/ppermute | solution.py:445
  4.0 31.4 %collective-permute-start.1 = (bf16[512,512]{1,0:T(8,128)(2,1)}, bf16[512,512]{1,0:T(8,128)(2,1)S(1)}, u32[]{:S(2)}, u32[]{:S(2)}) collective-permute-start(bf16[512,512]{1,0:T(8,128)(2,1)} %bitcast.35), channel_id=1, source_target_pairs={{0,6},{1,3},{2,0},{3,5},{4,2},{5,7},{6,4},{7,1},{8,14},{9,11},{10,... | collective-permute-start | bytes 1572872 | tf_op jit(solution)/shard_map/ppermute | solution.py:445
  7.1 28.2 %collective-permute-start.2 = (bf16[512,512]{1,0:T(8,128)(2,1)}, bf16[512,512]{1,0:T(8,128)(2,1)S(1)}, u32[]{:S(2)}, u32[]{:S(2)}) collective-permute-start(bf16[512,512]{1,0:T(8,128)(2,1)} %bitcast.36), channel_id=1, source_target_pairs={{0,1},{1,0},{2,3},{3,2},{4,5},{5,4},{6,7},{7,6},{8,9},{9,8},{10,11... | collective-permute-start | bytes 1572872 | tf_op jit(solution)/shard_map/ppermute | solution.py:445
  7.1 28.2 %collective-permute-start.3 = (bf16[512,512]{1,0:T(8,128)(2,1)}, bf16[512,512]{1,0:T(8,128)(2,1)S(1)}, u32[]{:S(2)}, u32[]{:S(2)}) collective-permute-start(bf16[512,512]{1,0:T(8,128)(2,1)} %bitcast.41), channel_id=1, source_target_pairs={{0,1},{1,0},{2,3},{3,2},{4,5},{5,4},{6,7},{7,6},{8,9},{9,8},{10,11... | collective-permute-start | bytes 1572872 | tf_op jit(solution)/shard_map/ppermute | solution.py:445
  7.6 32.3 %collective-permute-start.8 = (bf16[512,512]{1,0:T(8,128)(2,1)}, bf16[512,512]{1,0:T(8,128)(2,1)S(1)}, u32[]{:S(2)}, u32[]{:S(2)}) collective-permute-start(bf16[512,512]{1,0:T(8,128)(2,1)} %bitcast.42), channel_id=1, source_target_pairs={{0,2},{1,7},{2,4},{3,1},{4,6},{5,3},{6,0},{7,5},{8,10},{9,15},{10,... | collective-permute-start | bytes 1572872 | tf_op jit(solution)/shard_map/ppermute | solution.py:445
  10.4 1.6 %copy-start = (bf16[1,2,128,4096]{3,2,1,0:T(8,128)(2,1)S(1)}, bf16[1,2,128,4096]{3,2,1,0:T(8,128)(2,1)}, u32[]{:S(2)}) copy-start(bf16[1,2,128,4096]{3,2,1,0:T(8,128)(2,1)} %rows_s.3) | copy-start | bytes 6291460
  12.0 1.6 %copy-start.2 = (bf16[1,4,4096,64]{2,3,1,0:T(8,128)(2,1)S(1)}, bf16[1,4,4096,64]{2,3,1,0:T(8,128)(2,1)}, u32[]{:S(2)}) copy-start(bf16[1,4,4096,64]{2,3,1,0:T(8,128)(2,1)} %param.22) | copy-start | bytes 6291460
  13.5 1.2 copy-start.4
  14.8 0.7 copy-start.12
  15.5 5.1 %copy-start.7 = (bf16[1,512,512]{2,1,0:T(8,128)(2,1)S(1)}, bf16[1,512,512]{2,1,0:T(8,128)(2,1)}, u32[]{:S(2)}) copy-start(bf16[1,512,512]{2,1,0:T(8,128)(2,1)} %param.19) | copy-start | bytes 1572868
  15.5 53.4 %copy-start.1 = (bf16[1,2,128,4096]{3,2,1,0:T(8,128)(2,1)S(1)}, bf16[1,2,128,4096]{3,2,1,0:T(8,128)(2,1)}, u32[]{:S(2)}) copy-start(bf16[1,2,128,4096]{3,2,1,0:T(8,128)(2,1)} %rows_s.3) | copy-start | bytes 6291460
  15.5 53.4 %copy-start.3 = (bf16[1,4,4096,64]{2,3,1,0:T(8,128)(2,1)S(1)}, bf16[1,4,4096,64]{2,3,1,0:T(8,128)(2,1)}, u32[]{:S(2)}) copy-start(bf16[1,4,4096,64]{2,3,1,0:T(8,128)(2,1)} %param.22) | copy-start | bytes 6291460
  15.5 53.4 %copy-start.6 = (bf16[1,512,512]{2,1,0:T(8,128)(2,1)S(1)}, bf16[1,512,512]{2,1,0:T(8,128)(2,1)}, u32[]{:S(2)}) copy-start(bf16[1,512,512]{2,1,0:T(8,128)(2,1)} %param.20) | copy-start | bytes 1572868
  15.5 53.4 %copy-start.8 = (bf16[1,4,64,512]{3,2,1,0:T(8,128)(2,1)S(1)}, bf16[1,4,64,512]{3,2,1,0:T(8,128)(2,1)}, u32[]{:S(2)}) copy-start(bf16[1,4,64,512]{3,2,1,0:T(8,128)(2,1)} %param.23) | copy-start | bytes 786436
  15.5 53.4 %copy-start.9 = (bf16[1,128,4096]{2,1,0:T(8,128)(2,1)S(1)}, bf16[1,128,4096]{2,1,0:T(8,128)(2,1)}, u32[]{:S(2)}) copy-start(bf16[1,128,4096]{2,1,0:T(8,128)(2,1)} %param.13) | copy-start | bytes 3145732
  20.5 26.2 %collective-permute-start.10 = (bf16[512,512]{1,0:T(8,128)(2,1)S(1)}, bf16[512,512]{1,0:T(8,128)(2,1)S(1)}, u32[]{:S(2)}, u32[]{:S(2)}) collective-permute-start(bf16[512,512]{1,0:T(8,128)(2,1)S(1)} %bitcast.43), channel_id=1, source_target_pairs={{0,6},{1,3},{2,0},{3,5},{4,2},{5,7},{6,4},{7,1},{8,14},{9,11},{10,... | collective-permute-start | bytes 1572872 | tf_op jit(solution)/shard_map/ppermute | solution.py:445
  35.4 31.2 %collective-permute-start.6 = (bf16[512,512]{1,0:T(8,128)(2,1)S(1)}, bf16[512,512]{1,0:T(8,128)(2,1)S(1)}, u32[]{:S(2)}, u32[]{:S(2)}) collective-permute-start(bf16[512,512]{1,0:T(8,128)(2,1)S(1)} %collective-permute-done.refs_2_.refs_10_), channel_id=1, source_target_pairs={{0,2},{1,7},{2,4},{3,1},{4,6},{5,3},{6,0},{7,5},{8,10},{9,15},{10,... | collective-permute-start | bytes 1572872 | tf_op jit(solution)/shard_map/ppermute | solution.py:445
  39.4 27.2 %collective-permute-start.4 = (bf16[512,512]{1,0:T(8,128)(2,1)S(1)}, bf16[512,512]{1,0:T(8,128)(2,1)S(1)}, u32[]{:S(2)}, u32[]{:S(2)}) collective-permute-start(bf16[512,512]{1,0:T(8,128)(2,1)S(1)} %collective-permute-done.refs_2_.refs_10_), channel_id=1, source_target_pairs={{0,1},{1,0},{2,3},{3,2},{4,5},{5,4},{6,7},{7,6},{8,9},{9,8},{10,11... | collective-permute-start | bytes 1572872 | tf_op jit(solution)/shard_map/ppermute | solution.py:445
  39.4 27.7 %collective-permute-start.5 = (bf16[512,512]{1,0:T(8,128)(2,1)S(1)}, bf16[512,512]{1,0:T(8,128)(2,1)S(1)}, u32[]{:S(2)}, u32[]{:S(2)}) collective-permute-start(bf16[512,512]{1,0:T(8,128)(2,1)S(1)} %collective-permute-done.1.refs_4_.refs_12_), channel_id=1, source_target_pairs={{0,1},{1,0},{2,3},{3,2},{4,5},{5,4},{6,7},{7,6},{8,9},{9,8},{10,11... | collective-permute-start | bytes 1572872 | tf_op jit(solution)/shard_map/ppermute | solution.py:445
  39.9 27.2 %collective-permute-start.9 = (bf16[512,512]{1,0:T(8,128)(2,1)S(1)}, bf16[512,512]{1,0:T(8,128)(2,1)S(1)}, u32[]{:S(2)}, u32[]{:S(2)}) collective-permute-start(bf16[512,512]{1,0:T(8,128)(2,1)S(1)} %collective-permute-done.8.refs_10_.refs_2_), channel_id=1, source_target_pairs={{0,1},{1,0},{2,3},{3,2},{4,5},{5,4},{6,7},{7,6},{8,9},{9,8},{10,11... | collective-permute-start | bytes 1572872 | tf_op jit(solution)/shard_map/ppermute | solution.py:445
  46.7 21.4 %collective-permute-start.11 = (bf16[512,512]{1,0:T(8,128)(2,1)S(1)}, bf16[512,512]{1,0:T(8,128)(2,1)S(1)}, u32[]{:S(2)}, u32[]{:S(2)}) collective-permute-start(bf16[512,512]{1,0:T(8,128)(2,1)S(1)} %collective-permute-done.10.refs_12_.refs_4_), channel_id=1, source_target_pairs={{0,1},{1,0},{2,3},{3,2},{4,5},{5,4},{6,7},{7,6},{8,9},{9,8},{10,11... | collective-permute-start | bytes 1572872 | tf_op jit(solution)/shard_map/ppermute | solution.py:445
  66.6 2.3 %collective-permute-start.7 = (bf16[512,512]{1,0:T(8,128)(2,1)S(1)}, bf16[512,512]{1,0:T(8,128)(2,1)S(1)}, u32[]{:S(2)}, u32[]{:S(2)}) collective-permute-start(bf16[512,512]{1,0:T(8,128)(2,1)S(1)} %collective-permute-done.6.refs_6_.refs_14_), channel_id=1, source_target_pairs={{0,1},{1,0},{2,3},{3,2},{4,5},{5,4},{6,7},{7,6},{8,9},{9,8},{10,11... | collective-permute-start | bytes 1572872 | tf_op jit(solution)/shard_map/ppermute | solution.py:445
  66.6 14.7 %collective-permute-start.12 = (bf16[512,512]{1,0:T(8,128)(2,1)S(1)}, bf16[512,512]{1,0:T(8,128)(2,1)S(1)}, u32[]{:S(2)}, u32[]{:S(2)}) collective-permute-start(bf16[512,512]{1,0:T(8,128)(2,1)S(1)} %collective-permute-done.8.refs_10_.refs_2_), channel_id=1, source_target_pairs={{0,2},{1,7},{2,4},{3,1},{4,6},{5,3},{6,0},{7,5},{8,10},{9,15},{10,... | collective-permute-start | bytes 1572872 | tf_op jit(solution)/shard_map/ppermute | solution.py:445
  74.5 1.7 %collective-permute-start.13 = (bf16[4,64,640]{2,1,0:T(8,128)(2,1)S(1)}, bf16[4,64,640]{2,1,0:T(8,128)(2,1)S(1)}, u32[]{:S(2)}, u32[]{:S(2)}) collective-permute-start(bf16[4,64,640]{2,1,0:T(8,128)(2,1)S(1)} %shard_map.150), channel_id=1, source_target_pairs={{0,1},{1,0},{2,3},{3,2},{4,5},{5,4},{6,7},{7,6},{8,9},{9,8},{10,11... | collective-permute-start | bytes 983048 | tf_op jit(solution)/shard_map/ppermute | solution.py:445
  81.3 1.9 %collective-permute-start.14 = (bf16[512,512]{1,0:T(8,128)(2,1)S(1)}, bf16[512,512]{1,0:T(8,128)(2,1)S(1)}, u32[]{:S(2)}, u32[]{:S(2)}) collective-permute-start(bf16[512,512]{1,0:T(8,128)(2,1)S(1)} %collective-permute-done.12.far.refs_6_), channel_id=1, source_target_pairs={{0,1},{1,0},{2,3},{3,2},{4,5},{5,4},{6,7},{7,6},{8,9},{9,8},{10,11... | collective-permute-start | bytes 1572872 | tf_op jit(solution)/shard_map/ppermute | solution.py:445
  83.2 4.4 %copy-start.5 = (bf16[1,128,4096]{2,1,0:T(8,128)(2,1)S(1)}, bf16[1,128,4096]{2,1,0:T(8,128)(2,1)}, u32[]{:S(2)}) copy-start(bf16[1,128,4096]{2,1,0:T(8,128)(2,1)} %param.12) | copy-start | bytes 3145732
  85.0 32.0 %collective-permute-start.16 = (bf16[128,4224]{1,0:T(8,128)(2,1)S(1)}, bf16[128,4224]{1,0:T(8,128)(2,1)S(1)}, u32[]{:S(2)}, u32[]{:S(2)}) collective-permute-start(bf16[128,4224]{1,0:T(8,128)(2,1)S(1)} %shard_map.152), channel_id=1, source_target_pairs={{8,0},{16,8},{24,16},{32,24},{40,32},{48,40},{56,48},{64,56},{72,6... | collective-permute-start | bytes 3244040 | tf_op jit(solution)/shard_map/ppermute | solution.py:510
  89.2 44.1 %collective-permute-start.15 = (bf16[128,4224]{1,0:T(8,128)(2,1)S(1)}, bf16[128,4224]{1,0:T(8,128)(2,1)S(1)}, u32[]{:S(2)}, u32[]{:S(2)}) collective-permute-start(bf16[128,4224]{1,0:T(8,128)(2,1)S(1)} %shard_map.153.out), channel_id=1, source_target_pairs={{0,8},{8,16},{16,24},{24,32},{32,40},{40,48},{48,56},{56,64},{64,7... | collective-permute-start | bytes 3244040 | tf_op jit(solution)/shard_map/ppermute | solution.py:513
  94.8 22.2 %copy-start.10 = (bf16[128,4096]{1,0:T(8,128)(2,1)S(1)}, bf16[128,4096]{1,0:T(8,128)(2,1)}, u32[]{:S(2)}) copy-start(bf16[128,4096]{1,0:T(8,128)(2,1)} %target.1) | copy-start | bytes 3145732
  119.6 1.7 %collective-permute-start.17 = (bf16[4,64,640]{2,1,0:T(8,128)(2,1)S(1)}, bf16[4,64,640]{2,1,0:T(8,128)(2,1)S(1)}, u32[]{:S(2)}, u32[]{:S(2)}) collective-permute-start(bf16[4,64,640]{2,1,0:T(8,128)(2,1)S(1)} %get-tuple-element.69), channel_id=1, source_target_pairs={{0,1},{1,0},{2,3},{3,2},{4,5},{5,4},{6,7},{7,6},{8,9},{9,8},{10,11... | collective-permute-start | bytes 983048 | tf_op jit(solution)/shard_map/ppermute | solution.py:445
  122.0 16.4 %collective-permute-start.18 = (bf16[64,1152]{1,0:T(8,128)(2,1)S(1)}, bf16[64,1152]{1,0:T(8,128)(2,1)S(1)}, u32[]{:S(2)}, u32[]{:S(2)}) collective-permute-start(bf16[64,1152]{1,0:T(8,128)(2,1)S(1)} %get-tuple-element.71), channel_id=1, source_target_pairs={{0,4},{1,5},{2,6},{3,7},{4,0},{5,1},{6,2},{7,3},{8,12},{9,13},{10,... | collective-permute-start | bytes 442376 | tf_op jit(solution)/shard_map/ppermute | solution.py:401
  125.6 12.8 %collective-permute-start.19 = (bf16[64,1152]{1,0:T(8,128)(2,1)S(1)}, bf16[64,1152]{1,0:T(8,128)(2,1)S(1)}, u32[]{:S(2)}, u32[]{:S(2)}) collective-permute-start(bf16[64,1152]{1,0:T(8,128)(2,1)S(1)} %get-tuple-element.72), channel_id=1, source_target_pairs={{0,2},{1,3},{2,4},{3,5},{4,6},{5,7},{6,0},{7,1},{8,10},{9,11},{10,... | collective-permute-start | bytes 442376 | tf_op jit(solution)/shard_map/ppermute | solution.py:402
  126.3 12.1 %collective-permute-start.20 = (bf16[64,1152]{1,0:T(8,128)(2,1)S(1)}, bf16[64,1152]{1,0:T(8,128)(2,1)S(1)}, u32[]{:S(2)}, u32[]{:S(2)}) collective-permute-start(bf16[64,1152]{1,0:T(8,128)(2,1)S(1)} %get-tuple-element.73), channel_id=1, source_target_pairs={{0,6},{1,7},{2,0},{3,1},{4,2},{5,3},{6,4},{7,5},{8,14},{9,15},{10,... | collective-permute-start | bytes 442376 | tf_op jit(solution)/shard_map/ppermute | solution.py:403
  129.8 3.6 %copy-start.11 = (bf16[128,4096]{1,0:T(8,128)(2,1)S(1)}, bf16[128,4096]{1,0:T(8,128)(2,1)}, u32[]{:S(2)}) copy-start(bf16[128,4096]{1,0:T(8,128)(2,1)} %fresh.1) | copy-start | bytes 3145732

commit v10 on v9

--- a/solution.py
+++ b/solution.py
@@ -106,6 +106,7 @@
                 whole = rows_b[0, 0, part, :]
             else:
                 whole = jnp.where(last, rows_f[part, :], rows_s[0, 0, part, :])
+                refs[9][part, :] = whole
             whole = whole.astype(F32)
             scale = factor_of(whole)
             normed[part, :] = (whole * scale * gain[...]).astype(BF)
@@ -124,7 +125,7 @@
         prepare_kernel,
         (ahead, back, where),
         [rows, saved_of(saved, 0), saved_of(saved, 1), gain, down],
-        kinds * 3,
+        [*kinds * 3, shape((ROWS, WIDTH), BF)],
         6 * ROWS * WIDTH * LOWS,
     )
 
@@ -311,10 +312,9 @@
 
 
 def second_input_kernel(
-    where, sums, low, grad, rows_f, rows_s, factor, gain, down, d_values, d_low, *refs
+    where, sums, low, grad, rows, factor, gain, down, d_values, d_low, *refs
 ):
     blocks, out = refs[:8], refs[8]
-    last = where[9] == 1
     scale = factor[:, :1]
     values, lowered = d_values[...], d_low[...]
     inner = jnp.sum(values.astype(F32) * sums[...], axis=-1, keepdims=True)
@@ -322,17 +322,18 @@
     weight = scale * scale * inner * (1.0 / WIDTH)
     for i in range(8):
         span = columns(where[i])
-        rows = jnp.where(last, rows_f[:, span], rows_s[0, 0, :, span]).astype(F32)
         gained = gained_block(values, lowered, span, gain, down, blocks[i])
-        out[:, span] = (grad[:, span].astype(F32) + scale * gained - weight * rows).astype(BF)
-
-
-def second_input(where, sums, low, grad, rows, saved, factor, gain, down, d_values, d_low, blocks):
+        out[:, span] = (
+            grad[:, span].astype(F32) + scale * gained - weight * rows[:, span].astype(F32)
+        ).astype(BF)
+
+
+def second_input(where, sums, low, grad, rows, factor, gain, down, d_values, d_low, blocks):
     return call(
         second_input_kernel,
         (where,),
         [
-            sums, low, grad, rows, saved_of(saved, 1), factor, gain, down, d_values, d_low, *blocks
+            sums, low, grad, rows, factor, gain, down, d_values, d_low, *blocks
         ],
         [shape((ROWS, WIDTH), BF)],
         2 * ROWS * WIDTH * (VALUES + RANK),
@@ -340,20 +341,27 @@
 
 
 def forward_kernel(where, fresh, passed, gain, down, up, *refs):
-    vals, outs, (out, rows, normed) = refs[:8], refs[8:16], refs[16:]
+    vals, outs, (out, rows, gained) = refs[:8], refs[8:16], refs[16:]
     first = where[8] == 1
+    sums = []
     for top in range(0, ROWS, 32):
         part = slice(top, top + 32)
-        chosen = jnp.where(first, fresh[part, :], passed[part, :WIDTH])
-        whole = chosen.astype(F32)
-        rows[part, :] = chosen
-        normed[part, :] = (whole * factor_of(whole) * gain[...]).astype(BF)
+        total = jnp.zeros((32, 1), F32)
+        for left in range(0, WIDTH, PART):
+            span = slice(left, left + PART)
+            chosen = jnp.where(first, fresh[part, span], passed[part, span])
+            whole = chosen.astype(F32)
+            rows[part, span] = chosen
+            gained[part, span] = (whole * gain[:, span]).astype(BF)
+            total += jnp.sum(whole * whole, axis=-1, keepdims=True)
+        sums.append(total)
+    factor = lax.rsqrt(jnp.concatenate(sums, axis=0) * (1.0 / WIDTH) + EPS)
     ident = passed[:, WIDTH : WIDTH + 1].astype(F32).astype(jnp.int32)
-    low = only(dot_t(normed[...], down[...]), ident).astype(BF)
-    total = SCALE * dot(low, up[...])
-    for i in range(8):
-        total += dot(normed[:, columns(where[i])], vals[i][...])
-    values = total.astype(BF)
+    low = only(factor * dot_t(gained[...], down[...]), ident).astype(BF)
+    total = jnp.zeros((ROWS, VALUES), F32)
+    for i in range(8):
+        total += dot(gained[:, columns(where[i])], vals[i][...])
+    values = (factor * total + SCALE * dot(low, up[...])).astype(BF)
     for i in range(8):
         span = columns(where[i])
         out[:, span] = (rows[:, span].astype(F32) + dot(values, outs[i][...])).astype(BF)
@@ -481,7 +489,7 @@
     val_near, val_away = send(val_own, split_ring(1)), send(val_own, split_ring(-1))
     out_sibling, val_sibling = send(out_own, CORE), send(val_own, CORE)
 
-    normed_f, _, low_f, normed_b, factor_b, low_b, normed_n, factor_n, low_n = prepare(
+    normed_f, _, low_f, normed_b, factor_b, low_b, normed_n, factor_n, low_n, rows_n = prepare(
         ahead, back, where, rows, saved, gain, down
     )
     out_near, out_away, normed_f, out_sibling, val_sibling = lax.optimization_barrier(
@@ -522,7 +530,7 @@
     mine = pack(where, chosen_low, normed_n, d_values, d_low, False)
     terms = spread(where, first_sums, mine, received)
     bwd_out = second_input(
-        where, sums_n, low_n, grad_n, rows, saved, factor_n, gain, down, d_values, d_low, vals
+        where, sums_n, low_n, grad_n, rows_n, factor_n, gain, down, d_values, d_low, vals
     )
     fwd_out = forward(where, fresh, passed, gain, down, up, vals, outs)
     down_table, up_table = tables(ahead, back, where, relayed, terms)

time: 140 us -> 140 us (level)
    unnamed x26 -> x28, local copies, waits for them, and re-layouts: 5.16 us -> 5.17 us
  transfers between devices with their start and end apart: 21 -> 21, of which waited for: 10 -> 10; matrix products, arithmetic and copies ran while one was open for 0% -> 0% of each run, Pallas kernels for 19% -> 18%
where the time goes in v10:
time: 140 us; the launch traced here: 139 us
  starting transfers between devices  59.8 us (43%)
  waiting for transfers between devices  43.1 us (31%)
  Pallas kernels  28.6 us (20%)
  local copies, waits for them, and re-layouts  5.26 us (4%)
  between operations  2.1 us (2%)
    ppermute x16, starting transfers between devices, send(): return lax.ppermute(block, 'dp', pairs)  43.8 us
    pallas_call x14, Pallas kernels, call(): pl.pallas_call(kernel, out_shape=outs, grid_spec=pltpu.PrefetchScalarGrid...  28.6 us
    ppermute x16, waiting for transfers between devices, send(): return lax.ppermute(block, 'dp', pairs)  22.2 us
    ppermute x1, waiting for transfers between devices, body(): relayed = lax.ppermute(first_back, 'section', before)  20.9 us
    ppermute x1, starting transfers between devices, body(): passed = lax.ppermute(first_out, 'section', onward)  5.58 us
    unnamed x28, local copies, waits for them, and re-layouts  5.17 us
    ppermute x1, starting transfers between devices, spread(): lax.ppermute(two, 'dp', chips(2))  3.62 us
    ppermute x1, starting transfers between devices, spread(): lax.ppermute(three, 'dp', chips(3))  3.44 us
  transfers between devices with their start and end apart: 21, of which 10 were waited for; matrix products, arithmetic and copies ran while one was open for 0% of the time, Pallas kernels for 18%

profile of v10, /device:TPU:30, one launch (start us, length us, event | category | flops | bytes accessed | tf_op | source)
XLA Modules:
  0.0 138.8 jit_solution(3163947728817858231)
XLA Ops:
  0.6 3.3 %collective-permute-start = (bf16[512,512]{1,0:T(8,128)(2,1)}, bf16[512,512]{1,0:T(8,128)(2,1)S(1)}, u32[]{:S(2)}, u32[]{:S(2)}) collective-permute-start(bf16[512,512]{1,0:T(8,128)(2,1)} %bitcast.31), channel_id=1, source_target_pairs={{0,2},{1,7},{2,4},{3,1},{4,6},{5,3},{6,0},{7,5},{8,10},{9,15},{10,... | collective-permute-start | bytes 1572872 | tf_op jit(solution)/shard_map/ppermute | solution.py:453
  4.0 3.1 %collective-permute-start.1 = (bf16[512,512]{1,0:T(8,128)(2,1)}, bf16[512,512]{1,0:T(8,128)(2,1)S(1)}, u32[]{:S(2)}, u32[]{:S(2)}) collective-permute-start(bf16[512,512]{1,0:T(8,128)(2,1)} %bitcast.32), channel_id=1, source_target_pairs={{0,6},{1,3},{2,0},{3,5},{4,2},{5,7},{6,4},{7,1},{8,14},{9,11},{10,... | collective-permute-start | bytes 1572872 | tf_op jit(solution)/shard_map/ppermute | solution.py:453
  7.1 0.5 collective-permute-start.3
  7.6 1.4 collective-permute-start.8
  10.3 0.1 stack.51.where
  10.4 1.6 %copy-done = bf16[1,4,4096,64]{2,3,1,0:T(8,128)(2,1)S(1)} copy-done((bf16[1,4,4096,64]{2,3,1,0:T(8,128)(2,1)S(1)}, bf16[1,4,4096,64]{2,3,1,0:T(8,128)(2,1)}, u32[]{:S(2)}) %copy-start) | copy-done | bytes 2097176
  12.0 1.6 %copy-done.2 = bf16[1,2,128,4096]{3,2,1,0:T(8,128)(2,1)S(1)} copy-done((bf16[1,2,128,4096]{3,2,1,0:T(8,128)(2,1)S(1)}, bf16[1,2,128,4096]{3,2,1,0:T(8,128)(2,1)}, u32[]{:S(2)}) %copy-start.2) | copy-done | bytes 2097176
  13.5 1.2 copy-done.7
  14.8 0.7 copy-done.12
  15.5 0.0 copy-start.6
  15.5 0.0 copy-start.9
  15.5 4.2 %shard_map.147 = (bf16[128,4096]{1,0:T(8,128)(2,1)S(1)}, f32[128,128]{1,0:T(8,128)}, bf16[128,256]{1,0:T(8,128)(2,1)S(1)}, bf16[128,4096]{1,0:T(8,128)(2,1)S(1)}...) custom-call(s32[1]{0:T(128)S(6)} %copy.16.ahead, ...), custom_call_target="tpu_custom_call" | custom-call | flops 805306 | bytes 7356 | tf_op jit(solution)/shard_map/pallas_call | solution.py:52
  19.7 0.8 collective-permute-done.refs_2_.refs_10_
  20.5 6.2 %collective-permute-start.10 = (bf16[512,512]{1,0:T(8,128)(2,1)S(1)}, bf16[512,512]{1,0:T(8,128)(2,1)S(1)}, u32[]{:S(2)}, u32[]{:S(2)}) collective-permute-start(bf16[512,512]{1,0:T(8,128)(2,1)S(1)} %bitcast.40), channel_id=1, source_target_pairs={{0,6},{1,3},{2,0},{3,5},{4,2},{5,7},{6,4},{7,1},{8,14},{9,11},{10,... | collective-permute-start | bytes 1572872 | tf_op jit(solution)/shard_map/ppermute | solution.py:453
  26.8 8.6 %collective-permute-done.1.refs_4_.refs_12_ = bf16[512,512]{1,0:T(8,128)(2,1)S(1)} collective-permute-done((bf16[512,512]{1,0:T(8,128)(2,1)}, bf16[512,512]{1,0:T(8,128)(2,1)S(1)}, u32[]{:S(2)}, u32[]{:S(2)}) %collective-permute-start.1) | collective-permute-done | bytes 524320 | tf_op jit(solution)/shard_map/ppermute | solution.py:453
  35.4 4.0 %collective-permute-start.6 = (bf16[512,512]{1,0:T(8,128)(2,1)S(1)}, bf16[512,512]{1,0:T(8,128)(2,1)S(1)}, u32[]{:S(2)}, u32[]{:S(2)}) collective-permute-start(bf16[512,512]{1,0:T(8,128)(2,1)S(1)} %collective-permute-done.refs_2_.refs_10_), channel_id=1, source_target_pairs={{0,2},{1,7},{2,4},{3,1},{4,6},{5,3},{6,0},{7,5},{8,10},{9,15},{10,... | collective-permute-start | bytes 1572872 | tf_op jit(solution)/shard_map/ppermute | solution.py:453
  39.4 0.5 collective-permute-start.5
  39.9 3.8 %collective-permute-start.9 = (bf16[512,512]{1,0:T(8,128)(2,1)S(1)}, bf16[512,512]{1,0:T(8,128)(2,1)S(1)}, u32[]{:S(2)}, u32[]{:S(2)}) collective-permute-start(bf16[512,512]{1,0:T(8,128)(2,1)S(1)} %collective-permute-done.8.refs_10_.refs_2_), channel_id=1, source_target_pairs={{0,1},{1,0},{2,3},{3,2},{4,5},{5,4},{6,7},{7,6},{8,9},{9,8},{10,11... | collective-permute-start | bytes 1572872 | tf_op jit(solution)/shard_map/ppermute | solution.py:453
  43.7 3.0 %collective-permute-done.10.refs_12_.refs_4_ = bf16[512,512]{1,0:T(8,128)(2,1)S(1)} collective-permute-done((bf16[512,512]{1,0:T(8,128)(2,1)S(1)}, bf16[512,512]{1,0:T(8,128)(2,1)S(1)}, u32[]{:S(2)}, u32[]{:S(2)}) %collective-permute-start.10) | collective-permute-done | bytes 524320 | tf_op jit(solution)/shard_map/ppermute | solution.py:453
  46.7 19.9 %collective-permute-start.11 = (bf16[512,512]{1,0:T(8,128)(2,1)S(1)}, bf16[512,512]{1,0:T(8,128)(2,1)S(1)}, u32[]{:S(2)}, u32[]{:S(2)}) collective-permute-start(bf16[512,512]{1,0:T(8,128)(2,1)S(1)} %collective-permute-done.10.refs_12_.refs_4_), channel_id=1, source_target_pairs={{0,1},{1,0},{2,3},{3,2},{4,5},{5,4},{6,7},{7,6},{8,9},{9,8},{10,11... | collective-permute-start | bytes 1572872 | tf_op jit(solution)/shard_map/ppermute | solution.py:453
  66.6 0.5 collective-permute-start.12
  67.1 1.0 collective-permute-done.11.refs_13_.refs_5_
  68.1 0.7 collective-permute-done.7.refs_7_.refs_15_
  68.9 4.7 %shard_map.148 = (bf16[128,512]{1,0:T(8,128)(2,1)S(1)}, bf16[128,256]{1,0:T(8,128)(2,1)S(1)}, f32[6,128,512]{2,1,0:T(8,128)S(1)}, f32[128,128]{1,0:T(8,128)S(1)}, f32[128,512]{1,0:T(8,128)S(1)}) custom-call(s32[1]{0:T(128)S(6)} %copy.17.back, s32[10]{0:T(128)S(1)} %stack.51.where, bf16[128,4096]{1,0:T(8,128)(2,1)S(1)} %bitcast.51, ...), custom_call_target="tpu_custom_call" | custom-call | flops 1610612 | bytes 13975 | tf_op jit(solution)/shard_map/pallas_call | solution.py:52
  73.6 0.9 shard_map.150
  74.5 0.5 collective-permute-start.13
  75.0 0.9 shard_map.149.mine
  75.9 0.4 collective-permute-done.13.other
  76.2 0.1 shard_map.151.first
  76.3 4.9 %collective-permute-done.12.far.refs_6_ = bf16[512,512]{1,0:T(8,128)(2,1)S(1)} collective-permute-done((bf16[512,512]{1,0:T(8,128)(2,1)S(1)}, bf16[512,512]{1,0:T(8,128)(2,1)S(1)}, u32[]{:S(2)}, u32[]{:S(2)}) %collective-permute-start.12) | collective-permute-done | bytes 524320 | tf_op jit(solution)/shard_map/ppermute | solution.py:453
  81.3 1.9 %collective-permute-done.14.far_other.refs_7_ = bf16[512,512]{1,0:T(8,128)(2,1)S(1)} collective-permute-done((bf16[512,512]{1,0:T(8,128)(2,1)S(1)}, bf16[512,512]{1,0:T(8,128)(2,1)S(1)}, u32[]{:S(2)}, u32[]{:S(2)}) %collective-permute-start.14) | collective-permute-done | bytes 524320 | tf_op jit(solution)/shard_map/ppermute | solution.py:453
  83.2 1.8 %shard_map.152 = bf16[128,4224]{1,0:T(8,128)(2,1)S(1)} custom-call(s32[1]{0:T(128)S(6)} %copy.17.back, s32[10]{0:T(128)S(1)} %stack.51.where, f32[6,128,512]{2,1,0:T(8,128)S(1)} %get-tuple-element.49.kept, f32[128,128]{1,0:T(8,128)S(1)} %get-tuple-element.50.inner, bf16[128,512]{1,0:T(8,128)(2,1)S(1)} %get-tuple-element.51.d_values.values, ...), custom_call_target="tpu_custom_call" | custom-call | flops 268435 | bytes 8208 | tf_op jit(solution)/shard_map/pallas_call | solution.py:52
  85.0 2.7 %collective-permute-start.16 = (bf16[128,4224]{1,0:T(8,128)(2,1)S(1)}, bf16[128,4224]{1,0:T(8,128)(2,1)S(1)}, u32[]{:S(2)}, u32[]{:S(2)}) collective-permute-start(bf16[128,4224]{1,0:T(8,128)(2,1)S(1)} %shard_map.152), channel_id=1, source_target_pairs={{8,0},{16,8},{24,16},{32,24},{40,32},{48,40},{56,48},{64,56},{72,6... | collective-permute-start | bytes 3244040 | tf_op jit(solution)/shard_map/ppermute | solution.py:518
  87.6 1.6 %shard_map.153.out = bf16[128,4224]{1,0:T(8,128)(2,1)S(1)} custom-call(s32[1]{0:T(128)S(6)} %copy.16.ahead, s32[10]{0:T(128)S(1)} %stack.51.where, f32[128,512]{1,0:T(8,128)S(1)} %get-tuple-element.56.share, bf16[128,4096]{1,0:T(8,128)(2,1)S(1)} %get-tuple-element.42.normed, bf16[128,256]{1,0:T(8,128)(2,1)S(1)} %get-tuple-element.57.low, ...), custom_call_target="tpu_custom_call" | custom-call | flops 536870 | bytes 7929 | tf_op jit(solution)/shard_map/pallas_call | solution.py:52
  89.2 5.6 %collective-permute-start.15 = (bf16[128,4224]{1,0:T(8,128)(2,1)S(1)}, bf16[128,4224]{1,0:T(8,128)(2,1)S(1)}, u32[]{:S(2)}, u32[]{:S(2)}) collective-permute-start(bf16[128,4224]{1,0:T(8,128)(2,1)S(1)} %shard_map.153.out), channel_id=1, source_target_pairs={{0,8},{8,16},{16,24},{24,32},{32,40},{40,48},{48,56},{56,64},{64,7... | collective-permute-start | bytes 3244040 | tf_op jit(solution)/shard_map/ppermute | solution.py:521
  94.8 1.3 shard_map.155.sums
  96.1 20.9 %collective-permute-done.16.relayed = bf16[128,4224]{1,0:T(8,128)(2,1)S(1)} collective-permute-done((bf16[128,4224]{1,0:T(8,128)(2,1)S(1)}, bf16[128,4224]{1,0:T(8,128)(2,1)S(1)}, u32[]{:S(2)}, u32[]{:S(2)}) %collective-permute-start.16) | collective-permute-done | bytes 1081376 | tf_op jit(solution)/shard_map/ppermute | solution.py:518
  117.0 2.6 %shard_map.156 = (bf16[128,4096]{1,0:T(8,128)(2,1)S(1)}, bf16[128,512]{1,0:T(8,128)(2,1)S(1)}, bf16[128,256]{1,0:T(8,128)(2,1)S(1)}, bf16[128,256]{1,0:T(8,128)(2,1)S(1)}, bf16[4,64,640]{2,1,0:T(8,128)(2,1)S(1)}) custom-call(s32[1]{0:T(128)S(6)} %copy.16.ahead, s32[10]{0:T(128)S(1)} %stack.51.where, bf16[128,4224]{1,0:T(8,128)(2,1)S(1)} %collective-permute-done.16.relayed, ...), custom_call_target="tpu_custom_call" | custom-call | flops 603979 | bytes 8781 | tf_op jit(solution)/shard_map/pallas_call | solution.py:52
  119.6 0.1 collective-permute-start.17
  119.7 0.9 shard_map.158.mine
  120.6 0.7 collective-permute-done.17.other
  121.3 0.7 shard_map.159
  122.0 3.6 %collective-permute-start.18 = (bf16[64,1152]{1,0:T(8,128)(2,1)S(1)}, bf16[64,1152]{1,0:T(8,128)(2,1)S(1)}, u32[]{:S(2)}, u32[]{:S(2)}) collective-permute-start(bf16[64,1152]{1,0:T(8,128)(2,1)S(1)} %get-tuple-element.73), channel_id=1, source_target_pairs={{0,4},{1,5},{2,6},{3,7},{4,0},{5,1},{6,2},{7,3},{8,12},{9,13},{10,... | collective-permute-start | bytes 442376 | tf_op jit(solution)/shard_map/ppermute | solution.py:409
  125.6 0.7 collective-permute-start.19
  126.3 3.4 %collective-permute-start.20 = (bf16[64,1152]{1,0:T(8,128)(2,1)S(1)}, bf16[64,1152]{1,0:T(8,128)(2,1)S(1)}, u32[]{:S(2)}, u32[]{:S(2)}) collective-permute-start(bf16[64,1152]{1,0:T(8,128)(2,1)S(1)} %get-tuple-element.75), channel_id=1, source_target_pairs={{0,6},{1,7},{2,0},{3,1},{4,2},{5,3},{6,4},{7,5},{8,14},{9,15},{10,... | collective-permute-start | bytes 442376 | tf_op jit(solution)/shard_map/ppermute | solution.py:411
  129.8 3.5 %shard_map.157 = bf16[128,4096]{1,0:T(8,128)(2,1)} custom-call(s32[10]{0:T(128)S(1)} %stack.51.where, f32[128,512]{1,0:T(8,128)S(1)} %shard_map.155.sums, bf16[128,256]{1,0:T(8,128)(2,1)S(1)} %get-tuple-element.61.low, bf16[128,4096]{1,0:T(8,128)(2,1)S(1)} %get-tuple-element.64.grad, bf16[128,4096]{1,0:T(8,128)(2,1)S(1)} %get-tuple-element.65.rows, ...), custom_call_target="tpu_custom_call" | custom-call | flops 603979 | bytes 8994 | tf_op jit(solution)/shard_map/pallas_call | solution.py:52
  133.3 4.0 %shard_map.154 = bf16[128,4096]{1,0:T(8,128)(2,1)} custom-call(s32[10]{0:T(128)S(1)} %stack.51.where, bf16[128,4096]{1,0:T(8,128)(2,1)S(1)} %copy-done.11, bf16[128,4224]{1,0:T(8,128)(2,1)S(1)} %collective-permute-done.15.passed, f32[1,4096]{1,0:T(1,128)S(1)} %copy-done.13, bf16[256,4096]{1,0:T(8,128)(2,1)S(1)} %bitcast.30, bf16[256,512]{1,0:T(8,128)(2,1)S(1)} %bitcast.48, ...), custom_call_target="tpu_custom_call" | custom-call | flops 1073741 | bytes 12894 | tf_op jit(solution)/shard_map/pallas_call | solution.py:52
  137.3 1.5 %shard_map.160 = (f32[4,64,512]{2,1,0:T(8,128)}, f32[4,64,64]{2,1,0:T(8,128)}) custom-call(s32[1]{0:T(128)S(6)} %copy.16.ahead, s32[1]{0:T(128)S(6)} %copy.17.back, s32[10]{0:T(128)S(1)} %stack.51.where, bf16[128,4224]{1,0:T(8,128)(2,1)S(1)} %collective-permute-done.16.relayed, bf16[64,1152]{1,0:T(8,128)(2,1)S(1)} %get-tuple-element.72.refs_0_, ...), custom_call_target="tpu_custom_call" | custom-call | bytes 1671 | tf_op jit(solution)/shard_map/pallas_call | solution.py:52
  (37 shorter events, 0.1 us)
Async XLA Ops:
  0.6 19.9 %collective-permute-start = (bf16[512,512]{1,0:T(8,128)(2,1)}, bf16[512,512]{1,0:T(8,128)(2,1)S(1)}, u32[]{:S(2)}, u32[]{:S(2)}) collective-permute-start(bf16[512,512]{1,0:T(8,128)(2,1)} %bitcast.31), channel_id=1, source_target_pairs={{0,2},{1,7},{2,4},{3,1},{4,6},{5,3},{6,0},{7,5},{8,10},{9,15},{10,... | collective-permute-start | bytes 1572872 | tf_op jit(solution)/shard_map/ppermute | solution.py:453
  4.0 31.4 %collective-permute-start.1 = (bf16[512,512]{1,0:T(8,128)(2,1)}, bf16[512,512]{1,0:T(8,128)(2,1)S(1)}, u32[]{:S(2)}, u32[]{:S(2)}) collective-permute-start(bf16[512,512]{1,0:T(8,128)(2,1)} %bitcast.32), channel_id=1, source_target_pairs={{0,6},{1,3},{2,0},{3,5},{4,2},{5,7},{6,4},{7,1},{8,14},{9,11},{10,... | collective-permute-start | bytes 1572872 | tf_op jit(solution)/shard_map/ppermute | solution.py:453
  7.1 28.2 %collective-permute-start.2 = (bf16[512,512]{1,0:T(8,128)(2,1)}, bf16[512,512]{1,0:T(8,128)(2,1)S(1)}, u32[]{:S(2)}, u32[]{:S(2)}) collective-permute-start(bf16[512,512]{1,0:T(8,128)(2,1)} %bitcast.33), channel_id=1, source_target_pairs={{0,1},{1,0},{2,3},{3,2},{4,5},{5,4},{6,7},{7,6},{8,9},{9,8},{10,11... | collective-permute-start | bytes 1572872 | tf_op jit(solution)/shard_map/ppermute | solution.py:453
  7.1 28.2 %collective-permute-start.3 = (bf16[512,512]{1,0:T(8,128)(2,1)}, bf16[512,512]{1,0:T(8,128)(2,1)S(1)}, u32[]{:S(2)}, u32[]{:S(2)}) collective-permute-start(bf16[512,512]{1,0:T(8,128)(2,1)} %bitcast.38), channel_id=1, source_target_pairs={{0,1},{1,0},{2,3},{3,2},{4,5},{5,4},{6,7},{7,6},{8,9},{9,8},{10,11... | collective-permute-start | bytes 1572872 | tf_op jit(solution)/shard_map/ppermute | solution.py:453
  7.6 32.3 %collective-permute-start.8 = (bf16[512,512]{1,0:T(8,128)(2,1)}, bf16[512,512]{1,0:T(8,128)(2,1)S(1)}, u32[]{:S(2)}, u32[]{:S(2)}) collective-permute-start(bf16[512,512]{1,0:T(8,128)(2,1)} %bitcast.39), channel_id=1, source_target_pairs={{0,2},{1,7},{2,4},{3,1},{4,6},{5,3},{6,0},{7,5},{8,10},{9,15},{10,... | collective-permute-start | bytes 1572872 | tf_op jit(solution)/shard_map/ppermute | solution.py:453
  10.4 1.6 %copy-start = (bf16[1,4,4096,64]{2,3,1,0:T(8,128)(2,1)S(1)}, bf16[1,4,4096,64]{2,3,1,0:T(8,128)(2,1)}, u32[]{:S(2)}) copy-start(bf16[1,4,4096,64]{2,3,1,0:T(8,128)(2,1)} %param.22) | copy-start | bytes 6291460
  12.0 1.6 %copy-start.2 = (bf16[1,2,128,4096]{3,2,1,0:T(8,128)(2,1)S(1)}, bf16[1,2,128,4096]{3,2,1,0:T(8,128)(2,1)}, u32[]{:S(2)}) copy-start(bf16[1,2,128,4096]{3,2,1,0:T(8,128)(2,1)} %rows.3) | copy-start | bytes 6291460
  13.5 1.2 copy-start.7
  14.8 0.7 copy-start.12
  15.5 5.1 %copy-start.5 = (bf16[1,512,512]{2,1,0:T(8,128)(2,1)S(1)}, bf16[1,512,512]{2,1,0:T(8,128)(2,1)}, u32[]{:S(2)}) copy-start(bf16[1,512,512]{2,1,0:T(8,128)(2,1)} %param.19) | copy-start | bytes 1572868
  15.5 53.4 %copy-start.1 = (bf16[1,4,4096,64]{2,3,1,0:T(8,128)(2,1)S(1)}, bf16[1,4,4096,64]{2,3,1,0:T(8,128)(2,1)}, u32[]{:S(2)}) copy-start(bf16[1,4,4096,64]{2,3,1,0:T(8,128)(2,1)} %param.22) | copy-start | bytes 6291460
  15.5 53.4 %copy-start.3 = (bf16[1,2,128,4096]{3,2,1,0:T(8,128)(2,1)S(1)}, bf16[1,2,128,4096]{3,2,1,0:T(8,128)(2,1)}, u32[]{:S(2)}) copy-start(bf16[1,2,128,4096]{3,2,1,0:T(8,128)(2,1)} %rows.3) | copy-start | bytes 6291460
  15.5 53.4 %copy-start.4 = (bf16[1,512,512]{2,1,0:T(8,128)(2,1)S(1)}, bf16[1,512,512]{2,1,0:T(8,128)(2,1)}, u32[]{:S(2)}) copy-start(bf16[1,512,512]{2,1,0:T(8,128)(2,1)} %param.20) | copy-start | bytes 1572868
  15.5 53.4 %copy-start.6 = (bf16[1,4,64,512]{3,2,1,0:T(8,128)(2,1)S(1)}, bf16[1,4,64,512]{3,2,1,0:T(8,128)(2,1)}, u32[]{:S(2)}) copy-start(bf16[1,4,64,512]{3,2,1,0:T(8,128)(2,1)} %param.23) | copy-start | bytes 786436
  15.5 53.4 %copy-start.9 = (bf16[1,128,4096]{2,1,0:T(8,128)(2,1)S(1)}, bf16[1,128,4096]{2,1,0:T(8,128)(2,1)}, u32[]{:S(2)}) copy-start(bf16[1,128,4096]{2,1,0:T(8,128)(2,1)} %param.13) | copy-start | bytes 3145732
  20.5 26.2 %collective-permute-start.10 = (bf16[512,512]{1,0:T(8,128)(2,1)S(1)}, bf16[512,512]{1,0:T(8,128)(2,1)S(1)}, u32[]{:S(2)}, u32[]{:S(2)}) collective-permute-start(bf16[512,512]{1,0:T(8,128)(2,1)S(1)} %bitcast.40), channel_id=1, source_target_pairs={{0,6},{1,3},{2,0},{3,5},{4,2},{5,7},{6,4},{7,1},{8,14},{9,11},{10,... | collective-permute-start | bytes 1572872 | tf_op jit(solution)/shard_map/ppermute | solution.py:453
  35.4 31.2 %collective-permute-start.6 = (bf16[512,512]{1,0:T(8,128)(2,1)S(1)}, bf16[512,512]{1,0:T(8,128)(2,1)S(1)}, u32[]{:S(2)}, u32[]{:S(2)}) collective-permute-start(bf16[512,512]{1,0:T(8,128)(2,1)S(1)} %collective-permute-done.refs_2_.refs_10_), channel_id=1, source_target_pairs={{0,2},{1,7},{2,4},{3,1},{4,6},{5,3},{6,0},{7,5},{8,10},{9,15},{10,... | collective-permute-start | bytes 1572872 | tf_op jit(solution)/shard_map/ppermute | solution.py:453
  39.4 27.2 %collective-permute-start.4 = (bf16[512,512]{1,0:T(8,128)(2,1)S(1)}, bf16[512,512]{1,0:T(8,128)(2,1)S(1)}, u32[]{:S(2)}, u32[]{:S(2)}) collective-permute-start(bf16[512,512]{1,0:T(8,128)(2,1)S(1)} %collective-permute-done.refs_2_.refs_10_), channel_id=1, source_target_pairs={{0,1},{1,0},{2,3},{3,2},{4,5},{5,4},{6,7},{7,6},{8,9},{9,8},{10,11... | collective-permute-start | bytes 1572872 | tf_op jit(solution)/shard_map/ppermute | solution.py:453
  39.4 27.7 %collective-permute-start.5 = (bf16[512,512]{1,0:T(8,128)(2,1)S(1)}, bf16[512,512]{1,0:T(8,128)(2,1)S(1)}, u32[]{:S(2)}, u32[]{:S(2)}) collective-permute-start(bf16[512,512]{1,0:T(8,128)(2,1)S(1)} %collective-permute-done.1.refs_4_.refs_12_), channel_id=1, source_target_pairs={{0,1},{1,0},{2,3},{3,2},{4,5},{5,4},{6,7},{7,6},{8,9},{9,8},{10,11... | collective-permute-start | bytes 1572872 | tf_op jit(solution)/shard_map/ppermute | solution.py:453
  39.9 27.2 %collective-permute-start.9 = (bf16[512,512]{1,0:T(8,128)(2,1)S(1)}, bf16[512,512]{1,0:T(8,128)(2,1)S(1)}, u32[]{:S(2)}, u32[]{:S(2)}) collective-permute-start(bf16[512,512]{1,0:T(8,128)(2,1)S(1)} %collective-permute-done.8.refs_10_.refs_2_), channel_id=1, source_target_pairs={{0,1},{1,0},{2,3},{3,2},{4,5},{5,4},{6,7},{7,6},{8,9},{9,8},{10,11... | collective-permute-start | bytes 1572872 | tf_op jit(solution)/shard_map/ppermute | solution.py:453
  46.7 21.4 %collective-permute-start.11 = (bf16[512,512]{1,0:T(8,128)(2,1)S(1)}, bf16[512,512]{1,0:T(8,128)(2,1)S(1)}, u32[]{:S(2)}, u32[]{:S(2)}) collective-permute-start(bf16[512,512]{1,0:T(8,128)(2,1)S(1)} %collective-permute-done.10.refs_12_.refs_4_), channel_id=1, source_target_pairs={{0,1},{1,0},{2,3},{3,2},{4,5},{5,4},{6,7},{7,6},{8,9},{9,8},{10,11... | collective-permute-start | bytes 1572872 | tf_op jit(solution)/shard_map/ppermute | solution.py:453
  66.6 2.3 %collective-permute-start.7 = (bf16[512,512]{1,0:T(8,128)(2,1)S(1)}, bf16[512,512]{1,0:T(8,128)(2,1)S(1)}, u32[]{:S(2)}, u32[]{:S(2)}) collective-permute-start(bf16[512,512]{1,0:T(8,128)(2,1)S(1)} %collective-permute-done.6.refs_6_.refs_14_), channel_id=1, source_target_pairs={{0,1},{1,0},{2,3},{3,2},{4,5},{5,4},{6,7},{7,6},{8,9},{9,8},{10,11... | collective-permute-start | bytes 1572872 | tf_op jit(solution)/shard_map/ppermute | solution.py:453
  66.6 14.7 %collective-permute-start.12 = (bf16[512,512]{1,0:T(8,128)(2,1)S(1)}, bf16[512,512]{1,0:T(8,128)(2,1)S(1)}, u32[]{:S(2)}, u32[]{:S(2)}) collective-permute-start(bf16[512,512]{1,0:T(8,128)(2,1)S(1)} %collective-permute-done.8.refs_10_.refs_2_), channel_id=1, source_target_pairs={{0,2},{1,7},{2,4},{3,1},{4,6},{5,3},{6,0},{7,5},{8,10},{9,15},{10,... | collective-permute-start | bytes 1572872 | tf_op jit(solution)/shard_map/ppermute | solution.py:453
  74.5 8.7 %copy-start.13 = (f32[1,4096]{1,0:T(1,128)S(1)}, f32[1,4096]{1,0:T(1,128)}, u32[]{:S(2)}) copy-start(f32[1,4096]{1,0:T(1,128)} %gain.9) | copy-start | bytes 49156
  74.5 1.7 %collective-permute-start.13 = (bf16[4,64,640]{2,1,0:T(8,128)(2,1)S(1)}, bf16[4,64,640]{2,1,0:T(8,128)(2,1)S(1)}, u32[]{:S(2)}, u32[]{:S(2)}) collective-permute-start(bf16[4,64,640]{2,1,0:T(8,128)(2,1)S(1)} %shard_map.150), channel_id=1, source_target_pairs={{0,1},{1,0},{2,3},{3,2},{4,5},{5,4},{6,7},{7,6},{8,9},{9,8},{10,11... | collective-permute-start | bytes 983048 | tf_op jit(solution)/shard_map/ppermute | solution.py:453
  81.3 1.9 %collective-permute-start.14 = (bf16[512,512]{1,0:T(8,128)(2,1)S(1)}, bf16[512,512]{1,0:T(8,128)(2,1)S(1)}, u32[]{:S(2)}, u32[]{:S(2)}) collective-permute-start(bf16[512,512]{1,0:T(8,128)(2,1)S(1)} %collective-permute-done.12.far.refs_6_), channel_id=1, source_target_pairs={{0,1},{1,0},{2,3},{3,2},{4,5},{5,4},{6,7},{7,6},{8,9},{9,8},{10,11... | collective-permute-start | bytes 1572872 | tf_op jit(solution)/shard_map/ppermute | solution.py:453
  83.2 4.4 %copy-start.8 = (bf16[1,128,4096]{2,1,0:T(8,128)(2,1)S(1)}, bf16[1,128,4096]{2,1,0:T(8,128)(2,1)}, u32[]{:S(2)}) copy-start(bf16[1,128,4096]{2,1,0:T(8,128)(2,1)} %param.12) | copy-start | bytes 3145732
  85.0 32.0 %collective-permute-start.16 = (bf16[128,4224]{1,0:T(8,128)(2,1)S(1)}, bf16[128,4224]{1,0:T(8,128)(2,1)S(1)}, u32[]{:S(2)}, u32[]{:S(2)}) collective-permute-start(bf16[128,4224]{1,0:T(8,128)(2,1)S(1)} %shard_map.152), channel_id=1, source_target_pairs={{8,0},{16,8},{24,16},{32,24},{40,32},{48,40},{56,48},{64,56},{72,6... | collective-permute-start | bytes 3244040 | tf_op jit(solution)/shard_map/ppermute | solution.py:518
  89.2 44.1 %collective-permute-start.15 = (bf16[128,4224]{1,0:T(8,128)(2,1)S(1)}, bf16[128,4224]{1,0:T(8,128)(2,1)S(1)}, u32[]{:S(2)}, u32[]{:S(2)}) collective-permute-start(bf16[128,4224]{1,0:T(8,128)(2,1)S(1)} %shard_map.153.out), channel_id=1, source_target_pairs={{0,8},{8,16},{16,24},{24,32},{32,40},{40,48},{48,56},{56,64},{64,7... | collective-permute-start | bytes 3244040 | tf_op jit(solution)/shard_map/ppermute | solution.py:521
  94.8 22.2 %copy-start.10 = (bf16[128,4096]{1,0:T(8,128)(2,1)S(1)}, bf16[128,4096]{1,0:T(8,128)(2,1)}, u32[]{:S(2)}) copy-start(bf16[128,4096]{1,0:T(8,128)(2,1)} %target.1) | copy-start | bytes 3145732
  119.6 1.7 %collective-permute-start.17 = (bf16[4,64,640]{2,1,0:T(8,128)(2,1)S(1)}, bf16[4,64,640]{2,1,0:T(8,128)(2,1)S(1)}, u32[]{:S(2)}, u32[]{:S(2)}) collective-permute-start(bf16[4,64,640]{2,1,0:T(8,128)(2,1)S(1)} %get-tuple-element.71), channel_id=1, source_target_pairs={{0,1},{1,0},{2,3},{3,2},{4,5},{5,4},{6,7},{7,6},{8,9},{9,8},{10,11... | collective-permute-start | bytes 983048 | tf_op jit(solution)/shard_map/ppermute | solution.py:453
  122.0 15.3 %collective-permute-start.18 = (bf16[64,1152]{1,0:T(8,128)(2,1)S(1)}, bf16[64,1152]{1,0:T(8,128)(2,1)S(1)}, u32[]{:S(2)}, u32[]{:S(2)}) collective-permute-start(bf16[64,1152]{1,0:T(8,128)(2,1)S(1)} %get-tuple-element.73), channel_id=1, source_target_pairs={{0,4},{1,5},{2,6},{3,7},{4,0},{5,1},{6,2},{7,3},{8,12},{9,13},{10,... | collective-permute-start | bytes 442376 | tf_op jit(solution)/shard_map/ppermute | solution.py:409
  125.6 11.6 %collective-permute-start.19 = (bf16[64,1152]{1,0:T(8,128)(2,1)S(1)}, bf16[64,1152]{1,0:T(8,128)(2,1)S(1)}, u32[]{:S(2)}, u32[]{:S(2)}) collective-permute-start(bf16[64,1152]{1,0:T(8,128)(2,1)S(1)} %get-tuple-element.74), channel_id=1, source_target_pairs={{0,2},{1,3},{2,4},{3,5},{4,6},{5,7},{6,0},{7,1},{8,10},{9,11},{10,... | collective-permute-start | bytes 442376 | tf_op jit(solution)/shard_map/ppermute | solution.py:410
  126.3 10.9 %collective-permute-start.20 = (bf16[64,1152]{1,0:T(8,128)(2,1)S(1)}, bf16[64,1152]{1,0:T(8,128)(2,1)S(1)}, u32[]{:S(2)}, u32[]{:S(2)}) collective-permute-start(bf16[64,1152]{1,0:T(8,128)(2,1)S(1)} %get-tuple-element.75), channel_id=1, source_target_pairs={{0,6},{1,7},{2,0},{3,1},{4,2},{5,3},{6,4},{7,5},{8,14},{9,15},{10,... | collective-permute-start | bytes 442376 | tf_op jit(solution)/shard_map/ppermute | solution.py:411
  129.8 3.5 %copy-start.11 = (bf16[128,4096]{1,0:T(8,128)(2,1)S(1)}, bf16[128,4096]{1,0:T(8,128)(2,1)}, u32[]{:S(2)}) copy-start(bf16[128,4096]{1,0:T(8,128)(2,1)} %fresh.1) | copy-start | bytes 3145732

commit v11 on v9

--- a/solution.py
+++ b/solution.py
@@ -484,9 +484,7 @@
     normed_f, _, low_f, normed_b, factor_b, low_b, normed_n, factor_n, low_n = prepare(
         ahead, back, where, rows, saved, gain, down
     )
-    out_near, out_away, normed_f, out_sibling, val_sibling = lax.optimization_barrier(
-        (out_near, out_away, normed_f, out_sibling, val_sibling)
-    )
+    out_near, out_away, normed_f = lax.optimization_barrier((out_near, out_away, normed_f))
     out_far, val_far = send(out_near, split_ring(1)), send(val_near, split_ring(1))
     outs = [
         out_own, out_sibling, out_near, send(out_near, CORE), out_away, send(out_away, CORE)

time: 140 us -> 140 us (level)
  starting transfers between devices: 59.8 us -> 47.2 us
  waiting for transfers between devices: 43.1 us -> 55.2 us
    ppermute x16, starting transfers between devices: 43.8 us -> 31.6 us  [send(): return lax.ppermute(block, 'dp', pairs)]
    ppermute x16, waiting for transfers between devices: 22.2 us -> 34.3 us  [send(): return lax.ppermute(block, 'dp', pairs)]
  transfers between devices with their start and end apart: 21 -> 21, of which waited for: 10 -> 9; matrix products, arithmetic and copies ran while one was open for 0% -> 0% of each run, Pallas kernels for 19% -> 19%
where the time goes in v11:
time: 140 us; the launch traced here: 139 us
  waiting for transfers between devices  55.2 us (39%)
  starting transfers between devices  47.2 us (34%)
  Pallas kernels  29.7 us (21%)
  local copies, waits for them, and re-layouts  5.25 us (4%)
  between operations  2.1 us (2%)
    ppermute x16, waiting for transfers between devices, send(): return lax.ppermute(block, 'dp', pairs)  34.3 us
    ppermute x16, starting transfers between devices, send(): return lax.ppermute(block, 'dp', pairs)  31.6 us
    pallas_call x14, Pallas kernels, call(): pl.pallas_call(kernel, out_shape=outs, grid_spec=pltpu.PrefetchScalarGrid...  29.7 us
    ppermute x1, waiting for transfers between devices, body(): relayed = lax.ppermute(first_back, 'section', before)  20.9 us
    ppermute x1, starting transfers between devices, body(): passed = lax.ppermute(first_out, 'section', onward)  5.58 us
    unnamed x26, local copies, waits for them, and re-layouts  5.16 us
    ppermute x1, starting transfers between devices, spread(): lax.ppermute(two, 'dp', chips(2))  3.28 us
    ppermute x1, starting transfers between devices, spread(): lax.ppermute(three, 'dp', chips(3))  3.01 us
  transfers between devices with their start and end apart: 21, of which 9 were waited for; matrix products, arithmetic and copies ran while one was open for 0% of the time, Pallas kernels for 19%

profile of v11, /device:TPU:30, one launch (start us, length us, event | category | flops | bytes accessed | tf_op | source)
XLA Modules:
  0.0 139.5 jit_solution(3742947447928131426)
XLA Ops:
  0.6 3.3 %collective-permute-start = (bf16[512,512]{1,0:T(8,128)(2,1)}, bf16[512,512]{1,0:T(8,128)(2,1)S(1)}, u32[]{:S(2)}, u32[]{:S(2)}) collective-permute-start(bf16[512,512]{1,0:T(8,128)(2,1)} %bitcast.34), channel_id=1, source_target_pairs={{0,2},{1,7},{2,4},{3,1},{4,6},{5,3},{6,0},{7,5},{8,10},{9,15},{10,... | collective-permute-start | bytes 1572872 | tf_op jit(solution)/shard_map/ppermute | solution.py:445
  4.0 3.1 %collective-permute-start.1 = (bf16[512,512]{1,0:T(8,128)(2,1)}, bf16[512,512]{1,0:T(8,128)(2,1)S(1)}, u32[]{:S(2)}, u32[]{:S(2)}) collective-permute-start(bf16[512,512]{1,0:T(8,128)(2,1)} %bitcast.35), channel_id=1, source_target_pairs={{0,6},{1,3},{2,0},{3,5},{4,2},{5,7},{6,4},{7,1},{8,14},{9,11},{10,... | collective-permute-start | bytes 1572872 | tf_op jit(solution)/shard_map/ppermute | solution.py:445
  7.1 1.4 collective-permute-start.8
  8.5 2.8 %collective-permute-start.10 = (bf16[512,512]{1,0:T(8,128)(2,1)}, bf16[512,512]{1,0:T(8,128)(2,1)S(1)}, u32[]{:S(2)}, u32[]{:S(2)}) collective-permute-start(bf16[512,512]{1,0:T(8,128)(2,1)} %bitcast.42), channel_id=1, source_target_pairs={{0,6},{1,3},{2,0},{3,5},{4,2},{5,7},{6,4},{7,1},{8,14},{9,11},{10,... | collective-permute-start | bytes 1572872 | tf_op jit(solution)/shard_map/ppermute | solution.py:445
  11.2 0.0 collective-permute-start.2
  12.5 0.1 stack.51.where
  12.6 1.6 %copy-done = bf16[1,2,128,4096]{3,2,1,0:T(8,128)(2,1)S(1)} copy-done((bf16[1,2,128,4096]{3,2,1,0:T(8,128)(2,1)S(1)}, bf16[1,2,128,4096]{3,2,1,0:T(8,128)(2,1)}, u32[]{:S(2)}) %copy-start) | copy-done | bytes 2097176
  14.2 1.6 %copy-done.2 = bf16[1,4,4096,64]{2,3,1,0:T(8,128)(2,1)S(1)} copy-done((bf16[1,4,4096,64]{2,3,1,0:T(8,128)(2,1)S(1)}, bf16[1,4,4096,64]{2,3,1,0:T(8,128)(2,1)}, u32[]{:S(2)}) %copy-start.2) | copy-done | bytes 2097176
  15.8 1.2 copy-done.4
  17.0 0.7 copy-done.12
  17.8 0.0 copy-start.8
  17.8 0.0 copy-start.9
  17.8 4.1 %shard_map.147 = (bf16[128,4096]{1,0:T(8,128)(2,1)S(1)}, f32[128,128]{1,0:T(8,128)}, bf16[128,256]{1,0:T(8,128)(2,1)S(1)}, bf16[128,4096]{1,0:T(8,128)(2,1)S(1)}...) custom-call(s32[1]{0:T(128)S(6)} %copy.16.ahead, ...), custom_call_target="tpu_custom_call" | custom-call | flops 805306 | bytes 7356 | tf_op jit(solution)/shard_map/pallas_call | solution.py:52
  21.9 11.5 %collective-permute-start.7 = (bf16[512,512]{1,0:T(8,128)(2,1)S(1)}, bf16[512,512]{1,0:T(8,128)(2,1)S(1)}, u32[]{:S(2)}, u32[]{:S(2)}) collective-permute-start(bf16[512,512]{1,0:T(8,128)(2,1)S(1)} %bitcast.43), channel_id=1, source_target_pairs={{0,1},{1,0},{2,3},{3,2},{4,5},{5,4},{6,7},{7,6},{8,9},{9,8},{10,11... | collective-permute-start | bytes 1572872 | tf_op jit(solution)/shard_map/ppermute | solution.py:445
  33.5 7.6 %collective-permute-done.1.refs_4_.refs_12_ = bf16[512,512]{1,0:T(8,128)(2,1)S(1)} collective-permute-done((bf16[512,512]{1,0:T(8,128)(2,1)}, bf16[512,512]{1,0:T(8,128)(2,1)S(1)}, u32[]{:S(2)}, u32[]{:S(2)}) %collective-permute-start.1) | collective-permute-done | bytes 524320 | tf_op jit(solution)/shard_map/ppermute | solution.py:445
  41.1 3.2 %collective-permute-start.5 = (bf16[512,512]{1,0:T(8,128)(2,1)S(1)}, bf16[512,512]{1,0:T(8,128)(2,1)S(1)}, u32[]{:S(2)}, u32[]{:S(2)}) collective-permute-start(bf16[512,512]{1,0:T(8,128)(2,1)S(1)} %collective-permute-done.refs_2_.refs_10_), channel_id=1, source_target_pairs={{0,2},{1,7},{2,4},{3,1},{4,6},{5,3},{6,0},{7,5},{8,10},{9,15},{10,... | collective-permute-start | bytes 1572872 | tf_op jit(solution)/shard_map/ppermute | solution.py:445
  44.3 5.0 %collective-permute-start.3 = (bf16[512,512]{1,0:T(8,128)(2,1)S(1)}, bf16[512,512]{1,0:T(8,128)(2,1)S(1)}, u32[]{:S(2)}, u32[]{:S(2)}) collective-permute-start(bf16[512,512]{1,0:T(8,128)(2,1)S(1)} %collective-permute-done.refs_2_.refs_10_), channel_id=1, source_target_pairs={{0,1},{1,0},{2,3},{3,2},{4,5},{5,4},{6,7},{7,6},{8,9},{9,8},{10,11... | collective-permute-start | bytes 1572872 | tf_op jit(solution)/shard_map/ppermute | solution.py:445
  49.3 3.0 %collective-permute-done.10.refs_12_.refs_4_ = bf16[512,512]{1,0:T(8,128)(2,1)S(1)} collective-permute-done((bf16[512,512]{1,0:T(8,128)(2,1)}, bf16[512,512]{1,0:T(8,128)(2,1)S(1)}, u32[]{:S(2)}, u32[]{:S(2)}) %collective-permute-start.10) | collective-permute-done | bytes 524320 | tf_op jit(solution)/shard_map/ppermute | solution.py:445
  52.3 0.5 collective-permute-start.9
  52.9 0.1 collective-permute-start.11
  53.0 13.6 %collective-permute-done.5.refs_6_.refs_14_ = bf16[512,512]{1,0:T(8,128)(2,1)S(1)} collective-permute-done((bf16[512,512]{1,0:T(8,128)(2,1)S(1)}, bf16[512,512]{1,0:T(8,128)(2,1)S(1)}, u32[]{:S(2)}, u32[]{:S(2)}) %collective-permute-start.5) | collective-permute-done | bytes 524320 | tf_op jit(solution)/shard_map/ppermute | solution.py:445
  66.6 0.3 collective-permute-start.12
  66.9 1.6 %collective-permute-done.6.refs_7_.refs_15_ = bf16[512,512]{1,0:T(8,128)(2,1)S(1)} collective-permute-done((bf16[512,512]{1,0:T(8,128)(2,1)S(1)}, bf16[512,512]{1,0:T(8,128)(2,1)S(1)}, u32[]{:S(2)}, u32[]{:S(2)}) %collective-permute-start.6) | collective-permute-done | bytes 524320 | tf_op jit(solution)/shard_map/ppermute | solution.py:445
  68.5 4.7 %shard_map.148 = (bf16[128,512]{1,0:T(8,128)(2,1)S(1)}, bf16[128,256]{1,0:T(8,128)(2,1)S(1)}, f32[6,128,512]{2,1,0:T(8,128)S(1)}, f32[128,128]{1,0:T(8,128)S(1)}, f32[128,512]{1,0:T(8,128)S(1)}) custom-call(s32[1]{0:T(128)S(6)} %copy.17.back, s32[10]{0:T(128)S(1)} %stack.51.where, bf16[128,4096]{1,0:T(8,128)(2,1)S(1)} %bitcast.52, ...), custom_call_target="tpu_custom_call" | custom-call | flops 1610612 | bytes 13975 | tf_op jit(solution)/shard_map/pallas_call | solution.py:52
  73.2 0.9 shard_map.150
  74.1 0.2 collective-permute-start.13
  74.3 0.9 shard_map.149.mine
  75.2 0.6 collective-permute-done.13.other
  75.9 0.1 shard_map.151.first
  76.0 5.2 %collective-permute-done.12.far.refs_6_ = bf16[512,512]{1,0:T(8,128)(2,1)S(1)} collective-permute-done((bf16[512,512]{1,0:T(8,128)(2,1)S(1)}, bf16[512,512]{1,0:T(8,128)(2,1)S(1)}, u32[]{:S(2)}, u32[]{:S(2)}) %collective-permute-start.12) | collective-permute-done | bytes 524320 | tf_op jit(solution)/shard_map/ppermute | solution.py:445
  81.1 1.9 %collective-permute-done.14.far_other.refs_7_ = bf16[512,512]{1,0:T(8,128)(2,1)S(1)} collective-permute-done((bf16[512,512]{1,0:T(8,128)(2,1)S(1)}, bf16[512,512]{1,0:T(8,128)(2,1)S(1)}, u32[]{:S(2)}, u32[]{:S(2)}) %collective-permute-start.14) | collective-permute-done | bytes 524320 | tf_op jit(solution)/shard_map/ppermute | solution.py:445
  83.0 1.8 %shard_map.152 = bf16[128,4224]{1,0:T(8,128)(2,1)S(1)} custom-call(s32[1]{0:T(128)S(6)} %copy.17.back, s32[10]{0:T(128)S(1)} %stack.51.where, f32[6,128,512]{2,1,0:T(8,128)S(1)} %get-tuple-element.44.kept, f32[128,128]{1,0:T(8,128)S(1)} %get-tuple-element.45.inner, bf16[128,512]{1,0:T(8,128)(2,1)S(1)} %get-tuple-element.46.d_values.values, ...), custom_call_target="tpu_custom_call" | custom-call | flops 268435 | bytes 8208 | tf_op jit(solution)/shard_map/pallas_call | solution.py:52
  84.8 2.7 %collective-permute-start.16 = (bf16[128,4224]{1,0:T(8,128)(2,1)S(1)}, bf16[128,4224]{1,0:T(8,128)(2,1)S(1)}, u32[]{:S(2)}, u32[]{:S(2)}) collective-permute-start(bf16[128,4224]{1,0:T(8,128)(2,1)S(1)} %shard_map.152), channel_id=1, source_target_pairs={{8,0},{16,8},{24,16},{32,24},{40,32},{48,40},{56,48},{64,56},{72,6... | collective-permute-start | bytes 3244040 | tf_op jit(solution)/shard_map/ppermute | solution.py:508
  87.5 1.6 %shard_map.153.out = bf16[128,4224]{1,0:T(8,128)(2,1)S(1)} custom-call(s32[1]{0:T(128)S(6)} %copy.16.ahead, s32[10]{0:T(128)S(1)} %stack.51.where, f32[128,512]{1,0:T(8,128)S(1)} %get-tuple-element.51.share, bf16[128,4096]{1,0:T(8,128)(2,1)S(1)} %get-tuple-element.39.normed, bf16[128,256]{1,0:T(8,128)(2,1)S(1)} %get-tuple-element.52.low, ...), custom_call_target="tpu_custom_call" | custom-call | flops 536870 | bytes 7929 | tf_op jit(solution)/shard_map/pallas_call | solution.py:52
  89.1 5.6 %collective-permute-start.15 = (bf16[128,4224]{1,0:T(8,128)(2,1)S(1)}, bf16[128,4224]{1,0:T(8,128)(2,1)S(1)}, u32[]{:S(2)}, u32[]{:S(2)}) collective-permute-start(bf16[128,4224]{1,0:T(8,128)(2,1)S(1)} %shard_map.153.out), channel_id=1, source_target_pairs={{0,8},{8,16},{16,24},{24,32},{32,40},{40,48},{48,56},{56,64},{64,7... | collective-permute-start | bytes 3244040 | tf_op jit(solution)/shard_map/ppermute | solution.py:511
  94.7 1.3 shard_map.155.sums
  95.9 20.9 %collective-permute-done.16.relayed = bf16[128,4224]{1,0:T(8,128)(2,1)S(1)} collective-permute-done((bf16[128,4224]{1,0:T(8,128)(2,1)S(1)}, bf16[128,4224]{1,0:T(8,128)(2,1)S(1)}, u32[]{:S(2)}, u32[]{:S(2)}) %collective-permute-start.16) | collective-permute-done | bytes 1081376 | tf_op jit(solution)/shard_map/ppermute | solution.py:508
  116.8 2.6 %shard_map.156 = (bf16[128,4096]{1,0:T(8,128)(2,1)S(1)}, bf16[128,512]{1,0:T(8,128)(2,1)S(1)}, bf16[128,256]{1,0:T(8,128)(2,1)S(1)}, bf16[128,256]{1,0:T(8,128)(2,1)S(1)}, bf16[4,64,640]{2,1,0:T(8,128)(2,1)S(1)}) custom-call(s32[1]{0:T(128)S(6)} %copy.16.ahead, s32[10]{0:T(128)S(1)} %stack.51.where, bf16[128,4224]{1,0:T(8,128)(2,1)S(1)} %collective-permute-done.16.relayed, ...), custom_call_target="tpu_custom_call" | custom-call | flops 603979 | bytes 8781 | tf_op jit(solution)/shard_map/pallas_call | solution.py:52
  119.4 0.1 collective-permute-start.17
  119.5 0.9 shard_map.158.mine
  120.4 0.7 collective-permute-done.17.other
  121.1 0.7 shard_map.159
  121.8 3.3 %collective-permute-start.18 = (bf16[64,1152]{1,0:T(8,128)(2,1)S(1)}, bf16[64,1152]{1,0:T(8,128)(2,1)S(1)}, u32[]{:S(2)}, u32[]{:S(2)}) collective-permute-start(bf16[64,1152]{1,0:T(8,128)(2,1)S(1)} %get-tuple-element.67), channel_id=1, source_target_pairs={{0,4},{1,5},{2,6},{3,7},{4,0},{5,1},{6,2},{7,3},{8,12},{9,13},{10,... | collective-permute-start | bytes 442376 | tf_op jit(solution)/shard_map/ppermute | solution.py:401
  125.1 1.1 collective-permute-start.19
  126.3 3.0 %collective-permute-start.20 = (bf16[64,1152]{1,0:T(8,128)(2,1)S(1)}, bf16[64,1152]{1,0:T(8,128)(2,1)S(1)}, u32[]{:S(2)}, u32[]{:S(2)}) collective-permute-start(bf16[64,1152]{1,0:T(8,128)(2,1)S(1)} %get-tuple-element.69), channel_id=1, source_target_pairs={{0,6},{1,7},{2,0},{3,1},{4,2},{5,3},{6,4},{7,5},{8,14},{9,15},{10,... | collective-permute-start | bytes 442376 | tf_op jit(solution)/shard_map/ppermute | solution.py:403
  129.3 3.5 %shard_map.157 = bf16[128,4096]{1,0:T(8,128)(2,1)} custom-call(s32[10]{0:T(128)S(1)} %stack.51.where, f32[128,512]{1,0:T(8,128)S(1)} %shard_map.155.sums, bf16[128,256]{1,0:T(8,128)(2,1)S(1)} %get-tuple-element.56.low, bf16[128,4096]{1,0:T(8,128)(2,1)S(1)} %get-tuple-element.59.grad, bf16[128,4096]{1,0:T(8,128)(2,1)S(1)} %bitcast.33, ...), custom_call_target="tpu_custom_call" | custom-call | flops 603979 | bytes 11091 | tf_op jit(solution)/shard_map/pallas_call | solution.py:52
  132.8 5.1 %shard_map.154 = bf16[128,4096]{1,0:T(8,128)(2,1)} custom-call(s32[10]{0:T(128)S(1)} %stack.51.where, bf16[128,4096]{1,0:T(8,128)(2,1)S(1)} %copy-done.11, bf16[128,4224]{1,0:T(8,128)(2,1)S(1)} %collective-permute-done.15.passed, f32[1,4096]{1,0:T(1,128)S(1)} %copy-done.12, bf16[256,4096]{1,0:T(8,128)(2,1)S(1)} %bitcast.30, bf16[256,512]{1,0:T(8,128)(2,1)S(1)} %bitcast.51, ...), custom_call_target="tpu_custom_call" | custom-call | flops 1073741 | bytes 12894 | tf_op jit(solution)/shard_map/pallas_call | solution.py:52
  137.9 1.5 %shard_map.160 = (f32[4,64,512]{2,1,0:T(8,128)}, f32[4,64,64]{2,1,0:T(8,128)}) custom-call(s32[1]{0:T(128)S(6)} %copy.16.ahead, s32[1]{0:T(128)S(6)} %copy.17.back, s32[10]{0:T(128)S(1)} %stack.51.where, bf16[128,4224]{1,0:T(8,128)(2,1)S(1)} %collective-permute-done.16.relayed, bf16[64,1152]{1,0:T(8,128)(2,1)S(1)} %get-tuple-element.66.refs_0_, ...), custom_call_target="tpu_custom_call" | custom-call | bytes 1671 | tf_op jit(solution)/shard_map/pallas_call | solution.py:52
  (35 shorter events, 0.1 us)
Async XLA Ops:
  0.6 21.3 %collective-permute-start = (bf16[512,512]{1,0:T(8,128)(2,1)}, bf16[512,512]{1,0:T(8,128)(2,1)S(1)}, u32[]{:S(2)}, u32[]{:S(2)}) collective-permute-start(bf16[512,512]{1,0:T(8,128)(2,1)} %bitcast.34), channel_id=1, source_target_pairs={{0,2},{1,7},{2,4},{3,1},{4,6},{5,3},{6,0},{7,5},{8,10},{9,15},{10,... | collective-permute-start | bytes 1572872 | tf_op jit(solution)/shard_map/ppermute | solution.py:445
  4.0 37.1 %collective-permute-start.1 = (bf16[512,512]{1,0:T(8,128)(2,1)}, bf16[512,512]{1,0:T(8,128)(2,1)S(1)}, u32[]{:S(2)}, u32[]{:S(2)}) collective-permute-start(bf16[512,512]{1,0:T(8,128)(2,1)} %bitcast.35), channel_id=1, source_target_pairs={{0,6},{1,3},{2,0},{3,5},{4,2},{5,7},{6,4},{7,1},{8,14},{9,11},{10,... | collective-permute-start | bytes 1572872 | tf_op jit(solution)/shard_map/ppermute | solution.py:445
  7.1 37.2 %collective-permute-start.8 = (bf16[512,512]{1,0:T(8,128)(2,1)}, bf16[512,512]{1,0:T(8,128)(2,1)S(1)}, u32[]{:S(2)}, u32[]{:S(2)}) collective-permute-start(bf16[512,512]{1,0:T(8,128)(2,1)} %bitcast.41), channel_id=1, source_target_pairs={{0,2},{1,7},{2,4},{3,1},{4,6},{5,3},{6,0},{7,5},{8,10},{9,15},{10,... | collective-permute-start | bytes 1572872 | tf_op jit(solution)/shard_map/ppermute | solution.py:445
  8.5 43.9 %collective-permute-start.10 = (bf16[512,512]{1,0:T(8,128)(2,1)}, bf16[512,512]{1,0:T(8,128)(2,1)S(1)}, u32[]{:S(2)}, u32[]{:S(2)}) collective-permute-start(bf16[512,512]{1,0:T(8,128)(2,1)} %bitcast.42), channel_id=1, source_target_pairs={{0,6},{1,3},{2,0},{3,5},{4,2},{5,7},{6,4},{7,1},{8,14},{9,11},{10,... | collective-permute-start | bytes 1572872 | tf_op jit(solution)/shard_map/ppermute | solution.py:445
  11.2 41.1 %collective-permute-start.2 = (bf16[512,512]{1,0:T(8,128)(2,1)}, bf16[512,512]{1,0:T(8,128)(2,1)S(1)}, u32[]{:S(2)}, u32[]{:S(2)}) collective-permute-start(bf16[512,512]{1,0:T(8,128)(2,1)} %bitcast.36), channel_id=1, source_target_pairs={{0,1},{1,0},{2,3},{3,2},{4,5},{5,4},{6,7},{7,6},{8,9},{9,8},{10,11... | collective-permute-start | bytes 1572872 | tf_op jit(solution)/shard_map/ppermute | solution.py:445
  12.6 1.6 %copy-start = (bf16[1,2,128,4096]{3,2,1,0:T(8,128)(2,1)S(1)}, bf16[1,2,128,4096]{3,2,1,0:T(8,128)(2,1)}, u32[]{:S(2)}) copy-start(bf16[1,2,128,4096]{3,2,1,0:T(8,128)(2,1)} %rows_s.3) | copy-start | bytes 6291460
  14.2 1.6 %copy-start.2 = (bf16[1,4,4096,64]{2,3,1,0:T(8,128)(2,1)S(1)}, bf16[1,4,4096,64]{2,3,1,0:T(8,128)(2,1)}, u32[]{:S(2)}) copy-start(bf16[1,4,4096,64]{2,3,1,0:T(8,128)(2,1)} %param.22) | copy-start | bytes 6291460
  15.8 1.2 copy-start.4
  17.0 0.7 copy-start.12
  17.8 4.2 %copy-start.7 = (bf16[1,512,512]{2,1,0:T(8,128)(2,1)S(1)}, bf16[1,512,512]{2,1,0:T(8,128)(2,1)}, u32[]{:S(2)}) copy-start(bf16[1,512,512]{2,1,0:T(8,128)(2,1)} %param.19) | copy-start | bytes 1572868
  17.8 50.7 %copy-start.1 = (bf16[1,2,128,4096]{3,2,1,0:T(8,128)(2,1)S(1)}, bf16[1,2,128,4096]{3,2,1,0:T(8,128)(2,1)}, u32[]{:S(2)}) copy-start(bf16[1,2,128,4096]{3,2,1,0:T(8,128)(2,1)} %rows_s.3) | copy-start | bytes 6291460
  17.8 50.7 %copy-start.3 = (bf16[1,4,4096,64]{2,3,1,0:T(8,128)(2,1)S(1)}, bf16[1,4,4096,64]{2,3,1,0:T(8,128)(2,1)}, u32[]{:S(2)}) copy-start(bf16[1,4,4096,64]{2,3,1,0:T(8,128)(2,1)} %param.22) | copy-start | bytes 6291460
  17.8 50.7 %copy-start.6 = (bf16[1,512,512]{2,1,0:T(8,128)(2,1)S(1)}, bf16[1,512,512]{2,1,0:T(8,128)(2,1)}, u32[]{:S(2)}) copy-start(bf16[1,512,512]{2,1,0:T(8,128)(2,1)} %param.20) | copy-start | bytes 1572868
  17.8 50.7 %copy-start.8 = (bf16[1,4,64,512]{3,2,1,0:T(8,128)(2,1)S(1)}, bf16[1,4,64,512]{3,2,1,0:T(8,128)(2,1)}, u32[]{:S(2)}) copy-start(bf16[1,4,64,512]{3,2,1,0:T(8,128)(2,1)} %param.23) | copy-start | bytes 786436
  17.8 50.7 %copy-start.9 = (bf16[1,128,4096]{2,1,0:T(8,128)(2,1)S(1)}, bf16[1,128,4096]{2,1,0:T(8,128)(2,1)}, u32[]{:S(2)}) copy-start(bf16[1,128,4096]{2,1,0:T(8,128)(2,1)} %param.13) | copy-start | bytes 3145732
  21.9 30.9 %collective-permute-start.7 = (bf16[512,512]{1,0:T(8,128)(2,1)S(1)}, bf16[512,512]{1,0:T(8,128)(2,1)S(1)}, u32[]{:S(2)}, u32[]{:S(2)}) collective-permute-start(bf16[512,512]{1,0:T(8,128)(2,1)S(1)} %bitcast.43), channel_id=1, source_target_pairs={{0,1},{1,0},{2,3},{3,2},{4,5},{5,4},{6,7},{7,6},{8,9},{9,8},{10,11... | collective-permute-start | bytes 1572872 | tf_op jit(solution)/shard_map/ppermute | solution.py:445
  41.1 25.5 %collective-permute-start.5 = (bf16[512,512]{1,0:T(8,128)(2,1)S(1)}, bf16[512,512]{1,0:T(8,128)(2,1)S(1)}, u32[]{:S(2)}, u32[]{:S(2)}) collective-permute-start(bf16[512,512]{1,0:T(8,128)(2,1)S(1)} %collective-permute-done.refs_2_.refs_10_), channel_id=1, source_target_pairs={{0,2},{1,7},{2,4},{3,1},{4,6},{5,3},{6,0},{7,5},{8,10},{9,15},{10,... | collective-permute-start | bytes 1572872 | tf_op jit(solution)/shard_map/ppermute | solution.py:445
  44.3 22.3 %collective-permute-start.3 = (bf16[512,512]{1,0:T(8,128)(2,1)S(1)}, bf16[512,512]{1,0:T(8,128)(2,1)S(1)}, u32[]{:S(2)}, u32[]{:S(2)}) collective-permute-start(bf16[512,512]{1,0:T(8,128)(2,1)S(1)} %collective-permute-done.refs_2_.refs_10_), channel_id=1, source_target_pairs={{0,1},{1,0},{2,3},{3,2},{4,5},{5,4},{6,7},{7,6},{8,9},{9,8},{10,11... | collective-permute-start | bytes 1572872 | tf_op jit(solution)/shard_map/ppermute | solution.py:445
  52.3 14.5 %collective-permute-start.4 = (bf16[512,512]{1,0:T(8,128)(2,1)S(1)}, bf16[512,512]{1,0:T(8,128)(2,1)S(1)}, u32[]{:S(2)}, u32[]{:S(2)}) collective-permute-start(bf16[512,512]{1,0:T(8,128)(2,1)S(1)} %collective-permute-done.1.refs_4_.refs_12_), channel_id=1, source_target_pairs={{0,1},{1,0},{2,3},{3,2},{4,5},{5,4},{6,7},{7,6},{8,9},{9,8},{10,11... | collective-permute-start | bytes 1572872 | tf_op jit(solution)/shard_map/ppermute | solution.py:445
  52.3 14.5 %collective-permute-start.9 = (bf16[512,512]{1,0:T(8,128)(2,1)S(1)}, bf16[512,512]{1,0:T(8,128)(2,1)S(1)}, u32[]{:S(2)}, u32[]{:S(2)}) collective-permute-start(bf16[512,512]{1,0:T(8,128)(2,1)S(1)} %collective-permute-done.8.refs_10_.refs_2_), channel_id=1, source_target_pairs={{0,1},{1,0},{2,3},{3,2},{4,5},{5,4},{6,7},{7,6},{8,9},{9,8},{10,11... | collective-permute-start | bytes 1572872 | tf_op jit(solution)/shard_map/ppermute | solution.py:445
  52.9 14.0 %collective-permute-start.11 = (bf16[512,512]{1,0:T(8,128)(2,1)S(1)}, bf16[512,512]{1,0:T(8,128)(2,1)S(1)}, u32[]{:S(2)}, u32[]{:S(2)}) collective-permute-start(bf16[512,512]{1,0:T(8,128)(2,1)S(1)} %collective-permute-done.10.refs_12_.refs_4_), channel_id=1, source_target_pairs={{0,1},{1,0},{2,3},{3,2},{4,5},{5,4},{6,7},{7,6},{8,9},{9,8},{10,11... | collective-permute-start | bytes 1572872 | tf_op jit(solution)/shard_map/ppermute | solution.py:445
  66.6 1.9 %collective-permute-start.6 = (bf16[512,512]{1,0:T(8,128)(2,1)S(1)}, bf16[512,512]{1,0:T(8,128)(2,1)S(1)}, u32[]{:S(2)}, u32[]{:S(2)}) collective-permute-start(bf16[512,512]{1,0:T(8,128)(2,1)S(1)} %collective-permute-done.5.refs_6_.refs_14_), channel_id=1, source_target_pairs={{0,1},{1,0},{2,3},{3,2},{4,5},{5,4},{6,7},{7,6},{8,9},{9,8},{10,11... | collective-permute-start | bytes 1572872 | tf_op jit(solution)/shard_map/ppermute | solution.py:445
  66.6 14.6 %collective-permute-start.12 = (bf16[512,512]{1,0:T(8,128)(2,1)S(1)}, bf16[512,512]{1,0:T(8,128)(2,1)S(1)}, u32[]{:S(2)}, u32[]{:S(2)}) collective-permute-start(bf16[512,512]{1,0:T(8,128)(2,1)S(1)} %collective-permute-done.8.refs_10_.refs_2_), channel_id=1, source_target_pairs={{0,2},{1,7},{2,4},{3,1},{4,6},{5,3},{6,0},{7,5},{8,10},{9,15},{10,... | collective-permute-start | bytes 1572872 | tf_op jit(solution)/shard_map/ppermute | solution.py:445
  74.1 1.7 %collective-permute-start.13 = (bf16[4,64,640]{2,1,0:T(8,128)(2,1)S(1)}, bf16[4,64,640]{2,1,0:T(8,128)(2,1)S(1)}, u32[]{:S(2)}, u32[]{:S(2)}) collective-permute-start(bf16[4,64,640]{2,1,0:T(8,128)(2,1)S(1)} %shard_map.150), channel_id=1, source_target_pairs={{0,1},{1,0},{2,3},{3,2},{4,5},{5,4},{6,7},{7,6},{8,9},{9,8},{10,11... | collective-permute-start | bytes 983048 | tf_op jit(solution)/shard_map/ppermute | solution.py:445
  81.1 1.9 %collective-permute-start.14 = (bf16[512,512]{1,0:T(8,128)(2,1)S(1)}, bf16[512,512]{1,0:T(8,128)(2,1)S(1)}, u32[]{:S(2)}, u32[]{:S(2)}) collective-permute-start(bf16[512,512]{1,0:T(8,128)(2,1)S(1)} %collective-permute-done.12.far.refs_6_), channel_id=1, source_target_pairs={{0,1},{1,0},{2,3},{3,2},{4,5},{5,4},{6,7},{7,6},{8,9},{9,8},{10,11... | collective-permute-start | bytes 1572872 | tf_op jit(solution)/shard_map/ppermute | solution.py:445
  83.0 4.4 %copy-start.5 = (bf16[1,128,4096]{2,1,0:T(8,128)(2,1)S(1)}, bf16[1,128,4096]{2,1,0:T(8,128)(2,1)}, u32[]{:S(2)}) copy-start(bf16[1,128,4096]{2,1,0:T(8,128)(2,1)} %param.12) | copy-start | bytes 3145732
  84.8 32.0 %collective-permute-start.16 = (bf16[128,4224]{1,0:T(8,128)(2,1)S(1)}, bf16[128,4224]{1,0:T(8,128)(2,1)S(1)}, u32[]{:S(2)}, u32[]{:S(2)}) collective-permute-start(bf16[128,4224]{1,0:T(8,128)(2,1)S(1)} %shard_map.152), channel_id=1, source_target_pairs={{8,0},{16,8},{24,16},{32,24},{40,32},{48,40},{56,48},{64,56},{72,6... | collective-permute-start | bytes 3244040 | tf_op jit(solution)/shard_map/ppermute | solution.py:508
  89.1 43.7 %collective-permute-start.15 = (bf16[128,4224]{1,0:T(8,128)(2,1)S(1)}, bf16[128,4224]{1,0:T(8,128)(2,1)S(1)}, u32[]{:S(2)}, u32[]{:S(2)}) collective-permute-start(bf16[128,4224]{1,0:T(8,128)(2,1)S(1)} %shard_map.153.out), channel_id=1, source_target_pairs={{0,8},{8,16},{16,24},{24,32},{32,40},{40,48},{48,56},{56,64},{64,7... | collective-permute-start | bytes 3244040 | tf_op jit(solution)/shard_map/ppermute | solution.py:511
  94.7 22.2 %copy-start.10 = (bf16[128,4096]{1,0:T(8,128)(2,1)S(1)}, bf16[128,4096]{1,0:T(8,128)(2,1)}, u32[]{:S(2)}) copy-start(bf16[128,4096]{1,0:T(8,128)(2,1)} %target.1) | copy-start | bytes 3145732
  119.4 1.7 %collective-permute-start.17 = (bf16[4,64,640]{2,1,0:T(8,128)(2,1)S(1)}, bf16[4,64,640]{2,1,0:T(8,128)(2,1)S(1)}, u32[]{:S(2)}, u32[]{:S(2)}) collective-permute-start(bf16[4,64,640]{2,1,0:T(8,128)(2,1)S(1)} %get-tuple-element.65), channel_id=1, source_target_pairs={{0,1},{1,0},{2,3},{3,2},{4,5},{5,4},{6,7},{7,6},{8,9},{9,8},{10,11... | collective-permute-start | bytes 983048 | tf_op jit(solution)/shard_map/ppermute | solution.py:445
  121.8 16.1 %collective-permute-start.18 = (bf16[64,1152]{1,0:T(8,128)(2,1)S(1)}, bf16[64,1152]{1,0:T(8,128)(2,1)S(1)}, u32[]{:S(2)}, u32[]{:S(2)}) collective-permute-start(bf16[64,1152]{1,0:T(8,128)(2,1)S(1)} %get-tuple-element.67), channel_id=1, source_target_pairs={{0,4},{1,5},{2,6},{3,7},{4,0},{5,1},{6,2},{7,3},{8,12},{9,13},{10,... | collective-permute-start | bytes 442376 | tf_op jit(solution)/shard_map/ppermute | solution.py:401
  125.1 12.8 %collective-permute-start.19 = (bf16[64,1152]{1,0:T(8,128)(2,1)S(1)}, bf16[64,1152]{1,0:T(8,128)(2,1)S(1)}, u32[]{:S(2)}, u32[]{:S(2)}) collective-permute-start(bf16[64,1152]{1,0:T(8,128)(2,1)S(1)} %get-tuple-element.68), channel_id=1, source_target_pairs={{0,2},{1,3},{2,4},{3,5},{4,6},{5,7},{6,0},{7,1},{8,10},{9,11},{10,... | collective-permute-start | bytes 442376 | tf_op jit(solution)/shard_map/ppermute | solution.py:402
  126.3 11.7 %collective-permute-start.20 = (bf16[64,1152]{1,0:T(8,128)(2,1)S(1)}, bf16[64,1152]{1,0:T(8,128)(2,1)S(1)}, u32[]{:S(2)}, u32[]{:S(2)}) collective-permute-start(bf16[64,1152]{1,0:T(8,128)(2,1)S(1)} %get-tuple-element.69), channel_id=1, source_target_pairs={{0,6},{1,7},{2,0},{3,1},{4,2},{5,3},{6,4},{7,5},{8,14},{9,15},{10,... | collective-permute-start | bytes 442376 | tf_op jit(solution)/shard_map/ppermute | solution.py:403
  129.3 3.6 %copy-start.11 = (bf16[128,4096]{1,0:T(8,128)(2,1)S(1)}, bf16[128,4096]{1,0:T(8,128)(2,1)}, u32[]{:S(2)}) copy-start(bf16[128,4096]{1,0:T(8,128)(2,1)} %fresh.1) | copy-start | bytes 3145732
